TPU v7x, 32 devices: a whole 2x2x4 slice. The times are simulated.
32 devices in a mesh: grp: 2 (over y), ctx: 4 (over x, core), exp: 4 (over z).
Axes of the slice: x: 2, y: 2, z: 4, core: 2. Of those that a mesh axis runs over, the one named last changes fastest.
Arguments:
- queries: bfloat16 [8, 512, 4096], P(('grp', 'exp'), 'ctx'), parts along dimension 0, may hold values from -150 to 150
- keys: bfloat16 [8, 512, 256], P(('grp', 'exp'), 'ctx'), parts along dimension 0, may hold values from -5 to 5
- values: bfloat16 [8, 512, 256], P(('grp', 'exp'), 'ctx'), parts along dimension 0, may hold values from -6 to 6
- tree_parents: int32 [8, 4], P(('grp', 'exp')), parts along dimension 0, may hold values from 0 to 3, as said below
- routes: int32 [8, 512, 1], P(('grp', 'exp'), 'ctx'), parts along dimension 0, may hold values from 0 to 3; in each aligned block of 128 rows (0 to 127, 128 to 255, ..., all dimensions but the last counted through in order) at most 40 rows name the same one
- route_weight: float32 [8, 512, 1], P(('grp', 'exp'), 'ctx'), parts along dimension 0, may hold values from 0.3 to 1.5
- norm_gain: float32 [4096], replicated, may hold values from 0.5 to 1.5
- expert_in: bfloat16 [4, 4096, 2, 768], P('exp', 'ctx'), may hold values from -0.09375 to 0.09375
- expert_out: bfloat16 [4, 768, 4096], P('exp', None, 'ctx'), may hold values from -0.21875 to 0.21875
Outputs:
- layer_out: bfloat16 [8, 512, 4096], P(('grp', 'exp'), 'ctx'), parts along dimension 0
There are 2 independent parts, one for each index of `grp`. A program takes and returns all parts, laid end to end along the dimension named above; an argument that names none is the same for every part. Nothing has to cross between parts.
Inputs may be any that keep to these rules, and one draw needn't show every extreme that they name: `routes`: in each aligned block of 128 rows (the rows of one device), no expert is named by more than 40 rows, a bound that some block reaches. `tree_parents`: the parent of block b is a block of the same sequence at or before b; a block that is its own parent begins a new tree. The last block of the first sequence begins a tree.
All inputs are finite; a program needn't handle non-finite values.
Results may differ from a plain program's by a relative error of at most 0.022.
Values may be sent and summed in bfloat16 or wider, within the bound.
No kernel may reach another device: no remote copies, remote signals or barrier semaphores. Data moves between devices by JAX's collectives and lax.ppermute only.
A program may use at most 64 MiB of HBM per device.

v0:
```python
import math

import jax
import jax.numpy as jnp
from jax import lax
from jax.sharding import PartitionSpec as P

KV_HEADS = 2
HEAD_DIM = 128
TREE_BLOCK = 128


def ancestor_table(parent_ids):
    blocks = parent_ids.shape[0]
    block_ids = jnp.arange(blocks, dtype=jnp.int32)

    def follow(turn_index, held_state):
        current, reach_table = held_state
        current_hot = current[:, None] == block_ids[None, :]
        following = jnp.sum(jnp.where(current_hot, parent_ids[None, :], 0), axis=1)
        reached = (following[:, None] == block_ids[None, :]).astype(jnp.float32)
        return (following, jnp.maximum(reach_table, reached))

    start_table = (block_ids[:, None] == block_ids[None, :]).astype(jnp.float32)
    return lax.fori_loop(0, blocks, follow, (block_ids, start_table))[1]


def body(
    queries, keys, values, tree_parents, routes, route_weight, norm_gain, expert_in, expert_out
):
    tokens = queries.shape[1]
    model_width = queries.shape[2]
    groups = KV_HEADS
    head_size = HEAD_DIM
    per_group = model_width // (groups * head_size)
    blocks = tree_parents.shape[1]
    score_scale = 1.0 / math.sqrt(head_size)
    block_ids = jnp.arange(blocks, dtype=jnp.int32)
    ancestry = ancestor_table(tree_parents[0])
    query_pos = lax.axis_index("ctx") * tokens + jnp.arange(tokens, dtype=jnp.int32)
    query_block = query_pos // TREE_BLOCK
    query_hot = (query_block[:, None] == block_ids[None, :]).astype(jnp.float32)
    query_reach = jnp.dot(query_hot, ancestry, preferred_element_type=jnp.float32)
    query_heads = queries[0].reshape(tokens, groups, per_group, head_size)

    def update(running_state, key_rows, value_rows, allowed):
        running, denominator, weighted = running_state
        scores = (
            jnp.einsum(
                "tgjd,ngd->gjtn",
                query_heads,
                key_rows.reshape(tokens, groups, head_size),
                preferred_element_type=jnp.float32,
            )
            * score_scale
        )
        masked = jnp.where(allowed[None, None], scores, -1e30)
        new_peak = jnp.maximum(running, jnp.max(masked, axis=-1))
        exp_scores = jnp.where(allowed[None, None], jnp.exp(masked - new_peak[..., None]), 0.0)
        factor = jnp.exp(running - new_peak)
        denominator = denominator * factor + jnp.sum(exp_scores, axis=-1)
        value_heads = value_rows.reshape(tokens, groups, head_size).astype(jnp.float32)
        weighted = weighted * factor[..., None] + jnp.einsum(
            "gjtn,ngd->gjtd", exp_scores, value_heads, preferred_element_type=jnp.float32
        )
        return (new_peak, denominator, weighted)

    start_state = (
        jnp.full((groups, per_group, tokens), -1e30, jnp.float32),
        jnp.zeros((groups, per_group, tokens), jnp.float32),
        jnp.zeros((groups, per_group, tokens, head_size), jnp.float32),
    )
    key_part = lax.all_gather(keys[0], "ctx", axis=0, tiled=True)
    value_part = lax.all_gather(values[0], "ctx", axis=0, tiled=True)
    block_count = key_part.shape[0] // tokens

    def one_block(block_step, inner_state):
        offset = block_step * tokens
        key_rows = lax.dynamic_slice_in_dim(key_part, offset, tokens, 0)
        value_rows = lax.dynamic_slice_in_dim(value_part, offset, tokens, 0)
        key_pos = offset + jnp.arange(tokens, dtype=jnp.int32)
        key_block = key_pos // TREE_BLOCK
        key_hot = (key_block[:, None] == block_ids[None, :]).astype(jnp.float32)
        related = jnp.dot(query_reach, key_hot.T, preferred_element_type=jnp.float32) > 0.5
        causal = (query_block[:, None] != key_block[None, :]) | (
            key_pos[None, :] <= query_pos[:, None]
        )
        allowed = related & causal
        return update(inner_state, key_rows, value_rows, allowed)

    running, denominator, weighted = lax.fori_loop(0, block_count, one_block, start_state)
    attended = (
        jnp.transpose(weighted / denominator[..., None], (2, 0, 1, 3))
        .reshape(tokens, model_width)
        .astype(jnp.bfloat16)
    )
    values_f = attended.astype(jnp.float32)
    mean_square = jnp.mean(values_f * values_f, axis=-1, keepdims=True)
    moe_in = (values_f * lax.rsqrt(mean_square + 1e-06) * norm_gain).astype(jnp.bfloat16)
    top_count = routes.shape[2]
    experts = lax.axis_size("exp")
    capacity = max(2, 5 * tokens * top_count // (4 * experts))
    picks = routes[0].reshape(-1)
    expert_ids = jnp.arange(experts, dtype=jnp.int32)
    pick_hot = (picks[:, None] == expert_ids[None, :]).astype(jnp.int32)
    earlier = jnp.cumsum(pick_hot, axis=0) - pick_hot
    rank_in_expert = jnp.sum(earlier * pick_hot, axis=1)
    slot_of_pick = picks * capacity + rank_in_expert
    slot_count = experts * capacity
    slot_ids = jnp.arange(slot_count, dtype=jnp.int32)
    placement = (slot_ids[:, None] == slot_of_pick[None, :]).astype(jnp.bfloat16)
    pick_rows = jnp.repeat(moe_in, top_count, axis=0)
    outgoing = (
        jnp.dot(placement, pick_rows, preferred_element_type=jnp.float32)
        .astype(jnp.bfloat16)
        .reshape(experts, capacity, model_width)
    )
    arrived = lax.all_to_all(outgoing, "exp", split_axis=0, concat_axis=0, tiled=True)
    column_rows = arrived.reshape(slot_count, model_width)
    feature_cols = lax.all_to_all(column_rows, "ctx", split_axis=1, concat_axis=0, tiled=True)
    inner_width = expert_out.shape[1]
    gate_up_weight = expert_in[0].reshape(expert_in.shape[1], 2 * inner_width)
    down_weight = expert_out[0]
    gate_up = lax.psum_scatter(
        jnp.dot(feature_cols, gate_up_weight, preferred_element_type=jnp.float32).astype(
            jnp.bfloat16
        ),
        "ctx",
        scatter_dimension=0,
        tiled=True,
    ).astype(jnp.float32)
    hidden = (jax.nn.silu(gate_up[:, :inner_width]) * gate_up[:, inner_width:]).astype(jnp.bfloat16)
    expert_cols = jnp.dot(
        lax.all_gather(hidden, "ctx", axis=0, tiled=True),
        down_weight,
        preferred_element_type=jnp.float32,
    ).astype(jnp.bfloat16)
    expert_rows = lax.all_to_all(expert_cols, "ctx", split_axis=0, concat_axis=1, tiled=True)
    returned = lax.all_to_all(
        expert_rows.reshape(experts, capacity, model_width),
        "exp",
        split_axis=0,
        concat_axis=0,
        tiled=True,
    )
    pick_out = jnp.einsum(
        "sp,sd->pd",
        placement,
        returned.reshape(slot_count, model_width),
        preferred_element_type=jnp.float32,
    )
    mixed = jnp.sum(
        pick_out.reshape(tokens, top_count, model_width) * route_weight[0][..., None], axis=1
    )
    layer_rows = (values_f + mixed).astype(jnp.bfloat16)
    return layer_rows[None]


def solution(mesh):
    in_specs = (
        P(("grp", "exp"), "ctx", None),
        P(("grp", "exp"), "ctx", None),
        P(("grp", "exp"), "ctx", None),
        P(("grp", "exp"), None),
        P(("grp", "exp"), "ctx", None),
        P(("grp", "exp"), "ctx", None),
        P(),
        P("exp", "ctx", None, None),
        P("exp", None, "ctx"),
    )
    out_specs = P(("grp", "exp"), "ctx", None)
    return jax.shard_map(body, mesh=mesh, in_specs=in_specs, out_specs=out_specs, check_vma=False)
```

profile of v0, /device:TPU:0, one launch (start us, length us, event | category | flops | bytes accessed | tf_op | source)
XLA Modules:
  0.0 233.3 jit_solution(2885587250885024385)
XLA Ops:
  6.6 3.8 %while.36 = (s32[]{:T(128)}, s32[4]{0:T(128)S(1)}, bf16[4,4]{1,0:T(4,128)(2,1)S(1)}, s32[1,4]{1,0:T(1,128)}, s32[]{:T(128)}) while((s32[]{:T(128)}, s32[4]{0:T(128)S(1)}, bf16[4,4]{1,0:T(4,128)(2,1)S(1)}, s32[1,4]{1,0:T(1,128)}, s32[]{:T(128)}) %tuple.84), condition=%wide.region_2.3_spmd.clone.clone, body=%wide.region_0.2_spmd.clone.clone.sunk | while | flops 126 | bytes 221 | solution.py:25
  14.7 7.2 %all-gather.1 = bf16[1,512,256]{1,2,0:T(8,128)(2,1)S(1)} all-gather(bf16[1,128,256]{1,2,0:T(8,128)(2,1)S(1)} %copy.36), channel_id=3, replica_groups=mesh['grp'=2,'ctx'=4,'exp'=4] {'ctx'}, dimensions={1}, use_global_device_ids=true | all-gather | bytes 327680 | tf_op jit(solution)/shard_map/all_gather | solution.py:74
  21.9 5.9 %all-gather = bf16[1,512,256]{1,2,0:T(8,128)(2,1)S(1)} all-gather(bf16[1,128,256]{1,2,0:T(8,128)(2,1)S(1)} %copy.34), channel_id=2, replica_groups=mesh['grp'=2,'ctx'=4,'exp'=4] {'ctx'}, dimensions={1}, use_global_device_ids=true | all-gather | bytes 327680 | tf_op jit(solution)/shard_map/all_gather | solution.py:73
  27.8 2.3 copy.35
  30.1 1.6 copy.37
  31.9 19.0 %while.37 = (s32[]{:T(128)}, f32[2,16,128]{2,1,0:T(8,128)S(1)}, f32[2,16,128]{2,1,0:T(8,128)S(1)}, f32[2,16,128,128]{3,2,1,0:T(8,128)}, bf16[128,4]{0,1:T(4,128)...) while((s32[]{:T(128)}, f32[2,16,128]{2,1,0:T(8,128)S(1)}, ...), condition=%wide.region_6.7_spmd.clone.clone.clone, body=%wide.region_3.6_spmd.clone.clone.clone.sunk | while | flops 276537856 | bytes 29037828 | solution.py:91
  33.8 1.5 fusion.66
  35.3 1.3 copy-done.2
  38.5 1.5 fusion.66
  40.1 1.3 copy-done.2
  43.3 1.5 fusion.66
  44.8 1.3 copy-done.2
  48.0 1.5 fusion.66
  49.6 1.3 copy-done.2
  50.9 2.1 fusion.26
  53.2 1.2 copy.38
  54.5 1.4 copy-done.3
  55.8 1.5 convolution_convert_fusion
  57.3 36.6 %all_to_all.45 = bf16[4,40,4096]{2,1,0:T(8,128)(2,1)S(1)} all-to-all(bf16[4,40,4096]{2,1,0:T(8,128)(2,1)S(1)} %bitcast.93), channel_id=1, replica_groups=mesh['grp'=2,'ctx'=4,'exp'=4] {'exp'}, dimensions={0} | all-to-all | bytes 2621440 | tf_op jit(solution)/shard_map/all_to_all | solution.py:118
  93.9 1.9 all_to_all.33
  95.8 2.8 %copy.39 = bf16[160,4,1024]{2,0,1:T(8,128)(2,1)} copy(bf16[160,4,1024]{2,1,0:T(4,128)(2,1)} %all_to_all.33) | data formatting | bytes 2621440 | tf_op jit(solution)/shard_map/all_to_all | solution.py:120
  98.6 3.5 %all-to-all-start.1 = ((bf16[160,4,1024]{2,0,1:T(8,128)(2,1)}), bf16[160,4,1024]{2,0,1:T(8,128)(2,1)S(1)}, u32[]{:S(2)}, u32[]{:S(2)}) async-start(bf16[160,4,1024]{2,0,1:T(8,128)(2,1)} %copy.39), calls=%async_computation.1 | async-start | bytes 2621440 | tf_op jit(solution)/shard_map/all_to_all | solution.py:120
  102.2 4.1 %copy.49 = bf16[128,8,2,768]{3,1,2,0:T(8,128)(2,1)} copy(bf16[128,8,2,768]{3,2,1,0:T(2,128)(2,1)} %bitcast.96) | data formatting | bytes 6291456
  106.3 13.0 %all-to-all-done.1 = bf16[160,4,1024]{2,0,1:T(8,128)(2,1)S(1)} async-done(((bf16[160,4,1024]{2,0,1:T(8,128)(2,1)}), bf16[160,4,1024]{2,0,1:T(8,128)(2,1)S(1)}, u32[]{:S(2)}, u32[]{:S(2)}) %all-to-all-start.1) | async-done | bytes 1310752 | tf_op jit(solution)/shard_map/all_to_all | solution.py:120
  119.3 5.4 %convolution_convert_fusion.1 = bf16[640,1536]{1,0:T(8,128)(2,1)} fusion(bf16[640,1024]{1,0:T(8,128)(2,1)S(1)} %bitcast.100, bf16[1024,1536]{1,0:T(8,128)(2,1)} %bitcast.97), kind=kOutput, calls=%fused_computation.48 | convolution fusion | flops 2014248960 | bytes 6422528 | tf_op jit(solution)/shard_map/dot_general | solution.py:125
  124.8 29.0 %reduce-scatter.2.cloned.1.call-done = bf16[160,1536]{1,0:T(8,128)(2,1)} async-done(((bf16[640,1536]{1,0:T(8,128)(2,1)}), bf16[160,1536]{1,0:T(8,128)(2,1)}) %reduce-scatter.2.cloned.1.call-update) | async-done | bytes 491536 | tf_op jit(solution)/shard_map/reduce_scatter | solution.py:124
  155.0 9.3 %all_gather.11 = bf16[640,768]{1,0:T(8,128)(2,1)S(1)} all-gather(bf16[160,768]{1,0:T(8,128)(2,1)S(1)} %fusion.33), channel_id=1, replica_groups=mesh['grp'=2,'ctx'=4,'exp'=4] {'ctx'}, dimensions={0}, use_global_device_ids=true | all-gather | bytes 1228800 | tf_op jit(solution)/shard_map/all_gather | solution.py:134
  164.3 1.2 convolution_convert_fusion.2
  165.5 19.9 %all_to_all.46 = bf16[4,160,1024]{2,1,0:T(8,128)(2,1)S(1)} all-to-all(bf16[4,160,1024]{2,1,0:T(8,128)(2,1)S(1)} %bitcast.101), channel_id=1, replica_groups=mesh['grp'=2,'ctx'=4,'exp'=4] {'ctx'}, dimensions={0} | all-to-all | bytes 2621440 | tf_op jit(solution)/shard_map/all_to_all | solution.py:138
  186.4 1.8 reshape.144
  188.2 35.7 %all_to_all.47 = bf16[4,40,4096]{2,1,0:T(8,128)(2,1)S(1)} all-to-all(bf16[4,40,4096]{2,1,0:T(8,128)(2,1)} %reshape.144), channel_id=1, replica_groups=mesh['grp'=2,'ctx'=4,'exp'=4] {'exp'}, dimensions={0} | all-to-all | bytes 2621440 | tf_op jit(solution)/shard_map/all_to_all | solution.py:139
  223.9 2.5 %fusion.25 = bf16[1,128,4096]{2,1,0:T(8,128)(2,1)} fusion(bf16[160,4096]{1,0:T(8,128)(2,1)S(1)} %bitcast.92, f32[16,8,32,128]{3,2,1,0:T(8,128)S(1)} %bitcast.89, f32[128]{0:T(128)S(1)} %bitcast.104, s32[128]{0:T(128)S(1)} %multiply_add_fusion), kind=kOutput, calls=%fused_computation.47 | convolution fusion | flops 169365504 | bytes 4457472 | tf_op jit(solution)/shard_map/sp,sd->pd/dot_general | solution.py:146
  (89 shorter events, 18.2 us)
Async XLA Ops:
  6.5 157.7 %copy-start = (bf16[1,768,1024]{2,1,0:T(8,128)(2,1)S(1)}, bf16[1,768,1024]{2,1,0:T(8,128)(2,1)}, u32[]{:S(2)}) copy-start(bf16[1,768,1024]{2,1,0:T(8,128)(2,1)} %param.21) | copy-start | bytes 4718596
  32.2 1.6 copy-start.1
  35.3 1.4 copy-start.2
  36.9 1.6 copy-start.1
  40.1 1.4 copy-start.2
  41.7 1.6 copy-start.1
  44.8 1.4 copy-start.2
  46.4 1.6 copy-start.1
  49.5 1.4 copy-start.2
  53.2 2.6 %copy-start.5 = (f32[4096]{0:T(1024)S(1)}, f32[4096]{0:T(1024)}, u32[]{:S(2)}) copy-start(f32[4096]{0:T(1024)} %param.19) | copy-start | bytes 49156
  54.5 1.4 copy-start.3
  98.6 20.8 %all-to-all-start.1 = ((bf16[160,4,1024]{2,0,1:T(8,128)(2,1)}), bf16[160,4,1024]{2,0,1:T(8,128)(2,1)S(1)}, u32[]{:S(2)}, u32[]{:S(2)}) async-start(bf16[160,4,1024]{2,0,1:T(8,128)(2,1)} %copy.39), calls=%async_computation.1 | async-start | bytes 2621440 | tf_op jit(solution)/shard_map/all_to_all | solution.py:120
  102.1 51.6 %reduce-scatter.2.cloned.1.call-start = ((), (), s32[]{:S(2)}) async-start(), calls=%async_computation.5 | async-start | bytes 2457600 | tf_op jit(solution)/shard_map/reduce_scatter | solution.py:124
  186.4 37.5 %copy-start.6 = (f32[1,128,1]{1,2,0:T(1,128)S(1)}, f32[1,128,1]{1,2,0:T(1,128)}, u32[]{:S(2)}) copy-start(f32[1,128,1]{1,2,0:T(1,128)} %param.18) | copy-start | bytes 1540
  188.2 35.7 %copy-start.4 = (f32[128,2,16,128]{3,2,1,0:T(8,128)S(1)}, f32[128,2,16,128]{3,2,1,0:T(8,128)}, u32[]{:S(2)}) copy-start(f32[128,2,16,128]{3,2,1,0:T(8,128)} %copy-done.3) | copy-start | bytes 6291460
Sparse Core Ops, SparseCore 0:
  124.9 28.7 reduce-scatter.1
where the time goes:
time: 234 us; the launch traced here: 233 us
  blocking collectives  115 us (49%)
  waiting for transfers between devices  42 us (18%)
  local copies, waits for them, and re-layouts  27.3 us (12%)
  matrix products  19.7 us (8%)
  between operations  13.6 us (6%)
  other arithmetic  12.2 us (5%)
  starting transfers between devices  3.58 us (2%)
    all_to_all x1, blocking collectives, body(): lax.all_to_all(outgoing, 'exp', split_axis=0, concat_axis=0, tiled=True)  36.6 us
    all_to_all x1, blocking collectives, body(): lax.all_to_all(expert_rows.reshape(experts, capacity, model_width), 'exp'...  35.7 us
    reduce_scatter x1, waiting for transfers between devices, body(): lax.psum_scatter(jnp.dot(feature_cols, gate_up_weight, preferred_element_...  29 us
    all_to_all x1, blocking collectives, body(): lax.all_to_all(expert_cols, 'ctx', split_axis=0, concat_axis=1, tiled=True)  19.9 us
    all_to_all x1, waiting for transfers between devices, body(): lax.all_to_all(column_rows, 'ctx', split_axis=1, concat_axis=0, tiled=True)  13 us
    unnamed x15, local copies, waits for them, and re-layouts  11.3 us
    all_gather x1, blocking collectives, body(): lax.all_gather(hidden, 'ctx', axis=0, tiled=True)  9.27 us
    while x24, local copies, waits for them, and re-layouts  7.21 us
  transfers between devices with their start and end apart: 2, of which 2 were waited for; matrix products, arithmetic and copies ran while one was open for 2% of the time, Pallas kernels for 0%

commit v1 on v0

v1 whole, which is shorter than its diff:
```python
import functools
import math

import jax
import jax.numpy as jnp
from jax import lax
from jax.experimental import pallas as pl
from jax.experimental.pallas import tpu as pltpu
from jax.sharding import PartitionSpec as P

KV_HEADS = 2
HEAD_DIM = 128
TREE_BLOCK = 128
NEG = -1e30
VMEM_BYTES = 56 * 1024 * 1024


def params():
    return pltpu.CompilerParams(vmem_limit_bytes=VMEM_BYTES)


def placement_of(route_row, capacity, experts, first, relative):
    tokens = route_row.shape[1]
    if relative:
        route_row = lax.rem(route_row - first + experts, experts)
    rows = max(8, experts)
    expert_ids = lax.broadcasted_iota(jnp.int32, (rows, tokens), 0)
    hot = jnp.where(expert_ids == route_row, 1.0, 0.0)
    before = lax.broadcasted_iota(jnp.int32, (tokens, tokens), 0) < lax.broadcasted_iota(
        jnp.int32, (tokens, tokens), 1
    )
    earlier = jnp.dot(
        hot.astype(jnp.bfloat16),
        jnp.where(before, 1.0, 0.0).astype(jnp.bfloat16),
        preferred_element_type=jnp.float32,
    )
    rank = jnp.sum(earlier * hot, axis=0, keepdims=True).astype(jnp.int32)
    slot = route_row * capacity + rank
    slot_ids = lax.broadcasted_iota(jnp.int32, (experts * capacity, tokens), 0)
    return jnp.where(slot_ids == slot, 1.0, 0.0).astype(jnp.bfloat16)


def attention_kernel(
    n_ctx, experts, capacity, blocks_out, meta, parents, q_ref, route_ref, *refs
):
    kv = refs[: 2 * n_ctx]
    att_ref = refs[2 * n_ctx]
    out_refs = refs[2 * n_ctx + 1 : 2 * n_ctx + 1 + blocks_out]
    tokens = q_ref.shape[0]
    heads = q_ref.shape[1] // HEAD_DIM
    me = meta[1]
    reached = [jnp.int32(0)] * n_ctx
    current = me
    for _ in range(n_ctx):
        current = parents[current]
        for j in range(1, n_ctx):
            reached[j] = jnp.where(current == (me ^ j), jnp.int32(1), reached[j])
    causal = lax.broadcasted_iota(jnp.int32, (tokens, tokens), 1) <= lax.broadcasted_iota(
        jnp.int32, (tokens, tokens), 0
    )
    keys_t = jnp.concatenate([kv[2 * j][...] for j in range(n_ctx)], axis=0).T
    ones = jnp.ones((tokens, HEAD_DIM), jnp.bfloat16)
    values = jnp.concatenate(
        [jnp.concatenate([kv[2 * j + 1][...], ones], axis=1) for j in range(n_ctx)], axis=0
    )
    bias = jnp.concatenate(
        [jnp.where(causal, 0.0, NEG)]
        + [
            jnp.broadcast_to(jnp.where(reached[j] == 1, 0.0, NEG), (tokens, tokens))
            for j in range(1, n_ctx)
        ],
        axis=1,
    )
    scale = math.log2(math.e) / math.sqrt(HEAD_DIM)
    for h in range(heads):
        columns = slice(h * HEAD_DIM, (h + 1) * HEAD_DIM)
        scores = jnp.dot(q_ref[:, columns], keys_t, preferred_element_type=jnp.float32)
        scores = scores * scale + bias
        peak = jnp.max(scores, axis=1, keepdims=True)
        weights = jnp.exp2(scores - peak).astype(jnp.bfloat16)
        total = jnp.dot(weights, values, preferred_element_type=jnp.float32)
        att_ref[:, columns] = (total[:, :HEAD_DIM] / total[:, HEAD_DIM:]).astype(jnp.bfloat16)
    place = placement_of(route_ref[...], capacity, experts, meta[2], blocks_out > 1)
    packed = jnp.dot(place, att_ref[...], preferred_element_type=jnp.float32)
    rows = experts * capacity // blocks_out
    for k in range(blocks_out):
        out_refs[k][...] = packed[k * rows : (k + 1) * rows].astype(jnp.bfloat16)


def attention(meta, parents, queries, route_row, kvs, experts, capacity, blocks_out, half):
    n_ctx = len(kvs)
    tokens, width = queries.shape
    half_width = width // KV_HEADS
    rows = experts * capacity // blocks_out

    def pick(scalars):
        return scalars[0] if half == 0 else 1 - scalars[0]

    kv_specs, kv_args = [], []
    for kv in kvs:
        kv_specs.append(pl.BlockSpec((tokens, HEAD_DIM), lambda i, m, p: (0, pick(m))))
        kv_specs.append(pl.BlockSpec((tokens, HEAD_DIM), lambda i, m, p: (0, KV_HEADS + pick(m))))
        kv_args += [kv, kv]
    outs = pl.pallas_call(
        functools.partial(attention_kernel, n_ctx, experts, capacity, blocks_out),
        grid_spec=pltpu.PrefetchScalarGridSpec(
            num_scalar_prefetch=2,
            grid=(1,),
            in_specs=[
                pl.BlockSpec((tokens, half_width), lambda i, m, p: (0, pick(m))),
                pl.BlockSpec((1, tokens), lambda i, m, p: (0, 0)),
            ]
            + kv_specs,
            out_specs=[pl.BlockSpec((tokens, half_width), lambda i, m, p: (0, 0))]
            + [pl.BlockSpec((rows, half_width), lambda i, m, p: (0, 0))] * blocks_out,
        ),
        out_shape=[jax.ShapeDtypeStruct((tokens, half_width), jnp.bfloat16)]
        + [jax.ShapeDtypeStruct((rows, half_width), jnp.bfloat16)] * blocks_out,
        compiler_params=params(),
        name="attend_" + "ab"[half],
    )(meta, parents, queries, route_row, *kv_args)
    return outs[0], list(outs[1:])


def load_rows(row_refs, gain_ref, rows_scratch):
    rows = jnp.concatenate([r[...].astype(jnp.float32) for r in row_refs], axis=0)
    rows_scratch[...] = (rows * gain_ref[...]).astype(jnp.bfloat16)
    return jnp.sum(rows * rows, axis=1, keepdims=True)


def start_copies(sources, targets, sems):
    copies = [
        pltpu.make_async_copy(s, t, sems.at[i]) for i, (s, t) in enumerate(zip(sources, targets))
    ]
    for copy in copies:
        copy.start()
    return copies


def first_kernel(n_rows, n_in, offset_at, meta, gain_ref, *refs):
    row_refs, refs = refs[:n_rows], refs[n_rows:]
    w_refs, refs = refs[:n_in], refs[n_in:]
    sums_ref, squares_ref, rows_scratch, sems = refs[0], refs[1], refs[2], refs[3]
    w_scratch = refs[4:]
    copies = start_copies(w_refs, w_scratch, sems)
    squares = load_rows(row_refs, gain_ref, rows_scratch)
    squares_ref[...] = jnp.broadcast_to(squares, squares_ref.shape)
    for i in range(n_in):
        depth = w_refs[i].shape[0]
        offset = pl.multiple_of(meta[offset_at + i], 128)
        copies[i].wait()
        part = jnp.dot(
            rows_scratch[:, pl.ds(offset, depth)],
            w_scratch[i][...],
            preferred_element_type=jnp.float32,
        )
        sums_ref[...] = part if i == 0 else sums_ref[...] + part


def first_half(meta, gain, rows, weights, offset_at, slots):
    half_width = rows[0].shape[1]
    columns = weights[0].shape[1]
    return pl.pallas_call(
        functools.partial(first_kernel, len(rows), len(weights), offset_at),
        grid_spec=pltpu.PrefetchScalarGridSpec(
            num_scalar_prefetch=1,
            grid=(1,),
            in_specs=[pl.BlockSpec((1, half_width), lambda i, m: (0, m[0]))]
            + [pl.BlockSpec(r.shape, lambda i, m: (0, 0)) for r in rows]
            + [pl.BlockSpec(memory_space=pl.ANY)] * len(weights),
            out_specs=[
                pl.BlockSpec((slots, columns), lambda i, m: (0, 0)),
                pl.BlockSpec((slots, 128), lambda i, m: (0, 0)),
            ],
            scratch_shapes=[
                pltpu.VMEM((slots, half_width), jnp.bfloat16),
                pltpu.SemaphoreType.DMA((len(weights),)),
            ]
            + [pltpu.VMEM(w.shape, w.dtype) for w in weights],
        ),
        out_shape=[
            jax.ShapeDtypeStruct((slots, columns), jnp.float32),
            jax.ShapeDtypeStruct((slots, 128), jnp.float32),
        ],
        compiler_params=params(),
        name="gate_up_a",
    )(meta, gain, *rows, *weights)


def store_blocks(value, out_refs, offset, columns):
    rows = value.shape[0] // len(out_refs)
    for k, out in enumerate(out_refs):
        out[:, pl.ds(offset, columns)] = value[k * rows : (k + 1) * rows].astype(jnp.bfloat16)


def second_kernel(n_rows, n_in, n_out, blocks_out, in_at, out_at, meta, gain_ref, *refs):
    row_refs, refs = refs[:n_rows], refs[n_rows:]
    sums_ref, squares_ref, refs = refs[0], refs[1], refs[2:]
    w_refs, refs = refs[: n_in + n_out], refs[n_in + n_out :]
    hidden_ref, refs = refs[0], refs[1:]
    out_refs, refs = refs[:blocks_out], refs[blocks_out:]
    rows_scratch, sums_scratch, sems = refs[:3]
    w_scratch = refs[3:]
    copies = start_copies(w_refs, w_scratch, sems)
    squares = load_rows(row_refs, gain_ref, rows_scratch) + squares_ref[:, :1]
    sums_scratch[...] = sums_ref[...]
    for i in range(n_in):
        depth = w_refs[i].shape[0]
        offset = pl.multiple_of(meta[in_at + i], 128)
        copies[i].wait()
        sums_scratch[...] += jnp.dot(
            rows_scratch[:, pl.ds(offset, depth)],
            w_scratch[i][...],
            preferred_element_type=jnp.float32,
        )
    width = 2 * rows_scratch.shape[1]
    factor = lax.rsqrt(squares * (1.0 / width) + 1e-06)
    inner = hidden_ref.shape[1]
    gate = sums_scratch[:, :inner] * factor
    up = sums_scratch[:, inner:] * factor
    hidden = (gate / (1.0 + jnp.exp(-gate)) * up).astype(jnp.bfloat16)
    hidden_ref[...] = hidden
    for i in range(n_out):
        columns = w_refs[n_in + i].shape[1]
        offset = pl.multiple_of(meta[out_at + i], 128)
        copies[n_in + i].wait()
        value = jnp.dot(hidden, w_scratch[n_in + i][...], preferred_element_type=jnp.float32)
        store_blocks(value, out_refs, offset, columns)


def second_half(meta, gain, rows, sums, squares, w_in, w_out, in_at, out_at, blocks_out):
    half_width = rows[0].shape[1]
    slots, columns = sums.shape
    inner = columns // 2
    block_rows = slots // blocks_out
    weights = list(w_in) + list(w_out)
    outs = pl.pallas_call(
        functools.partial(
            second_kernel, len(rows), len(w_in), len(w_out), blocks_out, in_at, out_at
        ),
        grid_spec=pltpu.PrefetchScalarGridSpec(
            num_scalar_prefetch=1,
            grid=(1,),
            in_specs=[pl.BlockSpec((1, half_width), lambda i, m: (0, 1 - m[0]))]
            + [pl.BlockSpec(r.shape, lambda i, m: (0, 0)) for r in rows]
            + [pl.BlockSpec(sums.shape, lambda i, m: (0, 0))]
            + [pl.BlockSpec(squares.shape, lambda i, m: (0, 0))]
            + [pl.BlockSpec(memory_space=pl.ANY)] * len(weights),
            out_specs=[pl.BlockSpec((slots, inner), lambda i, m: (0, 0))]
            + [pl.BlockSpec((block_rows, half_width), lambda i, m: (0, 0))] * blocks_out,
            scratch_shapes=[
                pltpu.VMEM((slots, half_width), jnp.bfloat16),
                pltpu.VMEM(sums.shape, jnp.float32),
                pltpu.SemaphoreType.DMA((len(weights),)),
            ]
            + [pltpu.VMEM(w.shape, w.dtype) for w in weights],
        ),
        out_shape=[jax.ShapeDtypeStruct((slots, inner), jnp.bfloat16)]
        + [jax.ShapeDtypeStruct((block_rows, half_width), jnp.bfloat16)] * blocks_out,
        compiler_params=params(),
        name="gate_up_b_down_a",
    )(meta, gain, *rows, sums, squares, *weights)
    return outs[0], list(outs[1:])


def third_kernel(n_out, blocks_out, out_at, meta, hidden_ref, *refs):
    w_refs, refs = refs[:n_out], refs[n_out:]
    out_refs, refs = refs[:blocks_out], refs[blocks_out:]
    sems, w_scratch = refs[0], refs[1:]
    copies = start_copies(w_refs, w_scratch, sems)
    for i in range(n_out):
        columns = w_refs[i].shape[1]
        offset = pl.multiple_of(meta[out_at + i], 128)
        copies[i].wait()
        value = jnp.dot(hidden_ref[...], w_scratch[i][...], preferred_element_type=jnp.float32)
        store_blocks(value, out_refs, offset, columns)


def down_half(meta, hidden, weights, out_at, blocks_out, half_width):
    block_rows = hidden.shape[0] // blocks_out
    return pl.pallas_call(
        functools.partial(third_kernel, len(weights), blocks_out, out_at),
        grid_spec=pltpu.PrefetchScalarGridSpec(
            num_scalar_prefetch=1,
            grid=(1,),
            in_specs=[pl.BlockSpec(hidden.shape, lambda i, m: (0, 0))]
            + [pl.BlockSpec(memory_space=pl.ANY)] * len(weights),
            out_specs=[pl.BlockSpec((block_rows, half_width), lambda i, m: (0, 0))] * blocks_out,
            scratch_shapes=[pltpu.SemaphoreType.DMA((len(weights),))]
            + [pltpu.VMEM(w.shape, w.dtype) for w in weights],
        ),
        out_shape=[jax.ShapeDtypeStruct((block_rows, half_width), jnp.bfloat16)] * blocks_out,
        compiler_params=params(),
        name="down_b",
    )(meta, hidden, *weights)


def combine_kernel(experts, capacity, n_rows, meta, att_ref, route_ref, weight_ref, *refs):
    row_refs, out_ref = refs[:n_rows], refs[-1]
    tokens = att_ref.shape[0]
    place = placement_of(route_ref[...], capacity, experts, meta[2], n_rows > 1)
    rows = jnp.concatenate([r[...].astype(jnp.float32) for r in row_refs], axis=0)
    mine = lax.dot_general(
        place,
        rows.astype(jnp.bfloat16),
        (((0,), (0,)), ((), ())),
        preferred_element_type=jnp.float32,
    )
    diagonal = lax.broadcasted_iota(jnp.int32, (tokens, tokens), 0) == lax.broadcasted_iota(
        jnp.int32, (tokens, tokens), 1
    )
    weight = jnp.sum(jnp.where(diagonal, weight_ref[...], 0.0), axis=1, keepdims=True)
    out_ref[...] = (att_ref[...].astype(jnp.float32) + mine * weight).astype(jnp.bfloat16)


def combine(meta, att, route_row, weight_row, rows, experts, capacity, half, before):
    tokens, half_width = att.shape

    def pick(scalars):
        return scalars[0] if half == 0 else 1 - scalars[0]

    n_before = 0 if before is None else 1
    return pl.pallas_call(
        functools.partial(combine_kernel, experts, capacity, len(rows)),
        grid_spec=pltpu.PrefetchScalarGridSpec(
            num_scalar_prefetch=1,
            grid=(1,),
            in_specs=[
                pl.BlockSpec(att.shape, lambda i, m: (0, 0)),
                pl.BlockSpec(route_row.shape, lambda i, m: (0, 0)),
                pl.BlockSpec(weight_row.shape, lambda i, m: (0, 0)),
            ]
            + [pl.BlockSpec(r.shape, lambda i, m: (0, 0)) for r in rows]
            + [pl.BlockSpec(memory_space=pl.ANY)] * n_before,
            out_specs=pl.BlockSpec((tokens, half_width), lambda i, m: (0, pick(m))),
        ),
        out_shape=jax.ShapeDtypeStruct((tokens, KV_HEADS * half_width), jnp.bfloat16),
        input_output_aliases={4 + len(rows): 0} if n_before else {},
        compiler_params=params(),
        name="combine_" + "ab"[half],
    )(meta, att, route_row, weight_row, *rows, *([before] if n_before else []))


def swap(array, axis, size, bit):
    return lax.ppermute(array, axis, [(i, i ^ bit) for i in range(size)])


def body(
    queries, keys, values, tree_parents, routes, route_weight, norm_gain, expert_in, expert_out
):
    n_grp, n_ctx, n_exp = (lax.axis_size(name) for name in ("grp", "ctx", "exp"))
    grp, ctx, exp = (lax.axis_index(name) for name in ("grp", "ctx", "exp"))
    tokens, width = queries.shape[1:]
    assert tokens == TREE_BLOCK and tree_parents.shape[1] == n_ctx and routes.shape[2] == 1
    assert n_ctx & (n_ctx - 1) == 0 and n_ctx > 1
    capacity = max(2, 5 * tokens // (4 * n_exp))
    slots = n_exp * capacity
    shifted = n_exp <= 8 and capacity % 8 == 0
    blocks_out = n_exp if shifted else 1
    half_width = width // KV_HEADS
    top = n_ctx // 2
    low_bits = [1 << b for b in range(top.bit_length() - 1)]
    half = ctx // top

    depth = expert_in.shape[1]
    inner = expert_out.shape[1]
    columns = expert_out.shape[2]
    w_in = expert_in[0].reshape(depth, 2 * inner)
    w_out = expert_out[0]
    route_row = routes.reshape(1, tokens)
    weight_row = route_weight.reshape(1, tokens)
    gain = norm_gain.reshape(1, width)

    kv = jnp.concatenate([keys[0], values[0]], axis=1)
    near = [kv]
    far = [swap(kv, "ctx", n_ctx, top)]
    for bit in low_bits:
        near = near + [swap(x, "ctx", n_ctx, bit) for x in near]
        far = far + [swap(x, "ctx", n_ctx, bit) for x in far]
    kvs = near + far

    def spread(pieces):
        for bit in low_bits:
            pieces = pieces + [(swap(a, "ctx", n_ctx, bit), s ^ bit, o) for a, s, o in pieces]
        return pieces

    place = lax.rem(ctx, top)
    w_in_a = spread([(w_in, place, 0)])
    w_out_a = spread([(w_out, place, 0)])
    w_in_b, w_out_b = [], []
    parts = n_grp if n_grp == 2 else 1
    chunks = 2 if depth % 1024 == 0 else 1
    step = depth // (parts * chunks)
    for i in range(chunks):
        start = i * step
        mine = grp * (parts - 1) * (depth // 2) + start
        other = (1 - grp) * (parts - 1) * (depth // 2) + start
        piece = lax.dynamic_slice_in_dim(w_in, mine, step, 0)
        piece = swap(piece, "ctx", n_ctx, top)
        got = [(piece, place, mine)]
        if parts == 2:
            got.append((swap(piece, "grp", 2, 1), place, other))
        w_in_b += spread(got)
    step = columns // parts
    piece = lax.dynamic_slice_in_dim(w_out, grp * (parts - 1) * step, step, 1)
    piece = swap(piece, "ctx", n_ctx, top)
    got = [(piece, place, grp * (parts - 1) * step)]
    if parts == 2:
        got.append((swap(piece, "grp", 2, 1), place, (1 - grp) * step))
    w_out_b = spread(got)

    groups = (w_in_a, w_in_b, w_out_a, w_out_b)
    sizes = (depth, depth, columns, columns)
    scalars, starts = [half, ctx, exp], []
    for group, size in zip(groups, sizes):
        starts.append(len(scalars))
        scalars += [s * size + o for _, s, o in group]
    meta = jnp.stack([jnp.asarray(s, jnp.int32) for s in scalars])
    w_in_a, w_in_b, w_out_a, w_out_b = ([a for a, _, _ in group] for group in groups)

    def send(blocks, back):
        if not shifted:
            whole = blocks[0].reshape(n_exp, capacity, half_width)
            whole = lax.all_to_all(whole, "exp", 0, 0, tiled=True)
            return [whole.reshape(slots, half_width)]
        moved = [blocks[0]]
        for k in range(1, n_exp):
            shift = n_exp - k if back else k
            moved.append(
                lax.ppermute(blocks[k], "exp", [(i, (i + shift) % n_exp) for i in range(n_exp)])
            )
        return moved

    parents = tree_parents[0]
    att_a, packed_a = attention(
        meta, parents, queries[0], route_row, kvs, n_exp, capacity, blocks_out, 0
    )
    rows_a = send(packed_a, False)
    att_b, packed_b = attention(
        meta, parents, queries[0], route_row, kvs, n_exp, capacity, blocks_out, 1
    )
    rows_b = send(packed_b, False)
    sums, squares = first_half(meta, gain, rows_a, w_in_a, starts[0], slots)
    hidden, out_a = second_half(
        meta, gain, rows_b, sums, squares, w_in_b, w_out_a, starts[1], starts[2], blocks_out
    )
    back_a = send(out_a, True)
    out_b = down_half(meta, hidden, w_out_b, starts[3], blocks_out, half_width)
    back_b = send(out_b, True)
    done = combine(meta, att_a, route_row, weight_row, back_a, n_exp, capacity, 0, None)
    done = combine(meta, att_b, route_row, weight_row, back_b, n_exp, capacity, 1, done)
    return done[None]


def solution(mesh):
    in_specs = (
        P(("grp", "exp"), "ctx", None),
        P(("grp", "exp"), "ctx", None),
        P(("grp", "exp"), "ctx", None),
        P(("grp", "exp"), None),
        P(("grp", "exp"), "ctx", None),
        P(("grp", "exp"), "ctx", None),
        P(),
        P("exp", "ctx", None, None),
        P("exp", None, "ctx"),
    )
    out_specs = P(("grp", "exp"), "ctx", None)
    return jax.shard_map(body, mesh=mesh, in_specs=in_specs, out_specs=out_specs, check_vma=False)
```

time: 234 us -> 183 us (0.78)
  blocking collectives: 115 us -> 0 us
  waiting for transfers between devices: 42 us -> 93.5 us
  starting transfers between devices: 3.58 us -> 47 us
  Pallas kernels: 0 us -> 33.8 us
  matrix products: 19.7 us -> 0 us
  local copies, waits for them, and re-layouts: 27.3 us -> 8.49 us
  between operations: 13.6 us -> 0.27 us
  other arithmetic: 12.2 us -> 0.01 us
    ppermute x0 -> x29, waiting for transfers between devices: none -> 93.5 us  [the longest x17 72.5 us: swap(): return lax.ppermute(array, axis, [(i, i ^ bit) for i in range(size)])]
    all_to_all x3 -> x0, blocking collectives: 92.1 us -> none  [the longest x1 36.6 us: body(): lax.all_to_all(outgoing, 'exp', split_axis=0, concat_axis=0, tiled=True)]
    ppermute x0 -> x29, starting transfers between devices: none -> 47 us  [the longest x12 36 us: send(): lax.ppermute(blocks[k], 'exp', [(i, (i + shift) % n_exp) for i in range(n...]
    pallas_call x0 -> x7, Pallas kernels: none -> 33.8 us  [the longest x2 8.97 us: attention(): pl.pallas_call(functools.partial(attention_kernel, n_ctx, experts, capaci...]
    reduce_scatter x1 -> x0, waiting for transfers between devices: 29 us -> none  [body(): lax.psum_scatter(jnp.dot(feature_cols, gate_up_weight, preferred_element_...]
    all_gather x3 -> x0, blocking collectives: 22.4 us -> none  [the longest x1 9.27 us: body(): lax.all_gather(hidden, 'ctx', axis=0, tiled=True)]
    dot_general x17 -> x0, matrix products: 19.7 us -> none  [the longest x4 6.05 us: update(): jnp.einsum('gjtn,ngd->gjtd', exp_scores, value_heads, preferred_element_t...]
    all_to_all x1 -> x0, waiting for transfers between devices: 13 us -> none  [body(): lax.all_to_all(column_rows, 'ctx', split_axis=1, concat_axis=0, tiled=True)]
  transfers between devices with their start and end apart: 2 -> 29, of which waited for: 2 -> 12; matrix products, arithmetic and copies ran while one was open for 2% -> 1% of each run, Pallas kernels for 0% -> 17%
where the time goes in v1:
time: 183 us
  waiting for transfers between devices  93.5 us (51%)
  starting transfers between devices  47 us (26%)
  Pallas kernels  33.8 us (18%)
  local copies, waits for them, and re-layouts  8.49 us (5%)
    ppermute x17, waiting for transfers between devices, swap(): return lax.ppermute(array, axis, [(i, i ^ bit) for i in range(size)])  72.5 us
    ppermute x12, starting transfers between devices, send(): lax.ppermute(blocks[k], 'exp', [(i, (i + shift) % n_exp) for i in range(n...  36 us
    ppermute x12, waiting for transfers between devices, send(): lax.ppermute(blocks[k], 'exp', [(i, (i + shift) % n_exp) for i in range(n...  21 us
    ppermute x17, starting transfers between devices, swap(): return lax.ppermute(array, axis, [(i, i ^ bit) for i in range(size)])  10.9 us
    pallas_call x2, Pallas kernels, attention(): pl.pallas_call(functools.partial(attention_kernel, n_ctx, experts, capaci...  8.97 us
    pallas_call x1, Pallas kernels, second_half(): pl.pallas_call(functools.partial(second_kernel, len(rows), len(w_in), len...  7.2 us
    pallas_call x2, Pallas kernels, combine(): pl.pallas_call(functools.partial(combine_kernel, experts, capacity, len(r...  6.49 us
    pallas_call x1, Pallas kernels, first_half(): pl.pallas_call(functools.partial(first_kernel, len(rows), len(weights), o...  6.32 us
  transfers between devices with their start and end apart: 29, of which 12 were waited for; matrix products, arithmetic and copies ran while one was open for 1% of the time, Pallas kernels for 17%

profile of v1, /device:TPU:0, one launch (start us, length us, event | category | flops | bytes accessed | tf_op | source)
XLA Modules:
  0.0 183.0 jit_solution(16276596193424018080)
XLA Ops:
  0.0 2.5 %copy.11 = bf16[128,8,2,768]{3,1,2,0:T(8,128)(2,1)S(1)} copy(bf16[128,8,2,768]{3,2,1,0:T(2,128)(2,1)} %bitcast.34) | data formatting | bytes 6291456
  3.0 1.7 constant_dynamic-slice_fusion
  4.8 2.3 %collective-permute-start.10 = (bf16[256,1536]{1,0:T(8,128)(2,1)}, bf16[256,1536]{1,0:T(8,128)(2,1)}, u32[]{:S(2)}, u32[]{:S(2)}) collective-permute-start(bf16[256,1536]{1,0:T(8,128)(2,1)} %get-tuple-element.48), channel_id=1, source_target_pairs={{0,8},{4,12},{8,0},{12,4},{1,9},{5,13},{9,1},{13,5},{2,10},{6,14},... | collective-permute-start | bytes 2359304 | tf_op jit(solution)/shard_map/ppermute | solution.py:345
  7.4 20.8 %collective-permute-done.1.refs_4_.refs_5_ = bf16[128,512]{1,0:T(8,128)(2,1)S(1)} collective-permute-done((bf16[128,512]{1,0:T(8,128)(2,1)S(1)}, bf16[128,512]{1,0:T(8,128)(2,1)S(1)}, u32[]{:S(2)}, u32[]{:S(2)}) %collective-permute-start.1) | collective-permute-done | bytes 131104 | tf_op jit(solution)/shard_map/ppermute | solution.py:345
  29.7 4.5 %attend_b.1 = (bf16[128,2048]{1,0:T(8,128)(2,1)}, bf16[40,2048]{1,0:T(8,128)(2,1)}, bf16[40,2048]{1,0:T(8,128)(2,1)}, bf16[40,2048]{1,0:T(8,128)(2,1)}, bf16[40,2048]{1,0:T(8,128)(2,1)}) custom-call(s32[19]{0:T(128)} %stack.61.meta, s32[4]{0:T(128)} %bitcast.43, bf16[128,4096]{1,0:T(8,128)(2,1)} %bitcast.30, s32[1,128]{1,0:T(1,128)} %bitcast.39, ...), custom_call_target="tpu_custom_call" | custom-call | tf_op jit(solution)/shard_map/attend_b/pallas_call | solution.py:104
  34.2 1.8 collective-permute-start.3
  36.1 2.6 %collective-permute-start.4 = (bf16[40,2048]{1,0:T(8,128)(2,1)}, bf16[40,2048]{1,0:T(8,128)(2,1)S(1)}, u32[]{:S(2)}, u32[]{:S(2)}) collective-permute-start(bf16[40,2048]{1,0:T(8,128)(2,1)} %get-tuple-element.29), channel_id=1, source_target_pairs={{0,2},{1,3},{2,0},{3,1},{4,6},{5,7},{6,4},{7,5},{8,10},{9,11},{10,... | collective-permute-start | bytes 491528 | tf_op jit(solution)/shard_map/ppermute | solution.py:430
  38.7 1.3 collective-permute-start.5
  40.0 4.5 %attend_a.1 = (bf16[128,2048]{1,0:T(8,128)(2,1)}, bf16[40,2048]{1,0:T(8,128)(2,1)}, bf16[40,2048]{1,0:T(8,128)(2,1)}, bf16[40,2048]{1,0:T(8,128)(2,1)}, bf16[40,2048]{1,0:T(8,128)(2,1)}) custom-call(s32[19]{0:T(128)} %stack.61.meta, s32[4]{0:T(128)} %bitcast.44, bf16[128,4096]{1,0:T(8,128)(2,1)} %bitcast.31, s32[1,128]{1,0:T(1,128)} %bitcast.40, ...), custom_call_target="tpu_custom_call" | custom-call | tf_op jit(solution)/shard_map/attend_a/pallas_call | solution.py:104
  44.5 4.6 %collective-permute-start.6 = (bf16[40,2048]{1,0:T(8,128)(2,1)}, bf16[40,2048]{1,0:T(8,128)(2,1)S(1)}, u32[]{:S(2)}, u32[]{:S(2)}) collective-permute-start(bf16[40,2048]{1,0:T(8,128)(2,1)} %get-tuple-element.32), channel_id=1, source_target_pairs={{0,1},{1,2},{2,3},{3,0},{4,5},{5,6},{6,7},{7,4},{8,9},{9,10},{10,1... | collective-permute-start | bytes 491528 | tf_op jit(solution)/shard_map/ppermute | solution.py:430
  49.1 1.4 collective-permute-done.4.refs_2_
  51.5 1.6 collective-permute-start.14
  53.9 4.1 %collective-permute-start.8 = (bf16[40,2048]{1,0:T(8,128)(2,1)}, bf16[40,2048]{1,0:T(8,128)(2,1)S(1)}, u32[]{:S(2)}, u32[]{:S(2)}) collective-permute-start(bf16[40,2048]{1,0:T(8,128)(2,1)} %get-tuple-element.34), channel_id=1, source_target_pairs={{0,3},{1,0},{2,1},{3,2},{4,7},{5,4},{6,5},{7,6},{8,11},{9,8},{10,9... | collective-permute-start | bytes 491528 | tf_op jit(solution)/shard_map/ppermute | solution.py:430
  58.0 6.3 %collective-permute-done.7.refs_2_ = bf16[40,2048]{1,0:T(8,128)(2,1)S(1)} collective-permute-done((bf16[40,2048]{1,0:T(8,128)(2,1)}, bf16[40,2048]{1,0:T(8,128)(2,1)S(1)}, u32[]{:S(2)}, u32[]{:S(2)}) %collective-permute-start.7) | collective-permute-done | bytes 163872 | tf_op jit(solution)/shard_map/ppermute | solution.py:430
  64.3 1.5 collective-permute-start.19
  65.8 1.5 collective-permute-start.11
  67.8 4.3 %collective-permute-done.14.refs_10_ = bf16[256,1536]{1,0:T(8,128)(2,1)S(1)} collective-permute-done((bf16[256,1536]{1,0:T(8,128)(2,1)S(1)}, bf16[256,1536]{1,0:T(8,128)(2,1)S(1)}, u32[]{:S(2)}, u32[]{:S(2)}) %collective-permute-start.14) | collective-permute-done | bytes 786464 | tf_op jit(solution)/shard_map/ppermute | solution.py:345
  72.2 14.7 %collective-permute-done.19.refs_0_ = bf16[768,512]{1,0:T(8,128)(2,1)} collective-permute-done((bf16[768,512]{1,0:T(8,128)(2,1)S(1)}, bf16[768,512]{1,0:T(8,128)(2,1)}, u32[]{:S(2)}, u32[]{:S(2)}) %collective-permute-start.19) | collective-permute-done | bytes 786464 | tf_op jit(solution)/shard_map/ppermute | solution.py:345
  86.9 1.6 collective-permute-start.15
  89.0 18.5 %collective-permute-done.15.refs_11_ = bf16[256,1536]{1,0:T(8,128)(2,1)} collective-permute-done((bf16[256,1536]{1,0:T(8,128)(2,1)S(1)}, bf16[256,1536]{1,0:T(8,128)(2,1)}, u32[]{:S(2)}, u32[]{:S(2)}) %collective-permute-start.15) | collective-permute-done | bytes 786464 | tf_op jit(solution)/shard_map/ppermute | solution.py:345
  108.0 13.3 %collective-permute-done.20.refs_1_ = bf16[768,512]{1,0:T(8,128)(2,1)} collective-permute-done((bf16[768,512]{1,0:T(8,128)(2,1)}, bf16[768,512]{1,0:T(8,128)(2,1)}, u32[]{:S(2)}, u32[]{:S(2)}) %collective-permute-start.20) | collective-permute-done | bytes 786464 | tf_op jit(solution)/shard_map/ppermute | solution.py:345
  121.8 6.3 %gate_up_a.1 = (f32[160,1536]{1,0:T(8,128)}, f32[160,128]{1,0:T(8,128)}) custom-call(s32[19]{0:T(128)} %stack.61.meta, f32[1,4096]{1,0:T(1,128)} %bitcast.35, bf16[40,2048]{1,0:T(8,128)(2,1)} %get-tuple-element.31.refs_0_, bf16[40,2048]{1,0:T(8,128)(2,1)} %copy-done.12, bf16[40,2048]{1,0:T(8,128)(2,1)} %copy-done.13, bf16[40,2048]{1,0:T(8,128)(2,1)} %copy-done.14, ...), custom_call_target="tpu_custom_call" | custom-call | tf_op jit(solution)/shard_map/gate_up_a/pallas_call | solution.py:163
  129.4 7.2 %gate_up_b_down_a.1 = (bf16[160,768]{1,0:T(8,128)(2,1)}, bf16[40,2048]{1,0:T(8,128)(2,1)}, bf16[40,2048]{1,0:T(8,128)(2,1)}, bf16[40,2048]{1,0:T(8,128)(2,1)}, bf16[40,2048]{1,0:T(8,128)(2,1)}) custom-call(s32[19]{0:T(128)} %stack.61.meta, f32[1,4096]{1,0:T(1,128)} %bitcast.36, bf16[40,2048]{1,0:T(8,128)(2,1)} %get-tuple-element.27.refs_0_, ...), custom_call_target="tpu_custom_call" | custom-call | tf_op jit(solution)/shard_map/gate_up_b_down_a/pallas_call | solution.py:237
  136.6 4.6 %collective-permute-start.26 = (bf16[40,2048]{1,0:T(8,128)(2,1)}, bf16[40,2048]{1,0:T(8,128)(2,1)S(1)}, u32[]{:S(2)}, u32[]{:S(2)}) collective-permute-start(bf16[40,2048]{1,0:T(8,128)(2,1)} %get-tuple-element.44), channel_id=1, source_target_pairs={{0,3},{1,0},{2,1},{3,2},{4,7},{5,4},{6,5},{7,6},{8,11},{9,8},{10,9... | collective-permute-start | bytes 491528 | tf_op jit(solution)/shard_map/ppermute | solution.py:430
  141.2 8.9 %collective-permute-start.27 = (bf16[40,2048]{1,0:T(8,128)(2,1)}, bf16[40,2048]{1,0:T(8,128)(2,1)S(1)}, u32[]{:S(2)}, u32[]{:S(2)}) collective-permute-start(bf16[40,2048]{1,0:T(8,128)(2,1)} %get-tuple-element.45), channel_id=1, source_target_pairs={{0,2},{1,3},{2,0},{3,1},{4,6},{5,7},{6,4},{7,5},{8,10},{9,11},{10,... | collective-permute-start | bytes 491528 | tf_op jit(solution)/shard_map/ppermute | solution.py:430
  151.0 4.8 %down_b.1 = (bf16[40,2048]{1,0:T(8,128)(2,1)}, bf16[40,2048]{1,0:T(8,128)(2,1)}, bf16[40,2048]{1,0:T(8,128)(2,1)}, bf16[40,2048]{1,0:T(8,128)(2,1)}) custom-call(s32[19]{0:T(128)} %stack.61.meta, bf16[160,768]{1,0:T(8,128)(2,1)} %get-tuple-element.37.hidden_ref, bf16[768,512]{1,0:T(8,128)(2,1)} %collective-permute-done.19.refs_0_, ...), custom_call_target="tpu_custom_call" | custom-call | tf_op jit(solution)/shard_map/down_b/pallas_call | solution.py:281
  155.8 3.9 %collective-permute-start.23 = (bf16[40,2048]{1,0:T(8,128)(2,1)}, bf16[40,2048]{1,0:T(8,128)(2,1)S(1)}, u32[]{:S(2)}, u32[]{:S(2)}) collective-permute-start(bf16[40,2048]{1,0:T(8,128)(2,1)} %get-tuple-element.39), channel_id=1, source_target_pairs={{0,3},{1,0},{2,1},{3,2},{4,7},{5,4},{6,5},{7,6},{8,11},{9,8},{10,9... | collective-permute-start | bytes 491528 | tf_op jit(solution)/shard_map/ppermute | solution.py:430
  159.7 3.2 %collective-permute-start.25 = (bf16[40,2048]{1,0:T(8,128)(2,1)}, bf16[40,2048]{1,0:T(8,128)(2,1)S(1)}, u32[]{:S(2)}, u32[]{:S(2)}) collective-permute-start(bf16[40,2048]{1,0:T(8,128)(2,1)} %get-tuple-element.41), channel_id=1, source_target_pairs={{0,1},{1,2},{2,3},{3,0},{4,5},{5,6},{6,7},{7,4},{8,9},{9,10},{10,1... | collective-permute-start | bytes 491528 | tf_op jit(solution)/shard_map/ppermute | solution.py:430
  162.9 10.0 %collective-permute-done.27.refs_2_ = bf16[40,2048]{1,0:T(8,128)(2,1)S(1)} collective-permute-done((bf16[40,2048]{1,0:T(8,128)(2,1)}, bf16[40,2048]{1,0:T(8,128)(2,1)S(1)}, u32[]{:S(2)}, u32[]{:S(2)}) %collective-permute-start.27) | collective-permute-done | bytes 163872 | tf_op jit(solution)/shard_map/ppermute | solution.py:430
  173.6 3.2 %combine_a.1.refs_4_ = bf16[128,4096]{1,0:T(8,128)(2,1)} custom-call(s32[19]{0:T(128)} %stack.61.meta, bf16[128,2048]{1,0:T(8,128)(2,1)} %get-tuple-element.42.att_ref, s32[1,128]{1,0:T(1,128)} %bitcast.41, f32[1,128]{1,0:T(1,128)} %bitcast.45, bf16[40,2048]{1,0:T(8,128)(2,1)} %get-tuple-element.43.refs_0_, bf16[40,2048]{1,0:T(8,128)(2,1)} %copy-done.15, ...), custom_call_target="tpu_custom_call" | custom-call | tf_op jit(solution)/shard_map/combine_a/pallas_call | solution.py:323
  176.8 2.2 %collective-permute-done.24.refs_2_ = bf16[40,2048]{1,0:T(8,128)(2,1)S(1)} collective-permute-done((bf16[40,2048]{1,0:T(8,128)(2,1)}, bf16[40,2048]{1,0:T(8,128)(2,1)S(1)}, u32[]{:S(2)}, u32[]{:S(2)}) %collective-permute-start.24) | collective-permute-done | bytes 163872 | tf_op jit(solution)/shard_map/ppermute | solution.py:430
  179.7 3.2 %combine_b.1 = bf16[128,4096]{1,0:T(8,128)(2,1)} custom-call(s32[19]{0:T(128)} %stack.61.meta, bf16[128,2048]{1,0:T(8,128)(2,1)} %get-tuple-element.26.att_ref, s32[1,128]{1,0:T(1,128)} %bitcast.42, f32[1,128]{1,0:T(1,128)} %bitcast.46, bf16[40,2048]{1,0:T(8,128)(2,1)} %get-tuple-element.38.refs_0_, ...), custom_call_target="tpu_custom_call", output_to_operand_aliasing={{}: (8, {})} | custom-call | tf_op jit(solution)/shard_map/combine_b/pallas_call | solution.py:323
  (90 shorter events, 9.6 us)
Async XLA Ops:
  2.5 118.8 %collective-permute-start.9 = (bf16[1024,1536]{1,0:T(8,128)(2,1)S(1)}, bf16[1024,1536]{1,0:T(8,128)(2,1)}, u32[]{:S(2)}, u32[]{:S(2)}) collective-permute-start(bf16[1024,1536]{1,0:T(8,128)(2,1)S(1)} %bitcast.27), channel_id=1, source_target_pairs={{0,4},{4,0},{8,12},{12,8},{1,5},{5,1},{9,13},{13,9},{2,6},{6,2},{1... | collective-permute-start | bytes 9437192 | tf_op jit(solution)/shard_map/ppermute | solution.py:345
  4.8 61.1 %collective-permute-start.10 = (bf16[256,1536]{1,0:T(8,128)(2,1)}, bf16[256,1536]{1,0:T(8,128)(2,1)}, u32[]{:S(2)}, u32[]{:S(2)}) collective-permute-start(bf16[256,1536]{1,0:T(8,128)(2,1)} %get-tuple-element.48), channel_id=1, source_target_pairs={{0,8},{4,12},{8,0},{12,4},{1,9},{5,13},{9,1},{13,5},{2,10},{6,14},... | collective-permute-start | bytes 2359304 | tf_op jit(solution)/shard_map/ppermute | solution.py:345
  7.1 21.1 %collective-permute-start.1 = (bf16[128,512]{1,0:T(8,128)(2,1)S(1)}, bf16[128,512]{1,0:T(8,128)(2,1)S(1)}, u32[]{:S(2)}, u32[]{:S(2)}) collective-permute-start(bf16[128,512]{1,0:T(8,128)(2,1)S(1)} %pad_maximum_fusion.refs_0_.refs_1_), channel_id=1, source_target_pairs={{0,8},{4,12},{8,0},{12,4},{1,9},{5,13},{9,1},{13,5},{2,10},{6,14},... | collective-permute-start | bytes 393224 | tf_op jit(solution)/shard_map/ppermute | solution.py:345
  7.2 21.8 %collective-permute-start = (bf16[128,512]{1,0:T(8,128)(2,1)S(1)}, bf16[128,512]{1,0:T(8,128)(2,1)S(1)}, u32[]{:S(2)}, u32[]{:S(2)}) collective-permute-start(bf16[128,512]{1,0:T(8,128)(2,1)S(1)} %pad_maximum_fusion.refs_0_.refs_1_), channel_id=1, source_target_pairs={{0,4},{4,0},{8,12},{12,8},{1,5},{5,1},{9,13},{13,9},{2,6},{6,2},{1... | collective-permute-start | bytes 393224 | tf_op jit(solution)/shard_map/ppermute | solution.py:345
  28.3 1.5 collective-permute-start.2
  34.2 10.3 %collective-permute-start.3 = (bf16[40,2048]{1,0:T(8,128)(2,1)}, bf16[40,2048]{1,0:T(8,128)(2,1)S(1)}, u32[]{:S(2)}, u32[]{:S(2)}) collective-permute-start(bf16[40,2048]{1,0:T(8,128)(2,1)} %get-tuple-element.28), channel_id=1, source_target_pairs={{0,1},{1,2},{2,3},{3,0},{4,5},{5,6},{6,7},{7,4},{8,9},{9,10},{10,1... | collective-permute-start | bytes 491528 | tf_op jit(solution)/shard_map/ppermute | solution.py:430
  36.1 14.4 %collective-permute-start.4 = (bf16[40,2048]{1,0:T(8,128)(2,1)}, bf16[40,2048]{1,0:T(8,128)(2,1)S(1)}, u32[]{:S(2)}, u32[]{:S(2)}) collective-permute-start(bf16[40,2048]{1,0:T(8,128)(2,1)} %get-tuple-element.29), channel_id=1, source_target_pairs={{0,2},{1,3},{2,0},{3,1},{4,6},{5,7},{6,4},{7,5},{8,10},{9,11},{10,... | collective-permute-start | bytes 491528 | tf_op jit(solution)/shard_map/ppermute | solution.py:430
  38.7 12.9 %collective-permute-start.5 = (bf16[40,2048]{1,0:T(8,128)(2,1)}, bf16[40,2048]{1,0:T(8,128)(2,1)S(1)}, u32[]{:S(2)}, u32[]{:S(2)}) collective-permute-start(bf16[40,2048]{1,0:T(8,128)(2,1)} %get-tuple-element.30), channel_id=1, source_target_pairs={{0,3},{1,0},{2,1},{3,2},{4,7},{5,4},{6,5},{7,6},{8,11},{9,8},{10,9... | collective-permute-start | bytes 491528 | tf_op jit(solution)/shard_map/ppermute | solution.py:430
  44.5 9.3 %collective-permute-start.6 = (bf16[40,2048]{1,0:T(8,128)(2,1)}, bf16[40,2048]{1,0:T(8,128)(2,1)S(1)}, u32[]{:S(2)}, u32[]{:S(2)}) collective-permute-start(bf16[40,2048]{1,0:T(8,128)(2,1)} %get-tuple-element.32), channel_id=1, source_target_pairs={{0,1},{1,2},{2,3},{3,0},{4,5},{5,6},{6,7},{7,4},{8,9},{9,10},{10,1... | collective-permute-start | bytes 491528 | tf_op jit(solution)/shard_map/ppermute | solution.py:430
  50.5 13.8 %collective-permute-start.7 = (bf16[40,2048]{1,0:T(8,128)(2,1)}, bf16[40,2048]{1,0:T(8,128)(2,1)S(1)}, u32[]{:S(2)}, u32[]{:S(2)}) collective-permute-start(bf16[40,2048]{1,0:T(8,128)(2,1)} %get-tuple-element.33), channel_id=1, source_target_pairs={{0,2},{1,3},{2,0},{3,1},{4,6},{5,7},{6,4},{7,5},{8,10},{9,11},{10,... | collective-permute-start | bytes 491528 | tf_op jit(solution)/shard_map/ppermute | solution.py:430
  51.5 20.5 %collective-permute-start.14 = (bf16[256,1536]{1,0:T(8,128)(2,1)S(1)}, bf16[256,1536]{1,0:T(8,128)(2,1)S(1)}, u32[]{:S(2)}, u32[]{:S(2)}) collective-permute-start(bf16[256,1536]{1,0:T(8,128)(2,1)S(1)} %copy-done.10), channel_id=1, source_target_pairs={{0,8},{4,12},{8,0},{12,4},{1,9},{5,13},{9,1},{13,5},{2,10},{6,14},... | collective-permute-start | bytes 2359304 | tf_op jit(solution)/shard_map/ppermute | solution.py:345
  53.9 68.0 %copy-start.12 = (bf16[40,2048]{1,0:T(8,128)(2,1)}, bf16[40,2048]{1,0:T(8,128)(2,1)S(1)}, u32[]{:S(2)}) copy-start(bf16[40,2048]{1,0:T(8,128)(2,1)S(1)} %collective-permute-done.6.refs_1_) | copy-start | bytes 491524
  53.9 13.9 %collective-permute-start.8 = (bf16[40,2048]{1,0:T(8,128)(2,1)}, bf16[40,2048]{1,0:T(8,128)(2,1)S(1)}, u32[]{:S(2)}, u32[]{:S(2)}) collective-permute-start(bf16[40,2048]{1,0:T(8,128)(2,1)} %get-tuple-element.34), channel_id=1, source_target_pairs={{0,3},{1,0},{2,1},{3,2},{4,7},{5,4},{6,5},{7,6},{8,11},{9,8},{10,9... | collective-permute-start | bytes 491528 | tf_op jit(solution)/shard_map/ppermute | solution.py:430
  64.3 57.5 %copy-start.13 = (bf16[40,2048]{1,0:T(8,128)(2,1)}, bf16[40,2048]{1,0:T(8,128)(2,1)S(1)}, u32[]{:S(2)}) copy-start(bf16[40,2048]{1,0:T(8,128)(2,1)S(1)} %collective-permute-done.7.refs_2_) | copy-start | bytes 491524
  64.3 22.6 %collective-permute-start.19 = (bf16[768,512]{1,0:T(8,128)(2,1)S(1)}, bf16[768,512]{1,0:T(8,128)(2,1)}, u32[]{:S(2)}, u32[]{:S(2)}) collective-permute-start(bf16[768,512]{1,0:T(8,128)(2,1)S(1)} %dynamic-slice_bitcast_fusion), channel_id=1, source_target_pairs={{0,8},{4,12},{8,0},{12,4},{1,9},{5,13},{9,1},{13,5},{2,10},{6,14},... | collective-permute-start | bytes 2359304 | tf_op jit(solution)/shard_map/ppermute | solution.py:345
  65.8 22.7 %collective-permute-start.11 = (bf16[256,1536]{1,0:T(8,128)(2,1)}, bf16[256,1536]{1,0:T(8,128)(2,1)S(1)}, u32[]{:S(2)}, u32[]{:S(2)}) collective-permute-start(bf16[256,1536]{1,0:T(8,128)(2,1)} %collective-permute-done.10.refs_6_), channel_id=1, source_target_pairs={{0,16},{16,0},{1,17},{17,1},{2,18},{18,2},{3,19},{19,3},{4,20},{20... | collective-permute-start | bytes 2359304 | tf_op jit(solution)/shard_map/ppermute | solution.py:345
  67.8 20.8 %collective-permute-start.12 = (bf16[256,1536]{1,0:T(8,128)(2,1)}, bf16[256,1536]{1,0:T(8,128)(2,1)S(1)}, u32[]{:S(2)}, u32[]{:S(2)}) collective-permute-start(bf16[256,1536]{1,0:T(8,128)(2,1)} %collective-permute-done.10.refs_6_), channel_id=1, source_target_pairs={{0,4},{4,0},{8,12},{12,8},{1,5},{5,1},{9,13},{13,9},{2,6},{6,2},{1... | collective-permute-start | bytes 2359304 | tf_op jit(solution)/shard_map/ppermute | solution.py:345
  72.1 56.1 %copy-start.6 = (bf16[256,1536]{1,0:T(8,128)(2,1)}, bf16[256,1536]{1,0:T(8,128)(2,1)S(1)}, u32[]{:S(2)}) copy-start(bf16[256,1536]{1,0:T(8,128)(2,1)S(1)} %collective-permute-done.14.refs_10_) | copy-start | bytes 2359300
  72.1 56.1 %collective-permute-start.18 = (bf16[768,1024]{1,0:T(8,128)(2,1)S(1)}, bf16[768,1024]{1,0:T(8,128)(2,1)S(1)}, u32[]{:S(2)}, u32[]{:S(2)}) collective-permute-start(bf16[768,1024]{1,0:T(8,128)(2,1)S(1)} %bitcast.33), channel_id=1, source_target_pairs={{0,4},{4,0},{8,12},{12,8},{1,5},{5,1},{9,13},{13,9},{2,6},{6,2},{1... | collective-permute-start | bytes 4718600 | tf_op jit(solution)/shard_map/ppermute | solution.py:345
  86.9 20.6 %collective-permute-start.15 = (bf16[256,1536]{1,0:T(8,128)(2,1)S(1)}, bf16[256,1536]{1,0:T(8,128)(2,1)}, u32[]{:S(2)}, u32[]{:S(2)}) collective-permute-start(bf16[256,1536]{1,0:T(8,128)(2,1)S(1)} %collective-permute-done.14.refs_10_), channel_id=1, source_target_pairs={{0,16},{16,0},{1,17},{17,1},{2,18},{18,2},{3,19},{19,3},{4,20},{20... | collective-permute-start | bytes 2359304 | tf_op jit(solution)/shard_map/ppermute | solution.py:345
  88.6 19.0 %collective-permute-start.16 = (bf16[256,1536]{1,0:T(8,128)(2,1)S(1)}, bf16[256,1536]{1,0:T(8,128)(2,1)S(1)}, u32[]{:S(2)}, u32[]{:S(2)}) collective-permute-start(bf16[256,1536]{1,0:T(8,128)(2,1)S(1)} %collective-permute-done.14.refs_10_), channel_id=1, source_target_pairs={{0,4},{4,0},{8,12},{12,8},{1,5},{5,1},{9,13},{13,9},{2,6},{6,2},{1... | collective-permute-start | bytes 2359304 | tf_op jit(solution)/shard_map/ppermute | solution.py:345
  88.6 32.7 %collective-permute-start.20 = (bf16[768,512]{1,0:T(8,128)(2,1)}, bf16[768,512]{1,0:T(8,128)(2,1)}, u32[]{:S(2)}, u32[]{:S(2)}) collective-permute-start(bf16[768,512]{1,0:T(8,128)(2,1)} %collective-permute-done.19.refs_0_), channel_id=1, source_target_pairs={{0,16},{16,0},{1,17},{17,1},{2,18},{18,2},{3,19},{19,3},{4,20},{20... | collective-permute-start | bytes 2359304 | tf_op jit(solution)/shard_map/ppermute | solution.py:345
  107.5 20.7 %collective-permute-start.13 = (bf16[256,1536]{1,0:T(8,128)(2,1)S(1)}, bf16[256,1536]{1,0:T(8,128)(2,1)}, u32[]{:S(2)}, u32[]{:S(2)}) collective-permute-start(bf16[256,1536]{1,0:T(8,128)(2,1)S(1)} %collective-permute-done.11.refs_7_), channel_id=1, source_target_pairs={{0,4},{4,0},{8,12},{12,8},{1,5},{5,1},{9,13},{13,9},{2,6},{6,2},{1... | collective-permute-start | bytes 2359304 | tf_op jit(solution)/shard_map/ppermute | solution.py:345
  107.5 20.7 %collective-permute-start.17 = (bf16[256,1536]{1,0:T(8,128)(2,1)}, bf16[256,1536]{1,0:T(8,128)(2,1)}, u32[]{:S(2)}, u32[]{:S(2)}) collective-permute-start(bf16[256,1536]{1,0:T(8,128)(2,1)} %collective-permute-done.15.refs_11_), channel_id=1, source_target_pairs={{0,4},{4,0},{8,12},{12,8},{1,5},{5,1},{9,13},{13,9},{2,6},{6,2},{1... | collective-permute-start | bytes 2359304 | tf_op jit(solution)/shard_map/ppermute | solution.py:345
  121.3 28.8 %collective-permute-start.21 = (bf16[768,512]{1,0:T(8,128)(2,1)}, bf16[768,512]{1,0:T(8,128)(2,1)}, u32[]{:S(2)}, u32[]{:S(2)}) collective-permute-start(bf16[768,512]{1,0:T(8,128)(2,1)} %collective-permute-done.19.refs_0_), channel_id=1, source_target_pairs={{0,4},{4,0},{8,12},{12,8},{1,5},{5,1},{9,13},{13,9},{2,6},{6,2},{1... | collective-permute-start | bytes 2359304 | tf_op jit(solution)/shard_map/ppermute | solution.py:345
  121.3 28.8 %collective-permute-start.22 = (bf16[768,512]{1,0:T(8,128)(2,1)}, bf16[768,512]{1,0:T(8,128)(2,1)S(1)}, u32[]{:S(2)}, u32[]{:S(2)}) collective-permute-start(bf16[768,512]{1,0:T(8,128)(2,1)} %collective-permute-done.20.refs_1_), channel_id=1, source_target_pairs={{0,4},{4,0},{8,12},{12,8},{1,5},{5,1},{9,13},{13,9},{2,6},{6,2},{1... | collective-permute-start | bytes 2359304 | tf_op jit(solution)/shard_map/ppermute | solution.py:345
  136.6 23.1 %collective-permute-start.26 = (bf16[40,2048]{1,0:T(8,128)(2,1)}, bf16[40,2048]{1,0:T(8,128)(2,1)S(1)}, u32[]{:S(2)}, u32[]{:S(2)}) collective-permute-start(bf16[40,2048]{1,0:T(8,128)(2,1)} %get-tuple-element.44), channel_id=1, source_target_pairs={{0,3},{1,0},{2,1},{3,2},{4,7},{5,4},{6,5},{7,6},{8,11},{9,8},{10,9... | collective-permute-start | bytes 491528 | tf_op jit(solution)/shard_map/ppermute | solution.py:430
  141.2 31.7 %collective-permute-start.27 = (bf16[40,2048]{1,0:T(8,128)(2,1)}, bf16[40,2048]{1,0:T(8,128)(2,1)S(1)}, u32[]{:S(2)}, u32[]{:S(2)}) collective-permute-start(bf16[40,2048]{1,0:T(8,128)(2,1)} %get-tuple-element.45), channel_id=1, source_target_pairs={{0,2},{1,3},{2,0},{3,1},{4,6},{5,7},{6,4},{7,5},{8,10},{9,11},{10,... | collective-permute-start | bytes 491528 | tf_op jit(solution)/shard_map/ppermute | solution.py:430
  150.1 22.8 %collective-permute-start.28 = (bf16[40,2048]{1,0:T(8,128)(2,1)}, bf16[40,2048]{1,0:T(8,128)(2,1)S(1)}, u32[]{:S(2)}, u32[]{:S(2)}) collective-permute-start(bf16[40,2048]{1,0:T(8,128)(2,1)} %get-tuple-element.46), channel_id=1, source_target_pairs={{0,1},{1,2},{2,3},{3,0},{4,5},{5,6},{6,7},{7,4},{8,9},{9,10},{10,1... | collective-permute-start | bytes 491528 | tf_op jit(solution)/shard_map/ppermute | solution.py:430
  155.8 21.1 %collective-permute-start.23 = (bf16[40,2048]{1,0:T(8,128)(2,1)}, bf16[40,2048]{1,0:T(8,128)(2,1)S(1)}, u32[]{:S(2)}, u32[]{:S(2)}) collective-permute-start(bf16[40,2048]{1,0:T(8,128)(2,1)} %get-tuple-element.39), channel_id=1, source_target_pairs={{0,3},{1,0},{2,1},{3,2},{4,7},{5,4},{6,5},{7,6},{8,11},{9,8},{10,9... | collective-permute-start | bytes 491528 | tf_op jit(solution)/shard_map/ppermute | solution.py:430
  159.7 19.4 %collective-permute-start.24 = (bf16[40,2048]{1,0:T(8,128)(2,1)}, bf16[40,2048]{1,0:T(8,128)(2,1)S(1)}, u32[]{:S(2)}, u32[]{:S(2)}) collective-permute-start(bf16[40,2048]{1,0:T(8,128)(2,1)} %get-tuple-element.40), channel_id=1, source_target_pairs={{0,2},{1,3},{2,0},{3,1},{4,6},{5,7},{6,4},{7,5},{8,10},{9,11},{10,... | collective-permute-start | bytes 491528 | tf_op jit(solution)/shard_map/ppermute | solution.py:430
  159.7 19.4 %collective-permute-start.25 = (bf16[40,2048]{1,0:T(8,128)(2,1)}, bf16[40,2048]{1,0:T(8,128)(2,1)S(1)}, u32[]{:S(2)}, u32[]{:S(2)}) collective-permute-start(bf16[40,2048]{1,0:T(8,128)(2,1)} %get-tuple-element.41), channel_id=1, source_target_pairs={{0,1},{1,2},{2,3},{3,0},{4,5},{5,6},{6,7},{7,4},{8,9},{9,10},{10,1... | collective-permute-start | bytes 491528 | tf_op jit(solution)/shard_map/ppermute | solution.py:430
  (23 other events, 284.0 us)

commit v2 on v0

v2 whole, which is shorter than its diff:
```python
import functools
import math

import jax
import jax.numpy as jnp
from jax import lax
from jax.experimental import pallas as pl
from jax.experimental.pallas import tpu as pltpu
from jax.sharding import PartitionSpec as P

KV_HEADS = 2
HEAD_DIM = 128
TREE_BLOCK = 128
NEG = -1e30
MIB = 1024 * 1024
VMEM = pl.BlockSpec(memory_space=pltpu.VMEM)
SMEM = pl.BlockSpec(memory_space=pltpu.SMEM)


def call(kernel, name, args, specs, outs, scratch=(), mib=16, flops=1000):
    return pl.pallas_call(
        kernel,
        in_specs=specs,
        out_specs=[VMEM] * len(outs),
        out_shape=[jax.ShapeDtypeStruct(s, d) for s, d in outs],
        scratch_shapes=list(scratch),
        compiler_params=pltpu.CompilerParams(vmem_limit_bytes=mib * MIB),
        cost_estimate=pl.CostEstimate(flops=flops, bytes_accessed=1000, transcendentals=0),
        name=name,
    )(*args)


def placement_of(route_row, capacity, experts, first, relative):
    tokens = route_row.shape[1]
    if relative:
        route_row = lax.rem(route_row - first + experts, experts)
    rows = max(8, experts)
    expert_ids = lax.broadcasted_iota(jnp.int32, (rows, tokens), 0)
    hot = jnp.where(expert_ids == route_row, 1.0, 0.0)
    before = lax.broadcasted_iota(jnp.int32, (tokens, tokens), 0) < lax.broadcasted_iota(
        jnp.int32, (tokens, tokens), 1
    )
    earlier = jnp.dot(
        hot.astype(jnp.bfloat16),
        jnp.where(before, 1.0, 0.0).astype(jnp.bfloat16),
        preferred_element_type=jnp.float32,
    )
    rank = jnp.sum(earlier * hot, axis=0, keepdims=True).astype(jnp.int32)
    slot = route_row * capacity + rank
    slot_ids = lax.broadcasted_iota(jnp.int32, (experts * capacity, tokens), 0)
    return jnp.where(slot_ids == slot, 1.0, 0.0).astype(jnp.bfloat16)


def attention_kernel(n_ctx, experts, capacity, blocks_out, half, meta, parents, q_ref, route_ref, *refs):
    kv = refs[:n_ctx]
    att_ref = refs[n_ctx]
    out_refs = refs[n_ctx + 1 :]
    tokens, half_width = att_ref.shape
    heads = half_width // HEAD_DIM
    side = meta[0] if half == 0 else 1 - meta[0]
    me = meta[1]
    reached = [jnp.int32(0)] * n_ctx
    current = me
    for _ in range(n_ctx):
        current = parents[0, current]
        for j in range(1, n_ctx):
            reached[j] = jnp.where(current == (me ^ j), jnp.int32(1), reached[j])
    causal = lax.broadcasted_iota(jnp.int32, (tokens, tokens), 1) <= lax.broadcasted_iota(
        jnp.int32, (tokens, tokens), 0
    )
    key_at = pl.ds(pl.multiple_of(side * HEAD_DIM, HEAD_DIM), HEAD_DIM)
    value_at = pl.ds(pl.multiple_of((KV_HEADS + side) * HEAD_DIM, HEAD_DIM), HEAD_DIM)
    keys_t = jnp.concatenate([r[:, key_at] for r in kv], axis=0).T
    ones = jnp.ones((tokens, HEAD_DIM), jnp.bfloat16)
    values = jnp.concatenate(
        [jnp.concatenate([r[:, value_at], ones], axis=1) for r in kv], axis=0
    )
    bias = jnp.concatenate(
        [jnp.where(causal, 0.0, NEG)]
        + [
            jnp.broadcast_to(jnp.where(reached[j] == 1, 0.0, NEG), (tokens, tokens))
            for j in range(1, n_ctx)
        ],
        axis=1,
    )
    scale = math.log2(math.e) / math.sqrt(HEAD_DIM)
    for h in range(heads):
        columns = slice(h * HEAD_DIM, (h + 1) * HEAD_DIM)
        q_at = pl.ds(pl.multiple_of(side * half_width + h * HEAD_DIM, HEAD_DIM), HEAD_DIM)
        scores = jnp.dot(q_ref[:, q_at], keys_t, preferred_element_type=jnp.float32)
        scores = scores * scale + bias
        peak = jnp.max(scores, axis=1, keepdims=True)
        weights = jnp.exp2(scores - peak).astype(jnp.bfloat16)
        total = jnp.dot(weights, values, preferred_element_type=jnp.float32)
        att_ref[:, columns] = (total[:, :HEAD_DIM] / total[:, HEAD_DIM:]).astype(jnp.bfloat16)
    place = placement_of(route_ref[...], capacity, experts, meta[2], blocks_out > 1)
    packed = jnp.dot(place, att_ref[...], preferred_element_type=jnp.float32)
    rows = experts * capacity // blocks_out
    for k in range(blocks_out):
        out_refs[k][...] = packed[k * rows : (k + 1) * rows].astype(jnp.bfloat16)


def attention(meta, parents, queries, route_row, kvs, experts, capacity, blocks_out, half):
    tokens, width = queries.shape
    half_width = width // KV_HEADS
    rows = experts * capacity // blocks_out
    bf16 = jnp.bfloat16
    outs = call(
        functools.partial(attention_kernel, len(kvs), experts, capacity, blocks_out, half),
        "attend_" + "ab"[half],
        [meta, parents, queries, route_row, *kvs],
        [SMEM, SMEM] + [VMEM] * (2 + len(kvs)),
        [((tokens, half_width), bf16)] + [((rows, half_width), bf16)] * blocks_out,
        flops=2 * 10**9,
    )
    return outs[0], list(outs[1:])


def prepare_kernel(n_rows, half, meta, gain_ref, *refs):
    row_refs, (scaled_ref, squares_ref) = refs[:n_rows], refs[n_rows:]
    width = scaled_ref.shape[1]
    side = meta[0] if half == 0 else 1 - meta[0]
    gain = gain_ref[:, pl.ds(pl.multiple_of(side * width, width), width)]
    rows = jnp.concatenate([r[...].astype(jnp.float32) for r in row_refs], axis=0)
    scaled_ref[...] = (rows * gain).astype(jnp.bfloat16)
    squares = jnp.sum(rows * rows, axis=1, keepdims=True)
    squares_ref[...] = jnp.broadcast_to(squares, squares_ref.shape)


def prepare(meta, gain, rows, slots, half):
    return call(
        functools.partial(prepare_kernel, len(rows), half),
        "rows_" + "ab"[half],
        [meta, gain, *rows],
        [SMEM] + [VMEM] * (1 + len(rows)),
        [((slots, rows[0].shape[1]), jnp.bfloat16), ((slots, 128), jnp.float32)],
        flops=20 * 10**9,
    )


def add_products(meta, pieces, w_refs, rows_scratch, sums_ref, fresh):
    done = set()
    for (row_at, col_at), w_ref in zip(pieces, w_refs):
        depth, columns = w_ref.shape
        rows = rows_scratch[:, pl.ds(pl.multiple_of(meta[row_at], 128), depth)]
        part = jnp.dot(rows, w_ref[...], preferred_element_type=jnp.float32)
        where = pl.ds(pl.multiple_of(meta[col_at], 128), columns)
        if fresh and col_at not in done:
            sums_ref[:, where] = part
        else:
            sums_ref[:, where] += part
        done.add(col_at)


def first_kernel(pieces, meta, rows_ref, *refs):
    add_products(meta, pieces, refs[:-1], rows_ref, refs[-1], True)


def first_half(meta, rows, weights, pieces, inner):
    return call(
        functools.partial(first_kernel, pieces),
        "gate_up_a",
        [meta, rows, *weights],
        [SMEM] + [VMEM] * (1 + len(weights)),
        [((rows.shape[0], 2 * inner), jnp.float32)],
    )[0]


def store_down(meta, pieces, w_refs, hidden, out_refs):
    value, blocks = None, len(out_refs)
    for i, ((row_at, col_at), w_ref) in enumerate(zip(pieces, w_refs)):
        depth, columns = w_ref.shape
        rows = hidden[:, pl.ds(pl.multiple_of(meta[row_at], 128), depth)]
        part = jnp.dot(rows, w_ref[...], preferred_element_type=jnp.float32)
        value = part if value is None else value + part
        if i + 1 == len(pieces) or pieces[i + 1][1] != col_at:
            where = pl.ds(pl.multiple_of(meta[col_at], 128), columns)
            height = value.shape[0] // blocks
            for k, out in enumerate(out_refs):
                out[:, where] = value[k * height : (k + 1) * height].astype(jnp.bfloat16)
            value = None


def second_kernel(in_pieces, out_pieces, meta, rows_ref, start_ref, near_ref, far_ref, *refs):
    n_in, n_out = len(in_pieces), len(out_pieces)
    w_refs, refs = refs[: n_in + n_out], refs[n_in + n_out :]
    hidden_ref, out_refs, sums_ref = refs[0], refs[1:-1], refs[-1]
    sums_ref[...] = start_ref[...]
    add_products(meta, in_pieces, w_refs[:n_in], rows_ref, sums_ref, False)
    width = 2 * rows_ref.shape[1]
    squares = near_ref[:, :1] + far_ref[:, :1]
    factor = lax.rsqrt(squares * (1.0 / width) + 1e-06)
    inner = hidden_ref.shape[1]
    gate = sums_ref[:, :inner] * factor
    up = sums_ref[:, inner:] * factor
    hidden_ref[...] = (gate / (1.0 + jnp.exp(-gate)) * up).astype(jnp.bfloat16)
    store_down(meta, out_pieces, w_refs[n_in:], hidden_ref, out_refs)


def second_half(meta, rows, sums, near, far, w_in, in_pieces, w_out, out_pieces, blocks_out):
    slots, columns = sums.shape
    weights = list(w_in) + list(w_out)
    bf16 = jnp.bfloat16
    outs = call(
        functools.partial(second_kernel, in_pieces, out_pieces),
        "gate_up_b_down_a",
        [meta, rows, sums, near, far, *weights],
        [SMEM] + [VMEM] * (4 + len(weights)),
        [((slots, columns // 2), bf16)]
        + [((slots // blocks_out, rows.shape[1]), bf16)] * blocks_out,
        [pltpu.VMEM((slots, columns), jnp.float32)],
        flops=20 * 10**9,
    )
    return outs[0], list(outs[1:])


def third_kernel(pieces, meta, hidden_ref, *refs):
    store_down(meta, pieces, refs[: len(pieces)], hidden_ref, refs[len(pieces) :])


def down_half(meta, hidden, weights, pieces, blocks_out, half_width):
    outs = [((hidden.shape[0] // blocks_out, half_width), jnp.bfloat16)] * blocks_out
    return list(
        call(
            functools.partial(third_kernel, pieces),
            "down_b",
            [meta, hidden, *weights],
            [SMEM] + [VMEM] * (1 + len(weights)),
            outs,
        )
    )


def combine_kernel(experts, capacity, n_rows, last, meta, att_ref, route_ref, weight_ref, *refs):
    row_refs, out_ref = refs[:n_rows], refs[-1]
    tokens, half_width = att_ref.shape
    place = placement_of(route_ref[...], capacity, experts, meta[2], n_rows > 1)
    rows = jnp.concatenate([r[...].astype(jnp.float32) for r in row_refs], axis=0)
    mine = lax.dot_general(
        place,
        rows.astype(jnp.bfloat16),
        (((0,), (0,)), ((), ())),
        preferred_element_type=jnp.float32,
    )
    diagonal = lax.broadcasted_iota(jnp.int32, (tokens, tokens), 0) == lax.broadcasted_iota(
        jnp.int32, (tokens, tokens), 1
    )
    weight = jnp.sum(jnp.where(diagonal, weight_ref[...], 0.0), axis=1, keepdims=True)
    value = (att_ref[...].astype(jnp.float32) + mine * weight).astype(jnp.bfloat16)
    if last:
        before_ref = refs[n_rows]
        before_at = pl.multiple_of(meta[0] * half_width, half_width)
        mine_at = pl.multiple_of((1 - meta[0]) * half_width, half_width)
        out_ref[:, pl.ds(before_at, half_width)] = before_ref[...]
        out_ref[:, pl.ds(mine_at, half_width)] = value
    else:
        out_ref[...] = value


def combine(meta, att, route_row, weight_row, rows, experts, capacity, before):
    tokens, half_width = att.shape
    last = before is not None
    extra = [before] if last else []
    return call(
        functools.partial(combine_kernel, experts, capacity, len(rows), last),
        "combine_" + "ab"[last],
        [meta, att, route_row, weight_row, *rows, *extra],
        [SMEM] + [VMEM] * (3 + len(rows) + len(extra)),
        [((tokens, half_width * (1 + last)), jnp.bfloat16)],
        flops=20 * 10**9,
    )[0]


def swap(array, axis, size, bit):
    return lax.ppermute(array, axis, [(i, i ^ bit) for i in range(size)])


def after(array, *others):
    return lax.optimization_barrier((array, *others))[0]


def body(
    queries, keys, values, tree_parents, routes, route_weight, norm_gain, expert_in, expert_out
):
    n_grp, n_ctx, n_exp = (lax.axis_size(name) for name in ("grp", "ctx", "exp"))
    grp, ctx, exp = (lax.axis_index(name) for name in ("grp", "ctx", "exp"))
    tokens, width = queries.shape[1:]
    assert tokens == TREE_BLOCK and tree_parents.shape[1] == n_ctx and routes.shape[2] == 1
    assert n_ctx & (n_ctx - 1) == 0 and n_ctx > 1 and n_grp == 2
    capacity = max(2, 5 * tokens // (4 * n_exp))
    slots = n_exp * capacity
    shifted = n_exp <= 8 and capacity % 8 == 0
    blocks_out = n_exp if shifted else 1
    half_width = width // KV_HEADS
    top = n_ctx // 2
    low_bits = [1 << b for b in range(top.bit_length() - 1)]
    half = ctx // top

    depth = expert_in.shape[1]
    inner = expert_out.shape[1]
    columns = expert_out.shape[2]
    w_out = expert_out[0]
    route_row = routes.reshape(1, tokens)
    weight_row = route_weight.reshape(1, tokens)
    gain = norm_gain.reshape(1, width)

    kv = jnp.concatenate([keys[0], values[0]], axis=1)
    kv_far = swap(kv, "ctx", n_ctx, top)
    near, far = [kv], [kv_far]
    for bit in low_bits:
        near = near + [swap(x, "ctx", n_ctx, bit) for x in near]
        far = far + [swap(x, "ctx", n_ctx, bit) for x in far]
    kvs = near + far

    scalars = [half, ctx, exp, jnp.int32(0)]

    def note(value):
        scalars.append(jnp.asarray(value, jnp.int32))
        return len(scalars) - 1

    zero = 3
    shard = lax.rem(ctx, top)
    in_row = [note((shard ^ j) * depth) for j in range(top)]
    out_col = [note((shard ^ j) * columns) for j in range(top)]
    in_third, out_third = 2 * inner // 3, inner // 3
    in_cols = [note(grp * in_third), note((1 - grp) * in_third), note(2 * in_third)]
    out_rows = [note(grp * out_third), note((1 - grp) * out_third), note(2 * out_third)]
    meta = jnp.stack(scalars)

    def spread(array):
        found = [array]
        for bit in low_bits:
            found = found + [swap(a, "ctx", n_ctx, bit) for a in found]
        return found

    def send(blocks, back):
        if not shifted:
            whole = blocks[0].reshape(n_exp, capacity, half_width)
            whole = lax.all_to_all(whole, "exp", 0, 0, tiled=True)
            return [whole.reshape(slots, half_width)]
        moved = [blocks[0]]
        for k in range(1, n_exp):
            shift = n_exp - k if back else k
            moved.append(
                lax.ppermute(blocks[k], "exp", [(i, (i + shift) % n_exp) for i in range(n_exp)])
            )
        return moved

    w_in = expert_in[0].reshape(depth, 2 * inner)
    w_first = lax.dynamic_slice_in_dim(w_in, grp * in_third, in_third, 1)
    w_first = swap(after(w_first, kv_far), "ctx", n_ctx, top)
    w_direct = swap(after(w_in[:, 2 * in_third :], kv_far), "ctx", n_ctx, top)
    w_in_a = spread(after(w_in, kvs[-1]))

    att_a, packed_a = attention(
        meta,
        tree_parents,
        after(queries[0], w_in_a[-1]),
        route_row,
        kvs,
        n_exp,
        capacity,
        blocks_out,
        0,
    )
    rows_a = send(packed_a, False)
    att_b, packed_b = attention(
        meta,
        tree_parents,
        after(queries[0], att_a),
        route_row,
        kvs,
        n_exp,
        capacity,
        blocks_out,
        1,
    )
    rows_b = send([after(x, *rows_a) for x in packed_b], False)

    w_second = swap(after(w_first, *rows_a), "grp", 2, 1)
    scaled_a, squares_a = prepare(meta, gain, rows_a, slots, 0)
    sums = first_half(meta, scaled_a, w_in_a, [(r, zero) for r in in_row], inner)
    w_in_b = [spread(after(w_first, *rows_b))]
    w_out_a = spread(after(w_out, *rows_b))
    v_first = lax.dynamic_slice_in_dim(w_out, grp * out_third, out_third, 0)
    v_first = swap(after(v_first, *rows_b), "ctx", n_ctx, top)
    w_in_b.append(spread(after(w_direct, *rows_b)))
    w_in_b.append(spread(after(w_second, *rows_b)))
    w_in_b = list(zip(w_in_b[0], w_in_b[2], w_in_b[1]))
    scaled_b, squares_b = prepare(meta, gain, rows_b, slots, 1)

    in_pieces = [(r, c) for r in in_row for c in in_cols]
    hidden, out_a = second_half(
        meta,
        scaled_b,
        sums,
        squares_a,
        squares_b,
        [w for shard_pieces in w_in_b for w in shard_pieces],
        in_pieces,
        w_out_a,
        [(zero, c) for c in out_col],
        blocks_out,
    )
    back_a = send(out_a, True)
    v_direct = swap(after(w_out[2 * out_third :], hidden), "ctx", n_ctx, top)
    v_second = swap(after(v_first, hidden), "grp", 2, 1)
    w_out_b = list(zip(*[spread(after(v, *back_a)) for v in (v_first, v_second, v_direct)]))
    out_b = down_half(
        meta,
        after(hidden, *out_a),
        [w for shard_pieces in w_out_b for w in shard_pieces],
        [(r, c) for c in out_col for r in out_rows],
        blocks_out,
        half_width,
    )
    back_b = send(out_b, True)
    done = combine(meta, att_a, route_row, weight_row, back_a, n_exp, capacity, None)
    done = combine(meta, att_b, route_row, weight_row, back_b, n_exp, capacity, done)
    return done[None]


def solution(mesh):
    in_specs = (
        P(("grp", "exp"), "ctx", None),
        P(("grp", "exp"), "ctx", None),
        P(("grp", "exp"), "ctx", None),
        P(("grp", "exp"), None),
        P(("grp", "exp"), "ctx", None),
        P(("grp", "exp"), "ctx", None),
        P(),
        P("exp", "ctx", None, None),
        P("exp", None, "ctx"),
    )
    out_specs = P(("grp", "exp"), "ctx", None)
    return jax.shard_map(body, mesh=mesh, in_specs=in_specs, out_specs=out_specs, check_vma=False)
```

time: 234 us -> 119 us (0.51)
  blocking collectives: 115 us -> 0 us
  starting transfers between devices: 3.58 us -> 34.8 us
  local copies, waits for them, and re-layouts: 27.3 us -> 7.59 us
  matrix products: 19.7 us -> 0 us
  Pallas kernels: 0 us -> 18.2 us
  waiting for transfers between devices: 42 us -> 57.5 us
  between operations: 13.6 us -> 0.16 us
  other arithmetic: 12.2 us -> 0.88 us
    all_to_all x3 -> x0, blocking collectives: 92.1 us -> none  [the longest x1 36.6 us: body(): lax.all_to_all(outgoing, 'exp', split_axis=0, concat_axis=0, tiled=True)]
    ppermute x0 -> x29, waiting for transfers between devices: none -> 57.5 us  [the longest x12 35.2 us: send(): lax.ppermute(blocks[k], 'exp', [(i, (i + shift) % n_exp) for i in range(n...]
    ppermute x0 -> x29, starting transfers between devices: none -> 34.8 us  [the longest x12 21.5 us: send(): lax.ppermute(blocks[k], 'exp', [(i, (i + shift) % n_exp) for i in range(n...]
    reduce_scatter x1 -> x0, waiting for transfers between devices: 29 us -> none  [body(): lax.psum_scatter(jnp.dot(feature_cols, gate_up_weight, preferred_element_...]
    all_gather x3 -> x0, blocking collectives: 22.4 us -> none  [the longest x1 9.27 us: body(): lax.all_gather(hidden, 'ctx', axis=0, tiled=True)]
    dot_general x17 -> x0, matrix products: 19.7 us -> none  [the longest x4 6.05 us: update(): jnp.einsum('gjtn,ngd->gjtd', exp_scores, value_heads, preferred_element_t...]
    pallas_call x0 -> x9, Pallas kernels: none -> 18.2 us  [call(): pl.pallas_call(kernel, in_specs=specs, out_specs=[VMEM] * len(outs), out_...]
    all_to_all x1 -> x0, waiting for transfers between devices: 13 us -> none  [body(): lax.all_to_all(column_rows, 'ctx', split_axis=1, concat_axis=0, tiled=True)]
  transfers between devices with their start and end apart: 2 -> 29, of which waited for: 2 -> 15; matrix products, arithmetic and copies ran while one was open for 2% -> 5% of each run, Pallas kernels for 0% -> 13%
where the time goes in v2:
time: 119 us
  waiting for transfers between devices  57.5 us (48%)
  starting transfers between devices  34.8 us (29%)
  Pallas kernels  18.2 us (15%)
  local copies, waits for them, and re-layouts  7.59 us (6%)
    ppermute x12, waiting for transfers between devices, send(): lax.ppermute(blocks[k], 'exp', [(i, (i + shift) % n_exp) for i in range(n...  35.2 us
    ppermute x17, waiting for transfers between devices, swap(): return lax.ppermute(array, axis, [(i, i ^ bit) for i in range(size)])  22.3 us
    ppermute x12, starting transfers between devices, send(): lax.ppermute(blocks[k], 'exp', [(i, (i + shift) % n_exp) for i in range(n...  21.5 us
    pallas_call x9, Pallas kernels, call(): pl.pallas_call(kernel, in_specs=specs, out_specs=[VMEM] * len(outs), out_...  18.2 us
    ppermute x17, starting transfers between devices, swap(): return lax.ppermute(array, axis, [(i, i ^ bit) for i in range(size)])  13.3 us
    unnamed x17, local copies, waits for them, and re-layouts  3.72 us
  transfers between devices with their start and end apart: 29, of which 15 were waited for; matrix products, arithmetic and copies ran while one was open for 5% of the time, Pallas kernels for 13%

profile of v2, /device:TPU:0, one launch (start us, length us, event | category | flops | bytes accessed | tf_op | source)
XLA Modules:
  0.0 119.1 jit_solution(13363925717423856135)
XLA Ops:
  0.9 3.0 %collective-permute-start = (bf16[128,512]{1,0:T(8,128)(2,1)S(1)}, bf16[128,512]{1,0:T(8,128)(2,1)S(1)}, u32[]{:S(2)}, u32[]{:S(2)}) collective-permute-start(bf16[128,512]{1,0:T(8,128)(2,1)S(1)} %pad_maximum_fusion.refs_0_), channel_id=1, source_target_pairs={{0,8},{4,12},{8,0},{12,4},{1,9},{5,13},{9,1},{13,5},{2,10},{6,14},... | collective-permute-start | bytes 393224 | tf_op jit(solution)/shard_map/ppermute | solution.py:275
  3.9 3.5 %collective-permute-done.refs_2_ = bf16[128,512]{1,0:T(8,128)(2,1)S(1)} collective-permute-done((bf16[128,512]{1,0:T(8,128)(2,1)S(1)}, bf16[128,512]{1,0:T(8,128)(2,1)S(1)}, u32[]{:S(2)}, u32[]{:S(2)}) %collective-permute-start) | collective-permute-done | bytes 131104 | tf_op jit(solution)/shard_map/ppermute | solution.py:275
  7.4 2.5 %copy.10 = bf16[128,8,2,768]{3,1,2,0:T(8,128)(2,1)S(1)} copy(bf16[128,8,2,768]{3,2,1,0:T(2,128)(2,1)} %bitcast.39) | data formatting | bytes 6291456
  10.5 1.5 %fusion = (bf16[1024,512]{1,0:T(8,128)(2,1)}, bf16[1024,512]{1,0:T(8,128)(2,1)}) fusion(bf16[1024,1536]{1,0:T(8,128)(2,1)S(1)} %bitcast.25, s32[]{:T(128)S(6)} %select_n.12), kind=kLoop, calls=%fused_computation.4 | loop fusion | bytes 4194308 | tf_op jit(solution)/shard_map/slice | solution.py:352
  12.0 1.7 %collective-permute-start.10 = (bf16[1024,512]{1,0:T(8,128)(2,1)}, bf16[1024,512]{1,0:T(8,128)(2,1)}, u32[]{:S(2)}, u32[]{:S(2)}) collective-permute-start(bf16[1024,512]{1,0:T(8,128)(2,1)} %get-tuple-element.70), channel_id=1, source_target_pairs={{0,8},{4,12},{8,0},{12,4},{1,9},{5,13},{9,1},{13,5},{2,10},{6,14},... | collective-permute-start | bytes 3145736 | tf_op jit(solution)/shard_map/ppermute | solution.py:275
  13.7 2.3 %slice_bitcast_fusion = (bf16[256,1024]{1,0:T(8,128)(2,1)}, bf16[256,1024]{1,0:T(8,128)(2,1)}) fusion(bf16[1,768,1024]{2,1,0:T(8,128)(2,1)} %param.17, s32[]{:T(128)S(6)} %select_n.13), kind=kLoop, calls=%fused_computation | loop fusion | bytes 2097156 | tf_op jit(solution)/shard_map/slice | solution.py:406
  17.7 2.9 %attend_a.1 = (bf16[128,2048]{1,0:T(8,128)(2,1)S(1)}, bf16[40,2048]{1,0:T(8,128)(2,1)S(1)}, bf16[40,2048]{1,0:T(8,128)(2,1)S(1)}, bf16[40,2048]{1,0:T(8,128)(2,1)S(1)}, bf16[40,2048]{1,0:T(8,128)(2,1)S(1)}) custom-call(s32[14]{0:T(128)S(1)} %stack.41.meta, s32[1,4]{1,0:T(1,128)S(1)} %copy-done.3, bf16[128,4096]{1,0:T(8,128)(2,1)S(1)} %bitcast.29, ...), custom_call_target="tpu_custom_call" | custom-call | flops 2000000000 | bytes 1000 | tf_op jit(solution)/shard_map/attend_a/pallas_call | solution.py:21
  20.5 1.9 %collective-permute-start.4 = (bf16[40,2048]{1,0:T(8,128)(2,1)S(1)}, bf16[40,2048]{1,0:T(8,128)(2,1)S(1)}, u32[]{:S(2)}, u32[]{:S(2)}) collective-permute-start(bf16[40,2048]{1,0:T(8,128)(2,1)S(1)} %get-tuple-element.56), channel_id=1, source_target_pairs={{0,1},{1,2},{2,3},{3,0},{4,5},{5,6},{6,7},{7,4},{8,9},{9,10},{10,1... | collective-permute-start | bytes 491528 | tf_op jit(solution)/shard_map/ppermute | solution.py:345
  22.4 2.6 %collective-permute-start.5 = (bf16[40,2048]{1,0:T(8,128)(2,1)S(1)}, bf16[40,2048]{1,0:T(8,128)(2,1)S(1)}, u32[]{:S(2)}, u32[]{:S(2)}) collective-permute-start(bf16[40,2048]{1,0:T(8,128)(2,1)S(1)} %get-tuple-element.57), channel_id=1, source_target_pairs={{0,2},{1,3},{2,0},{3,1},{4,6},{5,7},{6,4},{7,5},{8,10},{9,11},{10,... | collective-permute-start | bytes 491528 | tf_op jit(solution)/shard_map/ppermute | solution.py:345
  25.0 1.4 %collective-permute-start.6 = (bf16[40,2048]{1,0:T(8,128)(2,1)S(1)}, bf16[40,2048]{1,0:T(8,128)(2,1)S(1)}, u32[]{:S(2)}, u32[]{:S(2)}) collective-permute-start(bf16[40,2048]{1,0:T(8,128)(2,1)S(1)} %get-tuple-element.58), channel_id=1, source_target_pairs={{0,3},{1,0},{2,1},{3,2},{4,7},{5,4},{6,5},{7,6},{8,11},{9,8},{10,9... | collective-permute-start | bytes 491528 | tf_op jit(solution)/shard_map/ppermute | solution.py:345
  26.4 2.9 %attend_b.1 = (bf16[128,2048]{1,0:T(8,128)(2,1)S(1)}, bf16[40,2048]{1,0:T(8,128)(2,1)S(1)}, bf16[40,2048]{1,0:T(8,128)(2,1)S(1)}, bf16[40,2048]{1,0:T(8,128)(2,1)S(1)}, bf16[40,2048]{1,0:T(8,128)(2,1)S(1)}) custom-call(s32[14]{0:T(128)S(1)} %stack.41.meta, s32[1,4]{1,0:T(1,128)S(1)} %copy-done.3, bf16[128,4096]{1,0:T(8,128)(2,1)S(1)} %bitcast.30, ...), custom_call_target="tpu_custom_call" | custom-call | flops 2000000000 | bytes 1000 | tf_op jit(solution)/shard_map/attend_b/pallas_call | solution.py:21
  29.5 6.6 %collective-permute-done.5.refs_2_ = bf16[40,2048]{1,0:T(8,128)(2,1)S(1)} collective-permute-done((bf16[40,2048]{1,0:T(8,128)(2,1)S(1)}, bf16[40,2048]{1,0:T(8,128)(2,1)S(1)}, u32[]{:S(2)}, u32[]{:S(2)}) %collective-permute-start.5) | collective-permute-done | bytes 163872 | tf_op jit(solution)/shard_map/ppermute | solution.py:345
  36.2 4.0 %collective-permute-start.7 = (bf16[40,2048]{1,0:T(8,128)(2,1)S(1)}, bf16[40,2048]{1,0:T(8,128)(2,1)S(1)}, u32[]{:S(2)}, u32[]{:S(2)}) collective-permute-start(bf16[40,2048]{1,0:T(8,128)(2,1)S(1)} %get-tuple-element.61), channel_id=1, source_target_pairs={{0,1},{1,2},{2,3},{3,0},{4,5},{5,6},{6,7},{7,4},{8,9},{9,10},{10,1... | collective-permute-start | bytes 491528 | tf_op jit(solution)/shard_map/ppermute | solution.py:345
  40.1 1.6 %collective-permute-start.8 = (bf16[40,2048]{1,0:T(8,128)(2,1)S(1)}, bf16[40,2048]{1,0:T(8,128)(2,1)S(1)}, u32[]{:S(2)}, u32[]{:S(2)}) collective-permute-start(bf16[40,2048]{1,0:T(8,128)(2,1)S(1)} %get-tuple-element.63), channel_id=1, source_target_pairs={{0,2},{1,3},{2,0},{3,1},{4,6},{5,7},{6,4},{7,5},{8,10},{9,11},{10,... | collective-permute-start | bytes 491528 | tf_op jit(solution)/shard_map/ppermute | solution.py:345
  42.5 1.5 %collective-permute-start.11 = (bf16[1024,512]{1,0:T(8,128)(2,1)}, bf16[1024,512]{1,0:T(8,128)(2,1)S(1)}, u32[]{:S(2)}, u32[]{:S(2)}) collective-permute-start(bf16[1024,512]{1,0:T(8,128)(2,1)} %collective-permute-done.10.refs_0_), channel_id=1, source_target_pairs={{0,16},{16,0},{1,17},{17,1},{2,18},{18,2},{3,19},{19,3},{4,20},{20... | collective-permute-start | bytes 3145736 | tf_op jit(solution)/shard_map/ppermute | solution.py:275
  44.8 3.2 %gate_up_a.1.start_ref = f32[160,1536]{1,0:T(8,128)S(1)} custom-call(s32[14]{0:T(128)S(1)} %stack.41.meta, bf16[160,2048]{1,0:T(8,128)(2,1)S(1)} %get-tuple-element.67.rows_ref, bf16[1024,1536]{1,0:T(8,128)(2,1)S(1)} %bitcast.26, bf16[1024,1536]{1,0:T(8,128)(2,1)} %collective-permute-done.2.refs_1_), custom_call_target="tpu_custom_call" | custom-call | flops 1000 | bytes 1000 | tf_op jit(solution)/shard_map/gate_up_a/pallas_call | solution.py:21
  48.1 4.0 %collective-permute-done.8.refs_2_ = bf16[40,2048]{1,0:T(8,128)(2,1)S(1)} collective-permute-done((bf16[40,2048]{1,0:T(8,128)(2,1)S(1)}, bf16[40,2048]{1,0:T(8,128)(2,1)S(1)}, u32[]{:S(2)}, u32[]{:S(2)}) %collective-permute-start.8) | collective-permute-done | bytes 163872 | tf_op jit(solution)/shard_map/ppermute | solution.py:345
  52.1 7.7 %collective-permute-done.12.refs_2_ = bf16[1024,512]{1,0:T(8,128)(2,1)S(1)} collective-permute-done((bf16[1024,512]{1,0:T(8,128)(2,1)}, bf16[1024,512]{1,0:T(8,128)(2,1)S(1)}, u32[]{:S(2)}, u32[]{:S(2)}) %collective-permute-start.12) | collective-permute-done | bytes 1048608 | tf_op jit(solution)/shard_map/ppermute | solution.py:275
  60.3 1.8 %collective-permute-start.17 = (bf16[256,1024]{1,0:T(8,128)(2,1)S(1)}, bf16[256,1024]{1,0:T(8,128)(2,1)S(1)}, u32[]{:S(2)}, u32[]{:S(2)}) collective-permute-start(bf16[256,1024]{1,0:T(8,128)(2,1)S(1)} %copy-done.7), channel_id=1, source_target_pairs={{0,8},{4,12},{8,0},{12,4},{1,9},{5,13},{9,1},{13,5},{2,10},{6,14},... | collective-permute-start | bytes 1572872 | tf_op jit(solution)/shard_map/ppermute | solution.py:275
  62.1 5.2 %collective-permute-done.11.refs_1_ = bf16[1024,512]{1,0:T(8,128)(2,1)S(1)} collective-permute-done((bf16[1024,512]{1,0:T(8,128)(2,1)}, bf16[1024,512]{1,0:T(8,128)(2,1)S(1)}, u32[]{:S(2)}, u32[]{:S(2)}) %collective-permute-start.11) | collective-permute-done | bytes 1048608 | tf_op jit(solution)/shard_map/ppermute | solution.py:275
  68.2 1.8 %collective-permute-done.14.refs_4_ = bf16[1024,512]{1,0:T(8,128)(2,1)S(1)} collective-permute-done((bf16[1024,512]{1,0:T(8,128)(2,1)S(1)}, bf16[1024,512]{1,0:T(8,128)(2,1)S(1)}, u32[]{:S(2)}, u32[]{:S(2)}) %collective-permute-start.14) | collective-permute-done | bytes 1048608 | tf_op jit(solution)/shard_map/ppermute | solution.py:275
  70.0 3.3 %gate_up_b_down_a.1 = (bf16[160,768]{1,0:T(8,128)(2,1)S(1)}, bf16[40,2048]{1,0:T(8,128)(2,1)S(1)}, bf16[40,2048]{1,0:T(8,128)(2,1)S(1)}, bf16[40,2048]{1,0:T(8,128)(2,1)S(1)}, bf16[40,2048]{1,0:T(8,128)(2,1)S(1)}) custom-call(s32[14]{0:T(128)S(1)} %stack.41.meta, bf16[160,2048]{1,0:T(8,128)(2,1)S(1)} %get-tuple-element.66.rows_ref, ...), custom_call_target="tpu_custom_call" | custom-call | flops 20000000000 | bytes 1000 | tf_op jit(solution)/shard_map/gate_up_b_down_a/pallas_call | solution.py:21
  74.6 1.7 %collective-permute-start.21 = (bf16[256,1024]{1,0:T(8,128)(2,1)S(1)}, bf16[256,1024]{1,0:T(8,128)(2,1)S(1)}, u32[]{:S(2)}, u32[]{:S(2)}) collective-permute-start(bf16[256,1024]{1,0:T(8,128)(2,1)S(1)} %collective-permute-done.17.refs_0_), channel_id=1, source_target_pairs={{0,16},{16,0},{1,17},{17,1},{2,18},{18,2},{3,19},{19,3},{4,20},{20... | collective-permute-start | bytes 1572872 | tf_op jit(solution)/shard_map/ppermute | solution.py:275
  76.4 1.5 %collective-permute-start.22 = (bf16[256,1024]{1,0:T(8,128)(2,1)S(1)}, bf16[256,1024]{1,0:T(8,128)(2,1)S(1)}, u32[]{:S(2)}, u32[]{:S(2)}) collective-permute-start(bf16[256,1024]{1,0:T(8,128)(2,1)S(1)} %copy-done.6), channel_id=1, source_target_pairs={{0,8},{4,12},{8,0},{12,4},{1,9},{5,13},{9,1},{13,5},{2,10},{6,14},... | collective-permute-start | bytes 1572872 | tf_op jit(solution)/shard_map/ppermute | solution.py:275
  77.9 3.6 %collective-permute-start.18 = (bf16[40,2048]{1,0:T(8,128)(2,1)S(1)}, bf16[40,2048]{1,0:T(8,128)(2,1)S(1)}, u32[]{:S(2)}, u32[]{:S(2)}) collective-permute-start(bf16[40,2048]{1,0:T(8,128)(2,1)S(1)} %get-tuple-element.80), channel_id=1, source_target_pairs={{0,3},{1,0},{2,1},{3,2},{4,7},{5,4},{6,5},{7,6},{8,11},{9,8},{10,9... | collective-permute-start | bytes 491528 | tf_op jit(solution)/shard_map/ppermute | solution.py:345
  82.5 3.6 %collective-permute-done.18.refs_1_ = bf16[40,2048]{1,0:T(8,128)(2,1)S(1)} collective-permute-done((bf16[40,2048]{1,0:T(8,128)(2,1)S(1)}, bf16[40,2048]{1,0:T(8,128)(2,1)S(1)}, u32[]{:S(2)}, u32[]{:S(2)}) %collective-permute-start.18) | collective-permute-done | bytes 163872 | tf_op jit(solution)/shard_map/ppermute | solution.py:345
  86.1 8.6 %collective-permute-done.19.refs_2_ = bf16[40,2048]{1,0:T(8,128)(2,1)S(1)} collective-permute-done((bf16[40,2048]{1,0:T(8,128)(2,1)S(1)}, bf16[40,2048]{1,0:T(8,128)(2,1)S(1)}, u32[]{:S(2)}, u32[]{:S(2)}) %collective-permute-start.19) | collective-permute-done | bytes 163872 | tf_op jit(solution)/shard_map/ppermute | solution.py:345
  95.3 1.3 %collective-permute-done.23.refs_3_ = bf16[256,1024]{1,0:T(8,128)(2,1)S(1)} collective-permute-done((bf16[256,1024]{1,0:T(8,128)(2,1)S(1)}, bf16[256,1024]{1,0:T(8,128)(2,1)S(1)}, u32[]{:S(2)}, u32[]{:S(2)}) %collective-permute-start.23) | collective-permute-done | bytes 524320 | tf_op jit(solution)/shard_map/ppermute | solution.py:275
  100.3 1.8 %collective-permute-start.27 = (bf16[40,2048]{1,0:T(8,128)(2,1)S(1)}, bf16[40,2048]{1,0:T(8,128)(2,1)S(1)}, u32[]{:S(2)}, u32[]{:S(2)}) collective-permute-start(bf16[40,2048]{1,0:T(8,128)(2,1)S(1)} %get-tuple-element.90), channel_id=1, source_target_pairs={{0,2},{1,3},{2,0},{3,1},{4,6},{5,7},{6,4},{7,5},{8,10},{9,11},{10,... | collective-permute-start | bytes 491528 | tf_op jit(solution)/shard_map/ppermute | solution.py:345
  102.1 1.9 %collective-permute-start.28 = (bf16[40,2048]{1,0:T(8,128)(2,1)S(1)}, bf16[40,2048]{1,0:T(8,128)(2,1)S(1)}, u32[]{:S(2)}, u32[]{:S(2)}) collective-permute-start(bf16[40,2048]{1,0:T(8,128)(2,1)S(1)} %get-tuple-element.91), channel_id=1, source_target_pairs={{0,1},{1,2},{2,3},{3,0},{4,5},{5,6},{6,7},{7,4},{8,9},{9,10},{10,1... | collective-permute-start | bytes 491528 | tf_op jit(solution)/shard_map/ppermute | solution.py:345
  105.7 11.4 %collective-permute-done.27.refs_2_ = bf16[40,2048]{1,0:T(8,128)(2,1)S(1)} collective-permute-done((bf16[40,2048]{1,0:T(8,128)(2,1)S(1)}, bf16[40,2048]{1,0:T(8,128)(2,1)S(1)}, u32[]{:S(2)}, u32[]{:S(2)}) %collective-permute-start.27) | collective-permute-done | bytes 163872 | tf_op jit(solution)/shard_map/ppermute | solution.py:345
  117.1 2.0 %combine_b.1 = bf16[128,4096]{1,0:T(8,128)(2,1)} custom-call(s32[14]{0:T(128)S(1)} %stack.41.meta, bf16[128,2048]{1,0:T(8,128)(2,1)S(1)} %get-tuple-element.53.att_ref, s32[1,128]{1,0:T(1,128)S(1)} %bitcast.36, f32[1,128]{1,0:T(1,128)S(1)} %bitcast.38, bf16[40,2048]{1,0:T(8,128)(2,1)S(1)} %get-tuple-element.88.refs_0_, ...), custom_call_target="tpu_custom_call" | custom-call | flops 20000000000 | bytes 1000 | tf_op jit(solution)/shard_map/combine_b/pallas_call | solution.py:21
  (56 shorter events, 14.5 us)
Async XLA Ops:
  0.9 6.5 %collective-permute-start = (bf16[128,512]{1,0:T(8,128)(2,1)S(1)}, bf16[128,512]{1,0:T(8,128)(2,1)S(1)}, u32[]{:S(2)}, u32[]{:S(2)}) collective-permute-start(bf16[128,512]{1,0:T(8,128)(2,1)S(1)} %pad_maximum_fusion.refs_0_), channel_id=1, source_target_pairs={{0,8},{4,12},{8,0},{12,4},{1,9},{5,13},{9,1},{13,5},{2,10},{6,14},... | collective-permute-start | bytes 393224 | tf_op jit(solution)/shard_map/ppermute | solution.py:275
  7.4 2.5 %collective-permute-start.1 = (bf16[128,512]{1,0:T(8,128)(2,1)S(1)}, bf16[128,512]{1,0:T(8,128)(2,1)S(1)}, u32[]{:S(2)}, u32[]{:S(2)}) collective-permute-start(bf16[128,512]{1,0:T(8,128)(2,1)S(1)} %collective-permute-done.refs_2_), channel_id=1, source_target_pairs={{0,4},{4,0},{8,12},{12,8},{1,5},{5,1},{9,13},{13,9},{2,6},{6,2},{1... | collective-permute-start | bytes 393224 | tf_op jit(solution)/shard_map/ppermute | solution.py:275
  9.9 6.5 %collective-permute-start.2 = (bf16[1024,1536]{1,0:T(8,128)(2,1)S(1)}, bf16[1024,1536]{1,0:T(8,128)(2,1)}, u32[]{:S(2)}, u32[]{:S(2)}) collective-permute-start(bf16[1024,1536]{1,0:T(8,128)(2,1)S(1)} %bitcast.24), channel_id=1, source_target_pairs={{0,4},{4,0},{8,12},{12,8},{1,5},{5,1},{9,13},{13,9},{2,6},{6,2},{1... | collective-permute-start | bytes 9437192 | tf_op jit(solution)/shard_map/ppermute | solution.py:275
  12.0 30.5 %collective-permute-start.10 = (bf16[1024,512]{1,0:T(8,128)(2,1)}, bf16[1024,512]{1,0:T(8,128)(2,1)}, u32[]{:S(2)}, u32[]{:S(2)}) collective-permute-start(bf16[1024,512]{1,0:T(8,128)(2,1)} %get-tuple-element.70), channel_id=1, source_target_pairs={{0,8},{4,12},{8,0},{12,4},{1,9},{5,13},{9,1},{13,5},{2,10},{6,14},... | collective-permute-start | bytes 3145736 | tf_op jit(solution)/shard_map/ppermute | solution.py:275
  13.7 2.7 %collective-permute-start.3 = (bf16[128,512]{1,0:T(8,128)(2,1)S(1)}, bf16[128,512]{1,0:T(8,128)(2,1)}, u32[]{:S(2)}, u32[]{:S(2)}) collective-permute-start(bf16[128,512]{1,0:T(8,128)(2,1)S(1)} %pad_maximum_fusion.refs_0_), channel_id=1, source_target_pairs={{0,4},{4,0},{8,12},{12,8},{1,5},{5,1},{9,13},{13,9},{2,6},{6,2},{1... | collective-permute-start | bytes 393224 | tf_op jit(solution)/shard_map/ppermute | solution.py:275
  16.1 43.7 %collective-permute-start.12 = (bf16[1024,512]{1,0:T(8,128)(2,1)}, bf16[1024,512]{1,0:T(8,128)(2,1)S(1)}, u32[]{:S(2)}, u32[]{:S(2)}) collective-permute-start(bf16[1024,512]{1,0:T(8,128)(2,1)} %get-tuple-element.74), channel_id=1, source_target_pairs={{0,8},{4,12},{8,0},{12,4},{1,9},{5,13},{9,1},{13,5},{2,10},{6,14},... | collective-permute-start | bytes 3145736 | tf_op jit(solution)/shard_map/ppermute | solution.py:275
  20.5 9.0 %collective-permute-start.4 = (bf16[40,2048]{1,0:T(8,128)(2,1)S(1)}, bf16[40,2048]{1,0:T(8,128)(2,1)S(1)}, u32[]{:S(2)}, u32[]{:S(2)}) collective-permute-start(bf16[40,2048]{1,0:T(8,128)(2,1)S(1)} %get-tuple-element.56), channel_id=1, source_target_pairs={{0,1},{1,2},{2,3},{3,0},{4,5},{5,6},{6,7},{7,4},{8,9},{9,10},{10,1... | collective-permute-start | bytes 491528 | tf_op jit(solution)/shard_map/ppermute | solution.py:345
  22.4 13.7 %collective-permute-start.5 = (bf16[40,2048]{1,0:T(8,128)(2,1)S(1)}, bf16[40,2048]{1,0:T(8,128)(2,1)S(1)}, u32[]{:S(2)}, u32[]{:S(2)}) collective-permute-start(bf16[40,2048]{1,0:T(8,128)(2,1)S(1)} %get-tuple-element.57), channel_id=1, source_target_pairs={{0,2},{1,3},{2,0},{3,1},{4,6},{5,7},{6,4},{7,5},{8,10},{9,11},{10,... | collective-permute-start | bytes 491528 | tf_op jit(solution)/shard_map/ppermute | solution.py:345
  25.0 19.0 %copy-start.2 = (f32[4096]{0:T(1024)S(1)}, f32[4096]{0:T(1024)}, u32[]{:S(2)}) copy-start(f32[4096]{0:T(1024)} %param.15) | copy-start | bytes 49156
  25.0 11.1 %collective-permute-start.6 = (bf16[40,2048]{1,0:T(8,128)(2,1)S(1)}, bf16[40,2048]{1,0:T(8,128)(2,1)S(1)}, u32[]{:S(2)}, u32[]{:S(2)}) collective-permute-start(bf16[40,2048]{1,0:T(8,128)(2,1)S(1)} %get-tuple-element.58), channel_id=1, source_target_pairs={{0,3},{1,0},{2,1},{3,2},{4,7},{5,4},{6,5},{7,6},{8,11},{9,8},{10,9... | collective-permute-start | bytes 491528 | tf_op jit(solution)/shard_map/ppermute | solution.py:345
  36.2 11.9 %collective-permute-start.7 = (bf16[40,2048]{1,0:T(8,128)(2,1)S(1)}, bf16[40,2048]{1,0:T(8,128)(2,1)S(1)}, u32[]{:S(2)}, u32[]{:S(2)}) collective-permute-start(bf16[40,2048]{1,0:T(8,128)(2,1)S(1)} %get-tuple-element.61), channel_id=1, source_target_pairs={{0,1},{1,2},{2,3},{3,0},{4,5},{5,6},{6,7},{7,4},{8,9},{9,10},{10,1... | collective-permute-start | bytes 491528 | tf_op jit(solution)/shard_map/ppermute | solution.py:345
  40.1 11.9 %collective-permute-start.8 = (bf16[40,2048]{1,0:T(8,128)(2,1)S(1)}, bf16[40,2048]{1,0:T(8,128)(2,1)S(1)}, u32[]{:S(2)}, u32[]{:S(2)}) collective-permute-start(bf16[40,2048]{1,0:T(8,128)(2,1)S(1)} %get-tuple-element.63), channel_id=1, source_target_pairs={{0,2},{1,3},{2,0},{3,1},{4,6},{5,7},{6,4},{7,5},{8,10},{9,11},{10,... | collective-permute-start | bytes 491528 | tf_op jit(solution)/shard_map/ppermute | solution.py:345
  41.8 10.3 %collective-permute-start.9 = (bf16[40,2048]{1,0:T(8,128)(2,1)S(1)}, bf16[40,2048]{1,0:T(8,128)(2,1)S(1)}, u32[]{:S(2)}, u32[]{:S(2)}) collective-permute-start(bf16[40,2048]{1,0:T(8,128)(2,1)S(1)} %get-tuple-element.65), channel_id=1, source_target_pairs={{0,3},{1,0},{2,1},{3,2},{4,7},{5,4},{6,5},{7,6},{8,11},{9,8},{10,9... | collective-permute-start | bytes 491528 | tf_op jit(solution)/shard_map/ppermute | solution.py:345
  42.5 24.8 %collective-permute-start.11 = (bf16[1024,512]{1,0:T(8,128)(2,1)}, bf16[1024,512]{1,0:T(8,128)(2,1)S(1)}, u32[]{:S(2)}, u32[]{:S(2)}) collective-permute-start(bf16[1024,512]{1,0:T(8,128)(2,1)} %collective-permute-done.10.refs_0_), channel_id=1, source_target_pairs={{0,16},{16,0},{1,17},{17,1},{2,18},{18,2},{3,19},{19,3},{4,20},{20... | collective-permute-start | bytes 3145736 | tf_op jit(solution)/shard_map/ppermute | solution.py:275
  44.8 15.5 %copy-start.7 = (bf16[256,1024]{1,0:T(8,128)(2,1)S(1)}, bf16[256,1024]{1,0:T(8,128)(2,1)}, u32[]{:S(2)}) copy-start(bf16[256,1024]{1,0:T(8,128)(2,1)} %get-tuple-element.78) | copy-start | bytes 1572868
  59.8 8.4 %collective-permute-start.13 = (bf16[1024,512]{1,0:T(8,128)(2,1)}, bf16[1024,512]{1,0:T(8,128)(2,1)S(1)}, u32[]{:S(2)}, u32[]{:S(2)}) collective-permute-start(bf16[1024,512]{1,0:T(8,128)(2,1)} %collective-permute-done.10.refs_0_), channel_id=1, source_target_pairs={{0,4},{4,0},{8,12},{12,8},{1,5},{5,1},{9,13},{13,9},{2,6},{6,2},{1... | collective-permute-start | bytes 3145736 | tf_op jit(solution)/shard_map/ppermute | solution.py:275
  59.8 8.4 %collective-permute-start.15 = (bf16[1024,512]{1,0:T(8,128)(2,1)S(1)}, bf16[1024,512]{1,0:T(8,128)(2,1)S(1)}, u32[]{:S(2)}, u32[]{:S(2)}) collective-permute-start(bf16[1024,512]{1,0:T(8,128)(2,1)S(1)} %collective-permute-done.12.refs_2_), channel_id=1, source_target_pairs={{0,4},{4,0},{8,12},{12,8},{1,5},{5,1},{9,13},{13,9},{2,6},{6,2},{1... | collective-permute-start | bytes 3145736 | tf_op jit(solution)/shard_map/ppermute | solution.py:275
  60.3 7.9 %collective-permute-start.16 = (bf16[768,1024]{1,0:T(8,128)(2,1)S(1)}, bf16[768,1024]{1,0:T(8,128)(2,1)S(1)}, u32[]{:S(2)}, u32[]{:S(2)}) collective-permute-start(bf16[768,1024]{1,0:T(8,128)(2,1)S(1)} %bitcast.27), channel_id=1, source_target_pairs={{0,4},{4,0},{8,12},{12,8},{1,5},{5,1},{9,13},{13,9},{2,6},{6,2},{1... | collective-permute-start | bytes 4718600 | tf_op jit(solution)/shard_map/ppermute | solution.py:275
  60.3 14.3 %collective-permute-start.17 = (bf16[256,1024]{1,0:T(8,128)(2,1)S(1)}, bf16[256,1024]{1,0:T(8,128)(2,1)S(1)}, u32[]{:S(2)}, u32[]{:S(2)}) collective-permute-start(bf16[256,1024]{1,0:T(8,128)(2,1)S(1)} %copy-done.7), channel_id=1, source_target_pairs={{0,8},{4,12},{8,0},{12,4},{1,9},{5,13},{9,1},{13,5},{2,10},{6,14},... | collective-permute-start | bytes 1572872 | tf_op jit(solution)/shard_map/ppermute | solution.py:275
  67.3 2.7 %collective-permute-start.14 = (bf16[1024,512]{1,0:T(8,128)(2,1)S(1)}, bf16[1024,512]{1,0:T(8,128)(2,1)S(1)}, u32[]{:S(2)}, u32[]{:S(2)}) collective-permute-start(bf16[1024,512]{1,0:T(8,128)(2,1)S(1)} %collective-permute-done.11.refs_1_), channel_id=1, source_target_pairs={{0,4},{4,0},{8,12},{12,8},{1,5},{5,1},{9,13},{13,9},{2,6},{6,2},{1... | collective-permute-start | bytes 3145736 | tf_op jit(solution)/shard_map/ppermute | solution.py:275
  73.3 30.8 %copy-start.5 = (f32[1,128,1]{1,2,0:T(1,128)S(1)}, f32[1,128,1]{1,2,0:T(1,128)}, u32[]{:S(2)}) copy-start(f32[1,128,1]{1,2,0:T(1,128)} %param.14) | copy-start | bytes 1540
  74.6 20.1 %collective-permute-start.21 = (bf16[256,1024]{1,0:T(8,128)(2,1)S(1)}, bf16[256,1024]{1,0:T(8,128)(2,1)S(1)}, u32[]{:S(2)}, u32[]{:S(2)}) collective-permute-start(bf16[256,1024]{1,0:T(8,128)(2,1)S(1)} %collective-permute-done.17.refs_0_), channel_id=1, source_target_pairs={{0,16},{16,0},{1,17},{17,1},{2,18},{18,2},{3,19},{19,3},{4,20},{20... | collective-permute-start | bytes 1572872 | tf_op jit(solution)/shard_map/ppermute | solution.py:275
  76.4 18.4 %collective-permute-start.22 = (bf16[256,1024]{1,0:T(8,128)(2,1)S(1)}, bf16[256,1024]{1,0:T(8,128)(2,1)S(1)}, u32[]{:S(2)}, u32[]{:S(2)}) collective-permute-start(bf16[256,1024]{1,0:T(8,128)(2,1)S(1)} %copy-done.6), channel_id=1, source_target_pairs={{0,8},{4,12},{8,0},{12,4},{1,9},{5,13},{9,1},{13,5},{2,10},{6,14},... | collective-permute-start | bytes 1572872 | tf_op jit(solution)/shard_map/ppermute | solution.py:275
  77.9 8.3 %collective-permute-start.18 = (bf16[40,2048]{1,0:T(8,128)(2,1)S(1)}, bf16[40,2048]{1,0:T(8,128)(2,1)S(1)}, u32[]{:S(2)}, u32[]{:S(2)}) collective-permute-start(bf16[40,2048]{1,0:T(8,128)(2,1)S(1)} %get-tuple-element.80), channel_id=1, source_target_pairs={{0,3},{1,0},{2,1},{3,2},{4,7},{5,4},{6,5},{7,6},{8,11},{9,8},{10,9... | collective-permute-start | bytes 491528 | tf_op jit(solution)/shard_map/ppermute | solution.py:345
  81.5 13.3 %collective-permute-start.19 = (bf16[40,2048]{1,0:T(8,128)(2,1)S(1)}, bf16[40,2048]{1,0:T(8,128)(2,1)S(1)}, u32[]{:S(2)}, u32[]{:S(2)}) collective-permute-start(bf16[40,2048]{1,0:T(8,128)(2,1)S(1)} %get-tuple-element.81), channel_id=1, source_target_pairs={{0,2},{1,3},{2,0},{3,1},{4,6},{5,7},{6,4},{7,5},{8,10},{9,11},{10,... | collective-permute-start | bytes 491528 | tf_op jit(solution)/shard_map/ppermute | solution.py:345
  81.5 13.3 %collective-permute-start.20 = (bf16[40,2048]{1,0:T(8,128)(2,1)S(1)}, bf16[40,2048]{1,0:T(8,128)(2,1)S(1)}, u32[]{:S(2)}, u32[]{:S(2)}) collective-permute-start(bf16[40,2048]{1,0:T(8,128)(2,1)S(1)} %get-tuple-element.82), channel_id=1, source_target_pairs={{0,1},{1,2},{2,3},{3,0},{4,5},{5,6},{6,7},{7,4},{8,9},{9,10},{10,1... | collective-permute-start | bytes 491528 | tf_op jit(solution)/shard_map/ppermute | solution.py:345
  94.7 1.9 %collective-permute-start.23 = (bf16[256,1024]{1,0:T(8,128)(2,1)S(1)}, bf16[256,1024]{1,0:T(8,128)(2,1)S(1)}, u32[]{:S(2)}, u32[]{:S(2)}) collective-permute-start(bf16[256,1024]{1,0:T(8,128)(2,1)S(1)} %collective-permute-done.17.refs_0_), channel_id=1, source_target_pairs={{0,4},{4,0},{8,12},{12,8},{1,5},{5,1},{9,13},{13,9},{2,6},{6,2},{1... | collective-permute-start | bytes 1572872 | tf_op jit(solution)/shard_map/ppermute | solution.py:275
  94.7 2.6 %collective-permute-start.24 = (bf16[256,1024]{1,0:T(8,128)(2,1)S(1)}, bf16[256,1024]{1,0:T(8,128)(2,1)S(1)}, u32[]{:S(2)}, u32[]{:S(2)}) collective-permute-start(bf16[256,1024]{1,0:T(8,128)(2,1)S(1)} %collective-permute-done.21.refs_1_), channel_id=1, source_target_pairs={{0,4},{4,0},{8,12},{12,8},{1,5},{5,1},{9,13},{13,9},{2,6},{6,2},{1... | collective-permute-start | bytes 1572872 | tf_op jit(solution)/shard_map/ppermute | solution.py:275
  95.2 2.9 %collective-permute-start.25 = (bf16[256,1024]{1,0:T(8,128)(2,1)S(1)}, bf16[256,1024]{1,0:T(8,128)(2,1)S(1)}, u32[]{:S(2)}, u32[]{:S(2)}) collective-permute-start(bf16[256,1024]{1,0:T(8,128)(2,1)S(1)} %collective-permute-done.22.refs_2_), channel_id=1, source_target_pairs={{0,4},{4,0},{8,12},{12,8},{1,5},{5,1},{9,13},{13,9},{2,6},{6,2},{1... | collective-permute-start | bytes 1572872 | tf_op jit(solution)/shard_map/ppermute | solution.py:275
  99.4 6.3 %collective-permute-start.26 = (bf16[40,2048]{1,0:T(8,128)(2,1)S(1)}, bf16[40,2048]{1,0:T(8,128)(2,1)S(1)}, u32[]{:S(2)}, u32[]{:S(2)}) collective-permute-start(bf16[40,2048]{1,0:T(8,128)(2,1)S(1)} %get-tuple-element.89), channel_id=1, source_target_pairs={{0,3},{1,0},{2,1},{3,2},{4,7},{5,4},{6,5},{7,6},{8,11},{9,8},{10,9... | collective-permute-start | bytes 491528 | tf_op jit(solution)/shard_map/ppermute | solution.py:345
  100.3 16.8 %collective-permute-start.27 = (bf16[40,2048]{1,0:T(8,128)(2,1)S(1)}, bf16[40,2048]{1,0:T(8,128)(2,1)S(1)}, u32[]{:S(2)}, u32[]{:S(2)}) collective-permute-start(bf16[40,2048]{1,0:T(8,128)(2,1)S(1)} %get-tuple-element.90), channel_id=1, source_target_pairs={{0,2},{1,3},{2,0},{3,1},{4,6},{5,7},{6,4},{7,5},{8,10},{9,11},{10,... | collective-permute-start | bytes 491528 | tf_op jit(solution)/shard_map/ppermute | solution.py:345
  102.1 15.0 %collective-permute-start.28 = (bf16[40,2048]{1,0:T(8,128)(2,1)S(1)}, bf16[40,2048]{1,0:T(8,128)(2,1)S(1)}, u32[]{:S(2)}, u32[]{:S(2)}) collective-permute-start(bf16[40,2048]{1,0:T(8,128)(2,1)S(1)} %get-tuple-element.91), channel_id=1, source_target_pairs={{0,1},{1,2},{2,3},{3,0},{4,5},{5,6},{6,7},{7,4},{8,9},{9,10},{10,1... | collective-permute-start | bytes 491528 | tf_op jit(solution)/shard_map/ppermute | solution.py:345
  (5 other events, 35.0 us)

commit v3 on v2

--- a/solution.py
+++ b/solution.py
@@ -139,17 +139,19 @@
 
 
 def add_products(meta, pieces, w_refs, rows_scratch, sums_ref, fresh):
-    done = set()
+    total = sums_ref.shape[1]
     for (row_at, col_at), w_ref in zip(pieces, w_refs):
         depth, columns = w_ref.shape
         rows = rows_scratch[:, pl.ds(pl.multiple_of(meta[row_at], 128), depth)]
         part = jnp.dot(rows, w_ref[...], preferred_element_type=jnp.float32)
-        where = pl.ds(pl.multiple_of(meta[col_at], 128), columns)
-        if fresh and col_at not in done:
-            sums_ref[:, where] = part
+        if columns == total:
+            sums_ref[...] = part if fresh else sums_ref[...] + part
+            fresh = False
         else:
-            sums_ref[:, where] += part
-        done.add(col_at)
+            unit = columns // 2
+            sums_ref[:, pl.ds(pl.multiple_of(meta[col_at], 128), unit)] += part[:, :unit]
+            up_at = pl.multiple_of(meta[col_at] + total // 2, 128)
+            sums_ref[:, pl.ds(up_at, unit)] += part[:, unit:]
 
 
 def first_kernel(pieces, meta, rows_ref, *refs):
@@ -306,7 +308,14 @@
 
     kv = jnp.concatenate([keys[0], values[0]], axis=1)
     kv_far = swap(kv, "ctx", n_ctx, top)
-    near, far = [kv], [kv_far]
+    unit = expert_out.shape[1] // 3
+
+    def third_of(array, start):
+        cut = lax.dynamic_slice_in_dim(array, start, unit, 2)
+        return cut.reshape(cut.shape[0], 2 * unit)
+
+    w_mine = third_of(expert_in[0], grp * unit)
+    near, far = [kv], [after(kv_far, w_mine)]
     for bit in low_bits:
         near = near + [swap(x, "ctx", n_ctx, bit) for x in near]
         far = far + [swap(x, "ctx", n_ctx, bit) for x in far]
@@ -322,9 +331,7 @@
     shard = lax.rem(ctx, top)
     in_row = [note((shard ^ j) * depth) for j in range(top)]
     out_col = [note((shard ^ j) * columns) for j in range(top)]
-    in_third, out_third = 2 * inner // 3, inner // 3
-    in_cols = [note(grp * in_third), note((1 - grp) * in_third), note(2 * in_third)]
-    out_rows = [note(grp * out_third), note((1 - grp) * out_third), note(2 * out_third)]
+    thirds = [note(grp * unit), note((1 - grp) * unit), note(2 * unit)]
     meta = jnp.stack(scalars)
 
     def spread(array):
@@ -346,11 +353,9 @@
             )
         return moved
 
-    w_in = expert_in[0].reshape(depth, 2 * inner)
-    w_first = lax.dynamic_slice_in_dim(w_in, grp * in_third, in_third, 1)
-    w_first = swap(after(w_first, kv_far), "ctx", n_ctx, top)
-    w_direct = swap(after(w_in[:, 2 * in_third :], kv_far), "ctx", n_ctx, top)
-    w_in_a = spread(after(w_in, kvs[-1]))
+    w_first = swap(w_mine, "ctx", n_ctx, top)
+    w_in = after(expert_in[0], kvs[-1]).reshape(depth, 2 * inner)
+    w_in_a = spread(after(w_in, *kvs[1:]))
 
     att_a, packed_a = attention(
         meta,
@@ -364,10 +369,11 @@
         0,
     )
     rows_a = send(packed_a, False)
+    w_direct = third_of(after(expert_in[0], att_a), 2 * unit)
     att_b, packed_b = attention(
         meta,
         tree_parents,
-        after(queries[0], att_a),
+        after(queries[0], att_a, w_direct),
         route_row,
         kvs,
         n_exp,
@@ -377,19 +383,20 @@
     )
     rows_b = send([after(x, *rows_a) for x in packed_b], False)
 
-    w_second = swap(after(w_first, *rows_a), "grp", 2, 1)
+    w_direct = swap(w_direct, "ctx", n_ctx, top)
+    w_second = swap(after(w_first, att_b), "grp", 2, 1)
     scaled_a, squares_a = prepare(meta, gain, rows_a, slots, 0)
     sums = first_half(meta, scaled_a, w_in_a, [(r, zero) for r in in_row], inner)
     w_in_b = [spread(after(w_first, *rows_b))]
     w_out_a = spread(after(w_out, *rows_b))
-    v_first = lax.dynamic_slice_in_dim(w_out, grp * out_third, out_third, 0)
+    v_first = lax.dynamic_slice_in_dim(after(w_out, *rows_a), grp * unit, unit, 0)
     v_first = swap(after(v_first, *rows_b), "ctx", n_ctx, top)
     w_in_b.append(spread(after(w_direct, *rows_b)))
     w_in_b.append(spread(after(w_second, *rows_b)))
     w_in_b = list(zip(w_in_b[0], w_in_b[2], w_in_b[1]))
     scaled_b, squares_b = prepare(meta, gain, rows_b, slots, 1)
 
-    in_pieces = [(r, c) for r in in_row for c in in_cols]
+    in_pieces = [(r, c) for r in in_row for c in thirds]
     hidden, out_a = second_half(
         meta,
         scaled_b,
@@ -403,19 +410,19 @@
         blocks_out,
     )
     back_a = send(out_a, True)
-    v_direct = swap(after(w_out[2 * out_third :], hidden), "ctx", n_ctx, top)
+    v_direct = swap(after(w_out[2 * unit :], hidden), "ctx", n_ctx, top)
     v_second = swap(after(v_first, hidden), "grp", 2, 1)
-    w_out_b = list(zip(*[spread(after(v, *back_a)) for v in (v_first, v_second, v_direct)]))
+    done = combine(meta, att_a, route_row, weight_row, back_a, n_exp, capacity, None)
+    w_out_b = list(zip(*[spread(after(v, done)) for v in (v_first, v_second, v_direct)]))
     out_b = down_half(
         meta,
         after(hidden, *out_a),
         [w for shard_pieces in w_out_b for w in shard_pieces],
-        [(r, c) for c in out_col for r in out_rows],
+        [(r, c) for c in out_col for r in thirds],
         blocks_out,
         half_width,
     )
     back_b = send(out_b, True)
-    done = combine(meta, att_a, route_row, weight_row, back_a, n_exp, capacity, None)
     done = combine(meta, att_b, route_row, weight_row, back_b, n_exp, capacity, done)
     return done[None]
 

time: 119 us -> 113 us (0.950)
  waiting for transfers between devices: 57.5 us -> 52.1 us
  starting transfers between devices: 34.8 us -> 32.9 us
  local copies, waits for them, and re-layouts: 7.59 us -> 9.14 us
    ppermute x17, waiting for transfers between devices: 22.3 us -> 17.6 us  [swap(): return lax.ppermute(array, axis, [(i, i ^ bit) for i in range(size)])]
    dynamic_slice x0 -> x3, local copies, waits for them, and re-layouts: none -> 4.18 us  [the longest x2 4.14 us: third_of(): cut = lax.dynamic_slice_in_dim(array, start, unit, 2)]
    slice x2 -> x1, local copies, waits for them, and re-layouts: 3.78 us -> 0.03 us  [body(): v_direct = swap(after(w_out[2 * unit:], hidden), 'ctx', n_ctx, top)]
    ppermute x12, starting transfers between devices: 21.5 us -> 18.6 us  [send(): lax.ppermute(blocks[k], 'exp', [(i, (i + shift) % n_exp) for i in range(n...]
    unnamed x17 -> x25, local copies, waits for them, and re-layouts: 3.72 us -> 4.84 us
  transfers between devices with their start and end apart: 29 -> 29, of which waited for: 15 -> 18; matrix products, arithmetic and copies ran while one was open for 5% -> 6% of each run, Pallas kernels for 13% -> 13%
where the time goes in v3:
time: 113 us
  waiting for transfers between devices  52.1 us (46%)
  starting transfers between devices  32.9 us (29%)
  Pallas kernels  17.4 us (15%)
  local copies, waits for them, and re-layouts  9.14 us (8%)
    ppermute x12, waiting for transfers between devices, send(): lax.ppermute(blocks[k], 'exp', [(i, (i + shift) % n_exp) for i in range(n...  34.5 us
    ppermute x12, starting transfers between devices, send(): lax.ppermute(blocks[k], 'exp', [(i, (i + shift) % n_exp) for i in range(n...  18.6 us
    ppermute x17, waiting for transfers between devices, swap(): return lax.ppermute(array, axis, [(i, i ^ bit) for i in range(size)])  17.6 us
    pallas_call x9, Pallas kernels, call(): pl.pallas_call(kernel, in_specs=specs, out_specs=[VMEM] * len(outs), out_...  17.4 us
    ppermute x17, starting transfers between devices, swap(): return lax.ppermute(array, axis, [(i, i ^ bit) for i in range(size)])  14.3 us
    unnamed x25, local copies, waits for them, and re-layouts  4.84 us
    dynamic_slice x2, local copies, waits for them, and re-layouts, third_of(): cut = lax.dynamic_slice_in_dim(array, start, unit, 2)  4.14 us
  transfers between devices with their start and end apart: 29, of which 18 were waited for; matrix products, arithmetic and copies ran while one was open for 6% of the time, Pallas kernels for 13%

profile of v3, /device:TPU:0, one launch (start us, length us, event | category | flops | bytes accessed | tf_op | source)
XLA Modules:
  0.0 112.7 jit_solution(12489444502695591241)
XLA Ops:
  0.9 3.0 %collective-permute-start = (bf16[128,512]{1,0:T(8,128)(2,1)S(1)}, bf16[128,512]{1,0:T(8,128)(2,1)S(1)}, u32[]{:S(2)}, u32[]{:S(2)}) collective-permute-start(bf16[128,512]{1,0:T(8,128)(2,1)S(1)} %pad_maximum_fusion.refs_0_), channel_id=1, source_target_pairs={{0,8},{4,12},{8,0},{12,4},{1,9},{5,13},{9,1},{13,5},{2,10},{6,14},... | collective-permute-start | bytes 393224 | tf_op jit(solution)/shard_map/ppermute | solution.py:277
  3.9 2.1 %constant_dynamic-slice_fusion.1 = bf16[1,1024,2,256]{3,2,1,0:T(2,128)(2,1)S(1)} fusion(bf16[1,1024,2,768]{3,2,1,0:T(2,128)(2,1)} %param.16, s32[]{:T(128)S(6)} %select_n.10), kind=kLoop, calls=%fused_computation.3 | loop fusion | bytes 2097156 | tf_op jit(solution)/shard_map/dynamic_slice | solution.py:314
  10.1 1.8 %collective-permute-start.10 = (bf16[1024,512]{1,0:T(8,128)(2,1)}, bf16[1024,512]{1,0:T(8,128)(2,1)}, u32[]{:S(2)}, u32[]{:S(2)}) collective-permute-start(bf16[1024,512]{1,0:T(8,128)(2,1)} %bitcast.19), channel_id=1, source_target_pairs={{0,8},{4,12},{8,0},{12,4},{1,9},{5,13},{9,1},{13,5},{2,10},{6,14},... | collective-permute-start | bytes 3145736 | tf_op jit(solution)/shard_map/ppermute | solution.py:277
  12.0 3.8 %collective-permute-done.3.refs_1_ = bf16[1024,1536]{1,0:T(8,128)(2,1)} collective-permute-done((bf16[1024,1536]{1,0:T(8,128)(2,1)S(1)}, bf16[1024,1536]{1,0:T(8,128)(2,1)}, u32[]{:S(2)}, u32[]{:S(2)}) %collective-permute-start.3) | collective-permute-done | bytes 3145760 | tf_op jit(solution)/shard_map/ppermute | solution.py:277
  17.9 2.5 %attend_a.1 = (bf16[128,2048]{1,0:T(8,128)(2,1)S(1)}, bf16[40,2048]{1,0:T(8,128)(2,1)S(1)}, bf16[40,2048]{1,0:T(8,128)(2,1)S(1)}, bf16[40,2048]{1,0:T(8,128)(2,1)S(1)}, bf16[40,2048]{1,0:T(8,128)(2,1)S(1)}) custom-call(s32[11]{0:T(128)S(1)} %stack.33.meta, s32[1,4]{1,0:T(1,128)S(1)} %copy-done.7, bf16[128,4096]{1,0:T(8,128)(2,1)S(1)} %bitcast.30, ...), custom_call_target="tpu_custom_call" | custom-call | flops 2000000000 | bytes 1000 | tf_op jit(solution)/shard_map/attend_a/pallas_call | solution.py:21
  20.4 2.0 %dynamic_slice.10 = bf16[1024,2,256]{2,1,0:T(2,128)(2,1)S(1)} slice(bf16[1024,2,768]{2,1,0:T(2,128)(2,1)} %bitcast.40), slice={[0:1024], [0:2], [512:768]} | slice | bytes 2097152 | tf_op jit(solution)/shard_map/dynamic_slice | solution.py:314
  22.7 1.8 %collective-permute-start.12 = (bf16[1024,512]{1,0:T(8,128)(2,1)S(1)}, bf16[1024,512]{1,0:T(8,128)(2,1)S(1)}, u32[]{:S(2)}, u32[]{:S(2)}) collective-permute-start(bf16[1024,512]{1,0:T(8,128)(2,1)S(1)} %bitcast.44), channel_id=1, source_target_pairs={{0,8},{4,12},{8,0},{12,4},{1,9},{5,13},{9,1},{13,5},{2,10},{6,14},... | collective-permute-start | bytes 3145736 | tf_op jit(solution)/shard_map/ppermute | solution.py:277
  24.5 1.6 %collective-permute-start.4 = (bf16[40,2048]{1,0:T(8,128)(2,1)S(1)}, bf16[40,2048]{1,0:T(8,128)(2,1)S(1)}, u32[]{:S(2)}, u32[]{:S(2)}) collective-permute-start(bf16[40,2048]{1,0:T(8,128)(2,1)S(1)} %get-tuple-element.61), channel_id=1, source_target_pairs={{0,1},{1,2},{2,3},{3,0},{4,5},{5,6},{6,7},{7,4},{8,9},{9,10},{10,1... | collective-permute-start | bytes 491528 | tf_op jit(solution)/shard_map/ppermute | solution.py:352
  26.1 2.6 %collective-permute-start.5 = (bf16[40,2048]{1,0:T(8,128)(2,1)S(1)}, bf16[40,2048]{1,0:T(8,128)(2,1)S(1)}, u32[]{:S(2)}, u32[]{:S(2)}) collective-permute-start(bf16[40,2048]{1,0:T(8,128)(2,1)S(1)} %get-tuple-element.62), channel_id=1, source_target_pairs={{0,2},{1,3},{2,0},{3,1},{4,6},{5,7},{6,4},{7,5},{8,10},{9,11},{10,... | collective-permute-start | bytes 491528 | tf_op jit(solution)/shard_map/ppermute | solution.py:352
  28.7 1.3 %collective-permute-start.6 = (bf16[40,2048]{1,0:T(8,128)(2,1)S(1)}, bf16[40,2048]{1,0:T(8,128)(2,1)S(1)}, u32[]{:S(2)}, u32[]{:S(2)}) collective-permute-start(bf16[40,2048]{1,0:T(8,128)(2,1)S(1)} %get-tuple-element.63), channel_id=1, source_target_pairs={{0,3},{1,0},{2,1},{3,2},{4,7},{5,4},{6,5},{7,6},{8,11},{9,8},{10,9... | collective-permute-start | bytes 491528 | tf_op jit(solution)/shard_map/ppermute | solution.py:352
  30.0 2.5 %attend_b.1 = (bf16[128,2048]{1,0:T(8,128)(2,1)S(1)}, bf16[40,2048]{1,0:T(8,128)(2,1)S(1)}, bf16[40,2048]{1,0:T(8,128)(2,1)S(1)}, bf16[40,2048]{1,0:T(8,128)(2,1)S(1)}, bf16[40,2048]{1,0:T(8,128)(2,1)S(1)}) custom-call(s32[11]{0:T(128)S(1)} %stack.33.meta, s32[1,4]{1,0:T(1,128)S(1)} %copy-done.7, bf16[128,4096]{1,0:T(8,128)(2,1)S(1)} %bitcast.31, ...), custom_call_target="tpu_custom_call" | custom-call | flops 2000000000 | bytes 1000 | tf_op jit(solution)/shard_map/attend_b/pallas_call | solution.py:21
  32.5 3.9 %collective-permute-done.10.refs_0_ = bf16[1024,512]{1,0:T(8,128)(2,1)} collective-permute-done((bf16[1024,512]{1,0:T(8,128)(2,1)}, bf16[1024,512]{1,0:T(8,128)(2,1)}, u32[]{:S(2)}, u32[]{:S(2)}) %collective-permute-start.10) | collective-permute-done | bytes 1048608 | tf_op jit(solution)/shard_map/ppermute | solution.py:277
  36.5 1.8 %collective-permute-start.11 = (bf16[1024,512]{1,0:T(8,128)(2,1)}, bf16[1024,512]{1,0:T(8,128)(2,1)S(1)}, u32[]{:S(2)}, u32[]{:S(2)}) collective-permute-start(bf16[1024,512]{1,0:T(8,128)(2,1)} %collective-permute-done.10.refs_0_), channel_id=1, source_target_pairs={{0,16},{16,0},{1,17},{17,1},{2,18},{18,2},{3,19},{19,3},{4,20},{20... | collective-permute-start | bytes 3145736 | tf_op jit(solution)/shard_map/ppermute | solution.py:277
  38.2 1.2 %collective-permute-done.5.refs_2_ = bf16[40,2048]{1,0:T(8,128)(2,1)S(1)} collective-permute-done((bf16[40,2048]{1,0:T(8,128)(2,1)S(1)}, bf16[40,2048]{1,0:T(8,128)(2,1)S(1)}, u32[]{:S(2)}, u32[]{:S(2)}) %collective-permute-start.5) | collective-permute-done | bytes 163872 | tf_op jit(solution)/shard_map/ppermute | solution.py:352
  39.5 5.0 %collective-permute-start.9 = (bf16[40,2048]{1,0:T(8,128)(2,1)S(1)}, bf16[40,2048]{1,0:T(8,128)(2,1)S(1)}, u32[]{:S(2)}, u32[]{:S(2)}) collective-permute-start(bf16[40,2048]{1,0:T(8,128)(2,1)S(1)} %get-tuple-element.70), channel_id=1, source_target_pairs={{0,3},{1,0},{2,1},{3,2},{4,7},{5,4},{6,5},{7,6},{8,11},{9,8},{10,9... | collective-permute-start | bytes 491528 | tf_op jit(solution)/shard_map/ppermute | solution.py:352
  45.9 3.2 %gate_up_a.1.start_ref = f32[160,1536]{1,0:T(8,128)S(1)} custom-call(s32[11]{0:T(128)S(1)} %stack.33.meta, bf16[160,2048]{1,0:T(8,128)(2,1)S(1)} %get-tuple-element.72.rows_ref, bf16[1024,1536]{1,0:T(8,128)(2,1)S(1)} %bitcast.26, bf16[1024,1536]{1,0:T(8,128)(2,1)} %collective-permute-done.3.refs_1_), custom_call_target="tpu_custom_call" | custom-call | flops 1000 | bytes 1000 | tf_op jit(solution)/shard_map/gate_up_a/pallas_call | solution.py:21
  49.2 10.3 %collective-permute-done.8.refs_2_ = bf16[40,2048]{1,0:T(8,128)(2,1)S(1)} collective-permute-done((bf16[40,2048]{1,0:T(8,128)(2,1)S(1)}, bf16[40,2048]{1,0:T(8,128)(2,1)S(1)}, u32[]{:S(2)}, u32[]{:S(2)}) %collective-permute-start.8) | collective-permute-done | bytes 163872 | tf_op jit(solution)/shard_map/ppermute | solution.py:352
  62.1 2.4 %collective-permute-done.13.refs_3_ = bf16[1024,512]{1,0:T(8,128)(2,1)S(1)} collective-permute-done((bf16[1024,512]{1,0:T(8,128)(2,1)}, bf16[1024,512]{1,0:T(8,128)(2,1)S(1)}, u32[]{:S(2)}, u32[]{:S(2)}) %collective-permute-start.13) | collective-permute-done | bytes 1048608 | tf_op jit(solution)/shard_map/ppermute | solution.py:277
  65.0 1.5 %collective-permute-done.14.refs_4_ = bf16[1024,512]{1,0:T(8,128)(2,1)S(1)} collective-permute-done((bf16[1024,512]{1,0:T(8,128)(2,1)S(1)}, bf16[1024,512]{1,0:T(8,128)(2,1)S(1)}, u32[]{:S(2)}, u32[]{:S(2)}) %collective-permute-start.14) | collective-permute-done | bytes 1048608 | tf_op jit(solution)/shard_map/ppermute | solution.py:277
  66.5 1.5 %collective-permute-done.15.refs_5_ = bf16[1024,512]{1,0:T(8,128)(2,1)S(1)} collective-permute-done((bf16[1024,512]{1,0:T(8,128)(2,1)S(1)}, bf16[1024,512]{1,0:T(8,128)(2,1)S(1)}, u32[]{:S(2)}, u32[]{:S(2)}) %collective-permute-start.15) | collective-permute-done | bytes 1048608 | tf_op jit(solution)/shard_map/ppermute | solution.py:277
  68.0 3.4 %gate_up_b_down_a.1 = (bf16[160,768]{1,0:T(8,128)(2,1)S(1)}, bf16[40,2048]{1,0:T(8,128)(2,1)S(1)}, bf16[40,2048]{1,0:T(8,128)(2,1)S(1)}, bf16[40,2048]{1,0:T(8,128)(2,1)S(1)}, bf16[40,2048]{1,0:T(8,128)(2,1)S(1)}) custom-call(s32[11]{0:T(128)S(1)} %stack.33.meta, bf16[160,2048]{1,0:T(8,128)(2,1)S(1)} %get-tuple-element.71.rows_ref, ...), custom_call_target="tpu_custom_call" | custom-call | flops 20000000000 | bytes 1000 | tf_op jit(solution)/shard_map/gate_up_b_down_a/pallas_call | solution.py:21
  72.3 1.9 %collective-permute-start.20 = (bf16[40,2048]{1,0:T(8,128)(2,1)S(1)}, bf16[40,2048]{1,0:T(8,128)(2,1)S(1)}, u32[]{:S(2)}, u32[]{:S(2)}) collective-permute-start(bf16[40,2048]{1,0:T(8,128)(2,1)S(1)} %get-tuple-element.86), channel_id=1, source_target_pairs={{0,1},{1,2},{2,3},{3,0},{4,5},{5,6},{6,7},{7,4},{8,9},{9,10},{10,1... | collective-permute-start | bytes 491528 | tf_op jit(solution)/shard_map/ppermute | solution.py:352
  74.3 1.6 %collective-permute-start.21 = (bf16[256,1024]{1,0:T(8,128)(2,1)S(1)}, bf16[256,1024]{1,0:T(8,128)(2,1)S(1)}, u32[]{:S(2)}, u32[]{:S(2)}) collective-permute-start(bf16[256,1024]{1,0:T(8,128)(2,1)S(1)} %collective-permute-done.17.refs_0_), channel_id=1, source_target_pairs={{0,16},{16,0},{1,17},{17,1},{2,18},{18,2},{3,19},{19,3},{4,20},{20... | collective-permute-start | bytes 1572872 | tf_op jit(solution)/shard_map/ppermute | solution.py:277
  75.8 1.5 %collective-permute-start.22 = (bf16[256,1024]{1,0:T(8,128)(2,1)S(1)}, bf16[256,1024]{1,0:T(8,128)(2,1)S(1)}, u32[]{:S(2)}, u32[]{:S(2)}) collective-permute-start(bf16[256,1024]{1,0:T(8,128)(2,1)S(1)} %slice_bitcast_fusion), channel_id=1, source_target_pairs={{0,8},{4,12},{8,0},{12,4},{1,9},{5,13},{9,1},{13,5},{2,10},{6,14},... | collective-permute-start | bytes 1572872 | tf_op jit(solution)/shard_map/ppermute | solution.py:277
  77.3 1.6 %collective-permute-done.18.refs_1_ = bf16[40,2048]{1,0:T(8,128)(2,1)S(1)} collective-permute-done((bf16[40,2048]{1,0:T(8,128)(2,1)S(1)}, bf16[40,2048]{1,0:T(8,128)(2,1)S(1)}, u32[]{:S(2)}, u32[]{:S(2)}) %collective-permute-start.18) | collective-permute-done | bytes 163872 | tf_op jit(solution)/shard_map/ppermute | solution.py:352
  79.0 8.3 %collective-permute-done.19.refs_2_ = bf16[40,2048]{1,0:T(8,128)(2,1)S(1)} collective-permute-done((bf16[40,2048]{1,0:T(8,128)(2,1)S(1)}, bf16[40,2048]{1,0:T(8,128)(2,1)S(1)}, u32[]{:S(2)}, u32[]{:S(2)}) %collective-permute-start.19) | collective-permute-done | bytes 163872 | tf_op jit(solution)/shard_map/ppermute | solution.py:352
  88.9 1.3 %collective-permute-done.23.refs_3_ = bf16[256,1024]{1,0:T(8,128)(2,1)S(1)} collective-permute-done((bf16[256,1024]{1,0:T(8,128)(2,1)S(1)}, bf16[256,1024]{1,0:T(8,128)(2,1)S(1)}, u32[]{:S(2)}, u32[]{:S(2)}) %collective-permute-start.23) | collective-permute-done | bytes 524320 | tf_op jit(solution)/shard_map/ppermute | solution.py:277
  94.0 1.7 %collective-permute-start.27 = (bf16[40,2048]{1,0:T(8,128)(2,1)S(1)}, bf16[40,2048]{1,0:T(8,128)(2,1)S(1)}, u32[]{:S(2)}, u32[]{:S(2)}) collective-permute-start(bf16[40,2048]{1,0:T(8,128)(2,1)S(1)} %get-tuple-element.94), channel_id=1, source_target_pairs={{0,2},{1,3},{2,0},{3,1},{4,6},{5,7},{6,4},{7,5},{8,10},{9,11},{10,... | collective-permute-start | bytes 491528 | tf_op jit(solution)/shard_map/ppermute | solution.py:352
  95.7 1.9 %collective-permute-start.28 = (bf16[40,2048]{1,0:T(8,128)(2,1)S(1)}, bf16[40,2048]{1,0:T(8,128)(2,1)S(1)}, u32[]{:S(2)}, u32[]{:S(2)}) collective-permute-start(bf16[40,2048]{1,0:T(8,128)(2,1)S(1)} %get-tuple-element.95), channel_id=1, source_target_pairs={{0,1},{1,2},{2,3},{3,0},{4,5},{5,6},{6,7},{7,4},{8,9},{9,10},{10,1... | collective-permute-start | bytes 491528 | tf_op jit(solution)/shard_map/ppermute | solution.py:352
  97.7 1.6 %collective-permute-done.26.refs_1_ = bf16[40,2048]{1,0:T(8,128)(2,1)S(1)} collective-permute-done((bf16[40,2048]{1,0:T(8,128)(2,1)S(1)}, bf16[40,2048]{1,0:T(8,128)(2,1)S(1)}, u32[]{:S(2)}, u32[]{:S(2)}) %collective-permute-start.26) | collective-permute-done | bytes 163872 | tf_op jit(solution)/shard_map/ppermute | solution.py:352
  99.3 11.4 %collective-permute-done.27.refs_2_ = bf16[40,2048]{1,0:T(8,128)(2,1)S(1)} collective-permute-done((bf16[40,2048]{1,0:T(8,128)(2,1)S(1)}, bf16[40,2048]{1,0:T(8,128)(2,1)S(1)}, u32[]{:S(2)}, u32[]{:S(2)}) %collective-permute-start.27) | collective-permute-done | bytes 163872 | tf_op jit(solution)/shard_map/ppermute | solution.py:352
  110.7 2.0 %combine_b.1 = bf16[128,4096]{1,0:T(8,128)(2,1)} custom-call(s32[11]{0:T(128)S(1)} %stack.33.meta, bf16[128,2048]{1,0:T(8,128)(2,1)S(1)} %get-tuple-element.58.att_ref, s32[1,128]{1,0:T(1,128)S(1)} %bitcast.37, f32[1,128]{1,0:T(1,128)S(1)} %bitcast.39, bf16[40,2048]{1,0:T(8,128)(2,1)S(1)} %get-tuple-element.92.refs_0_, ...), custom_call_target="tpu_custom_call" | custom-call | flops 20000000000 | bytes 1000 | tf_op jit(solution)/shard_map/combine_b/pallas_call | solution.py:21
  (66 shorter events, 18.4 us)
Async XLA Ops:
  0.9 6.5 %collective-permute-start = (bf16[128,512]{1,0:T(8,128)(2,1)S(1)}, bf16[128,512]{1,0:T(8,128)(2,1)S(1)}, u32[]{:S(2)}, u32[]{:S(2)}) collective-permute-start(bf16[128,512]{1,0:T(8,128)(2,1)S(1)} %pad_maximum_fusion.refs_0_), channel_id=1, source_target_pairs={{0,8},{4,12},{8,0},{12,4},{1,9},{5,13},{9,1},{13,5},{2,10},{6,14},... | collective-permute-start | bytes 393224 | tf_op jit(solution)/shard_map/ppermute | solution.py:277
  7.4 1.3 %collective-permute-start.1 = (bf16[128,512]{1,0:T(8,128)(2,1)S(1)}, bf16[128,512]{1,0:T(8,128)(2,1)S(1)}, u32[]{:S(2)}, u32[]{:S(2)}) collective-permute-start(bf16[128,512]{1,0:T(8,128)(2,1)S(1)} %collective-permute-done.refs_2_), channel_id=1, source_target_pairs={{0,4},{4,0},{8,12},{12,8},{1,5},{5,1},{9,13},{13,9},{2,6},{6,2},{1... | collective-permute-start | bytes 393224 | tf_op jit(solution)/shard_map/ppermute | solution.py:277
  7.4 1.9 %collective-permute-start.2 = (bf16[128,512]{1,0:T(8,128)(2,1)S(1)}, bf16[128,512]{1,0:T(8,128)(2,1)S(1)}, u32[]{:S(2)}, u32[]{:S(2)}) collective-permute-start(bf16[128,512]{1,0:T(8,128)(2,1)S(1)} %pad_maximum_fusion.refs_0_), channel_id=1, source_target_pairs={{0,4},{4,0},{8,12},{12,8},{1,5},{5,1},{9,13},{13,9},{2,6},{6,2},{1... | collective-permute-start | bytes 393224 | tf_op jit(solution)/shard_map/ppermute | solution.py:277
  10.0 5.8 %collective-permute-start.3 = (bf16[1024,1536]{1,0:T(8,128)(2,1)S(1)}, bf16[1024,1536]{1,0:T(8,128)(2,1)}, u32[]{:S(2)}, u32[]{:S(2)}) collective-permute-start(bf16[1024,1536]{1,0:T(8,128)(2,1)S(1)} %bitcast.25), channel_id=1, source_target_pairs={{0,4},{4,0},{8,12},{12,8},{1,5},{5,1},{9,13},{13,9},{2,6},{6,2},{1... | collective-permute-start | bytes 9437192 | tf_op jit(solution)/shard_map/ppermute | solution.py:277
  10.1 26.3 %collective-permute-start.10 = (bf16[1024,512]{1,0:T(8,128)(2,1)}, bf16[1024,512]{1,0:T(8,128)(2,1)}, u32[]{:S(2)}, u32[]{:S(2)}) collective-permute-start(bf16[1024,512]{1,0:T(8,128)(2,1)} %bitcast.19), channel_id=1, source_target_pairs={{0,8},{4,12},{8,0},{12,4},{1,9},{5,13},{9,1},{13,5},{2,10},{6,14},... | collective-permute-start | bytes 3145736 | tf_op jit(solution)/shard_map/ppermute | solution.py:277
  20.4 9.6 %copy-start.2 = (bf16[1,128,4096]{2,1,0:T(8,128)(2,1)S(1)}, bf16[1,128,4096]{2,1,0:T(8,128)(2,1)}, u32[]{:S(2)}) copy-start(bf16[1,128,4096]{2,1,0:T(8,128)(2,1)} %param.9) | copy-start | bytes 3145732
  22.7 38.0 %collective-permute-start.12 = (bf16[1024,512]{1,0:T(8,128)(2,1)S(1)}, bf16[1024,512]{1,0:T(8,128)(2,1)S(1)}, u32[]{:S(2)}, u32[]{:S(2)}) collective-permute-start(bf16[1024,512]{1,0:T(8,128)(2,1)S(1)} %bitcast.44), channel_id=1, source_target_pairs={{0,8},{4,12},{8,0},{12,4},{1,9},{5,13},{9,1},{13,5},{2,10},{6,14},... | collective-permute-start | bytes 3145736 | tf_op jit(solution)/shard_map/ppermute | solution.py:277
  24.5 13.7 %collective-permute-start.4 = (bf16[40,2048]{1,0:T(8,128)(2,1)S(1)}, bf16[40,2048]{1,0:T(8,128)(2,1)S(1)}, u32[]{:S(2)}, u32[]{:S(2)}) collective-permute-start(bf16[40,2048]{1,0:T(8,128)(2,1)S(1)} %get-tuple-element.61), channel_id=1, source_target_pairs={{0,1},{1,2},{2,3},{3,0},{4,5},{5,6},{6,7},{7,4},{8,9},{9,10},{10,1... | collective-permute-start | bytes 491528 | tf_op jit(solution)/shard_map/ppermute | solution.py:352
  26.1 13.4 %collective-permute-start.5 = (bf16[40,2048]{1,0:T(8,128)(2,1)S(1)}, bf16[40,2048]{1,0:T(8,128)(2,1)S(1)}, u32[]{:S(2)}, u32[]{:S(2)}) collective-permute-start(bf16[40,2048]{1,0:T(8,128)(2,1)S(1)} %get-tuple-element.62), channel_id=1, source_target_pairs={{0,2},{1,3},{2,0},{3,1},{4,6},{5,7},{6,4},{7,5},{8,10},{9,11},{10,... | collective-permute-start | bytes 491528 | tf_op jit(solution)/shard_map/ppermute | solution.py:352
  28.7 16.4 %copy-start.6 = (f32[4096]{0:T(1024)S(1)}, f32[4096]{0:T(1024)}, u32[]{:S(2)}) copy-start(f32[4096]{0:T(1024)} %param.15) | copy-start | bytes 49156
  28.7 10.8 %collective-permute-start.6 = (bf16[40,2048]{1,0:T(8,128)(2,1)S(1)}, bf16[40,2048]{1,0:T(8,128)(2,1)S(1)}, u32[]{:S(2)}, u32[]{:S(2)}) collective-permute-start(bf16[40,2048]{1,0:T(8,128)(2,1)S(1)} %get-tuple-element.63), channel_id=1, source_target_pairs={{0,3},{1,0},{2,1},{3,2},{4,7},{5,4},{6,5},{7,6},{8,11},{9,8},{10,9... | collective-permute-start | bytes 491528 | tf_op jit(solution)/shard_map/ppermute | solution.py:352
  36.5 24.3 %collective-permute-start.11 = (bf16[1024,512]{1,0:T(8,128)(2,1)}, bf16[1024,512]{1,0:T(8,128)(2,1)S(1)}, u32[]{:S(2)}, u32[]{:S(2)}) collective-permute-start(bf16[1024,512]{1,0:T(8,128)(2,1)} %collective-permute-done.10.refs_0_), channel_id=1, source_target_pairs={{0,16},{16,0},{1,17},{17,1},{2,18},{18,2},{3,19},{19,3},{4,20},{20... | collective-permute-start | bytes 3145736 | tf_op jit(solution)/shard_map/ppermute | solution.py:277
  39.5 9.7 %collective-permute-start.9 = (bf16[40,2048]{1,0:T(8,128)(2,1)S(1)}, bf16[40,2048]{1,0:T(8,128)(2,1)S(1)}, u32[]{:S(2)}, u32[]{:S(2)}) collective-permute-start(bf16[40,2048]{1,0:T(8,128)(2,1)S(1)} %get-tuple-element.70), channel_id=1, source_target_pairs={{0,3},{1,0},{2,1},{3,2},{4,7},{5,4},{6,5},{7,6},{8,11},{9,8},{10,9... | collective-permute-start | bytes 491528 | tf_op jit(solution)/shard_map/ppermute | solution.py:352
  44.5 15.0 %collective-permute-start.8 = (bf16[40,2048]{1,0:T(8,128)(2,1)S(1)}, bf16[40,2048]{1,0:T(8,128)(2,1)S(1)}, u32[]{:S(2)}, u32[]{:S(2)}) collective-permute-start(bf16[40,2048]{1,0:T(8,128)(2,1)S(1)} %get-tuple-element.68), channel_id=1, source_target_pairs={{0,2},{1,3},{2,0},{3,1},{4,6},{5,7},{6,4},{7,5},{8,10},{9,11},{10,... | collective-permute-start | bytes 491528 | tf_op jit(solution)/shard_map/ppermute | solution.py:352
  44.9 14.6 %collective-permute-start.7 = (bf16[40,2048]{1,0:T(8,128)(2,1)S(1)}, bf16[40,2048]{1,0:T(8,128)(2,1)S(1)}, u32[]{:S(2)}, u32[]{:S(2)}) collective-permute-start(bf16[40,2048]{1,0:T(8,128)(2,1)S(1)} %get-tuple-element.66), channel_id=1, source_target_pairs={{0,1},{1,2},{2,3},{3,0},{4,5},{5,6},{6,7},{7,4},{8,9},{9,10},{10,1... | collective-permute-start | bytes 491528 | tf_op jit(solution)/shard_map/ppermute | solution.py:352
  59.6 14.7 %collective-permute-start.17 = (bf16[256,1024]{1,0:T(8,128)(2,1)S(1)}, bf16[256,1024]{1,0:T(8,128)(2,1)S(1)}, u32[]{:S(2)}, u32[]{:S(2)}) collective-permute-start(bf16[256,1024]{1,0:T(8,128)(2,1)S(1)} %constant_dynamic-slice_fusion), channel_id=1, source_target_pairs={{0,8},{4,12},{8,0},{12,4},{1,9},{5,13},{9,1},{13,5},{2,10},{6,14},... | collective-permute-start | bytes 1572872 | tf_op jit(solution)/shard_map/ppermute | solution.py:277
  60.1 4.3 %collective-permute-start.13 = (bf16[1024,512]{1,0:T(8,128)(2,1)}, bf16[1024,512]{1,0:T(8,128)(2,1)S(1)}, u32[]{:S(2)}, u32[]{:S(2)}) collective-permute-start(bf16[1024,512]{1,0:T(8,128)(2,1)} %collective-permute-done.10.refs_0_), channel_id=1, source_target_pairs={{0,4},{4,0},{8,12},{12,8},{1,5},{5,1},{9,13},{13,9},{2,6},{6,2},{1... | collective-permute-start | bytes 3145736 | tf_op jit(solution)/shard_map/ppermute | solution.py:277
  60.1 4.9 %collective-permute-start.16 = (bf16[768,1024]{1,0:T(8,128)(2,1)S(1)}, bf16[768,1024]{1,0:T(8,128)(2,1)S(1)}, u32[]{:S(2)}, u32[]{:S(2)}) collective-permute-start(bf16[768,1024]{1,0:T(8,128)(2,1)S(1)} %bitcast.28), channel_id=1, source_target_pairs={{0,4},{4,0},{8,12},{12,8},{1,5},{5,1},{9,13},{13,9},{2,6},{6,2},{1... | collective-permute-start | bytes 4718600 | tf_op jit(solution)/shard_map/ppermute | solution.py:277
  60.7 5.8 %collective-permute-start.14 = (bf16[1024,512]{1,0:T(8,128)(2,1)S(1)}, bf16[1024,512]{1,0:T(8,128)(2,1)S(1)}, u32[]{:S(2)}, u32[]{:S(2)}) collective-permute-start(bf16[1024,512]{1,0:T(8,128)(2,1)S(1)} %collective-permute-done.11.refs_1_), channel_id=1, source_target_pairs={{0,4},{4,0},{8,12},{12,8},{1,5},{5,1},{9,13},{13,9},{2,6},{6,2},{1... | collective-permute-start | bytes 3145736 | tf_op jit(solution)/shard_map/ppermute | solution.py:277
  60.7 7.3 %collective-permute-start.15 = (bf16[1024,512]{1,0:T(8,128)(2,1)S(1)}, bf16[1024,512]{1,0:T(8,128)(2,1)S(1)}, u32[]{:S(2)}, u32[]{:S(2)}) collective-permute-start(bf16[1024,512]{1,0:T(8,128)(2,1)S(1)} %collective-permute-done.12.refs_2_), channel_id=1, source_target_pairs={{0,4},{4,0},{8,12},{12,8},{1,5},{5,1},{9,13},{13,9},{2,6},{6,2},{1... | collective-permute-start | bytes 3145736 | tf_op jit(solution)/shard_map/ppermute | solution.py:277
  68.0 19.2 %copy-start.9 = (f32[1,128,1]{1,2,0:T(1,128)S(1)}, f32[1,128,1]{1,2,0:T(1,128)}, u32[]{:S(2)}) copy-start(f32[1,128,1]{1,2,0:T(1,128)} %param.14) | copy-start | bytes 1540
  71.4 7.6 %collective-permute-start.18 = (bf16[40,2048]{1,0:T(8,128)(2,1)S(1)}, bf16[40,2048]{1,0:T(8,128)(2,1)S(1)}, u32[]{:S(2)}, u32[]{:S(2)}) collective-permute-start(bf16[40,2048]{1,0:T(8,128)(2,1)S(1)} %get-tuple-element.84), channel_id=1, source_target_pairs={{0,3},{1,0},{2,1},{3,2},{4,7},{5,4},{6,5},{7,6},{8,11},{9,8},{10,9... | collective-permute-start | bytes 491528 | tf_op jit(solution)/shard_map/ppermute | solution.py:352
  72.2 15.0 %collective-permute-start.19 = (bf16[40,2048]{1,0:T(8,128)(2,1)S(1)}, bf16[40,2048]{1,0:T(8,128)(2,1)S(1)}, u32[]{:S(2)}, u32[]{:S(2)}) collective-permute-start(bf16[40,2048]{1,0:T(8,128)(2,1)S(1)} %get-tuple-element.85), channel_id=1, source_target_pairs={{0,2},{1,3},{2,0},{3,1},{4,6},{5,7},{6,4},{7,5},{8,10},{9,11},{10,... | collective-permute-start | bytes 491528 | tf_op jit(solution)/shard_map/ppermute | solution.py:352
  72.3 15.0 %collective-permute-start.20 = (bf16[40,2048]{1,0:T(8,128)(2,1)S(1)}, bf16[40,2048]{1,0:T(8,128)(2,1)S(1)}, u32[]{:S(2)}, u32[]{:S(2)}) collective-permute-start(bf16[40,2048]{1,0:T(8,128)(2,1)S(1)} %get-tuple-element.86), channel_id=1, source_target_pairs={{0,1},{1,2},{2,3},{3,0},{4,5},{5,6},{6,7},{7,4},{8,9},{9,10},{10,1... | collective-permute-start | bytes 491528 | tf_op jit(solution)/shard_map/ppermute | solution.py:352
  74.3 14.1 %collective-permute-start.21 = (bf16[256,1024]{1,0:T(8,128)(2,1)S(1)}, bf16[256,1024]{1,0:T(8,128)(2,1)S(1)}, u32[]{:S(2)}, u32[]{:S(2)}) collective-permute-start(bf16[256,1024]{1,0:T(8,128)(2,1)S(1)} %collective-permute-done.17.refs_0_), channel_id=1, source_target_pairs={{0,16},{16,0},{1,17},{17,1},{2,18},{18,2},{3,19},{19,3},{4,20},{20... | collective-permute-start | bytes 1572872 | tf_op jit(solution)/shard_map/ppermute | solution.py:277
  75.8 13.0 %collective-permute-start.22 = (bf16[256,1024]{1,0:T(8,128)(2,1)S(1)}, bf16[256,1024]{1,0:T(8,128)(2,1)S(1)}, u32[]{:S(2)}, u32[]{:S(2)}) collective-permute-start(bf16[256,1024]{1,0:T(8,128)(2,1)S(1)} %slice_bitcast_fusion), channel_id=1, source_target_pairs={{0,8},{4,12},{8,0},{12,4},{1,9},{5,13},{9,1},{13,5},{2,10},{6,14},... | collective-permute-start | bytes 1572872 | tf_op jit(solution)/shard_map/ppermute | solution.py:277
  88.3 2.0 %collective-permute-start.23 = (bf16[256,1024]{1,0:T(8,128)(2,1)S(1)}, bf16[256,1024]{1,0:T(8,128)(2,1)S(1)}, u32[]{:S(2)}, u32[]{:S(2)}) collective-permute-start(bf16[256,1024]{1,0:T(8,128)(2,1)S(1)} %collective-permute-done.17.refs_0_), channel_id=1, source_target_pairs={{0,4},{4,0},{8,12},{12,8},{1,5},{5,1},{9,13},{13,9},{2,6},{6,2},{1... | collective-permute-start | bytes 1572872 | tf_op jit(solution)/shard_map/ppermute | solution.py:277
  88.3 2.6 %collective-permute-start.24 = (bf16[256,1024]{1,0:T(8,128)(2,1)S(1)}, bf16[256,1024]{1,0:T(8,128)(2,1)S(1)}, u32[]{:S(2)}, u32[]{:S(2)}) collective-permute-start(bf16[256,1024]{1,0:T(8,128)(2,1)S(1)} %collective-permute-done.21.refs_1_), channel_id=1, source_target_pairs={{0,4},{4,0},{8,12},{12,8},{1,5},{5,1},{9,13},{13,9},{2,6},{6,2},{1... | collective-permute-start | bytes 1572872 | tf_op jit(solution)/shard_map/ppermute | solution.py:277
  88.8 2.9 %collective-permute-start.25 = (bf16[256,1024]{1,0:T(8,128)(2,1)S(1)}, bf16[256,1024]{1,0:T(8,128)(2,1)S(1)}, u32[]{:S(2)}, u32[]{:S(2)}) collective-permute-start(bf16[256,1024]{1,0:T(8,128)(2,1)S(1)} %collective-permute-done.22.refs_2_), channel_id=1, source_target_pairs={{0,4},{4,0},{8,12},{12,8},{1,5},{5,1},{9,13},{13,9},{2,6},{6,2},{1... | collective-permute-start | bytes 1572872 | tf_op jit(solution)/shard_map/ppermute | solution.py:277
  93.0 6.3 %collective-permute-start.26 = (bf16[40,2048]{1,0:T(8,128)(2,1)S(1)}, bf16[40,2048]{1,0:T(8,128)(2,1)S(1)}, u32[]{:S(2)}, u32[]{:S(2)}) collective-permute-start(bf16[40,2048]{1,0:T(8,128)(2,1)S(1)} %get-tuple-element.93), channel_id=1, source_target_pairs={{0,3},{1,0},{2,1},{3,2},{4,7},{5,4},{6,5},{7,6},{8,11},{9,8},{10,9... | collective-permute-start | bytes 491528 | tf_op jit(solution)/shard_map/ppermute | solution.py:352
  94.0 16.6 %collective-permute-start.27 = (bf16[40,2048]{1,0:T(8,128)(2,1)S(1)}, bf16[40,2048]{1,0:T(8,128)(2,1)S(1)}, u32[]{:S(2)}, u32[]{:S(2)}) collective-permute-start(bf16[40,2048]{1,0:T(8,128)(2,1)S(1)} %get-tuple-element.94), channel_id=1, source_target_pairs={{0,2},{1,3},{2,0},{3,1},{4,6},{5,7},{6,4},{7,5},{8,10},{9,11},{10,... | collective-permute-start | bytes 491528 | tf_op jit(solution)/shard_map/ppermute | solution.py:352
  95.7 15.0 %collective-permute-start.28 = (bf16[40,2048]{1,0:T(8,128)(2,1)S(1)}, bf16[40,2048]{1,0:T(8,128)(2,1)S(1)}, u32[]{:S(2)}, u32[]{:S(2)}) collective-permute-start(bf16[40,2048]{1,0:T(8,128)(2,1)S(1)} %get-tuple-element.95), channel_id=1, source_target_pairs={{0,1},{1,2},{2,3},{3,0},{4,5},{5,6},{6,7},{7,4},{8,9},{9,10},{10,1... | collective-permute-start | bytes 491528 | tf_op jit(solution)/shard_map/ppermute | solution.py:352
  (8 other events, 34.6 us)

commit v4 on v2

v4 whole, which is shorter than its diff:
```python
import functools
import math

import jax
import jax.numpy as jnp
from jax import lax
from jax.experimental import pallas as pl
from jax.experimental.pallas import tpu as pltpu
from jax.sharding import PartitionSpec as P

KV_HEADS = 2
HEAD_DIM = 128
TREE_BLOCK = 128
NEG = -1e30
MIB = 1024 * 1024
VMEM = pl.BlockSpec(memory_space=pltpu.VMEM)
SMEM = pl.BlockSpec(memory_space=pltpu.SMEM)


def call(kernel, name, args, specs, outs, scratch=(), mib=16, flops=1000):
    return pl.pallas_call(
        kernel,
        in_specs=specs,
        out_specs=[VMEM] * len(outs),
        out_shape=[jax.ShapeDtypeStruct(s, d) for s, d in outs],
        scratch_shapes=list(scratch),
        compiler_params=pltpu.CompilerParams(vmem_limit_bytes=mib * MIB),
        cost_estimate=pl.CostEstimate(flops=flops, bytes_accessed=1000, transcendentals=0),
        name=name,
    )(*args)


def placement_of(route_row, capacity, experts, first, relative):
    tokens = route_row.shape[1]
    if relative:
        route_row = lax.rem(route_row - first + experts, experts)
    rows = max(8, experts)
    expert_ids = lax.broadcasted_iota(jnp.int32, (rows, tokens), 0)
    hot = jnp.where(expert_ids == route_row, 1.0, 0.0)
    before = lax.broadcasted_iota(jnp.int32, (tokens, tokens), 0) < lax.broadcasted_iota(
        jnp.int32, (tokens, tokens), 1
    )
    earlier = jnp.dot(
        hot.astype(jnp.bfloat16),
        jnp.where(before, 1.0, 0.0).astype(jnp.bfloat16),
        preferred_element_type=jnp.float32,
    )
    rank = jnp.sum(earlier * hot, axis=0, keepdims=True).astype(jnp.int32)
    slot = route_row * capacity + rank
    slot_ids = lax.broadcasted_iota(jnp.int32, (experts * capacity, tokens), 0)
    return jnp.where(slot_ids == slot, 1.0, 0.0)


def attention_kernel(n_ctx, experts, capacity, blocks_out, half, meta, parents, q_ref, route_ref, *refs):
    kv = refs[:n_ctx]
    att_ref = refs[n_ctx]
    out_refs = refs[n_ctx + 1 :]
    tokens, half_width = att_ref.shape
    heads = half_width // HEAD_DIM
    side = meta[0] if half == 0 else 1 - meta[0]
    me = meta[1]
    reached = [jnp.int32(0)] * n_ctx
    current = me
    for _ in range(n_ctx):
        current = parents[0, current]
        for j in range(1, n_ctx):
            reached[j] = jnp.where(current == (me ^ j), jnp.int32(1), reached[j])
    causal = lax.broadcasted_iota(jnp.int32, (tokens, tokens), 1) <= lax.broadcasted_iota(
        jnp.int32, (tokens, tokens), 0
    )
    key_at = pl.ds(pl.multiple_of(side * HEAD_DIM, HEAD_DIM), HEAD_DIM)
    value_at = pl.ds(pl.multiple_of((KV_HEADS + side) * HEAD_DIM, HEAD_DIM), HEAD_DIM)
    keys_t = jnp.concatenate([r[:, key_at] for r in kv], axis=0).T
    ones = jnp.ones((tokens, HEAD_DIM), jnp.bfloat16)
    values = jnp.concatenate(
        [jnp.concatenate([r[:, value_at], ones], axis=1) for r in kv], axis=0
    )
    bias = jnp.concatenate(
        [jnp.where(causal, 0.0, NEG)]
        + [
            jnp.broadcast_to(jnp.where(reached[j] == 1, 0.0, NEG), (tokens, tokens))
            for j in range(1, n_ctx)
        ],
        axis=1,
    )
    scale = math.log2(math.e) / math.sqrt(HEAD_DIM)
    for h in range(heads):
        columns = slice(h * HEAD_DIM, (h + 1) * HEAD_DIM)
        q_at = pl.ds(pl.multiple_of(side * half_width + h * HEAD_DIM, HEAD_DIM), HEAD_DIM)
        scores = jnp.dot(q_ref[:, q_at], keys_t, preferred_element_type=jnp.float32)
        scores = scores * scale + bias
        peak = jnp.max(scores, axis=1, keepdims=True)
        weights = jnp.exp2(scores - peak).astype(jnp.bfloat16)
        total = jnp.dot(weights, values, preferred_element_type=jnp.float32)
        att_ref[:, columns] = (total[:, :HEAD_DIM] / total[:, HEAD_DIM:]).astype(jnp.bfloat16)
    place = placement_of(route_ref[...], capacity, experts, meta[2], blocks_out > 1)
    packed = jnp.dot(place.astype(jnp.bfloat16), att_ref[...], preferred_element_type=jnp.float32)
    rows = experts * capacity // blocks_out
    for k in range(blocks_out):
        out_refs[k][...] = packed[k * rows : (k + 1) * rows].astype(jnp.bfloat16)


def attention(meta, parents, queries, route_row, kvs, experts, capacity, blocks_out, half):
    tokens, width = queries.shape
    half_width = width // KV_HEADS
    rows = experts * capacity // blocks_out
    bf16 = jnp.bfloat16
    outs = call(
        functools.partial(attention_kernel, len(kvs), experts, capacity, blocks_out, half),
        "attend_" + "ab"[half],
        [meta, parents, queries, route_row, *kvs],
        [SMEM, SMEM] + [VMEM] * (2 + len(kvs)),
        [((tokens, half_width), bf16)] + [((rows, half_width), bf16)] * blocks_out,
        flops=2 * 10**9,
    )
    return outs[0], list(outs[1:])


def products_kernel(n_rows, n_weights, row_at, packed, meta, gain_ref, *refs):
    row_refs, w_refs, refs = refs[:n_rows], refs[n_rows : n_rows + n_weights], refs[n_rows + n_weights :]
    scaled = refs[-1]
    width = scaled.shape[1]
    gain = gain_ref[:, pl.ds(pl.multiple_of(meta[0] * width, width), width)]
    rows = jnp.concatenate([r[...].astype(jnp.float32) for r in row_refs], axis=0)
    scaled[...] = (rows * gain).astype(jnp.bfloat16)
    squares = jnp.sum(rows * rows, axis=1, keepdims=True)
    squares = jnp.broadcast_to(squares, (scaled.shape[0], 128))
    sums = None
    for i, w_ref in enumerate(w_refs):
        features = pl.ds(pl.multiple_of(meta[row_at + i], 128), w_ref.shape[0])
        part = jnp.dot(scaled[:, features], w_ref[...], preferred_element_type=jnp.float32)
        sums = part if sums is None else sums + part
    if packed:
        columns = sums.shape[1]
        refs[0][:, :columns] = sums.astype(jnp.bfloat16)
        high = squares.astype(jnp.bfloat16)
        low = (squares - high.astype(jnp.float32)).astype(jnp.bfloat16)
        lane = lax.broadcasted_iota(jnp.int32, squares.shape, 1)
        refs[0][:, columns:] = jnp.where(
            lane < 64, high.astype(jnp.float32), low.astype(jnp.float32)
        ).astype(jnp.bfloat16)
    else:
        refs[0][...] = sums
        refs[1][...] = squares


def products(meta, gain, rows, weights, row_at, slots, packed):
    half_width = rows[0].shape[1]
    columns = weights[0].shape[1]
    f32, bf16 = jnp.float32, jnp.bfloat16
    outs = [((slots, columns + 128), bf16)] if packed else [((slots, columns), f32), ((slots, 128), f32)]
    return call(
        functools.partial(products_kernel, len(rows), len(weights), row_at, packed),
        "products_" + "ab"[packed],
        [meta, gain, *rows, *weights],
        [SMEM] + [VMEM] * (1 + len(rows) + len(weights)),
        outs,
        [pltpu.VMEM((slots, half_width), bf16)],
        flops=20 * 10**9,
    )


def store_down(meta, col_at, w_refs, hidden, out_refs):
    for i, w_ref in enumerate(w_refs):
        value = jnp.dot(hidden, w_ref[...], preferred_element_type=jnp.float32)
        where = pl.ds(pl.multiple_of(meta[col_at + i], 128), w_ref.shape[1])
        height = value.shape[0] // len(out_refs)
        for k, out in enumerate(out_refs):
            out[:, where] = value[k * height : (k + 1) * height].astype(jnp.bfloat16)


def finish_kernel(n_weights, col_at, width, meta, sums_ref, squares_ref, far_ref, *refs):
    w_refs, hidden_ref, out_refs = refs[:n_weights], refs[n_weights], refs[n_weights + 1 :]
    inner = hidden_ref.shape[1]
    squares = squares_ref[:, :1]
    for at in (0, 64):
        squares = squares + far_ref[:, 2 * inner + at : 2 * inner + at + 1].astype(jnp.float32)
    factor = lax.rsqrt(squares * (1.0 / width) + 1e-06)
    gate = (sums_ref[:, :inner] + far_ref[:, :inner].astype(jnp.float32)) * factor
    up = (sums_ref[:, inner:] + far_ref[:, inner : 2 * inner].astype(jnp.float32)) * factor
    hidden = (gate / (1.0 + jnp.exp(-gate)) * up).astype(jnp.bfloat16)
    hidden_ref[...] = hidden
    store_down(meta, col_at, w_refs, hidden, out_refs)


def finish(meta, sums, squares, far, weights, col_at, width, blocks_out):
    slots, columns = sums.shape
    bf16 = jnp.bfloat16
    outs = call(
        functools.partial(finish_kernel, len(weights), col_at, width),
        "hidden_down_a",
        [meta, sums, squares, far, *weights],
        [SMEM] + [VMEM] * (3 + len(weights)),
        [((slots, columns // 2), bf16)]
        + [((slots // blocks_out, width // KV_HEADS), bf16)] * blocks_out,
    )
    return outs[0], list(outs[1:])


def down_kernel(n_weights, col_at, meta, hidden_ref, *refs):
    store_down(meta, col_at, refs[:n_weights], hidden_ref[...], refs[n_weights:])


def down(meta, hidden, weights, col_at, width, blocks_out):
    outs = [((hidden.shape[0] // blocks_out, width // KV_HEADS), jnp.bfloat16)] * blocks_out
    return list(
        call(
            functools.partial(down_kernel, len(weights), col_at),
            "down_b",
            [meta, hidden, *weights],
            [SMEM] + [VMEM] * (1 + len(weights)),
            outs,
        )
    )


def combine_kernel(experts, capacity, n_rows, last, meta, att_ref, route_ref, weight_ref, *refs):
    row_refs, out_ref = refs[:n_rows], refs[-1]
    tokens, half_width = att_ref.shape
    place = placement_of(route_ref[...], capacity, experts, meta[2], n_rows > 1)
    height = place.shape[0] // n_rows
    mine = None
    for k, row_ref in enumerate(row_refs):
        part = lax.dot_general(
            place[k * height : (k + 1) * height].astype(jnp.bfloat16),
            row_ref[...],
            (((0,), (0,)), ((), ())),
            preferred_element_type=jnp.float32,
        )
        mine = part if mine is None else mine + part
    diagonal = lax.broadcasted_iota(jnp.int32, (tokens, tokens), 0) == lax.broadcasted_iota(
        jnp.int32, (tokens, tokens), 1
    )
    weight = jnp.sum(jnp.where(diagonal, weight_ref[...], 0.0), axis=1, keepdims=True)
    value = (att_ref[...].astype(jnp.float32) + mine * weight).astype(jnp.bfloat16)
    if last:
        before_ref = refs[n_rows]
        before_at = pl.multiple_of(meta[0] * half_width, half_width)
        mine_at = pl.multiple_of((1 - meta[0]) * half_width, half_width)
        out_ref[:, pl.ds(before_at, half_width)] = before_ref[...]
        out_ref[:, pl.ds(mine_at, half_width)] = value
    else:
        out_ref[...] = value


def combine(meta, att, route_row, weight_row, rows, experts, capacity, before):
    tokens, half_width = att.shape
    last = before is not None
    extra = [before] if last else []
    return call(
        functools.partial(combine_kernel, experts, capacity, len(rows), last),
        "combine_" + "ab"[last],
        [meta, att, route_row, weight_row, *rows, *extra],
        [SMEM] + [VMEM] * (3 + len(rows) + len(extra)),
        [((tokens, half_width * (1 + last)), jnp.bfloat16)],
        flops=20 * 10**9,
    )[0]


def swap(array, axis, size, bit):
    return lax.ppermute(array, axis, [(i, i ^ bit) for i in range(size)])


def after(array, *others):
    return lax.optimization_barrier((array, *others))[0]


def body(
    queries, keys, values, tree_parents, routes, route_weight, norm_gain, expert_in, expert_out
):
    n_ctx, n_exp = lax.axis_size("ctx"), lax.axis_size("exp")
    ctx, exp = lax.axis_index("ctx"), lax.axis_index("exp")
    tokens, width = queries.shape[1:]
    assert tokens == TREE_BLOCK and tree_parents.shape[1] == n_ctx and routes.shape[2] == 1
    assert n_ctx & (n_ctx - 1) == 0 and n_ctx > 1
    capacity = max(2, 5 * tokens // (4 * n_exp))
    slots = n_exp * capacity
    shifted = n_exp <= 8 and capacity % 8 == 0
    blocks_out = n_exp if shifted else 1
    half_width = width // KV_HEADS
    top = n_ctx // 2
    low_bits = [1 << b for b in range(top.bit_length() - 1)]
    half = ctx // top

    depth = expert_in.shape[1]
    inner = expert_out.shape[1]
    columns = expert_out.shape[2]
    route_row = routes.reshape(1, tokens)
    weight_row = route_weight.reshape(1, tokens)
    gain = norm_gain.reshape(1, width)

    w_in = expert_in[0].reshape(depth, 2 * inner)

    kv = jnp.concatenate([after(keys[0], w_in), values[0]], axis=1)
    near, far = [kv], [swap(kv, "ctx", n_ctx, top)]
    for bit in low_bits:
        near = near + [swap(x, "ctx", n_ctx, bit) for x in near]
        far = far + [swap(x, "ctx", n_ctx, bit) for x in far]
    kvs = near + far

    shards = [lax.rem(ctx, top) ^ j for j in range(top)]
    row_at, col_at = 3, 3 + top
    meta = jnp.stack([half, ctx, exp] + [j * depth for j in shards] + [j * columns for j in shards])

    def spread(array):
        found = [array]
        for bit in low_bits:
            found = found + [swap(a, "ctx", n_ctx, bit) for a in found]
        return found

    def send(blocks, back, cross):
        if not shifted:
            whole = blocks[0].reshape(n_exp, capacity, half_width)
            whole = lax.all_to_all(whole, "exp", 0, 0, tiled=True).reshape(slots, half_width)
            return [swap(whole, "ctx", n_ctx, top) if cross else whole]
        moved = []
        for k in range(n_exp):
            shift = (n_exp - k) % n_exp if back else k
            bit = top if cross else 0
            pairs = [
                (c * n_exp + e, (c ^ bit) * n_exp + (e + shift) % n_exp)
                for c in range(n_ctx)
                for e in range(n_exp)
            ]
            still = k == 0 and not cross
            moved.append(blocks[k] if still else lax.ppermute(blocks[k], ("ctx", "exp"), pairs))
        return moved

    def attend(queries, part):
        return attention(
            meta, tree_parents, queries, route_row, kvs, n_exp, capacity, blocks_out, part
        )

    att_b, packed_b = attend(queries[0], 1)
    rows_b = send(packed_b, False, True)
    att_a, packed_a = attend(after(queries[0], att_b), 0)
    rows_a = send(packed_a, False, False)

    w_ins = spread(after(w_in, *kvs[1:]))
    w_outs = spread(after(expert_out[0], *rows_b))
    rows_b = [after(r, att_a) for r in rows_b]
    far_sums = products(meta, gain, rows_b, w_ins, row_at, slots, True)[0]
    far_sums = swap(far_sums, "ctx", n_ctx, top)
    sums, squares = products(meta, gain, rows_a, w_ins, row_at, slots, False)
    hidden, out_a = finish(meta, sums, squares, far_sums, w_outs, col_at, width, blocks_out)
    back_a = send(out_a, True, False)
    out_b = down(meta, swap(hidden, "ctx", n_ctx, top), w_outs, col_at, width, blocks_out)
    back_b = send(out_b, True, True)
    done = combine(meta, att_a, route_row, weight_row, back_a, n_exp, capacity, None)
    done = combine(meta, att_b, route_row, weight_row, back_b, n_exp, capacity, done)
    return done[None]


def solution(mesh):
    in_specs = (
        P(("grp", "exp"), "ctx", None),
        P(("grp", "exp"), "ctx", None),
        P(("grp", "exp"), "ctx", None),
        P(("grp", "exp"), None),
        P(("grp", "exp"), "ctx", None),
        P(("grp", "exp"), "ctx", None),
        P(),
        P("exp", "ctx", None, None),
        P("exp", None, "ctx"),
    )
    out_specs = P(("grp", "exp"), "ctx", None)
    return jax.shard_map(body, mesh=mesh, in_specs=in_specs, out_specs=out_specs, check_vma=False)
```

time: 119 us -> 96.5 us (0.81)
  waiting for transfers between devices: 57.5 us -> 37.2 us
  local copies, waits for them, and re-layouts: 7.59 us -> 5.4 us
    ppermute x17 -> x7, waiting for transfers between devices: 22.3 us -> 12.2 us  [swap(): return lax.ppermute(array, axis, [(i, i ^ bit) for i in range(size)])]
    ppermute x12 -> x14, waiting for transfers between devices: 35.2 us -> 25 us  [send(): lax.ppermute(blocks[k], ('ctx', 'exp'), pairs)]
    ppermute x12 -> x14, starting transfers between devices: 21.5 us -> 29.5 us  [send(): lax.ppermute(blocks[k], ('ctx', 'exp'), pairs)]
    ppermute x17 -> x7, starting transfers between devices: 13.3 us -> 5.98 us  [swap(): return lax.ppermute(array, axis, [(i, i ^ bit) for i in range(size)])]
    slice x2 -> x0, local copies, waits for them, and re-layouts: 3.78 us -> none  [the longest x1 2.27 us: body(): v_direct = swap(after(w_out[2 * out_third:], hidden), 'ctx', n_ctx, top)]
    unnamed x17 -> x23, local copies, waits for them, and re-layouts: 3.72 us -> 5.32 us
    pallas_call x9 -> x8, Pallas kernels: 18.2 us -> 18 us  [call(): pl.pallas_call(kernel, in_specs=specs, out_specs=[VMEM] * len(outs), out_...]
  transfers between devices with their start and end apart: 29 -> 21, of which waited for: 15 -> 9; matrix products, arithmetic and copies ran while one was open for 5% -> 0% of each run, Pallas kernels for 13% -> 15%
where the time goes in v4:
time: 96.5 us; the launch traced here: 96.3 us
  waiting for transfers between devices  37.2 us (39%)
  starting transfers between devices  35.5 us (37%)
  Pallas kernels  18 us (19%)
  local copies, waits for them, and re-layouts  5.4 us (6%)
    ppermute x14, starting transfers between devices, send(): lax.ppermute(blocks[k], ('ctx', 'exp'), pairs)  29.5 us
    ppermute x14, waiting for transfers between devices, send(): lax.ppermute(blocks[k], ('ctx', 'exp'), pairs)  25 us
    pallas_call x8, Pallas kernels, call(): pl.pallas_call(kernel, in_specs=specs, out_specs=[VMEM] * len(outs), out_...  18 us
    ppermute x7, waiting for transfers between devices, swap(): return lax.ppermute(array, axis, [(i, i ^ bit) for i in range(size)])  12.2 us
    ppermute x7, starting transfers between devices, swap(): return lax.ppermute(array, axis, [(i, i ^ bit) for i in range(size)])  5.98 us
    unnamed x23, local copies, waits for them, and re-layouts  5.32 us
  transfers between devices with their start and end apart: 21, of which 9 were waited for; matrix products, arithmetic and copies ran while one was open for 0% of the time, Pallas kernels for 15%

profile of v4, /device:TPU:0, one launch (start us, length us, event | category | flops | bytes accessed | tf_op | source)
XLA Modules:
  0.0 96.3 jit_solution(14314554154606249440)
XLA Ops:
  0.0 2.5 %copy.10 = bf16[128,8,2,768]{3,1,2,0:T(8,128)(2,1)S(1)} copy(bf16[128,8,2,768]{3,2,1,0:T(2,128)(2,1)} %bitcast.32) | data formatting | bytes 6291456
  2.6 3.0 %collective-permute-start.1 = (bf16[128,512]{1,0:T(8,128)(2,1)S(1)}, bf16[128,512]{1,0:T(8,128)(2,1)S(1)}, u32[]{:S(2)}, u32[]{:S(2)}) collective-permute-start(bf16[128,512]{1,0:T(8,128)(2,1)S(1)} %pad_maximum_fusion.refs_0_), channel_id=1, source_target_pairs={{0,8},{4,12},{8,0},{12,4},{1,9},{5,13},{9,1},{13,5},{2,10},{6,14},... | collective-permute-start | bytes 393224 | tf_op jit(solution)/shard_map/ppermute | solution.py:261
  5.6 3.5 %collective-permute-done.1.refs_2_ = bf16[128,512]{1,0:T(8,128)(2,1)S(1)} collective-permute-done((bf16[128,512]{1,0:T(8,128)(2,1)S(1)}, bf16[128,512]{1,0:T(8,128)(2,1)S(1)}, u32[]{:S(2)}, u32[]{:S(2)}) %collective-permute-start.1) | collective-permute-done | bytes 131104 | tf_op jit(solution)/shard_map/ppermute | solution.py:261
  9.1 1.3 %collective-permute-done.2.refs_3_ = bf16[128,512]{1,0:T(8,128)(2,1)S(1)} collective-permute-done((bf16[128,512]{1,0:T(8,128)(2,1)S(1)}, bf16[128,512]{1,0:T(8,128)(2,1)S(1)}, u32[]{:S(2)}, u32[]{:S(2)}) %collective-permute-start.2) | collective-permute-done | bytes 131104 | tf_op jit(solution)/shard_map/ppermute | solution.py:261
  11.3 1.2 %copy-done.1 = bf16[1,128,4096]{2,1,0:T(8,128)(2,1)S(1)} copy-done((bf16[1,128,4096]{2,1,0:T(8,128)(2,1)S(1)}, bf16[1,128,4096]{2,1,0:T(8,128)(2,1)}, u32[]{:S(2)}) %copy-start.1) | copy-done | bytes 1048600
  12.6 0.9 copy-done.3
  13.5 2.5 %attend_b.1 = (bf16[128,2048]{1,0:T(8,128)(2,1)S(1)}, bf16[40,2048]{1,0:T(8,128)(2,1)S(1)}, bf16[40,2048]{1,0:T(8,128)(2,1)S(1)}, bf16[40,2048]{1,0:T(8,128)(2,1)S(1)}, bf16[40,2048]{1,0:T(8,128)(2,1)S(1)}) custom-call(s32[7]{0:T(128)S(1)} %stack.25.meta, s32[1,4]{1,0:T(1,128)S(1)} %copy-done.6, bf16[128,4096]{1,0:T(8,128)(2,1)S(1)} %bitcast.22, ...), custom_call_target="tpu_custom_call" | custom-call | flops 2000000000 | bytes 1000 | tf_op jit(solution)/shard_map/attend_b/pallas_call | solution.py:21
  15.9 1.8 %collective-permute-start.7 = (bf16[40,2048]{1,0:T(8,128)(2,1)S(1)}, bf16[40,2048]{1,0:T(8,128)(2,1)S(1)}, u32[]{:S(2)}, u32[]{:S(2)}) collective-permute-start(bf16[40,2048]{1,0:T(8,128)(2,1)S(1)} %get-tuple-element.44), channel_id=1, source_target_pairs={{0,8},{1,9},{2,10},{3,11},{4,12},{5,13},{6,14},{7,15},{8,0},{9,1},... | collective-permute-start | bytes 491528 | tf_op jit(solution)/shard_map/ppermute | solution.py:326
  17.7 1.6 %collective-permute-start.8 = (bf16[40,2048]{1,0:T(8,128)(2,1)S(1)}, bf16[40,2048]{1,0:T(8,128)(2,1)S(1)}, u32[]{:S(2)}, u32[]{:S(2)}) collective-permute-start(bf16[40,2048]{1,0:T(8,128)(2,1)S(1)} %get-tuple-element.47), channel_id=1, source_target_pairs={{0,9},{1,10},{2,11},{3,8},{4,13},{5,14},{6,15},{7,12},{8,1},{9,2},... | collective-permute-start | bytes 491528 | tf_op jit(solution)/shard_map/ppermute | solution.py:326
  19.3 3.5 %collective-permute-start.9 = (bf16[40,2048]{1,0:T(8,128)(2,1)S(1)}, bf16[40,2048]{1,0:T(8,128)(2,1)S(1)}, u32[]{:S(2)}, u32[]{:S(2)}) collective-permute-start(bf16[40,2048]{1,0:T(8,128)(2,1)S(1)} %get-tuple-element.49), channel_id=1, source_target_pairs={{0,10},{1,11},{2,8},{3,9},{4,14},{5,15},{6,12},{7,13},{8,2},{9,3},... | collective-permute-start | bytes 491528 | tf_op jit(solution)/shard_map/ppermute | solution.py:326
  22.8 1.3 %collective-permute-start.10 = (bf16[40,2048]{1,0:T(8,128)(2,1)S(1)}, bf16[40,2048]{1,0:T(8,128)(2,1)S(1)}, u32[]{:S(2)}, u32[]{:S(2)}) collective-permute-start(bf16[40,2048]{1,0:T(8,128)(2,1)S(1)} %get-tuple-element.51), channel_id=1, source_target_pairs={{0,11},{1,8},{2,9},{3,10},{4,15},{5,12},{6,13},{7,14},{8,3},{9,0},... | collective-permute-start | bytes 491528 | tf_op jit(solution)/shard_map/ppermute | solution.py:326
  24.1 2.5 %attend_a.1 = (bf16[128,2048]{1,0:T(8,128)(2,1)S(1)}, bf16[40,2048]{1,0:T(8,128)(2,1)S(1)}, bf16[40,2048]{1,0:T(8,128)(2,1)S(1)}, bf16[40,2048]{1,0:T(8,128)(2,1)S(1)}, bf16[40,2048]{1,0:T(8,128)(2,1)S(1)}) custom-call(s32[7]{0:T(128)S(1)} %stack.25.meta, s32[1,4]{1,0:T(1,128)S(1)} %copy-done.6, bf16[128,4096]{1,0:T(8,128)(2,1)S(1)} %bitcast.23, ...), custom_call_target="tpu_custom_call" | custom-call | flops 2000000000 | bytes 1000 | tf_op jit(solution)/shard_map/attend_a/pallas_call | solution.py:21
  26.6 5.6 %collective-permute-done.7.refs_0_ = bf16[40,2048]{1,0:T(8,128)(2,1)S(1)} collective-permute-done((bf16[40,2048]{1,0:T(8,128)(2,1)S(1)}, bf16[40,2048]{1,0:T(8,128)(2,1)S(1)}, u32[]{:S(2)}, u32[]{:S(2)}) %collective-permute-start.7) | collective-permute-done | bytes 163872 | tf_op jit(solution)/shard_map/ppermute | solution.py:326
  32.2 3.6 %collective-permute-start.4 = (bf16[40,2048]{1,0:T(8,128)(2,1)S(1)}, bf16[40,2048]{1,0:T(8,128)(2,1)S(1)}, u32[]{:S(2)}, u32[]{:S(2)}) collective-permute-start(bf16[40,2048]{1,0:T(8,128)(2,1)S(1)} %get-tuple-element.39), channel_id=1, source_target_pairs={{0,2},{1,3},{2,0},{3,1},{4,6},{5,7},{6,4},{7,5},{8,10},{9,11},{10,... | collective-permute-start | bytes 491528 | tf_op jit(solution)/shard_map/ppermute | solution.py:326
  35.8 3.1 %collective-permute-start.5 = (bf16[40,2048]{1,0:T(8,128)(2,1)S(1)}, bf16[40,2048]{1,0:T(8,128)(2,1)S(1)}, u32[]{:S(2)}, u32[]{:S(2)}) collective-permute-start(bf16[40,2048]{1,0:T(8,128)(2,1)S(1)} %get-tuple-element.40), channel_id=1, source_target_pairs={{0,3},{1,0},{2,1},{3,2},{4,7},{5,4},{6,5},{7,6},{8,11},{9,8},{10,9... | collective-permute-start | bytes 491528 | tf_op jit(solution)/shard_map/ppermute | solution.py:326
  38.9 3.3 %products_b.1 = bf16[160,1664]{1,0:T(8,128)(2,1)S(1)} custom-call(s32[7]{0:T(128)S(1)} %stack.25.meta, f32[1,4096]{1,0:T(1,128)S(1)} %bitcast.24, bf16[40,2048]{1,0:T(8,128)(2,1)S(1)} %collective-permute-done.7.refs_0_, bf16[40,2048]{1,0:T(8,128)(2,1)S(1)} %collective-permute-done.8.refs_1_, bf16[40,2048]{1,0:T(8,128)(2,1)S(1)} %collective-permute-done.9.refs_2_, ...), custom_call_target="tpu_custom_call" | custom-call | flops 20000000000 | bytes 1000 | tf_op jit(solution)/shard_map/products_b/pallas_call | solution.py:21
  42.2 1.4 %collective-permute-start.11 = (bf16[160,1664]{1,0:T(8,128)(2,1)S(1)}, bf16[160,1664]{1,0:T(8,128)(2,1)S(1)}, u32[]{:S(2)}, u32[]{:S(2)}) collective-permute-start(bf16[160,1664]{1,0:T(8,128)(2,1)S(1)} %products_b.1), channel_id=1, source_target_pairs={{0,8},{4,12},{8,0},{12,4},{1,9},{5,13},{9,1},{13,5},{2,10},{6,14},... | collective-permute-start | bytes 1597448 | tf_op jit(solution)/shard_map/ppermute | solution.py:261
  43.7 3.3 %collective-permute-done.4.refs_2_ = bf16[40,2048]{1,0:T(8,128)(2,1)S(1)} collective-permute-done((bf16[40,2048]{1,0:T(8,128)(2,1)S(1)}, bf16[40,2048]{1,0:T(8,128)(2,1)S(1)}, u32[]{:S(2)}, u32[]{:S(2)}) %collective-permute-start.4) | collective-permute-done | bytes 163872 | tf_op jit(solution)/shard_map/ppermute | solution.py:326
  46.9 3.3 %products_a.1 = (f32[160,1536]{1,0:T(8,128)S(1)}, f32[160,128]{1,0:T(8,128)S(1)}) custom-call(s32[7]{0:T(128)S(1)} %stack.25.meta, f32[1,4096]{1,0:T(1,128)S(1)} %bitcast.25, bf16[40,2048]{1,0:T(8,128)(2,1)S(1)} %get-tuple-element.37.refs_0_, bf16[40,2048]{1,0:T(8,128)(2,1)S(1)} %collective-permute-done.3.refs_1_, ...), custom_call_target="tpu_custom_call" | custom-call | flops 20000000000 | bytes 1000 | tf_op jit(solution)/shard_map/products_a/pallas_call | solution.py:21
  50.2 6.6 %collective-permute-done.11.far_ref = bf16[160,1664]{1,0:T(8,128)(2,1)S(1)} collective-permute-done((bf16[160,1664]{1,0:T(8,128)(2,1)S(1)}, bf16[160,1664]{1,0:T(8,128)(2,1)S(1)}, u32[]{:S(2)}, u32[]{:S(2)}) %collective-permute-start.11) | collective-permute-done | bytes 532512 | tf_op jit(solution)/shard_map/ppermute | solution.py:261
  56.8 1.5 %hidden_down_a.1 = (bf16[160,768]{1,0:T(8,128)(2,1)S(1)}, bf16[40,2048]{1,0:T(8,128)(2,1)S(1)}, bf16[40,2048]{1,0:T(8,128)(2,1)S(1)}, bf16[40,2048]{1,0:T(8,128)(2,1)S(1)}, bf16[40,2048]{1,0:T(8,128)(2,1)S(1)}) custom-call(s32[7]{0:T(128)S(1)} %stack.25.meta, f32[160,1536]{1,0:T(8,128)S(1)} %get-tuple-element.42.sums_ref, ...), custom_call_target="tpu_custom_call" | custom-call | flops 1000 | bytes 1000 | tf_op jit(solution)/shard_map/hidden_down_a/pallas_call | solution.py:21
  58.3 1.4 %collective-permute-start.13 = (bf16[160,768]{1,0:T(8,128)(2,1)S(1)}, bf16[160,768]{1,0:T(8,128)(2,1)S(1)}, u32[]{:S(2)}, u32[]{:S(2)}) collective-permute-start(bf16[160,768]{1,0:T(8,128)(2,1)S(1)} %get-tuple-element.54), channel_id=1, source_target_pairs={{0,8},{4,12},{8,0},{12,4},{1,9},{5,13},{9,1},{13,5},{2,10},{6,14},... | collective-permute-start | bytes 737288 | tf_op jit(solution)/shard_map/ppermute | solution.py:261
  59.8 5.4 %collective-permute-start.19 = (bf16[40,2048]{1,0:T(8,128)(2,1)S(1)}, bf16[40,2048]{1,0:T(8,128)(2,1)S(1)}, u32[]{:S(2)}, u32[]{:S(2)}) collective-permute-start(bf16[40,2048]{1,0:T(8,128)(2,1)S(1)} %get-tuple-element.61), channel_id=1, source_target_pairs={{0,2},{1,3},{2,0},{3,1},{4,6},{5,7},{6,4},{7,5},{8,10},{9,11},{10,... | collective-permute-start | bytes 491528 | tf_op jit(solution)/shard_map/ppermute | solution.py:326
  65.9 1.2 %down_b.1 = (bf16[40,2048]{1,0:T(8,128)(2,1)S(1)}, bf16[40,2048]{1,0:T(8,128)(2,1)S(1)}, bf16[40,2048]{1,0:T(8,128)(2,1)S(1)}, bf16[40,2048]{1,0:T(8,128)(2,1)S(1)}) custom-call(s32[7]{0:T(128)S(1)} %stack.25.meta, bf16[160,768]{1,0:T(8,128)(2,1)S(1)} %collective-permute-done.13.hidden_ref, bf16[768,1024]{1,0:T(8,128)(2,1)S(1)} %bitcast.18, ...), custom_call_target="tpu_custom_call" | custom-call | flops 1000 | bytes 1000 | tf_op jit(solution)/shard_map/down_b/pallas_call | solution.py:21
  67.2 1.4 %collective-permute-start.14 = (bf16[40,2048]{1,0:T(8,128)(2,1)S(1)}, bf16[40,2048]{1,0:T(8,128)(2,1)S(1)}, u32[]{:S(2)}, u32[]{:S(2)}) collective-permute-start(bf16[40,2048]{1,0:T(8,128)(2,1)S(1)} %get-tuple-element.55), channel_id=1, source_target_pairs={{0,8},{1,9},{2,10},{3,11},{4,12},{5,13},{6,14},{7,15},{8,0},{9,1},... | collective-permute-start | bytes 491528 | tf_op jit(solution)/shard_map/ppermute | solution.py:326
  68.6 3.2 %collective-permute-start.15 = (bf16[40,2048]{1,0:T(8,128)(2,1)S(1)}, bf16[40,2048]{1,0:T(8,128)(2,1)S(1)}, u32[]{:S(2)}, u32[]{:S(2)}) collective-permute-start(bf16[40,2048]{1,0:T(8,128)(2,1)S(1)} %get-tuple-element.56), channel_id=1, source_target_pairs={{0,11},{1,8},{2,9},{3,10},{4,15},{5,12},{6,13},{7,14},{8,3},{9,0},... | collective-permute-start | bytes 491528 | tf_op jit(solution)/shard_map/ppermute | solution.py:326
  71.8 4.5 %collective-permute-start.16 = (bf16[40,2048]{1,0:T(8,128)(2,1)S(1)}, bf16[40,2048]{1,0:T(8,128)(2,1)S(1)}, u32[]{:S(2)}, u32[]{:S(2)}) collective-permute-start(bf16[40,2048]{1,0:T(8,128)(2,1)S(1)} %get-tuple-element.57), channel_id=1, source_target_pairs={{0,10},{1,11},{2,8},{3,9},{4,14},{5,15},{6,12},{7,13},{8,2},{9,3},... | collective-permute-start | bytes 491528 | tf_op jit(solution)/shard_map/ppermute | solution.py:326
  76.3 9.5 %collective-permute-done.19.refs_2_ = bf16[40,2048]{1,0:T(8,128)(2,1)S(1)} collective-permute-done((bf16[40,2048]{1,0:T(8,128)(2,1)S(1)}, bf16[40,2048]{1,0:T(8,128)(2,1)S(1)}, u32[]{:S(2)}, u32[]{:S(2)}) %collective-permute-start.19) | collective-permute-done | bytes 163872 | tf_op jit(solution)/shard_map/ppermute | solution.py:326
  85.8 1.4 %combine_a.1.refs_4_ = bf16[128,2048]{1,0:T(8,128)(2,1)S(1)} custom-call(s32[7]{0:T(128)S(1)} %stack.25.meta, bf16[128,2048]{1,0:T(8,128)(2,1)S(1)} %get-tuple-element.45.att_ref, s32[1,128]{1,0:T(1,128)S(1)} %bitcast.28, f32[1,128]{1,0:T(1,128)S(1)} %bitcast.30, bf16[40,2048]{1,0:T(8,128)(2,1)S(1)} %get-tuple-element.59.refs_0_, ...), custom_call_target="tpu_custom_call" | custom-call | flops 20000000000 | bytes 1000 | tf_op jit(solution)/shard_map/combine_a/pallas_call | solution.py:21
  87.3 4.9 %collective-permute-done.16.refs_2_ = bf16[40,2048]{1,0:T(8,128)(2,1)S(1)} collective-permute-done((bf16[40,2048]{1,0:T(8,128)(2,1)S(1)}, bf16[40,2048]{1,0:T(8,128)(2,1)S(1)}, u32[]{:S(2)}, u32[]{:S(2)}) %collective-permute-start.16) | collective-permute-done | bytes 163872 | tf_op jit(solution)/shard_map/ppermute | solution.py:326
  92.2 1.7 %collective-permute-done.17.refs_3_ = bf16[40,2048]{1,0:T(8,128)(2,1)S(1)} collective-permute-done((bf16[40,2048]{1,0:T(8,128)(2,1)S(1)}, bf16[40,2048]{1,0:T(8,128)(2,1)S(1)}, u32[]{:S(2)}, u32[]{:S(2)}) %collective-permute-start.17) | collective-permute-done | bytes 163872 | tf_op jit(solution)/shard_map/ppermute | solution.py:326
  93.9 2.4 %combine_b.1 = bf16[128,4096]{1,0:T(8,128)(2,1)} custom-call(s32[7]{0:T(128)S(1)} %stack.25.meta, bf16[128,2048]{1,0:T(8,128)(2,1)S(1)} %get-tuple-element.35.att_ref, s32[1,128]{1,0:T(1,128)S(1)} %bitcast.29, f32[1,128]{1,0:T(1,128)S(1)} %bitcast.31, bf16[40,2048]{1,0:T(8,128)(2,1)S(1)} %collective-permute-done.14.refs_0_, ...), custom_call_target="tpu_custom_call" | custom-call | flops 20000000000 | bytes 1000 | tf_op jit(solution)/shard_map/combine_b/pallas_call | solution.py:21
  (43 shorter events, 1.8 us)
Async XLA Ops:
  0.0 2.5 %copy-start.9 = (bf16[1,128,256]{2,1,0:T(8,128)(2,1)S(1)}, bf16[1,128,256]{2,1,0:T(8,128)(2,1)}, u32[]{:S(2)}) copy-start(bf16[1,128,256]{2,1,0:T(8,128)(2,1)} %param.11) | copy-start | bytes 196612
  0.0 2.5 %copy-start.10 = (bf16[1,128,256]{2,1,0:T(8,128)(2,1)S(1)}, bf16[1,128,256]{2,1,0:T(8,128)(2,1)}, u32[]{:S(2)}) copy-start(bf16[1,128,256]{2,1,0:T(8,128)(2,1)} %param.10) | copy-start | bytes 196612
  0.0 11.3 %copy-start.6 = (s32[1,4]{1,0:T(1,128)S(1)}, s32[1,4]{1,0:T(1,128)}, u32[]{:S(2)}) copy-start(s32[1,4]{1,0:T(1,128)} %parents.3) | copy-start | bytes 52
  0.0 11.3 %copy-start.7 = (s32[1,128,1]{1,2,0:T(1,128)S(1)}, s32[1,128,1]{1,2,0:T(1,128)}, u32[]{:S(2)}) copy-start(s32[1,128,1]{1,2,0:T(1,128)} %param.13) | copy-start | bytes 1540
  2.6 6.5 %collective-permute-start.1 = (bf16[128,512]{1,0:T(8,128)(2,1)S(1)}, bf16[128,512]{1,0:T(8,128)(2,1)S(1)}, u32[]{:S(2)}, u32[]{:S(2)}) collective-permute-start(bf16[128,512]{1,0:T(8,128)(2,1)S(1)} %pad_maximum_fusion.refs_0_), channel_id=1, source_target_pairs={{0,8},{4,12},{8,0},{12,4},{1,9},{5,13},{9,1},{13,5},{2,10},{6,14},... | collective-permute-start | bytes 393224 | tf_op jit(solution)/shard_map/ppermute | solution.py:261
  5.6 3.5 %collective-permute-start = (bf16[128,512]{1,0:T(8,128)(2,1)S(1)}, bf16[128,512]{1,0:T(8,128)(2,1)S(1)}, u32[]{:S(2)}, u32[]{:S(2)}) collective-permute-start(bf16[128,512]{1,0:T(8,128)(2,1)S(1)} %pad_maximum_fusion.refs_0_), channel_id=1, source_target_pairs={{0,4},{4,0},{8,12},{12,8},{1,5},{5,1},{9,13},{13,9},{2,6},{6,2},{1... | collective-permute-start | bytes 393224 | tf_op jit(solution)/shard_map/ppermute | solution.py:261
  9.1 1.3 %collective-permute-start.2 = (bf16[128,512]{1,0:T(8,128)(2,1)S(1)}, bf16[128,512]{1,0:T(8,128)(2,1)S(1)}, u32[]{:S(2)}, u32[]{:S(2)}) collective-permute-start(bf16[128,512]{1,0:T(8,128)(2,1)S(1)} %collective-permute-done.1.refs_2_), channel_id=1, source_target_pairs={{0,4},{4,0},{8,12},{12,8},{1,5},{5,1},{9,13},{13,9},{2,6},{6,2},{1... | collective-permute-start | bytes 393224 | tf_op jit(solution)/shard_map/ppermute | solution.py:261
  10.4 0.7 copy-start.2
  11.1 27.8 %collective-permute-start.6 = (bf16[1024,1536]{1,0:T(8,128)(2,1)S(1)}, bf16[1024,1536]{1,0:T(8,128)(2,1)}, u32[]{:S(2)}, u32[]{:S(2)}) collective-permute-start(bf16[1024,1536]{1,0:T(8,128)(2,1)S(1)} %bitcast.19), channel_id=1, source_target_pairs={{0,4},{4,0},{8,12},{12,8},{1,5},{5,1},{9,13},{13,9},{2,6},{6,2},{1... | collective-permute-start | bytes 9437192 | tf_op jit(solution)/shard_map/ppermute | solution.py:261
  11.3 1.2 %copy-start.1 = (bf16[1,128,4096]{2,1,0:T(8,128)(2,1)S(1)}, bf16[1,128,4096]{2,1,0:T(8,128)(2,1)}, u32[]{:S(2)}) copy-start(bf16[1,128,4096]{2,1,0:T(8,128)(2,1)} %param.9) | copy-start | bytes 3145732
  12.5 0.9 copy-start.3
  13.5 10.7 %copy-start.4 = (bf16[128,512]{1,0:T(8,128)(2,1)S(1)}, bf16[128,512]{1,0:T(8,128)(2,1)}, u32[]{:S(2)}) copy-start(bf16[128,512]{1,0:T(8,128)(2,1)} %copy-done.2) | copy-start | bytes 393220
  15.9 16.3 %collective-permute-start.7 = (bf16[40,2048]{1,0:T(8,128)(2,1)S(1)}, bf16[40,2048]{1,0:T(8,128)(2,1)S(1)}, u32[]{:S(2)}, u32[]{:S(2)}) collective-permute-start(bf16[40,2048]{1,0:T(8,128)(2,1)S(1)} %get-tuple-element.44), channel_id=1, source_target_pairs={{0,8},{1,9},{2,10},{3,11},{4,12},{5,13},{6,14},{7,15},{8,0},{9,1},... | collective-permute-start | bytes 491528 | tf_op jit(solution)/shard_map/ppermute | solution.py:326
  17.7 14.5 %collective-permute-start.8 = (bf16[40,2048]{1,0:T(8,128)(2,1)S(1)}, bf16[40,2048]{1,0:T(8,128)(2,1)S(1)}, u32[]{:S(2)}, u32[]{:S(2)}) collective-permute-start(bf16[40,2048]{1,0:T(8,128)(2,1)S(1)} %get-tuple-element.47), channel_id=1, source_target_pairs={{0,9},{1,10},{2,11},{3,8},{4,13},{5,14},{6,15},{7,12},{8,1},{9,2},... | collective-permute-start | bytes 491528 | tf_op jit(solution)/shard_map/ppermute | solution.py:326
  19.3 16.5 %collective-permute-start.9 = (bf16[40,2048]{1,0:T(8,128)(2,1)S(1)}, bf16[40,2048]{1,0:T(8,128)(2,1)S(1)}, u32[]{:S(2)}, u32[]{:S(2)}) collective-permute-start(bf16[40,2048]{1,0:T(8,128)(2,1)S(1)} %get-tuple-element.49), channel_id=1, source_target_pairs={{0,10},{1,11},{2,8},{3,9},{4,14},{5,15},{6,12},{7,13},{8,2},{9,3},... | collective-permute-start | bytes 491528 | tf_op jit(solution)/shard_map/ppermute | solution.py:326
  22.8 16.1 %copy-start = (bf16[1,768,1024]{2,1,0:T(8,128)(2,1)S(1)}, bf16[1,768,1024]{2,1,0:T(8,128)(2,1)}, u32[]{:S(2)}) copy-start(bf16[1,768,1024]{2,1,0:T(8,128)(2,1)} %param.17) | copy-start | bytes 4718596
  22.8 16.1 %copy-start.5 = (f32[4096]{0:T(1024)S(1)}, f32[4096]{0:T(1024)}, u32[]{:S(2)}) copy-start(f32[4096]{0:T(1024)} %param.15) | copy-start | bytes 49156
  22.8 16.1 %collective-permute-start.10 = (bf16[40,2048]{1,0:T(8,128)(2,1)S(1)}, bf16[40,2048]{1,0:T(8,128)(2,1)S(1)}, u32[]{:S(2)}, u32[]{:S(2)}) collective-permute-start(bf16[40,2048]{1,0:T(8,128)(2,1)S(1)} %get-tuple-element.51), channel_id=1, source_target_pairs={{0,11},{1,8},{2,9},{3,10},{4,15},{5,12},{6,13},{7,14},{8,3},{9,0},... | collective-permute-start | bytes 491528 | tf_op jit(solution)/shard_map/ppermute | solution.py:326
  32.2 11.5 %collective-permute-start.3 = (bf16[40,2048]{1,0:T(8,128)(2,1)S(1)}, bf16[40,2048]{1,0:T(8,128)(2,1)S(1)}, u32[]{:S(2)}, u32[]{:S(2)}) collective-permute-start(bf16[40,2048]{1,0:T(8,128)(2,1)S(1)} %get-tuple-element.38), channel_id=1, source_target_pairs={{0,1},{1,2},{2,3},{3,0},{4,5},{5,6},{6,7},{7,4},{8,9},{9,10},{10,1... | collective-permute-start | bytes 491528 | tf_op jit(solution)/shard_map/ppermute | solution.py:326
  32.2 14.7 %collective-permute-start.4 = (bf16[40,2048]{1,0:T(8,128)(2,1)S(1)}, bf16[40,2048]{1,0:T(8,128)(2,1)S(1)}, u32[]{:S(2)}, u32[]{:S(2)}) collective-permute-start(bf16[40,2048]{1,0:T(8,128)(2,1)S(1)} %get-tuple-element.39), channel_id=1, source_target_pairs={{0,2},{1,3},{2,0},{3,1},{4,6},{5,7},{6,4},{7,5},{8,10},{9,11},{10,... | collective-permute-start | bytes 491528 | tf_op jit(solution)/shard_map/ppermute | solution.py:326
  35.8 11.1 %collective-permute-start.5 = (bf16[40,2048]{1,0:T(8,128)(2,1)S(1)}, bf16[40,2048]{1,0:T(8,128)(2,1)S(1)}, u32[]{:S(2)}, u32[]{:S(2)}) collective-permute-start(bf16[40,2048]{1,0:T(8,128)(2,1)S(1)} %get-tuple-element.40), channel_id=1, source_target_pairs={{0,3},{1,0},{2,1},{3,2},{4,7},{5,4},{6,5},{7,6},{8,11},{9,8},{10,9... | collective-permute-start | bytes 491528 | tf_op jit(solution)/shard_map/ppermute | solution.py:326
  38.9 11.3 %collective-permute-start.12 = (bf16[768,1024]{1,0:T(8,128)(2,1)S(1)}, bf16[768,1024]{1,0:T(8,128)(2,1)S(1)}, u32[]{:S(2)}, u32[]{:S(2)}) collective-permute-start(bf16[768,1024]{1,0:T(8,128)(2,1)S(1)} %bitcast.16), channel_id=1, source_target_pairs={{0,4},{4,0},{8,12},{12,8},{1,5},{5,1},{9,13},{13,9},{2,6},{6,2},{1... | collective-permute-start | bytes 4718600 | tf_op jit(solution)/shard_map/ppermute | solution.py:261
  42.2 14.6 %collective-permute-start.11 = (bf16[160,1664]{1,0:T(8,128)(2,1)S(1)}, bf16[160,1664]{1,0:T(8,128)(2,1)S(1)}, u32[]{:S(2)}, u32[]{:S(2)}) collective-permute-start(bf16[160,1664]{1,0:T(8,128)(2,1)S(1)} %products_b.1), channel_id=1, source_target_pairs={{0,8},{4,12},{8,0},{12,4},{1,9},{5,13},{9,1},{13,5},{2,10},{6,14},... | collective-permute-start | bytes 1597448 | tf_op jit(solution)/shard_map/ppermute | solution.py:261
  56.8 29.0 %copy-start.8 = (f32[1,128,1]{1,2,0:T(1,128)S(1)}, f32[1,128,1]{1,2,0:T(1,128)}, u32[]{:S(2)}) copy-start(f32[1,128,1]{1,2,0:T(1,128)} %param.14) | copy-start | bytes 1540
  58.3 7.6 %collective-permute-start.13 = (bf16[160,768]{1,0:T(8,128)(2,1)S(1)}, bf16[160,768]{1,0:T(8,128)(2,1)S(1)}, u32[]{:S(2)}, u32[]{:S(2)}) collective-permute-start(bf16[160,768]{1,0:T(8,128)(2,1)S(1)} %get-tuple-element.54), channel_id=1, source_target_pairs={{0,8},{4,12},{8,0},{12,4},{1,9},{5,13},{9,1},{13,5},{2,10},{6,14},... | collective-permute-start | bytes 737288 | tf_op jit(solution)/shard_map/ppermute | solution.py:261
  59.7 12.1 %collective-permute-start.18 = (bf16[40,2048]{1,0:T(8,128)(2,1)S(1)}, bf16[40,2048]{1,0:T(8,128)(2,1)S(1)}, u32[]{:S(2)}, u32[]{:S(2)}) collective-permute-start(bf16[40,2048]{1,0:T(8,128)(2,1)S(1)} %get-tuple-element.60), channel_id=1, source_target_pairs={{0,3},{1,0},{2,1},{3,2},{4,7},{5,4},{6,5},{7,6},{8,11},{9,8},{10,9... | collective-permute-start | bytes 491528 | tf_op jit(solution)/shard_map/ppermute | solution.py:326
  59.8 26.1 %collective-permute-start.19 = (bf16[40,2048]{1,0:T(8,128)(2,1)S(1)}, bf16[40,2048]{1,0:T(8,128)(2,1)S(1)}, u32[]{:S(2)}, u32[]{:S(2)}) collective-permute-start(bf16[40,2048]{1,0:T(8,128)(2,1)S(1)} %get-tuple-element.61), channel_id=1, source_target_pairs={{0,2},{1,3},{2,0},{3,1},{4,6},{5,7},{6,4},{7,5},{8,10},{9,11},{10,... | collective-permute-start | bytes 491528 | tf_op jit(solution)/shard_map/ppermute | solution.py:326
  65.2 20.7 %collective-permute-start.20 = (bf16[40,2048]{1,0:T(8,128)(2,1)S(1)}, bf16[40,2048]{1,0:T(8,128)(2,1)S(1)}, u32[]{:S(2)}, u32[]{:S(2)}) collective-permute-start(bf16[40,2048]{1,0:T(8,128)(2,1)S(1)} %get-tuple-element.62), channel_id=1, source_target_pairs={{0,1},{1,2},{2,3},{3,0},{4,5},{5,6},{6,7},{7,4},{8,9},{9,10},{10,1... | collective-permute-start | bytes 491528 | tf_op jit(solution)/shard_map/ppermute | solution.py:326
  67.2 20.1 %collective-permute-start.14 = (bf16[40,2048]{1,0:T(8,128)(2,1)S(1)}, bf16[40,2048]{1,0:T(8,128)(2,1)S(1)}, u32[]{:S(2)}, u32[]{:S(2)}) collective-permute-start(bf16[40,2048]{1,0:T(8,128)(2,1)S(1)} %get-tuple-element.55), channel_id=1, source_target_pairs={{0,8},{1,9},{2,10},{3,11},{4,12},{5,13},{6,14},{7,15},{8,0},{9,1},... | collective-permute-start | bytes 491528 | tf_op jit(solution)/shard_map/ppermute | solution.py:326
  68.6 18.7 %collective-permute-start.15 = (bf16[40,2048]{1,0:T(8,128)(2,1)S(1)}, bf16[40,2048]{1,0:T(8,128)(2,1)S(1)}, u32[]{:S(2)}, u32[]{:S(2)}) collective-permute-start(bf16[40,2048]{1,0:T(8,128)(2,1)S(1)} %get-tuple-element.56), channel_id=1, source_target_pairs={{0,11},{1,8},{2,9},{3,10},{4,15},{5,12},{6,13},{7,14},{8,3},{9,0},... | collective-permute-start | bytes 491528 | tf_op jit(solution)/shard_map/ppermute | solution.py:326
  71.8 20.4 %collective-permute-start.16 = (bf16[40,2048]{1,0:T(8,128)(2,1)S(1)}, bf16[40,2048]{1,0:T(8,128)(2,1)S(1)}, u32[]{:S(2)}, u32[]{:S(2)}) collective-permute-start(bf16[40,2048]{1,0:T(8,128)(2,1)S(1)} %get-tuple-element.57), channel_id=1, source_target_pairs={{0,10},{1,11},{2,8},{3,9},{4,14},{5,15},{6,12},{7,13},{8,2},{9,3},... | collective-permute-start | bytes 491528 | tf_op jit(solution)/shard_map/ppermute | solution.py:326
  85.8 8.1 %collective-permute-start.17 = (bf16[40,2048]{1,0:T(8,128)(2,1)S(1)}, bf16[40,2048]{1,0:T(8,128)(2,1)S(1)}, u32[]{:S(2)}, u32[]{:S(2)}) collective-permute-start(bf16[40,2048]{1,0:T(8,128)(2,1)S(1)} %get-tuple-element.58), channel_id=1, source_target_pairs={{0,9},{1,10},{2,11},{3,8},{4,13},{5,14},{6,15},{7,12},{8,1},{9,2},... | collective-permute-start | bytes 491528 | tf_op jit(solution)/shard_map/ppermute | solution.py:326

commit v5 on v4

--- a/solution.py
+++ b/solution.py
@@ -17,11 +17,11 @@
 SMEM = pl.BlockSpec(memory_space=pltpu.SMEM)
 
 
-def call(kernel, name, args, specs, outs, scratch=(), mib=16, flops=1000):
+def call(kernel, name, args, specs, outs, scratch=(), mib=16, flops=1000, out_space=pltpu.VMEM):
     return pl.pallas_call(
         kernel,
         in_specs=specs,
-        out_specs=[VMEM] * len(outs),
+        out_specs=[pl.BlockSpec(memory_space=out_space)] * len(outs),
         out_shape=[jax.ShapeDtypeStruct(s, d) for s, d in outs],
         scratch_shapes=list(scratch),
         compiler_params=pltpu.CompilerParams(vmem_limit_bytes=mib * MIB),
@@ -30,10 +30,16 @@
     )(*args)
 
 
+def shifts(experts):
+    return [experts // 2] + [s for s in range(1, experts) if 2 * s != experts] + [0]
+
+
 def placement_of(route_row, capacity, experts, first, relative):
     tokens = route_row.shape[1]
     if relative:
-        route_row = lax.rem(route_row - first + experts, experts)
+        shift = lax.rem(route_row - first + experts, experts)
+        for i, s in enumerate(shifts(experts)):
+            route_row = jnp.where(shift == s, i, route_row)
     rows = max(8, experts)
     expert_ids = lax.broadcasted_iota(jnp.int32, (rows, tokens), 0)
     hot = jnp.where(expert_ids == route_row, 1.0, 0.0)
@@ -51,7 +57,42 @@
     return jnp.where(slot_ids == slot, 1.0, 0.0)
 
 
-def attention_kernel(n_ctx, experts, capacity, blocks_out, half, meta, parents, q_ref, route_ref, *refs):
+def plan_kernel(experts, capacity, relative, meta, route_ref, weight_ref, q_hbm, *refs):
+    place_ref, back_ref, column_ref, q_ref, sem = refs
+    copy = pltpu.make_async_copy(q_hbm, q_ref, sem)
+    copy.start()
+    tokens = route_ref.shape[1]
+    place = placement_of(route_ref[...], capacity, experts, meta[2], relative)
+    place_ref[...] = place.astype(jnp.bfloat16)
+    back_ref[...] = place.T.astype(jnp.bfloat16)
+    diagonal = lax.broadcasted_iota(jnp.int32, (tokens, tokens), 0) == lax.broadcasted_iota(
+        jnp.int32, (tokens, tokens), 1
+    )
+    weight = jnp.sum(jnp.where(diagonal, weight_ref[...], 0.0), axis=1, keepdims=True)
+    column_ref[...] = jnp.broadcast_to(weight, column_ref.shape)
+    copy.wait()
+
+
+def plan(meta, route_row, weight_row, queries, experts, capacity, relative):
+    tokens = route_row.shape[1]
+    slots = experts * capacity
+    bf16 = jnp.bfloat16
+    return call(
+        functools.partial(plan_kernel, experts, capacity, relative),
+        "plan",
+        [meta, route_row, weight_row, queries],
+        [SMEM, VMEM, VMEM, pl.BlockSpec(memory_space=pl.ANY)],
+        [
+            ((slots, tokens), bf16),
+            ((tokens, slots), bf16),
+            ((tokens, 128), jnp.float32),
+            (queries.shape, bf16),
+        ],
+        [pltpu.SemaphoreType.DMA],
+    )
+
+
+def attention_kernel(n_ctx, half, meta, parents, q_ref, place_ref, *refs):
     kv = refs[:n_ctx]
     att_ref = refs[n_ctx]
     out_refs = refs[n_ctx + 1 :]
@@ -93,22 +134,21 @@
         weights = jnp.exp2(scores - peak).astype(jnp.bfloat16)
         total = jnp.dot(weights, values, preferred_element_type=jnp.float32)
         att_ref[:, columns] = (total[:, :HEAD_DIM] / total[:, HEAD_DIM:]).astype(jnp.bfloat16)
-    place = placement_of(route_ref[...], capacity, experts, meta[2], blocks_out > 1)
-    packed = jnp.dot(place.astype(jnp.bfloat16), att_ref[...], preferred_element_type=jnp.float32)
-    rows = experts * capacity // blocks_out
-    for k in range(blocks_out):
-        out_refs[k][...] = packed[k * rows : (k + 1) * rows].astype(jnp.bfloat16)
-
-
-def attention(meta, parents, queries, route_row, kvs, experts, capacity, blocks_out, half):
+    packed = jnp.dot(place_ref[...], att_ref[...], preferred_element_type=jnp.float32)
+    for k, out in enumerate(out_refs):
+        rows = out.shape[0]
+        out[...] = packed[k * rows : (k + 1) * rows].astype(jnp.bfloat16)
+
+
+def attention(meta, parents, queries, place, kvs, blocks_out, half):
     tokens, width = queries.shape
     half_width = width // KV_HEADS
-    rows = experts * capacity // blocks_out
+    rows = place.shape[0] // blocks_out
     bf16 = jnp.bfloat16
     outs = call(
-        functools.partial(attention_kernel, len(kvs), experts, capacity, blocks_out, half),
+        functools.partial(attention_kernel, len(kvs), half),
         "attend_" + "ab"[half],
-        [meta, parents, queries, route_row, *kvs],
+        [meta, parents, queries, place, *kvs],
         [SMEM, SMEM] + [VMEM] * (2 + len(kvs)),
         [((tokens, half_width), bf16)] + [((rows, half_width), bf16)] * blocks_out,
         flops=2 * 10**9,
@@ -214,46 +254,54 @@
     )
 
 
-def combine_kernel(experts, capacity, n_rows, last, meta, att_ref, route_ref, weight_ref, *refs):
-    row_refs, out_ref = refs[:n_rows], refs[-1]
-    tokens, half_width = att_ref.shape
-    place = placement_of(route_ref[...], capacity, experts, meta[2], n_rows > 1)
-    height = place.shape[0] // n_rows
-    mine = None
-    for k, row_ref in enumerate(row_refs):
-        part = lax.dot_general(
-            place[k * height : (k + 1) * height].astype(jnp.bfloat16),
-            row_ref[...],
-            (((0,), (0,)), ((), ())),
-            preferred_element_type=jnp.float32,
-        )
-        mine = part if mine is None else mine + part
-    diagonal = lax.broadcasted_iota(jnp.int32, (tokens, tokens), 0) == lax.broadcasted_iota(
-        jnp.int32, (tokens, tokens), 1
-    )
-    weight = jnp.sum(jnp.where(diagonal, weight_ref[...], 0.0), axis=1, keepdims=True)
-    value = (att_ref[...].astype(jnp.float32) + mine * weight).astype(jnp.bfloat16)
+def combine_kernel(last, meta, att_ref, back_ref, column_ref, *refs):
+    row_refs, refs = refs[: -1 - 3 * last], refs[-1 - 3 * last :]
+    half_width = att_ref.shape[1]
     if last:
-        before_ref = refs[n_rows]
+        before_ref, out_ref, value_ref, sems = refs
         before_at = pl.multiple_of(meta[0] * half_width, half_width)
         mine_at = pl.multiple_of((1 - meta[0]) * half_width, half_width)
-        out_ref[:, pl.ds(before_at, half_width)] = before_ref[...]
-        out_ref[:, pl.ds(mine_at, half_width)] = value
-    else:
-        out_ref[...] = value
-
-
-def combine(meta, att, route_row, weight_row, rows, experts, capacity, before):
+        copies = [
+            pltpu.make_async_copy(before_ref, out_ref.at[:, pl.ds(before_at, half_width)], sems.at[0])
+        ]
+        copies[0].start()
+    rows = jnp.concatenate([r[...].astype(jnp.float32) for r in row_refs], axis=0)
+    rows = rows.astype(jnp.bfloat16)
+    parts = 4 if last else 1
+    step = half_width // parts
+    for i in range(parts):
+        columns = slice(i * step, (i + 1) * step)
+        mine = jnp.dot(back_ref[...], rows[:, columns], preferred_element_type=jnp.float32)
+        value = att_ref[:, columns].astype(jnp.float32) + mine * column_ref[:, :1]
+        value = value.astype(jnp.bfloat16)
+        if last:
+            value_ref[:, columns] = value
+            place = out_ref.at[:, pl.ds(pl.multiple_of(mine_at + i * step, 128), step)]
+            copies.append(
+                pltpu.make_async_copy(value_ref.at[:, pl.ds(i * step, step)], place, sems.at[i + 1])
+            )
+            copies[-1].start()
+        else:
+            refs[0][:, columns] = value
+    if last:
+        for copy in copies:
+            copy.wait()
+
+
+def combine(meta, att, back, column, rows, before):
     tokens, half_width = att.shape
     last = before is not None
     extra = [before] if last else []
+    scratch = [pltpu.VMEM(att.shape, att.dtype), pltpu.SemaphoreType.DMA((5,))] if last else []
     return call(
-        functools.partial(combine_kernel, experts, capacity, len(rows), last),
+        functools.partial(combine_kernel, last),
         "combine_" + "ab"[last],
-        [meta, att, route_row, weight_row, *rows, *extra],
+        [meta, att, back, column, *rows, *extra],
         [SMEM] + [VMEM] * (3 + len(rows) + len(extra)),
         [((tokens, half_width * (1 + last)), jnp.bfloat16)],
+        scratch,
         flops=20 * 10**9,
+        out_space=pl.ANY if last else pltpu.VMEM,
     )[0]
 
 
@@ -289,18 +337,20 @@
     weight_row = route_weight.reshape(1, tokens)
     gain = norm_gain.reshape(1, width)
 
-    w_in = expert_in[0].reshape(depth, 2 * inner)
-
-    kv = jnp.concatenate([after(keys[0], w_in), values[0]], axis=1)
-    near, far = [kv], [swap(kv, "ctx", n_ctx, top)]
+
+    shards = [lax.rem(ctx, top) ^ j for j in range(top)]
+    row_at, col_at = 3, 3 + top
+    meta = jnp.stack([half, ctx, exp] + [j * depth for j in shards] + [j * columns for j in shards])
+    place, back, column, staged = plan(
+        meta, route_row, weight_row, queries[0], n_exp, capacity, shifted
+    )
+
+    kv = jnp.concatenate([keys[0], values[0]], axis=1)
+    near, far = [kv], [after(swap(kv, "ctx", n_ctx, top), place)]
     for bit in low_bits:
         near = near + [swap(x, "ctx", n_ctx, bit) for x in near]
         far = far + [swap(x, "ctx", n_ctx, bit) for x in far]
     kvs = near + far
-
-    shards = [lax.rem(ctx, top) ^ j for j in range(top)]
-    row_at, col_at = 3, 3 + top
-    meta = jnp.stack([half, ctx, exp] + [j * depth for j in shards] + [j * columns for j in shards])
 
     def spread(array):
         found = [array]
@@ -314,40 +364,37 @@
             whole = lax.all_to_all(whole, "exp", 0, 0, tiled=True).reshape(slots, half_width)
             return [swap(whole, "ctx", n_ctx, top) if cross else whole]
         moved = []
-        for k in range(n_exp):
-            shift = (n_exp - k) % n_exp if back else k
+        for block, distance in zip(blocks, shifts(n_exp)):
+            shift = (n_exp - distance) % n_exp if back else distance
             bit = top if cross else 0
             pairs = [
                 (c * n_exp + e, (c ^ bit) * n_exp + (e + shift) % n_exp)
                 for c in range(n_ctx)
                 for e in range(n_exp)
             ]
-            still = k == 0 and not cross
-            moved.append(blocks[k] if still else lax.ppermute(blocks[k], ("ctx", "exp"), pairs))
+            still = distance == 0 and not cross
+            moved.append(block if still else lax.ppermute(block, ("ctx", "exp"), pairs))
         return moved
 
     def attend(queries, part):
-        return attention(
-            meta, tree_parents, queries, route_row, kvs, n_exp, capacity, blocks_out, part
-        )
-
-    att_b, packed_b = attend(queries[0], 1)
+        return attention(meta, tree_parents, queries, place, kvs, blocks_out, part)
+
+    w_ins = [w.reshape(depth, 2 * inner) for w in spread(after(expert_in[0], *kvs[1:]))]
+    att_b, packed_b = attend(staged, 1)
     rows_b = send(packed_b, False, True)
-    att_a, packed_a = attend(after(queries[0], att_b), 0)
-    rows_a = send(packed_a, False, False)
-
-    w_ins = spread(after(w_in, *kvs[1:]))
-    w_outs = spread(after(expert_out[0], *rows_b))
+    att_a, packed_a = attend(after(staged, att_b, w_ins[-1]), 0)
     rows_b = [after(r, att_a) for r in rows_b]
     far_sums = products(meta, gain, rows_b, w_ins, row_at, slots, True)[0]
+    rows_a = send(packed_a, False, False)
     far_sums = swap(far_sums, "ctx", n_ctx, top)
+    w_outs = spread(after(expert_out[0], *rows_a))
     sums, squares = products(meta, gain, rows_a, w_ins, row_at, slots, False)
     hidden, out_a = finish(meta, sums, squares, far_sums, w_outs, col_at, width, blocks_out)
     back_a = send(out_a, True, False)
     out_b = down(meta, swap(hidden, "ctx", n_ctx, top), w_outs, col_at, width, blocks_out)
     back_b = send(out_b, True, True)
-    done = combine(meta, att_a, route_row, weight_row, back_a, n_exp, capacity, None)
-    done = combine(meta, att_b, route_row, weight_row, back_b, n_exp, capacity, done)
+    done = combine(meta, att_a, back, column, back_a, None)
+    done = combine(meta, att_b, back, column, back_b, done)
     return done[None]
 
 

time: 96.5 us -> 86.7 us (0.90)
  waiting for transfers between devices: 37.2 us -> 29.5 us
  Pallas kernels: 18 us -> 14.6 us
    ppermute x7, waiting for transfers between devices: 12.2 us -> 5.52 us  [swap(): return lax.ppermute(array, axis, [(i, i ^ bit) for i in range(size)])]
    pallas_call x8 -> x9, Pallas kernels: 18 us -> 14.6 us  [call(): pl.pallas_call(kernel, in_specs=specs, out_specs=[pl.BlockSpec(memory_spa...]
    ppermute x14, starting transfers between devices: 29.5 us -> 28.1 us  [send(): moved.append(block if still else lax.ppermute(block, ('ctx', 'exp'), pairs))]
    ppermute x7, starting transfers between devices: 5.98 us -> 7.05 us  [swap(): return lax.ppermute(array, axis, [(i, i ^ bit) for i in range(size)])]
    ppermute x14, waiting for transfers between devices: 25 us -> 24 us  [send(): moved.append(block if still else lax.ppermute(block, ('ctx', 'exp'), pairs))]
    unnamed x23 -> x14, local copies, waits for them, and re-layouts: 5.32 us -> 5.62 us
  transfers between devices with their start and end apart: 21 -> 21, of which waited for: 9 -> 10; matrix products, arithmetic and copies ran while one was open for 0% -> 4% of each run, Pallas kernels for 15% -> 13%
where the time goes in v5:
time: 86.7 us; the launch traced here: 85.9 us
  starting transfers between devices  35.1 us (40%)
  waiting for transfers between devices  29.5 us (34%)
  Pallas kernels  14.6 us (17%)
  local copies, waits for them, and re-layouts  5.71 us (7%)
  other arithmetic  0.88 us (1%)
    ppermute x14, starting transfers between devices, send(): moved.append(block if still else lax.ppermute(block, ('ctx', 'exp'), pairs))  28.1 us
    ppermute x14, waiting for transfers between devices, send(): moved.append(block if still else lax.ppermute(block, ('ctx', 'exp'), pairs))  24 us
    pallas_call x9, Pallas kernels, call(): pl.pallas_call(kernel, in_specs=specs, out_specs=[pl.BlockSpec(memory_spa...  14.6 us
    ppermute x7, starting transfers between devices, swap(): return lax.ppermute(array, axis, [(i, i ^ bit) for i in range(size)])  7.05 us
    unnamed x14, local copies, waits for them, and re-layouts  5.62 us
    ppermute x7, waiting for transfers between devices, swap(): return lax.ppermute(array, axis, [(i, i ^ bit) for i in range(size)])  5.52 us
  transfers between devices with their start and end apart: 21, of which 10 were waited for; matrix products, arithmetic and copies ran while one was open for 4% of the time, Pallas kernels for 13%

profile of v5, /device:TPU:0, one launch (start us, length us, event | category | flops | bytes accessed | tf_op | source)
XLA Modules:
  0.0 85.9 jit_solution(6172874785726408315)
XLA Ops:
  0.0 0.9 %pad_maximum_fusion.refs_0_ = bf16[128,512]{1,0:T(8,128)(2,1)S(1)} fusion(bf16[128,256]{1,0:T(8,128)(2,1)} %bitcast.33, bf16[128,256]{1,0:T(8,128)(2,1)} %bitcast.34), kind=kLoop, calls=%fused_computation | loop fusion | flops 262144 | bytes 262144 | tf_op jit(solution)/shard_map/concatenate | solution.py:348
  0.9 3.0 %collective-permute-start.1 = (bf16[128,512]{1,0:T(8,128)(2,1)S(1)}, bf16[128,512]{1,0:T(8,128)(2,1)S(1)}, u32[]{:S(2)}, u32[]{:S(2)}) collective-permute-start(bf16[128,512]{1,0:T(8,128)(2,1)S(1)} %pad_maximum_fusion.refs_0_), channel_id=1, source_target_pairs={{0,8},{4,12},{8,0},{12,4},{1,9},{5,13},{9,1},{13,5},{2,10},{6,14},... | collective-permute-start | bytes 393224 | tf_op jit(solution)/shard_map/ppermute | solution.py:309
  4.0 1.2 %copy-done.1 = bf16[1,128,4096]{2,1,0:T(8,128)(2,1)S(1)} copy-done((bf16[1,128,4096]{2,1,0:T(8,128)(2,1)S(1)}, bf16[1,128,4096]{2,1,0:T(8,128)(2,1)}, u32[]{:S(2)}) %copy-start.1) | copy-done | bytes 1048600
  6.5 0.9 %plan.1 = (bf16[160,128]{1,0:T(8,128)(2,1)S(1)}, bf16[128,160]{1,0:T(8,128)(2,1)S(1)}, f32[128,128]{1,0:T(8,128)S(1)}, bf16[128,4096]{1,0:T(8,128)(2,1)S(1)}) custom-call(s32[7]{0:T(128)S(1)} %stack.25.meta, s32[1,128]{1,0:T(1,128)S(1)} %bitcast.26, f32[1,128]{1,0:T(1,128)S(1)} %bitcast.27, bf16[128,4096]{1,0:T(8,128)(2,1)S(1)} %bitcast.25), custom_call_target="tpu_custom_call" | custom-call | flops 1000 | bytes 1000 | tf_op jit(solution)/shard_map/plan/pallas_call | solution.py:21
  8.0 1.0 %collective-permute-done.2.refs_3_ = bf16[128,512]{1,0:T(8,128)(2,1)S(1)} collective-permute-done((bf16[128,512]{1,0:T(8,128)(2,1)S(1)}, bf16[128,512]{1,0:T(8,128)(2,1)S(1)}, u32[]{:S(2)}, u32[]{:S(2)}) %collective-permute-start.2) | collective-permute-done | bytes 131104 | tf_op jit(solution)/shard_map/ppermute | solution.py:309
  9.4 2.5 %copy.11 = bf16[128,8,2,768]{3,1,2,0:T(8,128)(2,1)S(1)} copy(bf16[128,8,2,768]{3,2,1,0:T(2,128)(2,1)} %bitcast.31) | data formatting | bytes 6291456
  11.9 2.3 %attend_b.1 = (bf16[128,2048]{1,0:T(8,128)(2,1)S(1)}, bf16[40,2048]{1,0:T(8,128)(2,1)S(1)}, bf16[40,2048]{1,0:T(8,128)(2,1)S(1)}, bf16[40,2048]{1,0:T(8,128)(2,1)S(1)}, bf16[40,2048]{1,0:T(8,128)(2,1)S(1)}) custom-call(s32[7]{0:T(128)S(1)} %stack.25.meta, s32[1,4]{1,0:T(1,128)S(1)} %copy-done.5, bf16[128,4096]{1,0:T(8,128)(2,1)S(1)} %get-tuple-element.45.q_ref, ...), custom_call_target="tpu_custom_call" | custom-call | flops 2000000000 | bytes 1000 | tf_op jit(solution)/shard_map/attend_b/pallas_call | solution.py:21
  14.2 3.4 %collective-permute-start.7 = (bf16[40,2048]{1,0:T(8,128)(2,1)S(1)}, bf16[40,2048]{1,0:T(8,128)(2,1)S(1)}, u32[]{:S(2)}, u32[]{:S(2)}) collective-permute-start(bf16[40,2048]{1,0:T(8,128)(2,1)S(1)} %get-tuple-element.52), channel_id=1, source_target_pairs={{0,10},{1,11},{2,8},{3,9},{4,14},{5,15},{6,12},{7,13},{8,2},{9,3},... | collective-permute-start | bytes 491528 | tf_op jit(solution)/shard_map/ppermute | solution.py:376
  17.6 1.8 %collective-permute-start.8 = (bf16[40,2048]{1,0:T(8,128)(2,1)S(1)}, bf16[40,2048]{1,0:T(8,128)(2,1)S(1)}, u32[]{:S(2)}, u32[]{:S(2)}) collective-permute-start(bf16[40,2048]{1,0:T(8,128)(2,1)S(1)} %get-tuple-element.55), channel_id=1, source_target_pairs={{0,9},{1,10},{2,11},{3,8},{4,13},{5,14},{6,15},{7,12},{8,1},{9,2},... | collective-permute-start | bytes 491528 | tf_op jit(solution)/shard_map/ppermute | solution.py:376
  19.3 3.0 %collective-permute-start.9 = (bf16[40,2048]{1,0:T(8,128)(2,1)S(1)}, bf16[40,2048]{1,0:T(8,128)(2,1)S(1)}, u32[]{:S(2)}, u32[]{:S(2)}) collective-permute-start(bf16[40,2048]{1,0:T(8,128)(2,1)S(1)} %get-tuple-element.57), channel_id=1, source_target_pairs={{0,11},{1,8},{2,9},{3,10},{4,15},{5,12},{6,13},{7,14},{8,3},{9,0},... | collective-permute-start | bytes 491528 | tf_op jit(solution)/shard_map/ppermute | solution.py:376
  23.6 2.3 %attend_a.1 = (bf16[128,2048]{1,0:T(8,128)(2,1)S(1)}, bf16[40,2048]{1,0:T(8,128)(2,1)S(1)}, bf16[40,2048]{1,0:T(8,128)(2,1)S(1)}, bf16[40,2048]{1,0:T(8,128)(2,1)S(1)}, bf16[40,2048]{1,0:T(8,128)(2,1)S(1)}) custom-call(s32[7]{0:T(128)S(1)} %stack.25.meta, s32[1,4]{1,0:T(1,128)S(1)} %copy-done.5, bf16[128,4096]{1,0:T(8,128)(2,1)S(1)} %get-tuple-element.45.q_ref, ...), custom_call_target="tpu_custom_call" | custom-call | flops 2000000000 | bytes 1000 | tf_op jit(solution)/shard_map/attend_a/pallas_call | solution.py:21
  26.0 4.3 %collective-permute-done.7.refs_0_ = bf16[40,2048]{1,0:T(8,128)(2,1)S(1)} collective-permute-done((bf16[40,2048]{1,0:T(8,128)(2,1)S(1)}, bf16[40,2048]{1,0:T(8,128)(2,1)S(1)}, u32[]{:S(2)}, u32[]{:S(2)}) %collective-permute-start.7) | collective-permute-done | bytes 163872 | tf_op jit(solution)/shard_map/ppermute | solution.py:376
  30.3 3.8 %collective-permute-start.6 = (bf16[40,2048]{1,0:T(8,128)(2,1)S(1)}, bf16[40,2048]{1,0:T(8,128)(2,1)S(1)}, u32[]{:S(2)}, u32[]{:S(2)}) collective-permute-start(bf16[40,2048]{1,0:T(8,128)(2,1)S(1)} %get-tuple-element.48), channel_id=1, source_target_pairs={{0,3},{1,0},{2,1},{3,2},{4,7},{5,4},{6,5},{7,6},{8,11},{9,8},{10,9... | collective-permute-start | bytes 491528 | tf_op jit(solution)/shard_map/ppermute | solution.py:376
  34.1 1.2 %collective-permute-done.10.refs_3_ = bf16[40,2048]{1,0:T(8,128)(2,1)S(1)} collective-permute-done((bf16[40,2048]{1,0:T(8,128)(2,1)S(1)}, bf16[40,2048]{1,0:T(8,128)(2,1)S(1)}, u32[]{:S(2)}, u32[]{:S(2)}) %collective-permute-start.10) | collective-permute-done | bytes 163872 | tf_op jit(solution)/shard_map/ppermute | solution.py:376
  35.3 1.9 %products_b.1 = bf16[160,1664]{1,0:T(8,128)(2,1)S(1)} custom-call(s32[7]{0:T(128)S(1)} %stack.25.meta, f32[1,4096]{1,0:T(1,128)S(1)} %bitcast.28, bf16[40,2048]{1,0:T(8,128)(2,1)S(1)} %collective-permute-done.7.refs_0_, bf16[40,2048]{1,0:T(8,128)(2,1)S(1)} %collective-permute-done.8.refs_1_, bf16[40,2048]{1,0:T(8,128)(2,1)S(1)} %collective-permute-done.9.refs_2_, ...), custom_call_target="tpu_custom_call" | custom-call | flops 20000000000 | bytes 1000 | tf_op jit(solution)/shard_map/products_b/pallas_call | solution.py:21
  37.3 1.6 %collective-permute-start.11 = (bf16[160,1664]{1,0:T(8,128)(2,1)S(1)}, bf16[160,1664]{1,0:T(8,128)(2,1)S(1)}, u32[]{:S(2)}, u32[]{:S(2)}) collective-permute-start(bf16[160,1664]{1,0:T(8,128)(2,1)S(1)} %products_b.1), channel_id=1, source_target_pairs={{0,8},{4,12},{8,0},{12,4},{1,9},{5,13},{9,1},{13,5},{2,10},{6,14},... | collective-permute-start | bytes 1597448 | tf_op jit(solution)/shard_map/ppermute | solution.py:309
  38.8 5.3 %collective-permute-done.4.refs_0_ = bf16[40,2048]{1,0:T(8,128)(2,1)S(1)} collective-permute-done((bf16[40,2048]{1,0:T(8,128)(2,1)S(1)}, bf16[40,2048]{1,0:T(8,128)(2,1)S(1)}, u32[]{:S(2)}, u32[]{:S(2)}) %collective-permute-start.4) | collective-permute-done | bytes 163872 | tf_op jit(solution)/shard_map/ppermute | solution.py:376
  44.9 1.9 %products_a.1 = (f32[160,1536]{1,0:T(8,128)S(1)}, f32[160,128]{1,0:T(8,128)S(1)}) custom-call(s32[7]{0:T(128)S(1)} %stack.25.meta, f32[1,4096]{1,0:T(1,128)S(1)} %bitcast.29, bf16[40,2048]{1,0:T(8,128)(2,1)S(1)} %collective-permute-done.4.refs_0_, bf16[40,2048]{1,0:T(8,128)(2,1)S(1)} %collective-permute-done.5.refs_1_, ...), custom_call_target="tpu_custom_call" | custom-call | flops 20000000000 | bytes 1000 | tf_op jit(solution)/shard_map/products_a/pallas_call | solution.py:21
  46.8 4.5 %collective-permute-done.11.far_ref = bf16[160,1664]{1,0:T(8,128)(2,1)S(1)} collective-permute-done((bf16[160,1664]{1,0:T(8,128)(2,1)S(1)}, bf16[160,1664]{1,0:T(8,128)(2,1)S(1)}, u32[]{:S(2)}, u32[]{:S(2)}) %collective-permute-start.11) | collective-permute-done | bytes 532512 | tf_op jit(solution)/shard_map/ppermute | solution.py:309
  51.4 1.5 %hidden_down_a.1 = (bf16[160,768]{1,0:T(8,128)(2,1)S(1)}, bf16[40,2048]{1,0:T(8,128)(2,1)S(1)}, bf16[40,2048]{1,0:T(8,128)(2,1)S(1)}, bf16[40,2048]{1,0:T(8,128)(2,1)S(1)}, bf16[40,2048]{1,0:T(8,128)(2,1)S(1)}) custom-call(s32[7]{0:T(128)S(1)} %stack.25.meta, f32[160,1536]{1,0:T(8,128)S(1)} %get-tuple-element.50.sums_ref, ...), custom_call_target="tpu_custom_call" | custom-call | flops 1000 | bytes 1000 | tf_op jit(solution)/shard_map/hidden_down_a/pallas_call | solution.py:21
  52.8 1.6 %collective-permute-start.13 = (bf16[160,768]{1,0:T(8,128)(2,1)S(1)}, bf16[160,768]{1,0:T(8,128)(2,1)S(1)}, u32[]{:S(2)}, u32[]{:S(2)}) collective-permute-start(bf16[160,768]{1,0:T(8,128)(2,1)S(1)} %get-tuple-element.62), channel_id=1, source_target_pairs={{0,8},{4,12},{8,0},{12,4},{1,9},{5,13},{9,1},{13,5},{2,10},{6,14},... | collective-permute-start | bytes 737288 | tf_op jit(solution)/shard_map/ppermute | solution.py:309
  54.4 4.1 %collective-permute-start.18 = (bf16[40,2048]{1,0:T(8,128)(2,1)S(1)}, bf16[40,2048]{1,0:T(8,128)(2,1)S(1)}, u32[]{:S(2)}, u32[]{:S(2)}) collective-permute-start(bf16[40,2048]{1,0:T(8,128)(2,1)S(1)} %get-tuple-element.67), channel_id=1, source_target_pairs={{0,2},{1,3},{2,0},{3,1},{4,6},{5,7},{6,4},{7,5},{8,10},{9,11},{10,... | collective-permute-start | bytes 491528 | tf_op jit(solution)/shard_map/ppermute | solution.py:376
  58.5 3.0 %collective-permute-start.19 = (bf16[40,2048]{1,0:T(8,128)(2,1)S(1)}, bf16[40,2048]{1,0:T(8,128)(2,1)S(1)}, u32[]{:S(2)}, u32[]{:S(2)}) collective-permute-start(bf16[40,2048]{1,0:T(8,128)(2,1)S(1)} %get-tuple-element.68), channel_id=1, source_target_pairs={{0,3},{1,0},{2,1},{3,2},{4,7},{5,4},{6,5},{7,6},{8,11},{9,8},{10,9... | collective-permute-start | bytes 491528 | tf_op jit(solution)/shard_map/ppermute | solution.py:376
  61.5 1.2 %down_b.1 = (bf16[40,2048]{1,0:T(8,128)(2,1)S(1)}, bf16[40,2048]{1,0:T(8,128)(2,1)S(1)}, bf16[40,2048]{1,0:T(8,128)(2,1)S(1)}, bf16[40,2048]{1,0:T(8,128)(2,1)S(1)}) custom-call(s32[7]{0:T(128)S(1)} %stack.25.meta, bf16[160,768]{1,0:T(8,128)(2,1)S(1)} %collective-permute-done.13.hidden_ref, bf16[768,1024]{1,0:T(8,128)(2,1)S(1)} %bitcast.20, ...), custom_call_target="tpu_custom_call" | custom-call | flops 1000 | bytes 1000 | tf_op jit(solution)/shard_map/down_b/pallas_call | solution.py:21
  62.7 3.4 %collective-permute-start.14 = (bf16[40,2048]{1,0:T(8,128)(2,1)S(1)}, bf16[40,2048]{1,0:T(8,128)(2,1)S(1)}, u32[]{:S(2)}, u32[]{:S(2)}) collective-permute-start(bf16[40,2048]{1,0:T(8,128)(2,1)S(1)} %get-tuple-element.63), channel_id=1, source_target_pairs={{0,10},{1,11},{2,8},{3,9},{4,14},{5,15},{6,12},{7,13},{8,2},{9,3},... | collective-permute-start | bytes 491528 | tf_op jit(solution)/shard_map/ppermute | solution.py:376
  66.1 2.1 %collective-permute-start.15 = (bf16[40,2048]{1,0:T(8,128)(2,1)S(1)}, bf16[40,2048]{1,0:T(8,128)(2,1)S(1)}, u32[]{:S(2)}, u32[]{:S(2)}) collective-permute-start(bf16[40,2048]{1,0:T(8,128)(2,1)S(1)} %get-tuple-element.64), channel_id=1, source_target_pairs={{0,11},{1,8},{2,9},{3,10},{4,15},{5,12},{6,13},{7,14},{8,3},{9,0},... | collective-permute-start | bytes 491528 | tf_op jit(solution)/shard_map/ppermute | solution.py:376
  68.2 1.8 %collective-permute-done.18.refs_0_ = bf16[40,2048]{1,0:T(8,128)(2,1)S(1)} collective-permute-done((bf16[40,2048]{1,0:T(8,128)(2,1)S(1)}, bf16[40,2048]{1,0:T(8,128)(2,1)S(1)}, u32[]{:S(2)}, u32[]{:S(2)}) %collective-permute-start.18) | collective-permute-done | bytes 163872 | tf_op jit(solution)/shard_map/ppermute | solution.py:376
  70.0 1.6 %collective-permute-start.16 = (bf16[40,2048]{1,0:T(8,128)(2,1)S(1)}, bf16[40,2048]{1,0:T(8,128)(2,1)S(1)}, u32[]{:S(2)}, u32[]{:S(2)}) collective-permute-start(bf16[40,2048]{1,0:T(8,128)(2,1)S(1)} %get-tuple-element.65), channel_id=1, source_target_pairs={{0,9},{1,10},{2,11},{3,8},{4,13},{5,14},{6,15},{7,12},{8,1},{9,2},... | collective-permute-start | bytes 491528 | tf_op jit(solution)/shard_map/ppermute | solution.py:376
  71.6 1.2 %collective-permute-start.17 = (bf16[40,2048]{1,0:T(8,128)(2,1)S(1)}, bf16[40,2048]{1,0:T(8,128)(2,1)S(1)}, u32[]{:S(2)}, u32[]{:S(2)}) collective-permute-start(bf16[40,2048]{1,0:T(8,128)(2,1)S(1)} %get-tuple-element.66), channel_id=1, source_target_pairs={{0,8},{1,9},{2,10},{3,11},{4,12},{5,13},{6,14},{7,15},{8,0},{9,1},... | collective-permute-start | bytes 491528 | tf_op jit(solution)/shard_map/ppermute | solution.py:376
  72.8 0.9 %collective-permute-done.20.refs_2_ = bf16[40,2048]{1,0:T(8,128)(2,1)S(1)} collective-permute-done((bf16[40,2048]{1,0:T(8,128)(2,1)S(1)}, bf16[40,2048]{1,0:T(8,128)(2,1)S(1)}, u32[]{:S(2)}, u32[]{:S(2)}) %collective-permute-start.20) | collective-permute-done | bytes 163872 | tf_op jit(solution)/shard_map/ppermute | solution.py:376
  74.5 9.7 %collective-permute-done.14.refs_0_ = bf16[40,2048]{1,0:T(8,128)(2,1)S(1)} collective-permute-done((bf16[40,2048]{1,0:T(8,128)(2,1)S(1)}, bf16[40,2048]{1,0:T(8,128)(2,1)S(1)}, u32[]{:S(2)}, u32[]{:S(2)}) %collective-permute-start.14) | collective-permute-done | bytes 163872 | tf_op jit(solution)/shard_map/ppermute | solution.py:376
  84.2 1.7 %combine_b.1 = bf16[128,4096]{1,0:T(8,128)(2,1)} custom-call(s32[7]{0:T(128)S(1)} %stack.25.meta, bf16[128,2048]{1,0:T(8,128)(2,1)S(1)} %get-tuple-element.41.att_ref, bf16[128,160]{1,0:T(8,128)(2,1)S(1)} %get-tuple-element.42.back_ref, f32[128,128]{1,0:T(8,128)S(1)} %get-tuple-element.43.column_ref, bf16[40,2048]{1,0:T(8,128)(2,1)S(1)} %collective-permute-done.14.refs_0_, ...), custom_call_target="tpu_custom_call" | custom-call | flops 20000000000 | bytes 1000 | tf_op jit(solution)/shard_map/combine_b/pallas_call | solution.py:21
  (35 shorter events, 5.5 us)
Async XLA Ops:
  0.9 6.5 %collective-permute-start.1 = (bf16[128,512]{1,0:T(8,128)(2,1)S(1)}, bf16[128,512]{1,0:T(8,128)(2,1)S(1)}, u32[]{:S(2)}, u32[]{:S(2)}) collective-permute-start(bf16[128,512]{1,0:T(8,128)(2,1)S(1)} %pad_maximum_fusion.refs_0_), channel_id=1, source_target_pairs={{0,8},{4,12},{8,0},{12,4},{1,9},{5,13},{9,1},{13,5},{2,10},{6,14},... | collective-permute-start | bytes 393224 | tf_op jit(solution)/shard_map/ppermute | solution.py:309
  3.9 4.1 %collective-permute-start = (bf16[128,512]{1,0:T(8,128)(2,1)S(1)}, bf16[128,512]{1,0:T(8,128)(2,1)S(1)}, u32[]{:S(2)}, u32[]{:S(2)}) collective-permute-start(bf16[128,512]{1,0:T(8,128)(2,1)S(1)} %pad_maximum_fusion.refs_0_), channel_id=1, source_target_pairs={{0,4},{4,0},{8,12},{12,8},{1,5},{5,1},{9,13},{13,9},{2,6},{6,2},{1... | collective-permute-start | bytes 393224 | tf_op jit(solution)/shard_map/ppermute | solution.py:309
  4.0 1.2 %copy-start.1 = (bf16[1,128,4096]{2,1,0:T(8,128)(2,1)S(1)}, bf16[1,128,4096]{2,1,0:T(8,128)(2,1)}, u32[]{:S(2)}) copy-start(bf16[1,128,4096]{2,1,0:T(8,128)(2,1)} %param.9) | copy-start | bytes 3145732
  5.2 0.7 copy-start.2
  5.9 0.7 copy-start.3
  7.4 1.6 %collective-permute-start.2 = (bf16[128,512]{1,0:T(8,128)(2,1)S(1)}, bf16[128,512]{1,0:T(8,128)(2,1)S(1)}, u32[]{:S(2)}, u32[]{:S(2)}) collective-permute-start(bf16[128,512]{1,0:T(8,128)(2,1)S(1)} %collective-permute-done.1.refs_2_), channel_id=1, source_target_pairs={{0,4},{4,0},{8,12},{12,8},{1,5},{5,1},{9,13},{13,9},{2,6},{6,2},{1... | collective-permute-start | bytes 393224 | tf_op jit(solution)/shard_map/ppermute | solution.py:309
  9.0 14.0 %collective-permute-start.3 = (bf16[1024,2,768]{2,1,0:T(2,128)(2,1)}, bf16[1024,2,768]{2,1,0:T(2,128)(2,1)S(1)}, u32[]{:S(2)}, u32[]{:S(2)}) collective-permute-start(bf16[1024,2,768]{2,1,0:T(2,128)(2,1)} %bitcast.30), channel_id=1, source_target_pairs={{0,4},{4,0},{8,12},{12,8},{1,5},{5,1},{9,13},{13,9},{2,6},{6,2},{1... | collective-permute-start | bytes 9437192 | tf_op jit(solution)/shard_map/ppermute | solution.py:309
  9.4 2.5 %copy-start.5 = (s32[1,4]{1,0:T(1,128)S(1)}, s32[1,4]{1,0:T(1,128)}, u32[]{:S(2)}) copy-start(s32[1,4]{1,0:T(1,128)} %parents.3) | copy-start | bytes 52
  14.2 16.1 %collective-permute-start.7 = (bf16[40,2048]{1,0:T(8,128)(2,1)S(1)}, bf16[40,2048]{1,0:T(8,128)(2,1)S(1)}, u32[]{:S(2)}, u32[]{:S(2)}) collective-permute-start(bf16[40,2048]{1,0:T(8,128)(2,1)S(1)} %get-tuple-element.52), channel_id=1, source_target_pairs={{0,10},{1,11},{2,8},{3,9},{4,14},{5,15},{6,12},{7,13},{8,2},{9,3},... | collective-permute-start | bytes 491528 | tf_op jit(solution)/shard_map/ppermute | solution.py:376
  17.6 12.7 %collective-permute-start.8 = (bf16[40,2048]{1,0:T(8,128)(2,1)S(1)}, bf16[40,2048]{1,0:T(8,128)(2,1)S(1)}, u32[]{:S(2)}, u32[]{:S(2)}) collective-permute-start(bf16[40,2048]{1,0:T(8,128)(2,1)S(1)} %get-tuple-element.55), channel_id=1, source_target_pairs={{0,9},{1,10},{2,11},{3,8},{4,13},{5,14},{6,15},{7,12},{8,1},{9,2},... | collective-permute-start | bytes 491528 | tf_op jit(solution)/shard_map/ppermute | solution.py:376
  19.3 14.8 %collective-permute-start.9 = (bf16[40,2048]{1,0:T(8,128)(2,1)S(1)}, bf16[40,2048]{1,0:T(8,128)(2,1)S(1)}, u32[]{:S(2)}, u32[]{:S(2)}) collective-permute-start(bf16[40,2048]{1,0:T(8,128)(2,1)S(1)} %get-tuple-element.57), channel_id=1, source_target_pairs={{0,11},{1,8},{2,9},{3,10},{4,15},{5,12},{6,13},{7,14},{8,3},{9,0},... | collective-permute-start | bytes 491528 | tf_op jit(solution)/shard_map/ppermute | solution.py:376
  22.3 13.0 %collective-permute-start.10 = (bf16[40,2048]{1,0:T(8,128)(2,1)S(1)}, bf16[40,2048]{1,0:T(8,128)(2,1)S(1)}, u32[]{:S(2)}, u32[]{:S(2)}) collective-permute-start(bf16[40,2048]{1,0:T(8,128)(2,1)S(1)} %get-tuple-element.59), channel_id=1, source_target_pairs={{0,8},{1,9},{2,10},{3,11},{4,12},{5,13},{6,14},{7,15},{8,0},{9,1},... | collective-permute-start | bytes 491528 | tf_op jit(solution)/shard_map/ppermute | solution.py:376
  23.6 11.7 %copy-start.4 = (f32[4096]{0:T(1024)S(1)}, f32[4096]{0:T(1024)}, u32[]{:S(2)}) copy-start(f32[4096]{0:T(1024)} %param.15) | copy-start | bytes 49156
  25.9 18.1 %collective-permute-start.4 = (bf16[40,2048]{1,0:T(8,128)(2,1)S(1)}, bf16[40,2048]{1,0:T(8,128)(2,1)S(1)}, u32[]{:S(2)}, u32[]{:S(2)}) collective-permute-start(bf16[40,2048]{1,0:T(8,128)(2,1)S(1)} %get-tuple-element.46), channel_id=1, source_target_pairs={{0,2},{1,3},{2,0},{3,1},{4,6},{5,7},{6,4},{7,5},{8,10},{9,11},{10,... | collective-permute-start | bytes 491528 | tf_op jit(solution)/shard_map/ppermute | solution.py:376
  30.3 13.8 %collective-permute-start.5 = (bf16[40,2048]{1,0:T(8,128)(2,1)S(1)}, bf16[40,2048]{1,0:T(8,128)(2,1)S(1)}, u32[]{:S(2)}, u32[]{:S(2)}) collective-permute-start(bf16[40,2048]{1,0:T(8,128)(2,1)S(1)} %get-tuple-element.47), channel_id=1, source_target_pairs={{0,1},{1,2},{2,3},{3,0},{4,5},{5,6},{6,7},{7,4},{8,9},{9,10},{10,1... | collective-permute-start | bytes 491528 | tf_op jit(solution)/shard_map/ppermute | solution.py:376
  30.3 14.6 %collective-permute-start.6 = (bf16[40,2048]{1,0:T(8,128)(2,1)S(1)}, bf16[40,2048]{1,0:T(8,128)(2,1)S(1)}, u32[]{:S(2)}, u32[]{:S(2)}) collective-permute-start(bf16[40,2048]{1,0:T(8,128)(2,1)S(1)} %get-tuple-element.48), channel_id=1, source_target_pairs={{0,3},{1,0},{2,1},{3,2},{4,7},{5,4},{6,5},{7,6},{8,11},{9,8},{10,9... | collective-permute-start | bytes 491528 | tf_op jit(solution)/shard_map/ppermute | solution.py:376
  35.3 9.6 %copy-start = (bf16[1,768,1024]{2,1,0:T(8,128)(2,1)S(1)}, bf16[1,768,1024]{2,1,0:T(8,128)(2,1)}, u32[]{:S(2)}) copy-start(bf16[1,768,1024]{2,1,0:T(8,128)(2,1)} %param.17) | copy-start | bytes 4718596
  37.3 14.1 %collective-permute-start.11 = (bf16[160,1664]{1,0:T(8,128)(2,1)S(1)}, bf16[160,1664]{1,0:T(8,128)(2,1)S(1)}, u32[]{:S(2)}, u32[]{:S(2)}) collective-permute-start(bf16[160,1664]{1,0:T(8,128)(2,1)S(1)} %products_b.1), channel_id=1, source_target_pairs={{0,8},{4,12},{8,0},{12,4},{1,9},{5,13},{9,1},{13,5},{2,10},{6,14},... | collective-permute-start | bytes 1597448 | tf_op jit(solution)/shard_map/ppermute | solution.py:309
  44.9 6.5 %collective-permute-start.12 = (bf16[768,1024]{1,0:T(8,128)(2,1)S(1)}, bf16[768,1024]{1,0:T(8,128)(2,1)S(1)}, u32[]{:S(2)}, u32[]{:S(2)}) collective-permute-start(bf16[768,1024]{1,0:T(8,128)(2,1)S(1)} %bitcast.18), channel_id=1, source_target_pairs={{0,4},{4,0},{8,12},{12,8},{1,5},{5,1},{9,13},{13,9},{2,6},{6,2},{1... | collective-permute-start | bytes 4718600 | tf_op jit(solution)/shard_map/ppermute | solution.py:309
  52.8 8.6 %collective-permute-start.13 = (bf16[160,768]{1,0:T(8,128)(2,1)S(1)}, bf16[160,768]{1,0:T(8,128)(2,1)S(1)}, u32[]{:S(2)}, u32[]{:S(2)}) collective-permute-start(bf16[160,768]{1,0:T(8,128)(2,1)S(1)} %get-tuple-element.62), channel_id=1, source_target_pairs={{0,8},{4,12},{8,0},{12,4},{1,9},{5,13},{9,1},{13,5},{2,10},{6,14},... | collective-permute-start | bytes 737288 | tf_op jit(solution)/shard_map/ppermute | solution.py:309
  54.4 15.6 %collective-permute-start.18 = (bf16[40,2048]{1,0:T(8,128)(2,1)S(1)}, bf16[40,2048]{1,0:T(8,128)(2,1)S(1)}, u32[]{:S(2)}, u32[]{:S(2)}) collective-permute-start(bf16[40,2048]{1,0:T(8,128)(2,1)S(1)} %get-tuple-element.67), channel_id=1, source_target_pairs={{0,2},{1,3},{2,0},{3,1},{4,6},{5,7},{6,4},{7,5},{8,10},{9,11},{10,... | collective-permute-start | bytes 491528 | tf_op jit(solution)/shard_map/ppermute | solution.py:376
  58.5 13.1 %collective-permute-start.19 = (bf16[40,2048]{1,0:T(8,128)(2,1)S(1)}, bf16[40,2048]{1,0:T(8,128)(2,1)S(1)}, u32[]{:S(2)}, u32[]{:S(2)}) collective-permute-start(bf16[40,2048]{1,0:T(8,128)(2,1)S(1)} %get-tuple-element.68), channel_id=1, source_target_pairs={{0,3},{1,0},{2,1},{3,2},{4,7},{5,4},{6,5},{7,6},{8,11},{9,8},{10,9... | collective-permute-start | bytes 491528 | tf_op jit(solution)/shard_map/ppermute | solution.py:376
  61.5 12.2 %collective-permute-start.20 = (bf16[40,2048]{1,0:T(8,128)(2,1)S(1)}, bf16[40,2048]{1,0:T(8,128)(2,1)S(1)}, u32[]{:S(2)}, u32[]{:S(2)}) collective-permute-start(bf16[40,2048]{1,0:T(8,128)(2,1)S(1)} %get-tuple-element.69), channel_id=1, source_target_pairs={{0,1},{1,2},{2,3},{3,0},{4,5},{5,6},{6,7},{7,4},{8,9},{9,10},{10,1... | collective-permute-start | bytes 491528 | tf_op jit(solution)/shard_map/ppermute | solution.py:376
  62.7 21.5 %collective-permute-start.14 = (bf16[40,2048]{1,0:T(8,128)(2,1)S(1)}, bf16[40,2048]{1,0:T(8,128)(2,1)S(1)}, u32[]{:S(2)}, u32[]{:S(2)}) collective-permute-start(bf16[40,2048]{1,0:T(8,128)(2,1)S(1)} %get-tuple-element.63), channel_id=1, source_target_pairs={{0,10},{1,11},{2,8},{3,9},{4,14},{5,15},{6,12},{7,13},{8,2},{9,3},... | collective-permute-start | bytes 491528 | tf_op jit(solution)/shard_map/ppermute | solution.py:376
  66.1 18.1 %collective-permute-start.15 = (bf16[40,2048]{1,0:T(8,128)(2,1)S(1)}, bf16[40,2048]{1,0:T(8,128)(2,1)S(1)}, u32[]{:S(2)}, u32[]{:S(2)}) collective-permute-start(bf16[40,2048]{1,0:T(8,128)(2,1)S(1)} %get-tuple-element.64), channel_id=1, source_target_pairs={{0,11},{1,8},{2,9},{3,10},{4,15},{5,12},{6,13},{7,14},{8,3},{9,0},... | collective-permute-start | bytes 491528 | tf_op jit(solution)/shard_map/ppermute | solution.py:376
  70.0 14.2 %collective-permute-start.16 = (bf16[40,2048]{1,0:T(8,128)(2,1)S(1)}, bf16[40,2048]{1,0:T(8,128)(2,1)S(1)}, u32[]{:S(2)}, u32[]{:S(2)}) collective-permute-start(bf16[40,2048]{1,0:T(8,128)(2,1)S(1)} %get-tuple-element.65), channel_id=1, source_target_pairs={{0,9},{1,10},{2,11},{3,8},{4,13},{5,14},{6,15},{7,12},{8,1},{9,2},... | collective-permute-start | bytes 491528 | tf_op jit(solution)/shard_map/ppermute | solution.py:376
  71.6 12.7 %collective-permute-start.17 = (bf16[40,2048]{1,0:T(8,128)(2,1)S(1)}, bf16[40,2048]{1,0:T(8,128)(2,1)S(1)}, u32[]{:S(2)}, u32[]{:S(2)}) collective-permute-start(bf16[40,2048]{1,0:T(8,128)(2,1)S(1)} %get-tuple-element.66), channel_id=1, source_target_pairs={{0,8},{1,9},{2,10},{3,11},{4,12},{5,13},{6,14},{7,15},{8,0},{9,1},... | collective-permute-start | bytes 491528 | tf_op jit(solution)/shard_map/ppermute | solution.py:376

commit v6 on v5

--- a/solution.py
+++ b/solution.py
@@ -31,7 +31,7 @@
 
 
 def shifts(experts):
-    return [experts // 2] + [s for s in range(1, experts) if 2 * s != experts] + [0]
+    return [experts // 2, 0] + [s for s in range(1, experts) if 2 * s != experts]
 
 
 def placement_of(route_row, capacity, experts, first, relative):
@@ -57,20 +57,30 @@
     return jnp.where(slot_ids == slot, 1.0, 0.0)
 
 
-def plan_kernel(experts, capacity, relative, meta, route_ref, weight_ref, q_hbm, *refs):
-    place_ref, back_ref, column_ref, q_ref, sem = refs
-    copy = pltpu.make_async_copy(q_hbm, q_ref, sem)
-    copy.start()
+def start_copies(sources, targets, sems):
+    copies = [
+        pltpu.make_async_copy(s, t, sems.at[i]) for i, (s, t) in enumerate(zip(sources, targets))
+    ]
+    for copy in copies:
+        copy.start()
+    return copies
+
+
+def plan_kernel(experts, capacity, relative, meta, route_hbm, weight_hbm, q_hbm, *refs):
+    place_ref, back_ref, column_ref, q_ref, route_ref, weight_ref, sems = refs
+    copies = start_copies((route_hbm, weight_hbm, q_hbm), (route_ref, weight_ref, q_ref), sems)
     tokens = route_ref.shape[1]
+    copies[0].wait()
     place = placement_of(route_ref[...], capacity, experts, meta[2], relative)
     place_ref[...] = place.astype(jnp.bfloat16)
     back_ref[...] = place.T.astype(jnp.bfloat16)
     diagonal = lax.broadcasted_iota(jnp.int32, (tokens, tokens), 0) == lax.broadcasted_iota(
         jnp.int32, (tokens, tokens), 1
     )
+    copies[1].wait()
     weight = jnp.sum(jnp.where(diagonal, weight_ref[...], 0.0), axis=1, keepdims=True)
     column_ref[...] = jnp.broadcast_to(weight, column_ref.shape)
-    copy.wait()
+    copies[2].wait()
 
 
 def plan(meta, route_row, weight_row, queries, experts, capacity, relative):
@@ -81,18 +91,22 @@
         functools.partial(plan_kernel, experts, capacity, relative),
         "plan",
         [meta, route_row, weight_row, queries],
-        [SMEM, VMEM, VMEM, pl.BlockSpec(memory_space=pl.ANY)],
+        [SMEM] + [pl.BlockSpec(memory_space=pltpu.HBM)] * 3,
         [
             ((slots, tokens), bf16),
             ((tokens, slots), bf16),
             ((tokens, 128), jnp.float32),
             (queries.shape, bf16),
         ],
-        [pltpu.SemaphoreType.DMA],
-    )
-
-
-def attention_kernel(n_ctx, half, meta, parents, q_ref, place_ref, *refs):
+        [
+            pltpu.VMEM(route_row.shape, route_row.dtype),
+            pltpu.VMEM(weight_row.shape, weight_row.dtype),
+            pltpu.SemaphoreType.DMA((3,)),
+        ],
+    )
+
+
+def attention_kernel(n_ctx, half, parent_at, meta, q_ref, place_ref, *refs):
     kv = refs[:n_ctx]
     att_ref = refs[n_ctx]
     out_refs = refs[n_ctx + 1 :]
@@ -103,7 +117,7 @@
     reached = [jnp.int32(0)] * n_ctx
     current = me
     for _ in range(n_ctx):
-        current = parents[0, current]
+        current = meta[parent_at + current]
         for j in range(1, n_ctx):
             reached[j] = jnp.where(current == (me ^ j), jnp.int32(1), reached[j])
     causal = lax.broadcasted_iota(jnp.int32, (tokens, tokens), 1) <= lax.broadcasted_iota(
@@ -140,16 +154,16 @@
         out[...] = packed[k * rows : (k + 1) * rows].astype(jnp.bfloat16)
 
 
-def attention(meta, parents, queries, place, kvs, blocks_out, half):
+def attention(meta, parent_at, queries, place, kvs, blocks_out, half):
     tokens, width = queries.shape
     half_width = width // KV_HEADS
     rows = place.shape[0] // blocks_out
     bf16 = jnp.bfloat16
     outs = call(
-        functools.partial(attention_kernel, len(kvs), half),
+        functools.partial(attention_kernel, len(kvs), half, parent_at),
         "attend_" + "ab"[half],
-        [meta, parents, queries, place, *kvs],
-        [SMEM, SMEM] + [VMEM] * (2 + len(kvs)),
+        [meta, queries, place, *kvs],
+        [SMEM] + [VMEM] * (2 + len(kvs)),
         [((tokens, half_width), bf16)] + [((rows, half_width), bf16)] * blocks_out,
         flops=2 * 10**9,
     )
@@ -184,7 +198,8 @@
         refs[1][...] = squares
 
 
-def products(meta, gain, rows, weights, row_at, slots, packed):
+def products(meta, gain, rows, weights, row_at, packed):
+    slots = sum(r.shape[0] for r in rows)
     half_width = rows[0].shape[1]
     columns = weights[0].shape[1]
     f32, bf16 = jnp.float32, jnp.bfloat16
@@ -196,7 +211,7 @@
         [SMEM] + [VMEM] * (1 + len(rows) + len(weights)),
         outs,
         [pltpu.VMEM((slots, half_width), bf16)],
-        flops=20 * 10**9,
+        flops=20 * 10**9 if packed else 1000,
     )
 
 
@@ -209,28 +224,32 @@
             out[:, where] = value[k * height : (k + 1) * height].astype(jnp.bfloat16)
 
 
-def finish_kernel(n_weights, col_at, width, meta, sums_ref, squares_ref, far_ref, *refs):
+def finish_kernel(n_far, n_weights, col_at, width, meta, sums_ref, squares_ref, *refs):
+    far_refs, refs = refs[:n_far], refs[n_far:]
     w_refs, hidden_ref, out_refs = refs[:n_weights], refs[n_weights], refs[n_weights + 1 :]
     inner = hidden_ref.shape[1]
-    squares = squares_ref[:, :1]
-    for at in (0, 64):
-        squares = squares + far_ref[:, 2 * inner + at : 2 * inner + at + 1].astype(jnp.float32)
-    factor = lax.rsqrt(squares * (1.0 / width) + 1e-06)
-    gate = (sums_ref[:, :inner] + far_ref[:, :inner].astype(jnp.float32)) * factor
-    up = (sums_ref[:, inner:] + far_ref[:, inner : 2 * inner].astype(jnp.float32)) * factor
-    hidden = (gate / (1.0 + jnp.exp(-gate)) * up).astype(jnp.bfloat16)
-    hidden_ref[...] = hidden
-    store_down(meta, col_at, w_refs, hidden, out_refs)
+    start = 0
+    for far_ref in far_refs:
+        rows = slice(start, start + far_ref.shape[0])
+        start = rows.stop
+        squares = squares_ref[rows, :1]
+        for at in (0, 64):
+            squares = squares + far_ref[:, 2 * inner + at : 2 * inner + at + 1].astype(jnp.float32)
+        factor = lax.rsqrt(squares * (1.0 / width) + 1e-06)
+        gate = (sums_ref[rows, :inner] + far_ref[:, :inner].astype(jnp.float32)) * factor
+        up = (sums_ref[rows, inner:] + far_ref[:, inner : 2 * inner].astype(jnp.float32)) * factor
+        hidden_ref[rows] = (gate / (1.0 + jnp.exp(-gate)) * up).astype(jnp.bfloat16)
+    store_down(meta, col_at, w_refs, hidden_ref[...], out_refs)
 
 
 def finish(meta, sums, squares, far, weights, col_at, width, blocks_out):
     slots, columns = sums.shape
     bf16 = jnp.bfloat16
     outs = call(
-        functools.partial(finish_kernel, len(weights), col_at, width),
+        functools.partial(finish_kernel, len(far), len(weights), col_at, width),
         "hidden_down_a",
-        [meta, sums, squares, far, *weights],
-        [SMEM] + [VMEM] * (3 + len(weights)),
+        [meta, sums, squares, *far, *weights],
+        [SMEM] + [VMEM] * (2 + len(far) + len(weights)),
         [((slots, columns // 2), bf16)]
         + [((slots // blocks_out, width // KV_HEADS), bf16)] * blocks_out,
     )
@@ -340,7 +359,9 @@
 
     shards = [lax.rem(ctx, top) ^ j for j in range(top)]
     row_at, col_at = 3, 3 + top
+    parent_at = 3 + 2 * top
     meta = jnp.stack([half, ctx, exp] + [j * depth for j in shards] + [j * columns for j in shards])
+    meta = jnp.concatenate([meta, tree_parents[0]])
     place, back, column, staged = plan(
         meta, route_row, weight_row, queries[0], n_exp, capacity, shifted
     )
@@ -358,7 +379,7 @@
             found = found + [swap(a, "ctx", n_ctx, bit) for a in found]
         return found
 
-    def send(blocks, back, cross):
+    def send(blocks, back, cross, gates={}):
         if not shifted:
             whole = blocks[0].reshape(n_exp, capacity, half_width)
             whole = lax.all_to_all(whole, "exp", 0, 0, tiled=True).reshape(slots, half_width)
@@ -373,25 +394,42 @@
                 for e in range(n_exp)
             ]
             still = distance == 0 and not cross
+            if len(moved) in gates:
+                block = after(block, *gates[len(moved)](moved))
             moved.append(block if still else lax.ppermute(block, ("ctx", "exp"), pairs))
         return moved
 
     def attend(queries, part):
-        return attention(meta, tree_parents, queries, place, kvs, blocks_out, part)
-
-    w_ins = [w.reshape(depth, 2 * inner) for w in spread(after(expert_in[0], *kvs[1:]))]
+        return attention(meta, parent_at, queries, place, kvs, blocks_out, part)
+
+    w_raw = spread(after(expert_in[0], *kvs[1:]))
     att_b, packed_b = attend(staged, 1)
     rows_b = send(packed_b, False, True)
-    att_a, packed_a = attend(after(staged, att_b, w_ins[-1]), 0)
+    w_ins = [after(w, att_b).reshape(depth, 2 * inner) for w in w_raw]
+    w_outs = spread(after(expert_out[0], rows_b[0]))
+    att_a, packed_a = attend(after(staged, att_b, rows_b[0], *w_ins), 0)
     rows_b = [after(r, att_a) for r in rows_b]
-    far_sums = products(meta, gain, rows_b, w_ins, row_at, slots, True)[0]
-    rows_a = send(packed_a, False, False)
-    far_sums = swap(far_sums, "ctx", n_ctx, top)
-    w_outs = spread(after(expert_out[0], *rows_a))
-    sums, squares = products(meta, gain, rows_a, w_ins, row_at, slots, False)
-    hidden, out_a = finish(meta, sums, squares, far_sums, w_outs, col_at, width, blocks_out)
+    rows_b[-1] = after(rows_b[-1], w_outs[-1])
+    pair = len(rows_b) // 2 if len(rows_b) % 4 == 0 else len(rows_b)
+    groups = [rows_b[i : i + pair] for i in range(0, len(rows_b), pair)]
+    far_sums = [products(meta, gain, g, w_ins, row_at, True)[0] for g in groups]
+    gates = {2: lambda m: [far_sums[0]], 3: lambda m: [m[0]]} if shifted else {}
+    rows_a = send(packed_a, False, False, gates)
+    made = far_sums[-1]
+    far_sums = [swap(f, "ctx", n_ctx, top) for f in far_sums]
+    out_a, hiddens, moved = [], [], []
+    for i, far in enumerate(far_sums):
+        rows = [after(r, made, *hiddens) for r in rows_a[i * pair : (i + 1) * pair]]
+        sums, squares = products(meta, gain, rows, w_ins, row_at, False)
+        sums = after(sums, *moved)
+        hidden, blocks = finish(meta, sums, squares, [far], w_outs, col_at, width, len(rows))
+        out_a += blocks
+        hiddens.append(hidden)
+        moved.append(swap(hidden, "ctx", n_ctx, top))
     back_a = send(out_a, True, False)
-    out_b = down(meta, swap(hidden, "ctx", n_ctx, top), w_outs, col_at, width, blocks_out)
+    out_b = []
+    for hidden in moved:
+        out_b += down(meta, hidden, w_outs, col_at, width, pair)
     back_b = send(out_b, True, True)
     done = combine(meta, att_a, back, column, back_a, None)
     done = combine(meta, att_b, back, column, back_b, done)

time: 86.7 us -> 78.7 us (0.908)
  waiting for transfers between devices: 29.5 us -> 21.4 us
  Pallas kernels: 14.6 us -> 20.7 us
  starting transfers between devices: 35.1 us -> 30.9 us
  local copies, waits for them, and re-layouts: 5.71 us -> 4.46 us
    pallas_call x9 -> x13, Pallas kernels: 14.6 us -> 20.7 us  [call(): pl.pallas_call(kernel, in_specs=specs, out_specs=[pl.BlockSpec(memory_spa...]
    ppermute x14, waiting for transfers between devices: 24 us -> 18 us  [send(): moved.append(block if still else lax.ppermute(block, ('ctx', 'exp'), pairs))]
    ppermute x14, starting transfers between devices: 28.1 us -> 23.3 us  [send(): moved.append(block if still else lax.ppermute(block, ('ctx', 'exp'), pairs))]
    ppermute x7 -> x9, waiting for transfers between devices: 5.52 us -> 3.34 us  [swap(): return lax.ppermute(array, axis, [(i, i ^ bit) for i in range(size)])]
    unnamed x14, local copies, waits for them, and re-layouts: 5.62 us -> 3.72 us
    ppermute x7 -> x9, starting transfers between devices: 7.05 us -> 7.63 us  [swap(): return lax.ppermute(array, axis, [(i, i ^ bit) for i in range(size)])]
  transfers between devices with their start and end apart: 21 -> 23, of which waited for: 10 -> 9; matrix products, arithmetic and copies ran while one was open for 4% -> 2% of each run, Pallas kernels for 13% -> 24%
where the time goes in v6:
time: 78.7 us; the launch traced here: 78.5 us
  starting transfers between devices  30.9 us (39%)
  waiting for transfers between devices  21.4 us (27%)
  Pallas kernels  20.7 us (26%)
  local copies, waits for them, and re-layouts  4.46 us (6%)
  other arithmetic  0.88 us (1%)
    ppermute x14, starting transfers between devices, send(): moved.append(block if still else lax.ppermute(block, ('ctx', 'exp'), pairs))  23.3 us
    pallas_call x13, Pallas kernels, call(): pl.pallas_call(kernel, in_specs=specs, out_specs=[pl.BlockSpec(memory_spa...  20.7 us
    ppermute x14, waiting for transfers between devices, send(): moved.append(block if still else lax.ppermute(block, ('ctx', 'exp'), pairs))  18 us
    ppermute x9, starting transfers between devices, swap(): return lax.ppermute(array, axis, [(i, i ^ bit) for i in range(size)])  7.63 us
    unnamed x14, local copies, waits for them, and re-layouts  3.72 us
    ppermute x9, waiting for transfers between devices, swap(): return lax.ppermute(array, axis, [(i, i ^ bit) for i in range(size)])  3.34 us
  transfers between devices with their start and end apart: 23, of which 9 were waited for; matrix products, arithmetic and copies ran while one was open for 2% of the time, Pallas kernels for 24%

profile of v6, /device:TPU:0, one launch (start us, length us, event | category | flops | bytes accessed | tf_op | source)
XLA Modules:
  0.0 78.5 jit_solution(7882996441635474684)
XLA Ops:
  0.9 3.0 %collective-permute-start.1 = (bf16[128,512]{1,0:T(8,128)(2,1)S(1)}, bf16[128,512]{1,0:T(8,128)(2,1)S(1)}, u32[]{:S(2)}, u32[]{:S(2)}) collective-permute-start(bf16[128,512]{1,0:T(8,128)(2,1)S(1)} %pad_maximum_fusion.refs_0_), channel_id=1, source_target_pairs={{0,8},{4,12},{8,0},{12,4},{1,9},{5,13},{9,1},{13,5},{2,10},{6,14},... | collective-permute-start | bytes 393224 | tf_op jit(solution)/shard_map/ppermute | solution.py:328
  4.6 1.2 %copy-done.1 = bf16[1,128,4096]{2,1,0:T(8,128)(2,1)S(1)} copy-done((bf16[1,128,4096]{2,1,0:T(8,128)(2,1)S(1)}, bf16[1,128,4096]{2,1,0:T(8,128)(2,1)}, u32[]{:S(2)}) %copy-start.1) | copy-done | bytes 1048600
  7.2 1.0 %plan.1 = (bf16[160,128]{1,0:T(8,128)(2,1)S(1)}, bf16[128,160]{1,0:T(8,128)(2,1)S(1)}, f32[128,128]{1,0:T(8,128)S(1)}, bf16[128,4096]{1,0:T(8,128)(2,1)S(1)}) custom-call(s32[11]{0:T(128)S(1)} %concatenate.6.meta, s32[1,128]{1,0:T(1,128)S(1)} %bitcast.37, f32[1,128]{1,0:T(1,128)S(1)} %bitcast.38, bf16[128,4096]{1,0:T(8,128)(2,1)S(1)} %bitcast.32), custom_call_target="tpu_custom_call" | custom-call | flops 1000 | bytes 1000 | tf_op jit(solution)/shard_map/plan/pallas_call | solution.py:21
  8.7 1.0 %collective-permute-done.2.refs_3_ = bf16[128,512]{1,0:T(8,128)(2,1)S(1)} collective-permute-done((bf16[128,512]{1,0:T(8,128)(2,1)S(1)}, bf16[128,512]{1,0:T(8,128)(2,1)S(1)}, u32[]{:S(2)}, u32[]{:S(2)}) %collective-permute-start.2) | collective-permute-done | bytes 131104 | tf_op jit(solution)/shard_map/ppermute | solution.py:328
  10.1 2.3 %attend_b.1 = (bf16[128,2048]{1,0:T(8,128)(2,1)S(1)}, bf16[40,2048]{1,0:T(8,128)(2,1)S(1)}, bf16[40,2048]{1,0:T(8,128)(2,1)S(1)}, bf16[40,2048]{1,0:T(8,128)(2,1)S(1)}, bf16[40,2048]{1,0:T(8,128)(2,1)S(1)}) custom-call(s32[11]{0:T(128)S(1)} %concatenate.6.meta, bf16[128,4096]{1,0:T(8,128)(2,1)S(1)} %get-tuple-element.61.q_ref, ...), custom_call_target="tpu_custom_call" | custom-call | flops 2000000000 | bytes 1000 | tf_op jit(solution)/shard_map/attend_b/pallas_call | solution.py:21
  12.4 2.6 %collective-permute-start.3 = (bf16[40,2048]{1,0:T(8,128)(2,1)S(1)}, bf16[40,2048]{1,0:T(8,128)(2,1)S(1)}, u32[]{:S(2)}, u32[]{:S(2)}) collective-permute-start(bf16[40,2048]{1,0:T(8,128)(2,1)S(1)} %get-tuple-element.57), channel_id=1, source_target_pairs={{0,10},{1,11},{2,8},{3,9},{4,14},{5,15},{6,12},{7,13},{8,2},{9,3},... | collective-permute-start | bytes 491528 | tf_op jit(solution)/shard_map/ppermute | solution.py:399
  15.6 1.5 %collective-permute-start.9 = (bf16[40,2048]{1,0:T(8,128)(2,1)S(1)}, bf16[40,2048]{1,0:T(8,128)(2,1)S(1)}, u32[]{:S(2)}, u32[]{:S(2)}) collective-permute-start(bf16[40,2048]{1,0:T(8,128)(2,1)S(1)} %get-tuple-element.76), channel_id=1, source_target_pairs={{0,8},{1,9},{2,10},{3,11},{4,12},{5,13},{6,14},{7,15},{8,0},{9,1},... | collective-permute-start | bytes 491528 | tf_op jit(solution)/shard_map/ppermute | solution.py:399
  17.2 1.3 %collective-permute-start.7 = (bf16[40,2048]{1,0:T(8,128)(2,1)S(1)}, bf16[40,2048]{1,0:T(8,128)(2,1)S(1)}, u32[]{:S(2)}, u32[]{:S(2)}) collective-permute-start(bf16[40,2048]{1,0:T(8,128)(2,1)S(1)} %get-tuple-element.66), channel_id=1, source_target_pairs={{0,11},{1,8},{2,9},{3,10},{4,15},{5,12},{6,13},{7,14},{8,3},{9,0},... | collective-permute-start | bytes 491528 | tf_op jit(solution)/shard_map/ppermute | solution.py:399
  18.5 1.6 %collective-permute-start.6 = (bf16[40,2048]{1,0:T(8,128)(2,1)S(1)}, bf16[40,2048]{1,0:T(8,128)(2,1)S(1)}, u32[]{:S(2)}, u32[]{:S(2)}) collective-permute-start(bf16[40,2048]{1,0:T(8,128)(2,1)S(1)} %get-tuple-element.63), channel_id=1, source_target_pairs={{0,9},{1,10},{2,11},{3,8},{4,13},{5,14},{6,15},{7,12},{8,1},{9,2},... | collective-permute-start | bytes 491528 | tf_op jit(solution)/shard_map/ppermute | solution.py:399
  20.1 4.8 %collective-permute-done.3.refs_0_ = bf16[40,2048]{1,0:T(8,128)(2,1)S(1)} collective-permute-done((bf16[40,2048]{1,0:T(8,128)(2,1)S(1)}, bf16[40,2048]{1,0:T(8,128)(2,1)S(1)}, u32[]{:S(2)}, u32[]{:S(2)}) %collective-permute-start.3) | collective-permute-done | bytes 163872 | tf_op jit(solution)/shard_map/ppermute | solution.py:399
  25.5 2.3 %attend_a.1 = (bf16[128,2048]{1,0:T(8,128)(2,1)S(1)}, bf16[40,2048]{1,0:T(8,128)(2,1)S(1)}, bf16[40,2048]{1,0:T(8,128)(2,1)S(1)}, bf16[40,2048]{1,0:T(8,128)(2,1)S(1)}, bf16[40,2048]{1,0:T(8,128)(2,1)S(1)}) custom-call(s32[11]{0:T(128)S(1)} %concatenate.6.meta, bf16[128,4096]{1,0:T(8,128)(2,1)S(1)} %get-tuple-element.61.q_ref, ...), custom_call_target="tpu_custom_call" | custom-call | flops 2000000000 | bytes 1000 | tf_op jit(solution)/shard_map/attend_a/pallas_call | solution.py:21
  27.9 3.4 %collective-permute-done.9.refs_1_ = bf16[40,2048]{1,0:T(8,128)(2,1)S(1)} collective-permute-done((bf16[40,2048]{1,0:T(8,128)(2,1)S(1)}, bf16[40,2048]{1,0:T(8,128)(2,1)S(1)}, u32[]{:S(2)}, u32[]{:S(2)}) %collective-permute-start.9) | collective-permute-done | bytes 163872 | tf_op jit(solution)/shard_map/ppermute | solution.py:399
  31.3 1.8 %products_b.3 = bf16[80,1664]{1,0:T(8,128)(2,1)S(1)} custom-call(s32[11]{0:T(128)S(1)} %concatenate.6.meta, f32[1,4096]{1,0:T(1,128)S(1)} %bitcast.33, bf16[40,2048]{1,0:T(8,128)(2,1)S(1)} %collective-permute-done.3.refs_0_, bf16[40,2048]{1,0:T(8,128)(2,1)S(1)} %collective-permute-done.9.refs_1_, bf16[1024,1536]{1,0:T(8,128)(2,1)S(1)} %bitcast.19, ...), custom_call_target="tpu_custom_call" | custom-call | flops 20000000000 | bytes 1000 | tf_op jit(solution)/shard_map/products_b/pallas_call | solution.py:21
  33.1 1.3 %collective-permute-start.10 = (bf16[80,1664]{1,0:T(8,128)(2,1)S(1)}, bf16[80,1664]{1,0:T(8,128)(2,1)S(1)}, u32[]{:S(2)}, u32[]{:S(2)}) collective-permute-start(bf16[80,1664]{1,0:T(8,128)(2,1)S(1)} %products_b.3), channel_id=1, source_target_pairs={{0,8},{4,12},{8,0},{12,4},{1,9},{5,13},{9,1},{13,5},{2,10},{6,14},... | collective-permute-start | bytes 798728 | tf_op jit(solution)/shard_map/ppermute | solution.py:328
  34.5 1.8 %products_b.2 = bf16[80,1664]{1,0:T(8,128)(2,1)S(1)} custom-call(s32[11]{0:T(128)S(1)} %concatenate.6.meta, f32[1,4096]{1,0:T(1,128)S(1)} %bitcast.34, bf16[40,2048]{1,0:T(8,128)(2,1)S(1)} %collective-permute-done.6.refs_0_, bf16[40,2048]{1,0:T(8,128)(2,1)S(1)} %collective-permute-done.7.refs_1_, bf16[1024,1536]{1,0:T(8,128)(2,1)S(1)} %bitcast.20, ...), custom_call_target="tpu_custom_call" | custom-call | flops 20000000000 | bytes 1000 | tf_op jit(solution)/shard_map/products_b/pallas_call | solution.py:21
  37.1 3.4 %collective-permute-start.14 = (bf16[40,2048]{1,0:T(8,128)(2,1)S(1)}, bf16[40,2048]{1,0:T(8,128)(2,1)S(1)}, u32[]{:S(2)}, u32[]{:S(2)}) collective-permute-start(bf16[40,2048]{1,0:T(8,128)(2,1)S(1)} %get-tuple-element.82), channel_id=1, source_target_pairs={{0,1},{1,2},{2,3},{3,0},{4,5},{5,6},{6,7},{7,4},{8,9},{9,10},{10,1... | collective-permute-start | bytes 491528 | tf_op jit(solution)/shard_map/ppermute | solution.py:399
  40.6 1.1 %collective-permute-start.15 = (bf16[40,2048]{1,0:T(8,128)(2,1)S(1)}, bf16[40,2048]{1,0:T(8,128)(2,1)S(1)}, u32[]{:S(2)}, u32[]{:S(2)}) collective-permute-start(bf16[40,2048]{1,0:T(8,128)(2,1)S(1)} %get-tuple-element.85), channel_id=1, source_target_pairs={{0,3},{1,0},{2,1},{3,2},{4,7},{5,4},{6,5},{7,6},{8,11},{9,8},{10,9... | collective-permute-start | bytes 491528 | tf_op jit(solution)/shard_map/ppermute | solution.py:399
  41.7 1.8 %products_a.2 = (f32[80,1536]{1,0:T(8,128)S(1)}, f32[80,128]{1,0:T(8,128)S(1)}) custom-call(s32[11]{0:T(128)S(1)} %concatenate.6.meta, f32[1,4096]{1,0:T(1,128)S(1)} %bitcast.35, bf16[40,2048]{1,0:T(8,128)(2,1)S(1)} %collective-permute-done.5.refs_0_, bf16[40,2048]{1,0:T(8,128)(2,1)S(1)} %get-tuple-element.72.refs_1_, bf16[1024,1536]{1,0:T(8,128)(2,1)S(1)} %bitcast.21, ...), custom_call_target="tpu_custom_call" | custom-call | flops 1000 | bytes 1000 | tf_op jit(solution)/shard_map/products_a/pallas_call | solution.py:21
  43.5 1.4 %hidden_down_a.2 = (bf16[80,768]{1,0:T(8,128)(2,1)S(1)}, bf16[40,2048]{1,0:T(8,128)(2,1)S(1)}, bf16[40,2048]{1,0:T(8,128)(2,1)S(1)}) custom-call(s32[11]{0:T(128)S(1)} %concatenate.6.meta, f32[80,1536]{1,0:T(8,128)S(1)} %get-tuple-element.73.sums_ref, f32[80,128]{1,0:T(8,128)S(1)} %get-tuple-element.74.squares_ref, ...), custom_call_target="tpu_custom_call" | custom-call | flops 1000 | bytes 1000 | tf_op jit(solution)/shard_map/hidden_down_a/pallas_call | solution.py:21
  46.5 2.2 %collective-permute-done.15.refs_1_ = bf16[40,2048]{1,0:T(8,128)(2,1)S(1)} collective-permute-done((bf16[40,2048]{1,0:T(8,128)(2,1)S(1)}, bf16[40,2048]{1,0:T(8,128)(2,1)S(1)}, u32[]{:S(2)}, u32[]{:S(2)}) %collective-permute-start.15) | collective-permute-done | bytes 163872 | tf_op jit(solution)/shard_map/ppermute | solution.py:399
  48.7 1.8 %products_a.3 = (f32[80,1536]{1,0:T(8,128)S(1)}, f32[80,128]{1,0:T(8,128)S(1)}) custom-call(s32[11]{0:T(128)S(1)} %concatenate.6.meta, f32[1,4096]{1,0:T(1,128)S(1)} %bitcast.36, bf16[40,2048]{1,0:T(8,128)(2,1)S(1)} %collective-permute-done.14.refs_0_, bf16[40,2048]{1,0:T(8,128)(2,1)S(1)} %collective-permute-done.15.refs_1_, ...), custom_call_target="tpu_custom_call" | custom-call | flops 1000 | bytes 1000 | tf_op jit(solution)/shard_map/products_a/pallas_call | solution.py:21
  50.6 1.4 %hidden_down_a.3 = (bf16[80,768]{1,0:T(8,128)(2,1)S(1)}, bf16[40,2048]{1,0:T(8,128)(2,1)S(1)}, bf16[40,2048]{1,0:T(8,128)(2,1)S(1)}) custom-call(s32[11]{0:T(128)S(1)} %concatenate.6.meta, f32[80,1536]{1,0:T(8,128)S(1)} %get-tuple-element.88.sums_ref, f32[80,128]{1,0:T(8,128)S(1)} %get-tuple-element.89.squares_ref, ...), custom_call_target="tpu_custom_call" | custom-call | flops 1000 | bytes 1000 | tf_op jit(solution)/shard_map/hidden_down_a/pallas_call | solution.py:21
  52.0 4.4 %collective-permute-start.21 = (bf16[40,2048]{1,0:T(8,128)(2,1)S(1)}, bf16[40,2048]{1,0:T(8,128)(2,1)S(1)}, u32[]{:S(2)}, u32[]{:S(2)}) collective-permute-start(bf16[40,2048]{1,0:T(8,128)(2,1)S(1)} %get-tuple-element.95), channel_id=1, source_target_pairs={{0,3},{1,0},{2,1},{3,2},{4,7},{5,4},{6,5},{7,6},{8,11},{9,8},{10,9... | collective-permute-start | bytes 491528 | tf_op jit(solution)/shard_map/ppermute | solution.py:399
  57.1 1.2 %down_b.2 = (bf16[40,2048]{1,0:T(8,128)(2,1)S(1)}, bf16[40,2048]{1,0:T(8,128)(2,1)S(1)}) custom-call(s32[11]{0:T(128)S(1)} %concatenate.6.meta, bf16[80,768]{1,0:T(8,128)(2,1)S(1)} %collective-permute-done.11.hidden_ref, bf16[768,1024]{1,0:T(8,128)(2,1)S(1)} %bitcast.30, bf16[768,1024]{1,0:T(8,128)(2,1)S(1)} %collective-permute-done.8.refs_2_.refs_1_), custom_call_target="tpu_custom_call" | custom-call | flops 1000 | bytes 1000 | tf_op jit(solution)/shard_map/down_b/pallas_call | solution.py:21
  58.4 1.4 %collective-permute-start.12 = (bf16[40,2048]{1,0:T(8,128)(2,1)S(1)}, bf16[40,2048]{1,0:T(8,128)(2,1)S(1)}, u32[]{:S(2)}, u32[]{:S(2)}) collective-permute-start(bf16[40,2048]{1,0:T(8,128)(2,1)S(1)} %get-tuple-element.79), channel_id=1, source_target_pairs={{0,10},{1,11},{2,8},{3,9},{4,14},{5,15},{6,12},{7,13},{8,2},{9,3},... | collective-permute-start | bytes 491528 | tf_op jit(solution)/shard_map/ppermute | solution.py:399
  59.8 2.3 %collective-permute-done.17.hidden_ref = bf16[80,768]{1,0:T(8,128)(2,1)S(1)} collective-permute-done((bf16[80,768]{1,0:T(8,128)(2,1)S(1)}, bf16[80,768]{1,0:T(8,128)(2,1)S(1)}, u32[]{:S(2)}, u32[]{:S(2)}) %collective-permute-start.17) | collective-permute-done | bytes 122912 | tf_op jit(solution)/shard_map/ppermute | solution.py:328
  62.7 1.2 %down_b.3 = (bf16[40,2048]{1,0:T(8,128)(2,1)S(1)}, bf16[40,2048]{1,0:T(8,128)(2,1)S(1)}) custom-call(s32[11]{0:T(128)S(1)} %concatenate.6.meta, bf16[80,768]{1,0:T(8,128)(2,1)S(1)} %collective-permute-done.17.hidden_ref, bf16[768,1024]{1,0:T(8,128)(2,1)S(1)} %bitcast.31, bf16[768,1024]{1,0:T(8,128)(2,1)S(1)} %collective-permute-done.8.refs_2_.refs_1_), custom_call_target="tpu_custom_call" | custom-call | flops 1000 | bytes 1000 | tf_op jit(solution)/shard_map/down_b/pallas_call | solution.py:21
  64.0 4.7 %collective-permute-start.18 = (bf16[40,2048]{1,0:T(8,128)(2,1)S(1)}, bf16[40,2048]{1,0:T(8,128)(2,1)S(1)}, u32[]{:S(2)}, u32[]{:S(2)}) collective-permute-start(bf16[40,2048]{1,0:T(8,128)(2,1)S(1)} %get-tuple-element.91), channel_id=1, source_target_pairs={{0,11},{1,8},{2,9},{3,10},{4,15},{5,12},{6,13},{7,14},{8,3},{9,0},... | collective-permute-start | bytes 491528 | tf_op jit(solution)/shard_map/ppermute | solution.py:399
  69.6 3.5 %collective-permute-done.12.refs_0_ = bf16[40,2048]{1,0:T(8,128)(2,1)S(1)} collective-permute-done((bf16[40,2048]{1,0:T(8,128)(2,1)S(1)}, bf16[40,2048]{1,0:T(8,128)(2,1)S(1)}, u32[]{:S(2)}, u32[]{:S(2)}) %collective-permute-start.12) | collective-permute-done | bytes 163872 | tf_op jit(solution)/shard_map/ppermute | solution.py:399
  73.0 1.9 %collective-permute-done.13.refs_1_ = bf16[40,2048]{1,0:T(8,128)(2,1)S(1)} collective-permute-done((bf16[40,2048]{1,0:T(8,128)(2,1)S(1)}, bf16[40,2048]{1,0:T(8,128)(2,1)S(1)}, u32[]{:S(2)}, u32[]{:S(2)}) %collective-permute-start.13) | collective-permute-done | bytes 163872 | tf_op jit(solution)/shard_map/ppermute | solution.py:399
  75.0 1.9 %collective-permute-done.19.refs_3_ = bf16[40,2048]{1,0:T(8,128)(2,1)S(1)} collective-permute-done((bf16[40,2048]{1,0:T(8,128)(2,1)S(1)}, bf16[40,2048]{1,0:T(8,128)(2,1)S(1)}, u32[]{:S(2)}, u32[]{:S(2)}) %collective-permute-start.19) | collective-permute-done | bytes 163872 | tf_op jit(solution)/shard_map/ppermute | solution.py:399
  76.8 1.7 %combine_b.1 = bf16[128,4096]{1,0:T(8,128)(2,1)} custom-call(s32[11]{0:T(128)S(1)} %concatenate.6.meta, bf16[128,2048]{1,0:T(8,128)(2,1)S(1)} %get-tuple-element.54.att_ref, bf16[128,160]{1,0:T(8,128)(2,1)S(1)} %get-tuple-element.55.back_ref, f32[128,128]{1,0:T(8,128)S(1)} %get-tuple-element.56.column_ref, ...), custom_call_target="tpu_custom_call" | custom-call | flops 20000000000 | bytes 1000 | tf_op jit(solution)/shard_map/combine_b/pallas_call | solution.py:21
  (43 shorter events, 9.8 us)
Async XLA Ops:
  0.9 7.3 %collective-permute-start.1 = (bf16[128,512]{1,0:T(8,128)(2,1)S(1)}, bf16[128,512]{1,0:T(8,128)(2,1)S(1)}, u32[]{:S(2)}, u32[]{:S(2)}) collective-permute-start(bf16[128,512]{1,0:T(8,128)(2,1)S(1)} %pad_maximum_fusion.refs_0_), channel_id=1, source_target_pairs={{0,8},{4,12},{8,0},{12,4},{1,9},{5,13},{9,1},{13,5},{2,10},{6,14},... | collective-permute-start | bytes 393224 | tf_op jit(solution)/shard_map/ppermute | solution.py:328
  3.9 4.9 %collective-permute-start = (bf16[128,512]{1,0:T(8,128)(2,1)S(1)}, bf16[128,512]{1,0:T(8,128)(2,1)S(1)}, u32[]{:S(2)}, u32[]{:S(2)}) collective-permute-start(bf16[128,512]{1,0:T(8,128)(2,1)S(1)} %pad_maximum_fusion.refs_0_), channel_id=1, source_target_pairs={{0,4},{4,0},{8,12},{12,8},{1,5},{5,1},{9,13},{13,9},{2,6},{6,2},{1... | collective-permute-start | bytes 393224 | tf_op jit(solution)/shard_map/ppermute | solution.py:328
  4.6 1.2 %copy-start.1 = (bf16[1,128,4096]{2,1,0:T(8,128)(2,1)S(1)}, bf16[1,128,4096]{2,1,0:T(8,128)(2,1)}, u32[]{:S(2)}) copy-start(bf16[1,128,4096]{2,1,0:T(8,128)(2,1)} %param.9) | copy-start | bytes 3145732
  5.9 0.7 copy-start.3
  6.5 0.7 copy-start.4
  8.2 1.6 %collective-permute-start.2 = (bf16[128,512]{1,0:T(8,128)(2,1)S(1)}, bf16[128,512]{1,0:T(8,128)(2,1)S(1)}, u32[]{:S(2)}, u32[]{:S(2)}) collective-permute-start(bf16[128,512]{1,0:T(8,128)(2,1)S(1)} %collective-permute-done.1.refs_2_), channel_id=1, source_target_pairs={{0,4},{4,0},{8,12},{12,8},{1,5},{5,1},{9,13},{13,9},{2,6},{6,2},{1... | collective-permute-start | bytes 393224 | tf_op jit(solution)/shard_map/ppermute | solution.py:328
  9.7 15.2 %collective-permute-start.4 = (bf16[1024,2,768]{2,1,0:T(2,128)(2,1)}, bf16[1024,2,768]{2,1,0:T(2,128)(2,1)S(1)}, u32[]{:S(2)}, u32[]{:S(2)}) collective-permute-start(bf16[1024,2,768]{2,1,0:T(2,128)(2,1)} %bitcast.39), channel_id=1, source_target_pairs={{0,4},{4,0},{8,12},{12,8},{1,5},{5,1},{9,13},{13,9},{2,6},{6,2},{1... | collective-permute-start | bytes 9437192 | tf_op jit(solution)/shard_map/ppermute | solution.py:328
  10.1 5.0 %copy-start.5 = (bf16[1,1024,2,768]{3,2,1,0:T(2,128)(2,1)S(1)}, bf16[1,1024,2,768]{3,2,1,0:T(2,128)(2,1)}, u32[]{:S(2)}) copy-start(bf16[1,1024,2,768]{3,2,1,0:T(2,128)(2,1)} %param.16) | copy-start | bytes 9437188
  12.4 12.5 %collective-permute-start.3 = (bf16[40,2048]{1,0:T(8,128)(2,1)S(1)}, bf16[40,2048]{1,0:T(8,128)(2,1)S(1)}, u32[]{:S(2)}, u32[]{:S(2)}) collective-permute-start(bf16[40,2048]{1,0:T(8,128)(2,1)S(1)} %get-tuple-element.57), channel_id=1, source_target_pairs={{0,10},{1,11},{2,8},{3,9},{4,14},{5,15},{6,12},{7,13},{8,2},{9,3},... | collective-permute-start | bytes 491528 | tf_op jit(solution)/shard_map/ppermute | solution.py:399
  15.0 9.8 %copy-start = (bf16[1,768,1024]{2,1,0:T(8,128)(2,1)S(1)}, bf16[1,768,1024]{2,1,0:T(8,128)(2,1)}, u32[]{:S(2)}) copy-start(bf16[1,768,1024]{2,1,0:T(8,128)(2,1)} %param.17) | copy-start | bytes 4718596
  15.6 15.7 %collective-permute-start.9 = (bf16[40,2048]{1,0:T(8,128)(2,1)S(1)}, bf16[40,2048]{1,0:T(8,128)(2,1)S(1)}, u32[]{:S(2)}, u32[]{:S(2)}) collective-permute-start(bf16[40,2048]{1,0:T(8,128)(2,1)S(1)} %get-tuple-element.76), channel_id=1, source_target_pairs={{0,8},{1,9},{2,10},{3,11},{4,12},{5,13},{6,14},{7,15},{8,0},{9,1},... | collective-permute-start | bytes 491528 | tf_op jit(solution)/shard_map/ppermute | solution.py:399
  17.2 17.3 %collective-permute-start.7 = (bf16[40,2048]{1,0:T(8,128)(2,1)S(1)}, bf16[40,2048]{1,0:T(8,128)(2,1)S(1)}, u32[]{:S(2)}, u32[]{:S(2)}) collective-permute-start(bf16[40,2048]{1,0:T(8,128)(2,1)S(1)} %get-tuple-element.66), channel_id=1, source_target_pairs={{0,11},{1,8},{2,9},{3,10},{4,15},{5,12},{6,13},{7,14},{8,3},{9,0},... | collective-permute-start | bytes 491528 | tf_op jit(solution)/shard_map/ppermute | solution.py:399
  18.5 16.0 %collective-permute-start.6 = (bf16[40,2048]{1,0:T(8,128)(2,1)S(1)}, bf16[40,2048]{1,0:T(8,128)(2,1)S(1)}, u32[]{:S(2)}, u32[]{:S(2)}) collective-permute-start(bf16[40,2048]{1,0:T(8,128)(2,1)S(1)} %get-tuple-element.63), channel_id=1, source_target_pairs={{0,9},{1,10},{2,11},{3,8},{4,13},{5,14},{6,15},{7,12},{8,1},{9,2},... | collective-permute-start | bytes 491528 | tf_op jit(solution)/shard_map/ppermute | solution.py:399
  24.9 9.6 %collective-permute-start.8 = (bf16[768,1024]{1,0:T(8,128)(2,1)S(1)}, bf16[768,1024]{1,0:T(8,128)(2,1)S(1)}, u32[]{:S(2)}, u32[]{:S(2)}) collective-permute-start(bf16[768,1024]{1,0:T(8,128)(2,1)S(1)} %bitcast.27), channel_id=1, source_target_pairs={{0,4},{4,0},{8,12},{12,8},{1,5},{5,1},{9,13},{13,9},{2,6},{6,2},{1... | collective-permute-start | bytes 4718600 | tf_op jit(solution)/shard_map/ppermute | solution.py:328
  25.5 5.8 %copy-start.2 = (f32[4096]{0:T(1024)S(1)}, f32[4096]{0:T(1024)}, u32[]{:S(2)}) copy-start(f32[4096]{0:T(1024)} %param.15) | copy-start | bytes 49156
  27.8 12.8 %collective-permute-start.5 = (bf16[40,2048]{1,0:T(8,128)(2,1)S(1)}, bf16[40,2048]{1,0:T(8,128)(2,1)S(1)}, u32[]{:S(2)}, u32[]{:S(2)}) collective-permute-start(bf16[40,2048]{1,0:T(8,128)(2,1)S(1)} %get-tuple-element.62), channel_id=1, source_target_pairs={{0,2},{1,3},{2,0},{3,1},{4,6},{5,7},{6,4},{7,5},{8,10},{9,11},{10,... | collective-permute-start | bytes 491528 | tf_op jit(solution)/shard_map/ppermute | solution.py:399
  33.1 10.4 %collective-permute-start.10 = (bf16[80,1664]{1,0:T(8,128)(2,1)S(1)}, bf16[80,1664]{1,0:T(8,128)(2,1)S(1)}, u32[]{:S(2)}, u32[]{:S(2)}) collective-permute-start(bf16[80,1664]{1,0:T(8,128)(2,1)S(1)} %products_b.3), channel_id=1, source_target_pairs={{0,8},{4,12},{8,0},{12,4},{1,9},{5,13},{9,1},{13,5},{2,10},{6,14},... | collective-permute-start | bytes 798728 | tf_op jit(solution)/shard_map/ppermute | solution.py:328
  36.3 14.3 %collective-permute-start.16 = (bf16[80,1664]{1,0:T(8,128)(2,1)S(1)}, bf16[80,1664]{1,0:T(8,128)(2,1)S(1)}, u32[]{:S(2)}, u32[]{:S(2)}) collective-permute-start(bf16[80,1664]{1,0:T(8,128)(2,1)S(1)} %products_b.2), channel_id=1, source_target_pairs={{0,8},{4,12},{8,0},{12,4},{1,9},{5,13},{9,1},{13,5},{2,10},{6,14},... | collective-permute-start | bytes 798728 | tf_op jit(solution)/shard_map/ppermute | solution.py:328
  37.1 8.9 %collective-permute-start.14 = (bf16[40,2048]{1,0:T(8,128)(2,1)S(1)}, bf16[40,2048]{1,0:T(8,128)(2,1)S(1)}, u32[]{:S(2)}, u32[]{:S(2)}) collective-permute-start(bf16[40,2048]{1,0:T(8,128)(2,1)S(1)} %get-tuple-element.82), channel_id=1, source_target_pairs={{0,1},{1,2},{2,3},{3,0},{4,5},{5,6},{6,7},{7,4},{8,9},{9,10},{10,1... | collective-permute-start | bytes 491528 | tf_op jit(solution)/shard_map/ppermute | solution.py:399
  40.6 8.2 %collective-permute-start.15 = (bf16[40,2048]{1,0:T(8,128)(2,1)S(1)}, bf16[40,2048]{1,0:T(8,128)(2,1)S(1)}, u32[]{:S(2)}, u32[]{:S(2)}) collective-permute-start(bf16[40,2048]{1,0:T(8,128)(2,1)S(1)} %get-tuple-element.85), channel_id=1, source_target_pairs={{0,3},{1,0},{2,1},{3,2},{4,7},{5,4},{6,5},{7,6},{8,11},{9,8},{10,9... | collective-permute-start | bytes 491528 | tf_op jit(solution)/shard_map/ppermute | solution.py:399
  44.9 5.7 %collective-permute-start.11 = (bf16[80,768]{1,0:T(8,128)(2,1)S(1)}, bf16[80,768]{1,0:T(8,128)(2,1)S(1)}, u32[]{:S(2)}, u32[]{:S(2)}) collective-permute-start(bf16[80,768]{1,0:T(8,128)(2,1)S(1)} %get-tuple-element.78), channel_id=1, source_target_pairs={{0,8},{4,12},{8,0},{12,4},{1,9},{5,13},{9,1},{13,5},{2,10},{6,14},... | collective-permute-start | bytes 368648 | tf_op jit(solution)/shard_map/ppermute | solution.py:328
  46.1 17.9 %collective-permute-start.20 = (bf16[40,2048]{1,0:T(8,128)(2,1)S(1)}, bf16[40,2048]{1,0:T(8,128)(2,1)S(1)}, u32[]{:S(2)}, u32[]{:S(2)}) collective-permute-start(bf16[40,2048]{1,0:T(8,128)(2,1)S(1)} %get-tuple-element.93), channel_id=1, source_target_pairs={{0,2},{1,3},{2,0},{3,1},{4,6},{5,7},{6,4},{7,5},{8,10},{9,11},{10,... | collective-permute-start | bytes 491528 | tf_op jit(solution)/shard_map/ppermute | solution.py:399
  52.0 16.7 %collective-permute-start.21 = (bf16[40,2048]{1,0:T(8,128)(2,1)S(1)}, bf16[40,2048]{1,0:T(8,128)(2,1)S(1)}, u32[]{:S(2)}, u32[]{:S(2)}) collective-permute-start(bf16[40,2048]{1,0:T(8,128)(2,1)S(1)} %get-tuple-element.95), channel_id=1, source_target_pairs={{0,3},{1,0},{2,1},{3,2},{4,7},{5,4},{6,5},{7,6},{8,11},{9,8},{10,9... | collective-permute-start | bytes 491528 | tf_op jit(solution)/shard_map/ppermute | solution.py:399
  56.4 12.3 %collective-permute-start.22 = (bf16[40,2048]{1,0:T(8,128)(2,1)S(1)}, bf16[40,2048]{1,0:T(8,128)(2,1)S(1)}, u32[]{:S(2)}, u32[]{:S(2)}) collective-permute-start(bf16[40,2048]{1,0:T(8,128)(2,1)S(1)} %get-tuple-element.96), channel_id=1, source_target_pairs={{0,1},{1,2},{2,3},{3,0},{4,5},{5,6},{6,7},{7,4},{8,9},{9,10},{10,1... | collective-permute-start | bytes 491528 | tf_op jit(solution)/shard_map/ppermute | solution.py:399
  56.4 5.7 %collective-permute-start.17 = (bf16[80,768]{1,0:T(8,128)(2,1)S(1)}, bf16[80,768]{1,0:T(8,128)(2,1)S(1)}, u32[]{:S(2)}, u32[]{:S(2)}) collective-permute-start(bf16[80,768]{1,0:T(8,128)(2,1)S(1)} %get-tuple-element.90), channel_id=1, source_target_pairs={{0,8},{4,12},{8,0},{12,4},{1,9},{5,13},{9,1},{13,5},{2,10},{6,14},... | collective-permute-start | bytes 368648 | tf_op jit(solution)/shard_map/ppermute | solution.py:328
  58.4 14.7 %collective-permute-start.12 = (bf16[40,2048]{1,0:T(8,128)(2,1)S(1)}, bf16[40,2048]{1,0:T(8,128)(2,1)S(1)}, u32[]{:S(2)}, u32[]{:S(2)}) collective-permute-start(bf16[40,2048]{1,0:T(8,128)(2,1)S(1)} %get-tuple-element.79), channel_id=1, source_target_pairs={{0,10},{1,11},{2,8},{3,9},{4,14},{5,15},{6,12},{7,13},{8,2},{9,3},... | collective-permute-start | bytes 491528 | tf_op jit(solution)/shard_map/ppermute | solution.py:399
  62.1 12.8 %collective-permute-start.13 = (bf16[40,2048]{1,0:T(8,128)(2,1)S(1)}, bf16[40,2048]{1,0:T(8,128)(2,1)S(1)}, u32[]{:S(2)}, u32[]{:S(2)}) collective-permute-start(bf16[40,2048]{1,0:T(8,128)(2,1)S(1)} %get-tuple-element.80), channel_id=1, source_target_pairs={{0,8},{1,9},{2,10},{3,11},{4,12},{5,13},{6,14},{7,15},{8,0},{9,1},... | collective-permute-start | bytes 491528 | tf_op jit(solution)/shard_map/ppermute | solution.py:399
  64.0 11.0 %collective-permute-start.18 = (bf16[40,2048]{1,0:T(8,128)(2,1)S(1)}, bf16[40,2048]{1,0:T(8,128)(2,1)S(1)}, u32[]{:S(2)}, u32[]{:S(2)}) collective-permute-start(bf16[40,2048]{1,0:T(8,128)(2,1)S(1)} %get-tuple-element.91), channel_id=1, source_target_pairs={{0,11},{1,8},{2,9},{3,10},{4,15},{5,12},{6,13},{7,14},{8,3},{9,0},... | collective-permute-start | bytes 491528 | tf_op jit(solution)/shard_map/ppermute | solution.py:399
  68.7 8.1 %collective-permute-start.19 = (bf16[40,2048]{1,0:T(8,128)(2,1)S(1)}, bf16[40,2048]{1,0:T(8,128)(2,1)S(1)}, u32[]{:S(2)}, u32[]{:S(2)}) collective-permute-start(bf16[40,2048]{1,0:T(8,128)(2,1)S(1)} %get-tuple-element.92), channel_id=1, source_target_pairs={{0,9},{1,10},{2,11},{3,8},{4,13},{5,14},{6,15},{7,12},{8,1},{9,2},... | collective-permute-start | bytes 491528 | tf_op jit(solution)/shard_map/ppermute | solution.py:399

commit v7 on v6

--- a/solution.py
+++ b/solution.py
@@ -57,52 +57,24 @@
     return jnp.where(slot_ids == slot, 1.0, 0.0)
 
 
-def start_copies(sources, targets, sems):
-    copies = [
-        pltpu.make_async_copy(s, t, sems.at[i]) for i, (s, t) in enumerate(zip(sources, targets))
-    ]
-    for copy in copies:
-        copy.start()
-    return copies
-
-
-def plan_kernel(experts, capacity, relative, meta, route_hbm, weight_hbm, q_hbm, *refs):
-    place_ref, back_ref, column_ref, q_ref, route_ref, weight_ref, sems = refs
-    copies = start_copies((route_hbm, weight_hbm, q_hbm), (route_ref, weight_ref, q_ref), sems)
-    tokens = route_ref.shape[1]
-    copies[0].wait()
+def plan_kernel(experts, capacity, relative, meta, route_ref, *refs):
+    place_ref, back_ref = refs
     place = placement_of(route_ref[...], capacity, experts, meta[2], relative)
     place_ref[...] = place.astype(jnp.bfloat16)
     back_ref[...] = place.T.astype(jnp.bfloat16)
-    diagonal = lax.broadcasted_iota(jnp.int32, (tokens, tokens), 0) == lax.broadcasted_iota(
-        jnp.int32, (tokens, tokens), 1
-    )
-    copies[1].wait()
-    weight = jnp.sum(jnp.where(diagonal, weight_ref[...], 0.0), axis=1, keepdims=True)
-    column_ref[...] = jnp.broadcast_to(weight, column_ref.shape)
-    copies[2].wait()
-
-
-def plan(meta, route_row, weight_row, queries, experts, capacity, relative):
+
+
+def plan(meta, route_row, experts, capacity, relative):
     tokens = route_row.shape[1]
     slots = experts * capacity
     bf16 = jnp.bfloat16
     return call(
         functools.partial(plan_kernel, experts, capacity, relative),
         "plan",
-        [meta, route_row, weight_row, queries],
-        [SMEM] + [pl.BlockSpec(memory_space=pltpu.HBM)] * 3,
-        [
-            ((slots, tokens), bf16),
-            ((tokens, slots), bf16),
-            ((tokens, 128), jnp.float32),
-            (queries.shape, bf16),
-        ],
-        [
-            pltpu.VMEM(route_row.shape, route_row.dtype),
-            pltpu.VMEM(weight_row.shape, weight_row.dtype),
-            pltpu.SemaphoreType.DMA((3,)),
-        ],
+        [meta, route_row],
+        [SMEM, VMEM],
+        [((slots, tokens), bf16), ((tokens, slots), bf16)],
+        flops=3 * 10**9,
     )
 
 
@@ -273,9 +245,9 @@
     )
 
 
-def combine_kernel(last, meta, att_ref, back_ref, column_ref, *refs):
-    row_refs, refs = refs[: -1 - 3 * last], refs[-1 - 3 * last :]
-    half_width = att_ref.shape[1]
+def combine_kernel(last, meta, att_ref, back_ref, weight_ref, *refs):
+    row_refs, refs = refs[: -2 - 2 * last], refs[-2 - 2 * last :]
+    tokens, half_width = att_ref.shape
     if last:
         before_ref, out_ref, value_ref, sems = refs
         before_at = pl.multiple_of(meta[0] * half_width, half_width)
@@ -284,6 +256,13 @@
             pltpu.make_async_copy(before_ref, out_ref.at[:, pl.ds(before_at, half_width)], sems.at[0])
         ]
         copies[0].start()
+        weight = weight_ref[:, :1]
+    else:
+        diagonal = lax.broadcasted_iota(jnp.int32, (tokens, tokens), 0) == lax.broadcasted_iota(
+            jnp.int32, (tokens, tokens), 1
+        )
+        weight = jnp.sum(jnp.where(diagonal, weight_ref[...], 0.0), axis=1, keepdims=True)
+        refs[1][...] = jnp.broadcast_to(weight, refs[1].shape)
     rows = jnp.concatenate([r[...].astype(jnp.float32) for r in row_refs], axis=0)
     rows = rows.astype(jnp.bfloat16)
     parts = 4 if last else 1
@@ -291,7 +270,7 @@
     for i in range(parts):
         columns = slice(i * step, (i + 1) * step)
         mine = jnp.dot(back_ref[...], rows[:, columns], preferred_element_type=jnp.float32)
-        value = att_ref[:, columns].astype(jnp.float32) + mine * column_ref[:, :1]
+        value = att_ref[:, columns].astype(jnp.float32) + mine * weight
         value = value.astype(jnp.bfloat16)
         if last:
             value_ref[:, columns] = value
@@ -307,21 +286,25 @@
             copy.wait()
 
 
-def combine(meta, att, back, column, rows, before):
+def combine(meta, att, back, weight, rows, before):
     tokens, half_width = att.shape
     last = before is not None
     extra = [before] if last else []
+    if last:
+        outs = [((tokens, KV_HEADS * half_width), jnp.bfloat16)]
+    else:
+        outs = [((tokens, half_width), jnp.bfloat16), ((tokens, 128), jnp.float32)]
     scratch = [pltpu.VMEM(att.shape, att.dtype), pltpu.SemaphoreType.DMA((5,))] if last else []
     return call(
         functools.partial(combine_kernel, last),
         "combine_" + "ab"[last],
-        [meta, att, back, column, *rows, *extra],
+        [meta, att, back, weight, *rows, *extra],
         [SMEM] + [VMEM] * (3 + len(rows) + len(extra)),
-        [((tokens, half_width * (1 + last)), jnp.bfloat16)],
+        outs,
         scratch,
         flops=20 * 10**9,
         out_space=pl.ANY if last else pltpu.VMEM,
-    )[0]
+    )
 
 
 def swap(array, axis, size, bit):
@@ -362,9 +345,8 @@
     parent_at = 3 + 2 * top
     meta = jnp.stack([half, ctx, exp] + [j * depth for j in shards] + [j * columns for j in shards])
     meta = jnp.concatenate([meta, tree_parents[0]])
-    place, back, column, staged = plan(
-        meta, route_row, weight_row, queries[0], n_exp, capacity, shifted
-    )
+    place, back = plan(meta, route_row, n_exp, capacity, shifted)
+    staged = queries[0]
 
     kv = jnp.concatenate([keys[0], values[0]], axis=1)
     near, far = [kv], [after(swap(kv, "ctx", n_ctx, top), place)]
@@ -431,8 +413,8 @@
     for hidden in moved:
         out_b += down(meta, hidden, w_outs, col_at, width, pair)
     back_b = send(out_b, True, True)
-    done = combine(meta, att_a, back, column, back_a, None)
-    done = combine(meta, att_b, back, column, back_b, done)
+    done, column = combine(meta, att_a, back, weight_row, back_a, None)
+    done = combine(meta, att_b, back, column, back_b, done)[0]
     return done[None]
 
 

time: 78.7 us -> 77.9 us (0.990)
  local copies, waits for them, and re-layouts: 4.46 us -> 2.58 us
  waiting for transfers between devices: 21.4 us -> 22.4 us
    unnamed x14, local copies, waits for them, and re-layouts: 3.72 us -> 1.85 us
    ppermute x9, waiting for transfers between devices: 3.34 us -> 4.71 us  [swap(): return lax.ppermute(array, axis, [(i, i ^ bit) for i in range(size)])]
    ppermute x9, starting transfers between devices: 7.63 us -> 8.42 us  [swap(): return lax.ppermute(array, axis, [(i, i ^ bit) for i in range(size)])]
where the time goes in v7:
time: 77.9 us; the launch traced here: 77.7 us
  starting transfers between devices  31.3 us (40%)
  waiting for transfers between devices  22.4 us (29%)
  Pallas kernels  20.4 us (26%)
  local copies, waits for them, and re-layouts  2.58 us (3%)
  other arithmetic  0.88 us (1%)
    ppermute x14, starting transfers between devices, send(): moved.append(block if still else lax.ppermute(block, ('ctx', 'exp'), pairs))  22.8 us
    pallas_call x13, Pallas kernels, call(): pl.pallas_call(kernel, in_specs=specs, out_specs=[pl.BlockSpec(memory_spa...  20.4 us
    ppermute x14, waiting for transfers between devices, send(): moved.append(block if still else lax.ppermute(block, ('ctx', 'exp'), pairs))  17.7 us
    ppermute x9, starting transfers between devices, swap(): return lax.ppermute(array, axis, [(i, i ^ bit) for i in range(size)])  8.42 us
    ppermute x9, waiting for transfers between devices, swap(): return lax.ppermute(array, axis, [(i, i ^ bit) for i in range(size)])  4.71 us
    unnamed x14, local copies, waits for them, and re-layouts  1.85 us
  transfers between devices with their start and end apart: 23, of which 9 were waited for; matrix products, arithmetic and copies ran while one was open for 2% of the time, Pallas kernels for 24%

profile of v7, /device:TPU:0, one launch (start us, length us, event | category | flops | bytes accessed | tf_op | source)
XLA Modules:
  0.0 77.7 jit_solution(1278012977405216102)
XLA Ops:
  0.0 0.9 %pad_maximum_fusion.refs_0_ = bf16[128,512]{1,0:T(8,128)(2,1)S(1)} fusion(bf16[128,256]{1,0:T(8,128)(2,1)} %bitcast.43, bf16[128,256]{1,0:T(8,128)(2,1)} %bitcast.44), kind=kLoop, calls=%fused_computation | loop fusion | flops 262144 | bytes 262144 | tf_op jit(solution)/shard_map/concatenate | solution.py:351
  0.9 3.0 %collective-permute-start.1 = (bf16[128,512]{1,0:T(8,128)(2,1)S(1)}, bf16[128,512]{1,0:T(8,128)(2,1)S(1)}, u32[]{:S(2)}, u32[]{:S(2)}) collective-permute-start(bf16[128,512]{1,0:T(8,128)(2,1)S(1)} %pad_maximum_fusion.refs_0_), channel_id=1, source_target_pairs={{0,8},{4,12},{8,0},{12,4},{1,9},{5,13},{9,1},{13,5},{2,10},{6,14},... | collective-permute-start | bytes 393224 | tf_op jit(solution)/shard_map/ppermute | solution.py:311
  6.1 1.3 %collective-permute-done.1.refs_2_ = bf16[128,512]{1,0:T(8,128)(2,1)S(1)} collective-permute-done((bf16[128,512]{1,0:T(8,128)(2,1)S(1)}, bf16[128,512]{1,0:T(8,128)(2,1)S(1)}, u32[]{:S(2)}, u32[]{:S(2)}) %collective-permute-start.1) | collective-permute-done | bytes 131104 | tf_op jit(solution)/shard_map/ppermute | solution.py:311
  7.4 1.3 %collective-permute-done.2.refs_3_ = bf16[128,512]{1,0:T(8,128)(2,1)S(1)} collective-permute-done((bf16[128,512]{1,0:T(8,128)(2,1)S(1)}, bf16[128,512]{1,0:T(8,128)(2,1)S(1)}, u32[]{:S(2)}, u32[]{:S(2)}) %collective-permute-start.2) | collective-permute-done | bytes 131104 | tf_op jit(solution)/shard_map/ppermute | solution.py:311
  8.9 2.3 %attend_b.1 = (bf16[128,2048]{1,0:T(8,128)(2,1)S(1)}, bf16[40,2048]{1,0:T(8,128)(2,1)S(1)}, bf16[40,2048]{1,0:T(8,128)(2,1)S(1)}, bf16[40,2048]{1,0:T(8,128)(2,1)S(1)}, bf16[40,2048]{1,0:T(8,128)(2,1)S(1)}) custom-call(s32[11]{0:T(128)S(1)} %concatenate.6.meta, bf16[128,4096]{1,0:T(8,128)(2,1)S(1)} %bitcast.36, ...), custom_call_target="tpu_custom_call" | custom-call | flops 2000000000 | bytes 1000 | tf_op jit(solution)/shard_map/attend_b/pallas_call | solution.py:21
  11.2 3.8 %collective-permute-start.3 = (bf16[40,2048]{1,0:T(8,128)(2,1)S(1)}, bf16[40,2048]{1,0:T(8,128)(2,1)S(1)}, u32[]{:S(2)}, u32[]{:S(2)}) collective-permute-start(bf16[40,2048]{1,0:T(8,128)(2,1)S(1)} %get-tuple-element.55), channel_id=1, source_target_pairs={{0,10},{1,11},{2,8},{3,9},{4,14},{5,15},{6,12},{7,13},{8,2},{9,3},... | collective-permute-start | bytes 491528 | tf_op jit(solution)/shard_map/ppermute | solution.py:381
  16.2 2.3 %collective-permute-start.7 = (bf16[40,2048]{1,0:T(8,128)(2,1)S(1)}, bf16[40,2048]{1,0:T(8,128)(2,1)S(1)}, u32[]{:S(2)}, u32[]{:S(2)}) collective-permute-start(bf16[40,2048]{1,0:T(8,128)(2,1)S(1)} %get-tuple-element.64), channel_id=1, source_target_pairs={{0,11},{1,8},{2,9},{3,10},{4,15},{5,12},{6,13},{7,14},{8,3},{9,0},... | collective-permute-start | bytes 491528 | tf_op jit(solution)/shard_map/ppermute | solution.py:381
  19.2 4.5 %collective-permute-done.3.refs_0_ = bf16[40,2048]{1,0:T(8,128)(2,1)S(1)} collective-permute-done((bf16[40,2048]{1,0:T(8,128)(2,1)S(1)}, bf16[40,2048]{1,0:T(8,128)(2,1)S(1)}, u32[]{:S(2)}, u32[]{:S(2)}) %collective-permute-start.3) | collective-permute-done | bytes 163872 | tf_op jit(solution)/shard_map/ppermute | solution.py:381
  24.2 2.3 %attend_a.1 = (bf16[128,2048]{1,0:T(8,128)(2,1)S(1)}, bf16[40,2048]{1,0:T(8,128)(2,1)S(1)}, bf16[40,2048]{1,0:T(8,128)(2,1)S(1)}, bf16[40,2048]{1,0:T(8,128)(2,1)S(1)}, bf16[40,2048]{1,0:T(8,128)(2,1)S(1)}) custom-call(s32[11]{0:T(128)S(1)} %concatenate.6.meta, bf16[128,4096]{1,0:T(8,128)(2,1)S(1)} %bitcast.37, ...), custom_call_target="tpu_custom_call" | custom-call | flops 2000000000 | bytes 1000 | tf_op jit(solution)/shard_map/attend_a/pallas_call | solution.py:21
  26.9 4.4 %collective-permute-done.9.refs_1_ = bf16[40,2048]{1,0:T(8,128)(2,1)S(1)} collective-permute-done((bf16[40,2048]{1,0:T(8,128)(2,1)S(1)}, bf16[40,2048]{1,0:T(8,128)(2,1)S(1)}, u32[]{:S(2)}, u32[]{:S(2)}) %collective-permute-start.9) | collective-permute-done | bytes 163872 | tf_op jit(solution)/shard_map/ppermute | solution.py:381
  31.3 1.8 %products_b.3 = bf16[80,1664]{1,0:T(8,128)(2,1)S(1)} custom-call(s32[11]{0:T(128)S(1)} %concatenate.6.meta, f32[1,4096]{1,0:T(1,128)S(1)} %bitcast.32, bf16[40,2048]{1,0:T(8,128)(2,1)S(1)} %collective-permute-done.3.refs_0_, bf16[40,2048]{1,0:T(8,128)(2,1)S(1)} %collective-permute-done.9.refs_1_, bf16[1024,1536]{1,0:T(8,128)(2,1)S(1)} %bitcast.19, ...), custom_call_target="tpu_custom_call" | custom-call | flops 20000000000 | bytes 1000 | tf_op jit(solution)/shard_map/products_b/pallas_call | solution.py:21
  33.7 1.8 %products_b.2 = bf16[80,1664]{1,0:T(8,128)(2,1)S(1)} custom-call(s32[11]{0:T(128)S(1)} %concatenate.6.meta, f32[1,4096]{1,0:T(1,128)S(1)} %bitcast.33, bf16[40,2048]{1,0:T(8,128)(2,1)S(1)} %collective-permute-done.6.refs_0_, bf16[40,2048]{1,0:T(8,128)(2,1)S(1)} %collective-permute-done.7.refs_1_, bf16[1024,1536]{1,0:T(8,128)(2,1)S(1)} %bitcast.20, ...), custom_call_target="tpu_custom_call" | custom-call | flops 20000000000 | bytes 1000 | tf_op jit(solution)/shard_map/products_b/pallas_call | solution.py:21
  35.6 1.5 %collective-permute-start.15 = (bf16[80,1664]{1,0:T(8,128)(2,1)S(1)}, bf16[80,1664]{1,0:T(8,128)(2,1)S(1)}, u32[]{:S(2)}, u32[]{:S(2)}) collective-permute-start(bf16[80,1664]{1,0:T(8,128)(2,1)S(1)} %products_b.2), channel_id=1, source_target_pairs={{0,8},{4,12},{8,0},{12,4},{1,9},{5,13},{9,1},{13,5},{2,10},{6,14},... | collective-permute-start | bytes 798728 | tf_op jit(solution)/shard_map/ppermute | solution.py:311
  37.1 2.7 %collective-permute-start.12 = (bf16[40,2048]{1,0:T(8,128)(2,1)S(1)}, bf16[40,2048]{1,0:T(8,128)(2,1)S(1)}, u32[]{:S(2)}, u32[]{:S(2)}) collective-permute-start(bf16[40,2048]{1,0:T(8,128)(2,1)S(1)} %get-tuple-element.79), channel_id=1, source_target_pairs={{0,1},{1,2},{2,3},{3,0},{4,5},{5,6},{6,7},{7,4},{8,9},{9,10},{10,1... | collective-permute-start | bytes 491528 | tf_op jit(solution)/shard_map/ppermute | solution.py:381
  39.8 1.1 %collective-permute-start.13 = (bf16[40,2048]{1,0:T(8,128)(2,1)S(1)}, bf16[40,2048]{1,0:T(8,128)(2,1)S(1)}, u32[]{:S(2)}, u32[]{:S(2)}) collective-permute-start(bf16[40,2048]{1,0:T(8,128)(2,1)S(1)} %get-tuple-element.83), channel_id=1, source_target_pairs={{0,3},{1,0},{2,1},{3,2},{4,7},{5,4},{6,5},{7,6},{8,11},{9,8},{10,9... | collective-permute-start | bytes 491528 | tf_op jit(solution)/shard_map/ppermute | solution.py:381
  40.9 1.8 %products_a.2 = (f32[80,1536]{1,0:T(8,128)S(1)}, f32[80,128]{1,0:T(8,128)S(1)}) custom-call(s32[11]{0:T(128)S(1)} %concatenate.6.meta, f32[1,4096]{1,0:T(1,128)S(1)} %bitcast.34, bf16[40,2048]{1,0:T(8,128)(2,1)S(1)} %collective-permute-done.5.refs_0_, bf16[40,2048]{1,0:T(8,128)(2,1)S(1)} %get-tuple-element.70.refs_1_, bf16[1024,1536]{1,0:T(8,128)(2,1)S(1)} %bitcast.21, ...), custom_call_target="tpu_custom_call" | custom-call | flops 1000 | bytes 1000 | tf_op jit(solution)/shard_map/products_a/pallas_call | solution.py:21
  42.8 1.4 %hidden_down_a.2 = (bf16[80,768]{1,0:T(8,128)(2,1)S(1)}, bf16[40,2048]{1,0:T(8,128)(2,1)S(1)}, bf16[40,2048]{1,0:T(8,128)(2,1)S(1)}) custom-call(s32[11]{0:T(128)S(1)} %concatenate.6.meta, f32[80,1536]{1,0:T(8,128)S(1)} %get-tuple-element.71.sums_ref, f32[80,128]{1,0:T(8,128)S(1)} %get-tuple-element.72.squares_ref, ...), custom_call_target="tpu_custom_call" | custom-call | flops 1000 | bytes 1000 | tf_op jit(solution)/shard_map/hidden_down_a/pallas_call | solution.py:21
  44.2 1.5 %collective-permute-start.14 = (bf16[80,768]{1,0:T(8,128)(2,1)S(1)}, bf16[80,768]{1,0:T(8,128)(2,1)S(1)}, u32[]{:S(2)}, u32[]{:S(2)}) collective-permute-start(bf16[80,768]{1,0:T(8,128)(2,1)S(1)} %get-tuple-element.80), channel_id=1, source_target_pairs={{0,8},{4,12},{8,0},{12,4},{1,9},{5,13},{9,1},{13,5},{2,10},{6,14},... | collective-permute-start | bytes 368648 | tf_op jit(solution)/shard_map/ppermute | solution.py:311
  46.3 1.6 %collective-permute-done.13.refs_1_ = bf16[40,2048]{1,0:T(8,128)(2,1)S(1)} collective-permute-done((bf16[40,2048]{1,0:T(8,128)(2,1)S(1)}, bf16[40,2048]{1,0:T(8,128)(2,1)S(1)}, u32[]{:S(2)}, u32[]{:S(2)}) %collective-permute-start.13) | collective-permute-done | bytes 163872 | tf_op jit(solution)/shard_map/ppermute | solution.py:381
  47.9 1.8 %products_a.3 = (f32[80,1536]{1,0:T(8,128)S(1)}, f32[80,128]{1,0:T(8,128)S(1)}) custom-call(s32[11]{0:T(128)S(1)} %concatenate.6.meta, f32[1,4096]{1,0:T(1,128)S(1)} %bitcast.35, bf16[40,2048]{1,0:T(8,128)(2,1)S(1)} %collective-permute-done.12.refs_0_, bf16[40,2048]{1,0:T(8,128)(2,1)S(1)} %collective-permute-done.13.refs_1_, ...), custom_call_target="tpu_custom_call" | custom-call | flops 1000 | bytes 1000 | tf_op jit(solution)/shard_map/products_a/pallas_call | solution.py:21
  49.7 1.4 %hidden_down_a.3 = (bf16[80,768]{1,0:T(8,128)(2,1)S(1)}, bf16[40,2048]{1,0:T(8,128)(2,1)S(1)}, bf16[40,2048]{1,0:T(8,128)(2,1)S(1)}) custom-call(s32[11]{0:T(128)S(1)} %concatenate.6.meta, f32[80,1536]{1,0:T(8,128)S(1)} %get-tuple-element.86.sums_ref, f32[80,128]{1,0:T(8,128)S(1)} %get-tuple-element.87.squares_ref, ...), custom_call_target="tpu_custom_call" | custom-call | flops 1000 | bytes 1000 | tf_op jit(solution)/shard_map/hidden_down_a/pallas_call | solution.py:21
  51.2 4.4 %collective-permute-start.16 = (bf16[40,2048]{1,0:T(8,128)(2,1)S(1)}, bf16[40,2048]{1,0:T(8,128)(2,1)S(1)}, u32[]{:S(2)}, u32[]{:S(2)}) collective-permute-start(bf16[40,2048]{1,0:T(8,128)(2,1)S(1)} %get-tuple-element.88), channel_id=1, source_target_pairs={{0,3},{1,0},{2,1},{3,2},{4,7},{5,4},{6,5},{7,6},{8,11},{9,8},{10,9... | collective-permute-start | bytes 491528 | tf_op jit(solution)/shard_map/ppermute | solution.py:381
  55.5 1.6 %collective-permute-start.20 = (bf16[80,768]{1,0:T(8,128)(2,1)S(1)}, bf16[80,768]{1,0:T(8,128)(2,1)S(1)}, u32[]{:S(2)}, u32[]{:S(2)}) collective-permute-start(bf16[80,768]{1,0:T(8,128)(2,1)S(1)} %get-tuple-element.93), channel_id=1, source_target_pairs={{0,8},{4,12},{8,0},{12,4},{1,9},{5,13},{9,1},{13,5},{2,10},{6,14},... | collective-permute-start | bytes 368648 | tf_op jit(solution)/shard_map/ppermute | solution.py:311
  57.1 1.2 %down_b.2 = (bf16[40,2048]{1,0:T(8,128)(2,1)S(1)}, bf16[40,2048]{1,0:T(8,128)(2,1)S(1)}) custom-call(s32[11]{0:T(128)S(1)} %concatenate.6.meta, bf16[80,768]{1,0:T(8,128)(2,1)S(1)} %collective-permute-done.14.hidden_ref, bf16[768,1024]{1,0:T(8,128)(2,1)S(1)} %bitcast.30, bf16[768,1024]{1,0:T(8,128)(2,1)S(1)} %collective-permute-done.8.refs_2_.refs_1_), custom_call_target="tpu_custom_call" | custom-call | flops 1000 | bytes 1000 | tf_op jit(solution)/shard_map/down_b/pallas_call | solution.py:21
  58.9 2.0 %collective-permute-done.20.hidden_ref = bf16[80,768]{1,0:T(8,128)(2,1)S(1)} collective-permute-done((bf16[80,768]{1,0:T(8,128)(2,1)S(1)}, bf16[80,768]{1,0:T(8,128)(2,1)S(1)}, u32[]{:S(2)}, u32[]{:S(2)}) %collective-permute-start.20) | collective-permute-done | bytes 122912 | tf_op jit(solution)/shard_map/ppermute | solution.py:311
  61.0 2.0 %collective-permute-start.19 = (bf16[40,2048]{1,0:T(8,128)(2,1)S(1)}, bf16[40,2048]{1,0:T(8,128)(2,1)S(1)}, u32[]{:S(2)}, u32[]{:S(2)}) collective-permute-start(bf16[40,2048]{1,0:T(8,128)(2,1)S(1)} %get-tuple-element.92), channel_id=1, source_target_pairs={{0,8},{1,9},{2,10},{3,11},{4,12},{5,13},{6,14},{7,15},{8,0},{9,1},... | collective-permute-start | bytes 491528 | tf_op jit(solution)/shard_map/ppermute | solution.py:381
  62.9 1.2 %down_b.3 = (bf16[40,2048]{1,0:T(8,128)(2,1)S(1)}, bf16[40,2048]{1,0:T(8,128)(2,1)S(1)}) custom-call(s32[11]{0:T(128)S(1)} %concatenate.6.meta, bf16[80,768]{1,0:T(8,128)(2,1)S(1)} %collective-permute-done.20.hidden_ref, bf16[768,1024]{1,0:T(8,128)(2,1)S(1)} %bitcast.31, bf16[768,1024]{1,0:T(8,128)(2,1)S(1)} %collective-permute-done.8.refs_2_.refs_1_), custom_call_target="tpu_custom_call" | custom-call | flops 1000 | bytes 1000 | tf_op jit(solution)/shard_map/down_b/pallas_call | solution.py:21
  64.2 3.9 %collective-permute-start.21 = (bf16[40,2048]{1,0:T(8,128)(2,1)S(1)}, bf16[40,2048]{1,0:T(8,128)(2,1)S(1)}, u32[]{:S(2)}, u32[]{:S(2)}) collective-permute-start(bf16[40,2048]{1,0:T(8,128)(2,1)S(1)} %get-tuple-element.94), channel_id=1, source_target_pairs={{0,11},{1,8},{2,9},{3,10},{4,15},{5,12},{6,13},{7,14},{8,3},{9,0},... | collective-permute-start | bytes 491528 | tf_op jit(solution)/shard_map/ppermute | solution.py:381
  68.9 4.1 %collective-permute-done.18.refs_0_ = bf16[40,2048]{1,0:T(8,128)(2,1)S(1)} collective-permute-done((bf16[40,2048]{1,0:T(8,128)(2,1)S(1)}, bf16[40,2048]{1,0:T(8,128)(2,1)S(1)}, u32[]{:S(2)}, u32[]{:S(2)}) %collective-permute-start.18) | collective-permute-done | bytes 163872 | tf_op jit(solution)/shard_map/ppermute | solution.py:381
  73.0 1.4 %collective-permute-done.19.refs_1_ = bf16[40,2048]{1,0:T(8,128)(2,1)S(1)} collective-permute-done((bf16[40,2048]{1,0:T(8,128)(2,1)S(1)}, bf16[40,2048]{1,0:T(8,128)(2,1)S(1)}, u32[]{:S(2)}, u32[]{:S(2)}) %collective-permute-start.19) | collective-permute-done | bytes 163872 | tf_op jit(solution)/shard_map/ppermute | solution.py:381
  74.4 1.8 %collective-permute-done.22.refs_3_ = bf16[40,2048]{1,0:T(8,128)(2,1)S(1)} collective-permute-done((bf16[40,2048]{1,0:T(8,128)(2,1)S(1)}, bf16[40,2048]{1,0:T(8,128)(2,1)S(1)}, u32[]{:S(2)}, u32[]{:S(2)}) %collective-permute-start.22) | collective-permute-done | bytes 163872 | tf_op jit(solution)/shard_map/ppermute | solution.py:381
  76.1 1.6 %combine_b.1 = bf16[128,4096]{1,0:T(8,128)(2,1)} custom-call(s32[11]{0:T(128)S(1)} %concatenate.6.meta, bf16[128,2048]{1,0:T(8,128)(2,1)S(1)} %get-tuple-element.53.att_ref, bf16[128,160]{1,0:T(8,128)(2,1)S(1)} %get-tuple-element.54.back_ref, f32[128,128]{1,0:T(8,128)S(1)} %get-tuple-element.90.weight_ref, ...), custom_call_target="tpu_custom_call" | custom-call | flops 20000000000 | bytes 1000 | tf_op jit(solution)/shard_map/combine_b/pallas_call | solution.py:21
  (43 shorter events, 7.7 us)
Async XLA Ops:
  0.9 6.5 %collective-permute-start.1 = (bf16[128,512]{1,0:T(8,128)(2,1)S(1)}, bf16[128,512]{1,0:T(8,128)(2,1)S(1)}, u32[]{:S(2)}, u32[]{:S(2)}) collective-permute-start(bf16[128,512]{1,0:T(8,128)(2,1)S(1)} %pad_maximum_fusion.refs_0_), channel_id=1, source_target_pairs={{0,8},{4,12},{8,0},{12,4},{1,9},{5,13},{9,1},{13,5},{2,10},{6,14},... | collective-permute-start | bytes 393224 | tf_op jit(solution)/shard_map/ppermute | solution.py:311
  3.9 3.5 %collective-permute-start = (bf16[128,512]{1,0:T(8,128)(2,1)S(1)}, bf16[128,512]{1,0:T(8,128)(2,1)S(1)}, u32[]{:S(2)}, u32[]{:S(2)}) collective-permute-start(bf16[128,512]{1,0:T(8,128)(2,1)S(1)} %pad_maximum_fusion.refs_0_), channel_id=1, source_target_pairs={{0,4},{4,0},{8,12},{12,8},{1,5},{5,1},{9,13},{13,9},{2,6},{6,2},{1... | collective-permute-start | bytes 393224 | tf_op jit(solution)/shard_map/ppermute | solution.py:311
  4.6 0.7 copy-start.3
  5.3 3.5 %copy-start.5 = (bf16[1,1024,2,768]{3,2,1,0:T(2,128)(2,1)S(1)}, bf16[1,1024,2,768]{3,2,1,0:T(2,128)(2,1)}, u32[]{:S(2)}) copy-start(bf16[1,1024,2,768]{3,2,1,0:T(2,128)(2,1)} %param.16) | copy-start | bytes 9437188
  5.3 3.6 %copy-start.2 = (bf16[1,128,4096]{2,1,0:T(8,128)(2,1)S(1)}, bf16[1,128,4096]{2,1,0:T(8,128)(2,1)}, u32[]{:S(2)}) copy-start(bf16[1,128,4096]{2,1,0:T(8,128)(2,1)} %param.9) | copy-start | bytes 3145732
  7.4 1.3 %collective-permute-start.2 = (bf16[128,512]{1,0:T(8,128)(2,1)S(1)}, bf16[128,512]{1,0:T(8,128)(2,1)S(1)}, u32[]{:S(2)}, u32[]{:S(2)}) collective-permute-start(bf16[128,512]{1,0:T(8,128)(2,1)S(1)} %collective-permute-done.1.refs_2_), channel_id=1, source_target_pairs={{0,4},{4,0},{8,12},{12,8},{1,5},{5,1},{9,13},{13,9},{2,6},{6,2},{1... | collective-permute-start | bytes 393224 | tf_op jit(solution)/shard_map/ppermute | solution.py:311
  8.7 14.9 %collective-permute-start.4 = (bf16[1024,2,768]{2,1,0:T(2,128)(2,1)S(1)}, bf16[1024,2,768]{2,1,0:T(2,128)(2,1)S(1)}, u32[]{:S(2)}, u32[]{:S(2)}) collective-permute-start(bf16[1024,2,768]{2,1,0:T(2,128)(2,1)S(1)} %bitcast.40), channel_id=1, source_target_pairs={{0,4},{4,0},{8,12},{12,8},{1,5},{5,1},{9,13},{13,9},{2,6},{6,2},{1... | collective-permute-start | bytes 9437192 | tf_op jit(solution)/shard_map/ppermute | solution.py:311
  11.2 12.4 %collective-permute-start.3 = (bf16[40,2048]{1,0:T(8,128)(2,1)S(1)}, bf16[40,2048]{1,0:T(8,128)(2,1)S(1)}, u32[]{:S(2)}, u32[]{:S(2)}) collective-permute-start(bf16[40,2048]{1,0:T(8,128)(2,1)S(1)} %get-tuple-element.55), channel_id=1, source_target_pairs={{0,10},{1,11},{2,8},{3,9},{4,14},{5,15},{6,12},{7,13},{8,2},{9,3},... | collective-permute-start | bytes 491528 | tf_op jit(solution)/shard_map/ppermute | solution.py:381
  15.0 8.6 %copy-start = (bf16[1,768,1024]{2,1,0:T(8,128)(2,1)S(1)}, bf16[1,768,1024]{2,1,0:T(8,128)(2,1)}, u32[]{:S(2)}) copy-start(bf16[1,768,1024]{2,1,0:T(8,128)(2,1)} %param.17) | copy-start | bytes 4718596
  15.6 15.6 %collective-permute-start.9 = (bf16[40,2048]{1,0:T(8,128)(2,1)S(1)}, bf16[40,2048]{1,0:T(8,128)(2,1)S(1)}, u32[]{:S(2)}, u32[]{:S(2)}) collective-permute-start(bf16[40,2048]{1,0:T(8,128)(2,1)S(1)} %get-tuple-element.74), channel_id=1, source_target_pairs={{0,8},{1,9},{2,10},{3,11},{4,12},{5,13},{6,14},{7,15},{8,0},{9,1},... | collective-permute-start | bytes 491528 | tf_op jit(solution)/shard_map/ppermute | solution.py:381
  16.2 17.5 %collective-permute-start.7 = (bf16[40,2048]{1,0:T(8,128)(2,1)S(1)}, bf16[40,2048]{1,0:T(8,128)(2,1)S(1)}, u32[]{:S(2)}, u32[]{:S(2)}) collective-permute-start(bf16[40,2048]{1,0:T(8,128)(2,1)S(1)} %get-tuple-element.64), channel_id=1, source_target_pairs={{0,11},{1,8},{2,9},{3,10},{4,15},{5,12},{6,13},{7,14},{8,3},{9,0},... | collective-permute-start | bytes 491528 | tf_op jit(solution)/shard_map/ppermute | solution.py:381
  18.5 15.2 %collective-permute-start.6 = (bf16[40,2048]{1,0:T(8,128)(2,1)S(1)}, bf16[40,2048]{1,0:T(8,128)(2,1)S(1)}, u32[]{:S(2)}, u32[]{:S(2)}) collective-permute-start(bf16[40,2048]{1,0:T(8,128)(2,1)S(1)} %get-tuple-element.62), channel_id=1, source_target_pairs={{0,9},{1,10},{2,11},{3,8},{4,13},{5,14},{6,15},{7,12},{8,1},{9,2},... | collective-permute-start | bytes 491528 | tf_op jit(solution)/shard_map/ppermute | solution.py:381
  23.6 10.1 %collective-permute-start.8 = (bf16[768,1024]{1,0:T(8,128)(2,1)S(1)}, bf16[768,1024]{1,0:T(8,128)(2,1)S(1)}, u32[]{:S(2)}, u32[]{:S(2)}) collective-permute-start(bf16[768,1024]{1,0:T(8,128)(2,1)S(1)} %bitcast.27), channel_id=1, source_target_pairs={{0,4},{4,0},{8,12},{12,8},{1,5},{5,1},{9,13},{13,9},{2,6},{6,2},{1... | collective-permute-start | bytes 4718600 | tf_op jit(solution)/shard_map/ppermute | solution.py:311
  24.2 7.0 %copy-start.1 = (f32[4096]{0:T(1024)S(1)}, f32[4096]{0:T(1024)}, u32[]{:S(2)}) copy-start(f32[4096]{0:T(1024)} %param.15) | copy-start | bytes 49156
  26.6 13.2 %collective-permute-start.5 = (bf16[40,2048]{1,0:T(8,128)(2,1)S(1)}, bf16[40,2048]{1,0:T(8,128)(2,1)S(1)}, u32[]{:S(2)}, u32[]{:S(2)}) collective-permute-start(bf16[40,2048]{1,0:T(8,128)(2,1)S(1)} %get-tuple-element.61), channel_id=1, source_target_pairs={{0,2},{1,3},{2,0},{3,1},{4,6},{5,7},{6,4},{7,5},{8,10},{9,11},{10,... | collective-permute-start | bytes 491528 | tf_op jit(solution)/shard_map/ppermute | solution.py:381
  33.1 9.7 %collective-permute-start.10 = (bf16[80,1664]{1,0:T(8,128)(2,1)S(1)}, bf16[80,1664]{1,0:T(8,128)(2,1)S(1)}, u32[]{:S(2)}, u32[]{:S(2)}) collective-permute-start(bf16[80,1664]{1,0:T(8,128)(2,1)S(1)} %products_b.3), channel_id=1, source_target_pairs={{0,8},{4,12},{8,0},{12,4},{1,9},{5,13},{9,1},{13,5},{2,10},{6,14},... | collective-permute-start | bytes 798728 | tf_op jit(solution)/shard_map/ppermute | solution.py:311
  35.6 14.1 %collective-permute-start.15 = (bf16[80,1664]{1,0:T(8,128)(2,1)S(1)}, bf16[80,1664]{1,0:T(8,128)(2,1)S(1)}, u32[]{:S(2)}, u32[]{:S(2)}) collective-permute-start(bf16[80,1664]{1,0:T(8,128)(2,1)S(1)} %products_b.2), channel_id=1, source_target_pairs={{0,8},{4,12},{8,0},{12,4},{1,9},{5,13},{9,1},{13,5},{2,10},{6,14},... | collective-permute-start | bytes 798728 | tf_op jit(solution)/shard_map/ppermute | solution.py:311
  37.1 8.6 %collective-permute-start.12 = (bf16[40,2048]{1,0:T(8,128)(2,1)S(1)}, bf16[40,2048]{1,0:T(8,128)(2,1)S(1)}, u32[]{:S(2)}, u32[]{:S(2)}) collective-permute-start(bf16[40,2048]{1,0:T(8,128)(2,1)S(1)} %get-tuple-element.79), channel_id=1, source_target_pairs={{0,1},{1,2},{2,3},{3,0},{4,5},{5,6},{6,7},{7,4},{8,9},{9,10},{10,1... | collective-permute-start | bytes 491528 | tf_op jit(solution)/shard_map/ppermute | solution.py:381
  39.8 8.1 %collective-permute-start.13 = (bf16[40,2048]{1,0:T(8,128)(2,1)S(1)}, bf16[40,2048]{1,0:T(8,128)(2,1)S(1)}, u32[]{:S(2)}, u32[]{:S(2)}) collective-permute-start(bf16[40,2048]{1,0:T(8,128)(2,1)S(1)} %get-tuple-element.83), channel_id=1, source_target_pairs={{0,3},{1,0},{2,1},{3,2},{4,7},{5,4},{6,5},{7,6},{8,11},{9,8},{10,9... | collective-permute-start | bytes 491528 | tf_op jit(solution)/shard_map/ppermute | solution.py:381
  44.2 5.5 %collective-permute-start.14 = (bf16[80,768]{1,0:T(8,128)(2,1)S(1)}, bf16[80,768]{1,0:T(8,128)(2,1)S(1)}, u32[]{:S(2)}, u32[]{:S(2)}) collective-permute-start(bf16[80,768]{1,0:T(8,128)(2,1)S(1)} %get-tuple-element.80), channel_id=1, source_target_pairs={{0,8},{4,12},{8,0},{12,4},{1,9},{5,13},{9,1},{13,5},{2,10},{6,14},... | collective-permute-start | bytes 368648 | tf_op jit(solution)/shard_map/ppermute | solution.py:311
  45.7 18.4 %collective-permute-start.11 = (bf16[40,2048]{1,0:T(8,128)(2,1)S(1)}, bf16[40,2048]{1,0:T(8,128)(2,1)S(1)}, u32[]{:S(2)}, u32[]{:S(2)}) collective-permute-start(bf16[40,2048]{1,0:T(8,128)(2,1)S(1)} %get-tuple-element.76), channel_id=1, source_target_pairs={{0,2},{1,3},{2,0},{3,1},{4,6},{5,7},{6,4},{7,5},{8,10},{9,11},{10,... | collective-permute-start | bytes 491528 | tf_op jit(solution)/shard_map/ppermute | solution.py:381
  51.2 16.9 %collective-permute-start.16 = (bf16[40,2048]{1,0:T(8,128)(2,1)S(1)}, bf16[40,2048]{1,0:T(8,128)(2,1)S(1)}, u32[]{:S(2)}, u32[]{:S(2)}) collective-permute-start(bf16[40,2048]{1,0:T(8,128)(2,1)S(1)} %get-tuple-element.88), channel_id=1, source_target_pairs={{0,3},{1,0},{2,1},{3,2},{4,7},{5,4},{6,5},{7,6},{8,11},{9,8},{10,9... | collective-permute-start | bytes 491528 | tf_op jit(solution)/shard_map/ppermute | solution.py:381
  55.5 12.5 %collective-permute-start.17 = (bf16[40,2048]{1,0:T(8,128)(2,1)S(1)}, bf16[40,2048]{1,0:T(8,128)(2,1)S(1)}, u32[]{:S(2)}, u32[]{:S(2)}) collective-permute-start(bf16[40,2048]{1,0:T(8,128)(2,1)S(1)} %get-tuple-element.89), channel_id=1, source_target_pairs={{0,1},{1,2},{2,3},{3,0},{4,5},{5,6},{6,7},{7,4},{8,9},{9,10},{10,1... | collective-permute-start | bytes 491528 | tf_op jit(solution)/shard_map/ppermute | solution.py:381
  55.5 12.5 %copy-start.4 = (f32[1,128,1]{1,2,0:T(1,128)S(1)}, f32[1,128,1]{1,2,0:T(1,128)}, u32[]{:S(2)}) copy-start(f32[1,128,1]{1,2,0:T(1,128)} %param.14) | copy-start | bytes 1540
  55.5 5.4 %collective-permute-start.20 = (bf16[80,768]{1,0:T(8,128)(2,1)S(1)}, bf16[80,768]{1,0:T(8,128)(2,1)S(1)}, u32[]{:S(2)}, u32[]{:S(2)}) collective-permute-start(bf16[80,768]{1,0:T(8,128)(2,1)S(1)} %get-tuple-element.93), channel_id=1, source_target_pairs={{0,8},{4,12},{8,0},{12,4},{1,9},{5,13},{9,1},{13,5},{2,10},{6,14},... | collective-permute-start | bytes 368648 | tf_op jit(solution)/shard_map/ppermute | solution.py:311
  58.4 14.6 %collective-permute-start.18 = (bf16[40,2048]{1,0:T(8,128)(2,1)S(1)}, bf16[40,2048]{1,0:T(8,128)(2,1)S(1)}, u32[]{:S(2)}, u32[]{:S(2)}) collective-permute-start(bf16[40,2048]{1,0:T(8,128)(2,1)S(1)} %get-tuple-element.91), channel_id=1, source_target_pairs={{0,10},{1,11},{2,8},{3,9},{4,14},{5,15},{6,12},{7,13},{8,2},{9,3},... | collective-permute-start | bytes 491528 | tf_op jit(solution)/shard_map/ppermute | solution.py:381
  61.0 13.4 %collective-permute-start.19 = (bf16[40,2048]{1,0:T(8,128)(2,1)S(1)}, bf16[40,2048]{1,0:T(8,128)(2,1)S(1)}, u32[]{:S(2)}, u32[]{:S(2)}) collective-permute-start(bf16[40,2048]{1,0:T(8,128)(2,1)S(1)} %get-tuple-element.92), channel_id=1, source_target_pairs={{0,8},{1,9},{2,10},{3,11},{4,12},{5,13},{6,14},{7,15},{8,0},{9,1},... | collective-permute-start | bytes 491528 | tf_op jit(solution)/shard_map/ppermute | solution.py:381
  64.2 10.2 %collective-permute-start.21 = (bf16[40,2048]{1,0:T(8,128)(2,1)S(1)}, bf16[40,2048]{1,0:T(8,128)(2,1)S(1)}, u32[]{:S(2)}, u32[]{:S(2)}) collective-permute-start(bf16[40,2048]{1,0:T(8,128)(2,1)S(1)} %get-tuple-element.94), channel_id=1, source_target_pairs={{0,11},{1,8},{2,9},{3,10},{4,15},{5,12},{6,13},{7,14},{8,3},{9,0},... | collective-permute-start | bytes 491528 | tf_op jit(solution)/shard_map/ppermute | solution.py:381
  68.0 8.1 %collective-permute-start.22 = (bf16[40,2048]{1,0:T(8,128)(2,1)S(1)}, bf16[40,2048]{1,0:T(8,128)(2,1)S(1)}, u32[]{:S(2)}, u32[]{:S(2)}) collective-permute-start(bf16[40,2048]{1,0:T(8,128)(2,1)S(1)} %get-tuple-element.95), channel_id=1, source_target_pairs={{0,9},{1,10},{2,11},{3,8},{4,13},{5,14},{6,15},{7,12},{8,1},{9,2},... | collective-permute-start | bytes 491528 | tf_op jit(solution)/shard_map/ppermute | solution.py:381

commit v8 on v7

--- a/solution.py
+++ b/solution.py
@@ -339,14 +339,12 @@
     weight_row = route_weight.reshape(1, tokens)
     gain = norm_gain.reshape(1, width)
 
-
     shards = [lax.rem(ctx, top) ^ j for j in range(top)]
     row_at, col_at = 3, 3 + top
     parent_at = 3 + 2 * top
     meta = jnp.stack([half, ctx, exp] + [j * depth for j in shards] + [j * columns for j in shards])
     meta = jnp.concatenate([meta, tree_parents[0]])
     place, back = plan(meta, route_row, n_exp, capacity, shifted)
-    staged = queries[0]
 
     kv = jnp.concatenate([keys[0], values[0]], axis=1)
     near, far = [kv], [after(swap(kv, "ctx", n_ctx, top), place)]
@@ -385,11 +383,11 @@
         return attention(meta, parent_at, queries, place, kvs, blocks_out, part)
 
     w_raw = spread(after(expert_in[0], *kvs[1:]))
-    att_b, packed_b = attend(staged, 1)
+    att_b, packed_b = attend(queries[0], 1)
     rows_b = send(packed_b, False, True)
     w_ins = [after(w, att_b).reshape(depth, 2 * inner) for w in w_raw]
     w_outs = spread(after(expert_out[0], rows_b[0]))
-    att_a, packed_a = attend(after(staged, att_b, rows_b[0], *w_ins), 0)
+    att_a, packed_a = attend(after(queries[0], att_b, rows_b[0], *w_ins), 0)
     rows_b = [after(r, att_a) for r in rows_b]
     rows_b[-1] = after(rows_b[-1], w_outs[-1])
     pair = len(rows_b) // 2 if len(rows_b) % 4 == 0 else len(rows_b)

time: 77.9 us -> 77.9 us (level)
  no operation moved by 1% of the time
where the time goes in v8:
time: 77.9 us; the launch traced here: 77.7 us
  starting transfers between devices  31.3 us (40%)
  waiting for transfers between devices  22.4 us (29%)
  Pallas kernels  20.4 us (26%)
  local copies, waits for them, and re-layouts  2.58 us (3%)
  other arithmetic  0.88 us (1%)
    ppermute x14, starting transfers between devices, send(): moved.append(block if still else lax.ppermute(block, ('ctx', 'exp'), pairs))  22.8 us
    pallas_call x13, Pallas kernels, call(): pl.pallas_call(kernel, in_specs=specs, out_specs=[pl.BlockSpec(memory_spa...  20.4 us
    ppermute x14, waiting for transfers between devices, send(): moved.append(block if still else lax.ppermute(block, ('ctx', 'exp'), pairs))  17.7 us
    ppermute x9, starting transfers between devices, swap(): return lax.ppermute(array, axis, [(i, i ^ bit) for i in range(size)])  8.42 us
    ppermute x9, waiting for transfers between devices, swap(): return lax.ppermute(array, axis, [(i, i ^ bit) for i in range(size)])  4.71 us
    unnamed x14, local copies, waits for them, and re-layouts  1.85 us
  transfers between devices with their start and end apart: 23, of which 9 were waited for; matrix products, arithmetic and copies ran while one was open for 2% of the time, Pallas kernels for 24%

profile of v8, /device:TPU:0, one launch (start us, length us, event | category | flops | bytes accessed | tf_op | source)
XLA Modules:
  0.0 77.7 jit_solution(1278012977405216102)
XLA Ops:
  0.0 0.9 %pad_maximum_fusion.refs_0_ = bf16[128,512]{1,0:T(8,128)(2,1)S(1)} fusion(bf16[128,256]{1,0:T(8,128)(2,1)} %bitcast.43, bf16[128,256]{1,0:T(8,128)(2,1)} %bitcast.44), kind=kLoop, calls=%fused_computation | loop fusion | flops 262144 | bytes 262144 | tf_op jit(solution)/shard_map/concatenate | solution.py:349
  0.9 3.0 %collective-permute-start.1 = (bf16[128,512]{1,0:T(8,128)(2,1)S(1)}, bf16[128,512]{1,0:T(8,128)(2,1)S(1)}, u32[]{:S(2)}, u32[]{:S(2)}) collective-permute-start(bf16[128,512]{1,0:T(8,128)(2,1)S(1)} %pad_maximum_fusion.refs_0_), channel_id=1, source_target_pairs={{0,8},{4,12},{8,0},{12,4},{1,9},{5,13},{9,1},{13,5},{2,10},{6,14},... | collective-permute-start | bytes 393224 | tf_op jit(solution)/shard_map/ppermute | solution.py:311
  6.1 1.3 %collective-permute-done.1.refs_2_ = bf16[128,512]{1,0:T(8,128)(2,1)S(1)} collective-permute-done((bf16[128,512]{1,0:T(8,128)(2,1)S(1)}, bf16[128,512]{1,0:T(8,128)(2,1)S(1)}, u32[]{:S(2)}, u32[]{:S(2)}) %collective-permute-start.1) | collective-permute-done | bytes 131104 | tf_op jit(solution)/shard_map/ppermute | solution.py:311
  7.4 1.3 %collective-permute-done.2.refs_3_ = bf16[128,512]{1,0:T(8,128)(2,1)S(1)} collective-permute-done((bf16[128,512]{1,0:T(8,128)(2,1)S(1)}, bf16[128,512]{1,0:T(8,128)(2,1)S(1)}, u32[]{:S(2)}, u32[]{:S(2)}) %collective-permute-start.2) | collective-permute-done | bytes 131104 | tf_op jit(solution)/shard_map/ppermute | solution.py:311
  8.9 2.3 %attend_b.1 = (bf16[128,2048]{1,0:T(8,128)(2,1)S(1)}, bf16[40,2048]{1,0:T(8,128)(2,1)S(1)}, bf16[40,2048]{1,0:T(8,128)(2,1)S(1)}, bf16[40,2048]{1,0:T(8,128)(2,1)S(1)}, bf16[40,2048]{1,0:T(8,128)(2,1)S(1)}) custom-call(s32[11]{0:T(128)S(1)} %concatenate.6.meta, bf16[128,4096]{1,0:T(8,128)(2,1)S(1)} %bitcast.36, ...), custom_call_target="tpu_custom_call" | custom-call | flops 2000000000 | bytes 1000 | tf_op jit(solution)/shard_map/attend_b/pallas_call | solution.py:21
  11.2 3.8 %collective-permute-start.3 = (bf16[40,2048]{1,0:T(8,128)(2,1)S(1)}, bf16[40,2048]{1,0:T(8,128)(2,1)S(1)}, u32[]{:S(2)}, u32[]{:S(2)}) collective-permute-start(bf16[40,2048]{1,0:T(8,128)(2,1)S(1)} %get-tuple-element.55), channel_id=1, source_target_pairs={{0,10},{1,11},{2,8},{3,9},{4,14},{5,15},{6,12},{7,13},{8,2},{9,3},... | collective-permute-start | bytes 491528 | tf_op jit(solution)/shard_map/ppermute | solution.py:379
  16.2 2.3 %collective-permute-start.7 = (bf16[40,2048]{1,0:T(8,128)(2,1)S(1)}, bf16[40,2048]{1,0:T(8,128)(2,1)S(1)}, u32[]{:S(2)}, u32[]{:S(2)}) collective-permute-start(bf16[40,2048]{1,0:T(8,128)(2,1)S(1)} %get-tuple-element.64), channel_id=1, source_target_pairs={{0,11},{1,8},{2,9},{3,10},{4,15},{5,12},{6,13},{7,14},{8,3},{9,0},... | collective-permute-start | bytes 491528 | tf_op jit(solution)/shard_map/ppermute | solution.py:379
  19.2 4.5 %collective-permute-done.3.refs_0_ = bf16[40,2048]{1,0:T(8,128)(2,1)S(1)} collective-permute-done((bf16[40,2048]{1,0:T(8,128)(2,1)S(1)}, bf16[40,2048]{1,0:T(8,128)(2,1)S(1)}, u32[]{:S(2)}, u32[]{:S(2)}) %collective-permute-start.3) | collective-permute-done | bytes 163872 | tf_op jit(solution)/shard_map/ppermute | solution.py:379
  24.2 2.3 %attend_a.1 = (bf16[128,2048]{1,0:T(8,128)(2,1)S(1)}, bf16[40,2048]{1,0:T(8,128)(2,1)S(1)}, bf16[40,2048]{1,0:T(8,128)(2,1)S(1)}, bf16[40,2048]{1,0:T(8,128)(2,1)S(1)}, bf16[40,2048]{1,0:T(8,128)(2,1)S(1)}) custom-call(s32[11]{0:T(128)S(1)} %concatenate.6.meta, bf16[128,4096]{1,0:T(8,128)(2,1)S(1)} %bitcast.37, ...), custom_call_target="tpu_custom_call" | custom-call | flops 2000000000 | bytes 1000 | tf_op jit(solution)/shard_map/attend_a/pallas_call | solution.py:21
  26.9 4.4 %collective-permute-done.9.refs_1_ = bf16[40,2048]{1,0:T(8,128)(2,1)S(1)} collective-permute-done((bf16[40,2048]{1,0:T(8,128)(2,1)S(1)}, bf16[40,2048]{1,0:T(8,128)(2,1)S(1)}, u32[]{:S(2)}, u32[]{:S(2)}) %collective-permute-start.9) | collective-permute-done | bytes 163872 | tf_op jit(solution)/shard_map/ppermute | solution.py:379
  31.3 1.8 %products_b.3 = bf16[80,1664]{1,0:T(8,128)(2,1)S(1)} custom-call(s32[11]{0:T(128)S(1)} %concatenate.6.meta, f32[1,4096]{1,0:T(1,128)S(1)} %bitcast.32, bf16[40,2048]{1,0:T(8,128)(2,1)S(1)} %collective-permute-done.3.refs_0_, bf16[40,2048]{1,0:T(8,128)(2,1)S(1)} %collective-permute-done.9.refs_1_, bf16[1024,1536]{1,0:T(8,128)(2,1)S(1)} %bitcast.19, ...), custom_call_target="tpu_custom_call" | custom-call | flops 20000000000 | bytes 1000 | tf_op jit(solution)/shard_map/products_b/pallas_call | solution.py:21
  33.7 1.8 %products_b.2 = bf16[80,1664]{1,0:T(8,128)(2,1)S(1)} custom-call(s32[11]{0:T(128)S(1)} %concatenate.6.meta, f32[1,4096]{1,0:T(1,128)S(1)} %bitcast.33, bf16[40,2048]{1,0:T(8,128)(2,1)S(1)} %collective-permute-done.6.refs_0_, bf16[40,2048]{1,0:T(8,128)(2,1)S(1)} %collective-permute-done.7.refs_1_, bf16[1024,1536]{1,0:T(8,128)(2,1)S(1)} %bitcast.20, ...), custom_call_target="tpu_custom_call" | custom-call | flops 20000000000 | bytes 1000 | tf_op jit(solution)/shard_map/products_b/pallas_call | solution.py:21
  35.6 1.5 %collective-permute-start.15 = (bf16[80,1664]{1,0:T(8,128)(2,1)S(1)}, bf16[80,1664]{1,0:T(8,128)(2,1)S(1)}, u32[]{:S(2)}, u32[]{:S(2)}) collective-permute-start(bf16[80,1664]{1,0:T(8,128)(2,1)S(1)} %products_b.2), channel_id=1, source_target_pairs={{0,8},{4,12},{8,0},{12,4},{1,9},{5,13},{9,1},{13,5},{2,10},{6,14},... | collective-permute-start | bytes 798728 | tf_op jit(solution)/shard_map/ppermute | solution.py:311
  37.1 2.7 %collective-permute-start.12 = (bf16[40,2048]{1,0:T(8,128)(2,1)S(1)}, bf16[40,2048]{1,0:T(8,128)(2,1)S(1)}, u32[]{:S(2)}, u32[]{:S(2)}) collective-permute-start(bf16[40,2048]{1,0:T(8,128)(2,1)S(1)} %get-tuple-element.79), channel_id=1, source_target_pairs={{0,1},{1,2},{2,3},{3,0},{4,5},{5,6},{6,7},{7,4},{8,9},{9,10},{10,1... | collective-permute-start | bytes 491528 | tf_op jit(solution)/shard_map/ppermute | solution.py:379
  39.8 1.1 %collective-permute-start.13 = (bf16[40,2048]{1,0:T(8,128)(2,1)S(1)}, bf16[40,2048]{1,0:T(8,128)(2,1)S(1)}, u32[]{:S(2)}, u32[]{:S(2)}) collective-permute-start(bf16[40,2048]{1,0:T(8,128)(2,1)S(1)} %get-tuple-element.83), channel_id=1, source_target_pairs={{0,3},{1,0},{2,1},{3,2},{4,7},{5,4},{6,5},{7,6},{8,11},{9,8},{10,9... | collective-permute-start | bytes 491528 | tf_op jit(solution)/shard_map/ppermute | solution.py:379
  40.9 1.8 %products_a.2 = (f32[80,1536]{1,0:T(8,128)S(1)}, f32[80,128]{1,0:T(8,128)S(1)}) custom-call(s32[11]{0:T(128)S(1)} %concatenate.6.meta, f32[1,4096]{1,0:T(1,128)S(1)} %bitcast.34, bf16[40,2048]{1,0:T(8,128)(2,1)S(1)} %collective-permute-done.5.refs_0_, bf16[40,2048]{1,0:T(8,128)(2,1)S(1)} %get-tuple-element.70.refs_1_, bf16[1024,1536]{1,0:T(8,128)(2,1)S(1)} %bitcast.21, ...), custom_call_target="tpu_custom_call" | custom-call | flops 1000 | bytes 1000 | tf_op jit(solution)/shard_map/products_a/pallas_call | solution.py:21
  42.8 1.4 %hidden_down_a.2 = (bf16[80,768]{1,0:T(8,128)(2,1)S(1)}, bf16[40,2048]{1,0:T(8,128)(2,1)S(1)}, bf16[40,2048]{1,0:T(8,128)(2,1)S(1)}) custom-call(s32[11]{0:T(128)S(1)} %concatenate.6.meta, f32[80,1536]{1,0:T(8,128)S(1)} %get-tuple-element.71.sums_ref, f32[80,128]{1,0:T(8,128)S(1)} %get-tuple-element.72.squares_ref, ...), custom_call_target="tpu_custom_call" | custom-call | flops 1000 | bytes 1000 | tf_op jit(solution)/shard_map/hidden_down_a/pallas_call | solution.py:21
  44.2 1.5 %collective-permute-start.14 = (bf16[80,768]{1,0:T(8,128)(2,1)S(1)}, bf16[80,768]{1,0:T(8,128)(2,1)S(1)}, u32[]{:S(2)}, u32[]{:S(2)}) collective-permute-start(bf16[80,768]{1,0:T(8,128)(2,1)S(1)} %get-tuple-element.80), channel_id=1, source_target_pairs={{0,8},{4,12},{8,0},{12,4},{1,9},{5,13},{9,1},{13,5},{2,10},{6,14},... | collective-permute-start | bytes 368648 | tf_op jit(solution)/shard_map/ppermute | solution.py:311
  46.3 1.6 %collective-permute-done.13.refs_1_ = bf16[40,2048]{1,0:T(8,128)(2,1)S(1)} collective-permute-done((bf16[40,2048]{1,0:T(8,128)(2,1)S(1)}, bf16[40,2048]{1,0:T(8,128)(2,1)S(1)}, u32[]{:S(2)}, u32[]{:S(2)}) %collective-permute-start.13) | collective-permute-done | bytes 163872 | tf_op jit(solution)/shard_map/ppermute | solution.py:379
  47.9 1.8 %products_a.3 = (f32[80,1536]{1,0:T(8,128)S(1)}, f32[80,128]{1,0:T(8,128)S(1)}) custom-call(s32[11]{0:T(128)S(1)} %concatenate.6.meta, f32[1,4096]{1,0:T(1,128)S(1)} %bitcast.35, bf16[40,2048]{1,0:T(8,128)(2,1)S(1)} %collective-permute-done.12.refs_0_, bf16[40,2048]{1,0:T(8,128)(2,1)S(1)} %collective-permute-done.13.refs_1_, ...), custom_call_target="tpu_custom_call" | custom-call | flops 1000 | bytes 1000 | tf_op jit(solution)/shard_map/products_a/pallas_call | solution.py:21
  49.7 1.4 %hidden_down_a.3 = (bf16[80,768]{1,0:T(8,128)(2,1)S(1)}, bf16[40,2048]{1,0:T(8,128)(2,1)S(1)}, bf16[40,2048]{1,0:T(8,128)(2,1)S(1)}) custom-call(s32[11]{0:T(128)S(1)} %concatenate.6.meta, f32[80,1536]{1,0:T(8,128)S(1)} %get-tuple-element.86.sums_ref, f32[80,128]{1,0:T(8,128)S(1)} %get-tuple-element.87.squares_ref, ...), custom_call_target="tpu_custom_call" | custom-call | flops 1000 | bytes 1000 | tf_op jit(solution)/shard_map/hidden_down_a/pallas_call | solution.py:21
  51.2 4.4 %collective-permute-start.16 = (bf16[40,2048]{1,0:T(8,128)(2,1)S(1)}, bf16[40,2048]{1,0:T(8,128)(2,1)S(1)}, u32[]{:S(2)}, u32[]{:S(2)}) collective-permute-start(bf16[40,2048]{1,0:T(8,128)(2,1)S(1)} %get-tuple-element.88), channel_id=1, source_target_pairs={{0,3},{1,0},{2,1},{3,2},{4,7},{5,4},{6,5},{7,6},{8,11},{9,8},{10,9... | collective-permute-start | bytes 491528 | tf_op jit(solution)/shard_map/ppermute | solution.py:379
  55.5 1.6 %collective-permute-start.20 = (bf16[80,768]{1,0:T(8,128)(2,1)S(1)}, bf16[80,768]{1,0:T(8,128)(2,1)S(1)}, u32[]{:S(2)}, u32[]{:S(2)}) collective-permute-start(bf16[80,768]{1,0:T(8,128)(2,1)S(1)} %get-tuple-element.93), channel_id=1, source_target_pairs={{0,8},{4,12},{8,0},{12,4},{1,9},{5,13},{9,1},{13,5},{2,10},{6,14},... | collective-permute-start | bytes 368648 | tf_op jit(solution)/shard_map/ppermute | solution.py:311
  57.1 1.2 %down_b.2 = (bf16[40,2048]{1,0:T(8,128)(2,1)S(1)}, bf16[40,2048]{1,0:T(8,128)(2,1)S(1)}) custom-call(s32[11]{0:T(128)S(1)} %concatenate.6.meta, bf16[80,768]{1,0:T(8,128)(2,1)S(1)} %collective-permute-done.14.hidden_ref, bf16[768,1024]{1,0:T(8,128)(2,1)S(1)} %bitcast.30, bf16[768,1024]{1,0:T(8,128)(2,1)S(1)} %collective-permute-done.8.refs_2_.refs_1_), custom_call_target="tpu_custom_call" | custom-call | flops 1000 | bytes 1000 | tf_op jit(solution)/shard_map/down_b/pallas_call | solution.py:21
  58.9 2.0 %collective-permute-done.20.hidden_ref = bf16[80,768]{1,0:T(8,128)(2,1)S(1)} collective-permute-done((bf16[80,768]{1,0:T(8,128)(2,1)S(1)}, bf16[80,768]{1,0:T(8,128)(2,1)S(1)}, u32[]{:S(2)}, u32[]{:S(2)}) %collective-permute-start.20) | collective-permute-done | bytes 122912 | tf_op jit(solution)/shard_map/ppermute | solution.py:311
  61.0 2.0 %collective-permute-start.19 = (bf16[40,2048]{1,0:T(8,128)(2,1)S(1)}, bf16[40,2048]{1,0:T(8,128)(2,1)S(1)}, u32[]{:S(2)}, u32[]{:S(2)}) collective-permute-start(bf16[40,2048]{1,0:T(8,128)(2,1)S(1)} %get-tuple-element.92), channel_id=1, source_target_pairs={{0,8},{1,9},{2,10},{3,11},{4,12},{5,13},{6,14},{7,15},{8,0},{9,1},... | collective-permute-start | bytes 491528 | tf_op jit(solution)/shard_map/ppermute | solution.py:379
  62.9 1.2 %down_b.3 = (bf16[40,2048]{1,0:T(8,128)(2,1)S(1)}, bf16[40,2048]{1,0:T(8,128)(2,1)S(1)}) custom-call(s32[11]{0:T(128)S(1)} %concatenate.6.meta, bf16[80,768]{1,0:T(8,128)(2,1)S(1)} %collective-permute-done.20.hidden_ref, bf16[768,1024]{1,0:T(8,128)(2,1)S(1)} %bitcast.31, bf16[768,1024]{1,0:T(8,128)(2,1)S(1)} %collective-permute-done.8.refs_2_.refs_1_), custom_call_target="tpu_custom_call" | custom-call | flops 1000 | bytes 1000 | tf_op jit(solution)/shard_map/down_b/pallas_call | solution.py:21
  64.2 3.9 %collective-permute-start.21 = (bf16[40,2048]{1,0:T(8,128)(2,1)S(1)}, bf16[40,2048]{1,0:T(8,128)(2,1)S(1)}, u32[]{:S(2)}, u32[]{:S(2)}) collective-permute-start(bf16[40,2048]{1,0:T(8,128)(2,1)S(1)} %get-tuple-element.94), channel_id=1, source_target_pairs={{0,11},{1,8},{2,9},{3,10},{4,15},{5,12},{6,13},{7,14},{8,3},{9,0},... | collective-permute-start | bytes 491528 | tf_op jit(solution)/shard_map/ppermute | solution.py:379
  68.9 4.1 %collective-permute-done.18.refs_0_ = bf16[40,2048]{1,0:T(8,128)(2,1)S(1)} collective-permute-done((bf16[40,2048]{1,0:T(8,128)(2,1)S(1)}, bf16[40,2048]{1,0:T(8,128)(2,1)S(1)}, u32[]{:S(2)}, u32[]{:S(2)}) %collective-permute-start.18) | collective-permute-done | bytes 163872 | tf_op jit(solution)/shard_map/ppermute | solution.py:379
  73.0 1.4 %collective-permute-done.19.refs_1_ = bf16[40,2048]{1,0:T(8,128)(2,1)S(1)} collective-permute-done((bf16[40,2048]{1,0:T(8,128)(2,1)S(1)}, bf16[40,2048]{1,0:T(8,128)(2,1)S(1)}, u32[]{:S(2)}, u32[]{:S(2)}) %collective-permute-start.19) | collective-permute-done | bytes 163872 | tf_op jit(solution)/shard_map/ppermute | solution.py:379
  74.4 1.8 %collective-permute-done.22.refs_3_ = bf16[40,2048]{1,0:T(8,128)(2,1)S(1)} collective-permute-done((bf16[40,2048]{1,0:T(8,128)(2,1)S(1)}, bf16[40,2048]{1,0:T(8,128)(2,1)S(1)}, u32[]{:S(2)}, u32[]{:S(2)}) %collective-permute-start.22) | collective-permute-done | bytes 163872 | tf_op jit(solution)/shard_map/ppermute | solution.py:379
  76.1 1.6 %combine_b.1 = bf16[128,4096]{1,0:T(8,128)(2,1)} custom-call(s32[11]{0:T(128)S(1)} %concatenate.6.meta, bf16[128,2048]{1,0:T(8,128)(2,1)S(1)} %get-tuple-element.53.att_ref, bf16[128,160]{1,0:T(8,128)(2,1)S(1)} %get-tuple-element.54.back_ref, f32[128,128]{1,0:T(8,128)S(1)} %get-tuple-element.90.weight_ref, ...), custom_call_target="tpu_custom_call" | custom-call | flops 20000000000 | bytes 1000 | tf_op jit(solution)/shard_map/combine_b/pallas_call | solution.py:21
  (43 shorter events, 7.7 us)
Async XLA Ops:
  0.9 6.5 %collective-permute-start.1 = (bf16[128,512]{1,0:T(8,128)(2,1)S(1)}, bf16[128,512]{1,0:T(8,128)(2,1)S(1)}, u32[]{:S(2)}, u32[]{:S(2)}) collective-permute-start(bf16[128,512]{1,0:T(8,128)(2,1)S(1)} %pad_maximum_fusion.refs_0_), channel_id=1, source_target_pairs={{0,8},{4,12},{8,0},{12,4},{1,9},{5,13},{9,1},{13,5},{2,10},{6,14},... | collective-permute-start | bytes 393224 | tf_op jit(solution)/shard_map/ppermute | solution.py:311
  3.9 3.5 %collective-permute-start = (bf16[128,512]{1,0:T(8,128)(2,1)S(1)}, bf16[128,512]{1,0:T(8,128)(2,1)S(1)}, u32[]{:S(2)}, u32[]{:S(2)}) collective-permute-start(bf16[128,512]{1,0:T(8,128)(2,1)S(1)} %pad_maximum_fusion.refs_0_), channel_id=1, source_target_pairs={{0,4},{4,0},{8,12},{12,8},{1,5},{5,1},{9,13},{13,9},{2,6},{6,2},{1... | collective-permute-start | bytes 393224 | tf_op jit(solution)/shard_map/ppermute | solution.py:311
  4.6 0.7 copy-start.3
  5.3 3.5 %copy-start.5 = (bf16[1,1024,2,768]{3,2,1,0:T(2,128)(2,1)S(1)}, bf16[1,1024,2,768]{3,2,1,0:T(2,128)(2,1)}, u32[]{:S(2)}) copy-start(bf16[1,1024,2,768]{3,2,1,0:T(2,128)(2,1)} %param.16) | copy-start | bytes 9437188
  5.3 3.6 %copy-start.2 = (bf16[1,128,4096]{2,1,0:T(8,128)(2,1)S(1)}, bf16[1,128,4096]{2,1,0:T(8,128)(2,1)}, u32[]{:S(2)}) copy-start(bf16[1,128,4096]{2,1,0:T(8,128)(2,1)} %param.9) | copy-start | bytes 3145732
  7.4 1.3 %collective-permute-start.2 = (bf16[128,512]{1,0:T(8,128)(2,1)S(1)}, bf16[128,512]{1,0:T(8,128)(2,1)S(1)}, u32[]{:S(2)}, u32[]{:S(2)}) collective-permute-start(bf16[128,512]{1,0:T(8,128)(2,1)S(1)} %collective-permute-done.1.refs_2_), channel_id=1, source_target_pairs={{0,4},{4,0},{8,12},{12,8},{1,5},{5,1},{9,13},{13,9},{2,6},{6,2},{1... | collective-permute-start | bytes 393224 | tf_op jit(solution)/shard_map/ppermute | solution.py:311
  8.7 14.9 %collective-permute-start.4 = (bf16[1024,2,768]{2,1,0:T(2,128)(2,1)S(1)}, bf16[1024,2,768]{2,1,0:T(2,128)(2,1)S(1)}, u32[]{:S(2)}, u32[]{:S(2)}) collective-permute-start(bf16[1024,2,768]{2,1,0:T(2,128)(2,1)S(1)} %bitcast.40), channel_id=1, source_target_pairs={{0,4},{4,0},{8,12},{12,8},{1,5},{5,1},{9,13},{13,9},{2,6},{6,2},{1... | collective-permute-start | bytes 9437192 | tf_op jit(solution)/shard_map/ppermute | solution.py:311
  11.2 12.4 %collective-permute-start.3 = (bf16[40,2048]{1,0:T(8,128)(2,1)S(1)}, bf16[40,2048]{1,0:T(8,128)(2,1)S(1)}, u32[]{:S(2)}, u32[]{:S(2)}) collective-permute-start(bf16[40,2048]{1,0:T(8,128)(2,1)S(1)} %get-tuple-element.55), channel_id=1, source_target_pairs={{0,10},{1,11},{2,8},{3,9},{4,14},{5,15},{6,12},{7,13},{8,2},{9,3},... | collective-permute-start | bytes 491528 | tf_op jit(solution)/shard_map/ppermute | solution.py:379
  15.0 8.6 %copy-start = (bf16[1,768,1024]{2,1,0:T(8,128)(2,1)S(1)}, bf16[1,768,1024]{2,1,0:T(8,128)(2,1)}, u32[]{:S(2)}) copy-start(bf16[1,768,1024]{2,1,0:T(8,128)(2,1)} %param.17) | copy-start | bytes 4718596
  15.6 15.6 %collective-permute-start.9 = (bf16[40,2048]{1,0:T(8,128)(2,1)S(1)}, bf16[40,2048]{1,0:T(8,128)(2,1)S(1)}, u32[]{:S(2)}, u32[]{:S(2)}) collective-permute-start(bf16[40,2048]{1,0:T(8,128)(2,1)S(1)} %get-tuple-element.74), channel_id=1, source_target_pairs={{0,8},{1,9},{2,10},{3,11},{4,12},{5,13},{6,14},{7,15},{8,0},{9,1},... | collective-permute-start | bytes 491528 | tf_op jit(solution)/shard_map/ppermute | solution.py:379
  16.2 17.5 %collective-permute-start.7 = (bf16[40,2048]{1,0:T(8,128)(2,1)S(1)}, bf16[40,2048]{1,0:T(8,128)(2,1)S(1)}, u32[]{:S(2)}, u32[]{:S(2)}) collective-permute-start(bf16[40,2048]{1,0:T(8,128)(2,1)S(1)} %get-tuple-element.64), channel_id=1, source_target_pairs={{0,11},{1,8},{2,9},{3,10},{4,15},{5,12},{6,13},{7,14},{8,3},{9,0},... | collective-permute-start | bytes 491528 | tf_op jit(solution)/shard_map/ppermute | solution.py:379
  18.5 15.2 %collective-permute-start.6 = (bf16[40,2048]{1,0:T(8,128)(2,1)S(1)}, bf16[40,2048]{1,0:T(8,128)(2,1)S(1)}, u32[]{:S(2)}, u32[]{:S(2)}) collective-permute-start(bf16[40,2048]{1,0:T(8,128)(2,1)S(1)} %get-tuple-element.62), channel_id=1, source_target_pairs={{0,9},{1,10},{2,11},{3,8},{4,13},{5,14},{6,15},{7,12},{8,1},{9,2},... | collective-permute-start | bytes 491528 | tf_op jit(solution)/shard_map/ppermute | solution.py:379
  23.6 10.1 %collective-permute-start.8 = (bf16[768,1024]{1,0:T(8,128)(2,1)S(1)}, bf16[768,1024]{1,0:T(8,128)(2,1)S(1)}, u32[]{:S(2)}, u32[]{:S(2)}) collective-permute-start(bf16[768,1024]{1,0:T(8,128)(2,1)S(1)} %bitcast.27), channel_id=1, source_target_pairs={{0,4},{4,0},{8,12},{12,8},{1,5},{5,1},{9,13},{13,9},{2,6},{6,2},{1... | collective-permute-start | bytes 4718600 | tf_op jit(solution)/shard_map/ppermute | solution.py:311
  24.2 7.0 %copy-start.1 = (f32[4096]{0:T(1024)S(1)}, f32[4096]{0:T(1024)}, u32[]{:S(2)}) copy-start(f32[4096]{0:T(1024)} %param.15) | copy-start | bytes 49156
  26.6 13.2 %collective-permute-start.5 = (bf16[40,2048]{1,0:T(8,128)(2,1)S(1)}, bf16[40,2048]{1,0:T(8,128)(2,1)S(1)}, u32[]{:S(2)}, u32[]{:S(2)}) collective-permute-start(bf16[40,2048]{1,0:T(8,128)(2,1)S(1)} %get-tuple-element.61), channel_id=1, source_target_pairs={{0,2},{1,3},{2,0},{3,1},{4,6},{5,7},{6,4},{7,5},{8,10},{9,11},{10,... | collective-permute-start | bytes 491528 | tf_op jit(solution)/shard_map/ppermute | solution.py:379
  33.1 9.7 %collective-permute-start.10 = (bf16[80,1664]{1,0:T(8,128)(2,1)S(1)}, bf16[80,1664]{1,0:T(8,128)(2,1)S(1)}, u32[]{:S(2)}, u32[]{:S(2)}) collective-permute-start(bf16[80,1664]{1,0:T(8,128)(2,1)S(1)} %products_b.3), channel_id=1, source_target_pairs={{0,8},{4,12},{8,0},{12,4},{1,9},{5,13},{9,1},{13,5},{2,10},{6,14},... | collective-permute-start | bytes 798728 | tf_op jit(solution)/shard_map/ppermute | solution.py:311
  35.6 14.1 %collective-permute-start.15 = (bf16[80,1664]{1,0:T(8,128)(2,1)S(1)}, bf16[80,1664]{1,0:T(8,128)(2,1)S(1)}, u32[]{:S(2)}, u32[]{:S(2)}) collective-permute-start(bf16[80,1664]{1,0:T(8,128)(2,1)S(1)} %products_b.2), channel_id=1, source_target_pairs={{0,8},{4,12},{8,0},{12,4},{1,9},{5,13},{9,1},{13,5},{2,10},{6,14},... | collective-permute-start | bytes 798728 | tf_op jit(solution)/shard_map/ppermute | solution.py:311
  37.1 8.6 %collective-permute-start.12 = (bf16[40,2048]{1,0:T(8,128)(2,1)S(1)}, bf16[40,2048]{1,0:T(8,128)(2,1)S(1)}, u32[]{:S(2)}, u32[]{:S(2)}) collective-permute-start(bf16[40,2048]{1,0:T(8,128)(2,1)S(1)} %get-tuple-element.79), channel_id=1, source_target_pairs={{0,1},{1,2},{2,3},{3,0},{4,5},{5,6},{6,7},{7,4},{8,9},{9,10},{10,1... | collective-permute-start | bytes 491528 | tf_op jit(solution)/shard_map/ppermute | solution.py:379
  39.8 8.1 %collective-permute-start.13 = (bf16[40,2048]{1,0:T(8,128)(2,1)S(1)}, bf16[40,2048]{1,0:T(8,128)(2,1)S(1)}, u32[]{:S(2)}, u32[]{:S(2)}) collective-permute-start(bf16[40,2048]{1,0:T(8,128)(2,1)S(1)} %get-tuple-element.83), channel_id=1, source_target_pairs={{0,3},{1,0},{2,1},{3,2},{4,7},{5,4},{6,5},{7,6},{8,11},{9,8},{10,9... | collective-permute-start | bytes 491528 | tf_op jit(solution)/shard_map/ppermute | solution.py:379
  44.2 5.5 %collective-permute-start.14 = (bf16[80,768]{1,0:T(8,128)(2,1)S(1)}, bf16[80,768]{1,0:T(8,128)(2,1)S(1)}, u32[]{:S(2)}, u32[]{:S(2)}) collective-permute-start(bf16[80,768]{1,0:T(8,128)(2,1)S(1)} %get-tuple-element.80), channel_id=1, source_target_pairs={{0,8},{4,12},{8,0},{12,4},{1,9},{5,13},{9,1},{13,5},{2,10},{6,14},... | collective-permute-start | bytes 368648 | tf_op jit(solution)/shard_map/ppermute | solution.py:311
  45.7 18.4 %collective-permute-start.11 = (bf16[40,2048]{1,0:T(8,128)(2,1)S(1)}, bf16[40,2048]{1,0:T(8,128)(2,1)S(1)}, u32[]{:S(2)}, u32[]{:S(2)}) collective-permute-start(bf16[40,2048]{1,0:T(8,128)(2,1)S(1)} %get-tuple-element.76), channel_id=1, source_target_pairs={{0,2},{1,3},{2,0},{3,1},{4,6},{5,7},{6,4},{7,5},{8,10},{9,11},{10,... | collective-permute-start | bytes 491528 | tf_op jit(solution)/shard_map/ppermute | solution.py:379
  51.2 16.9 %collective-permute-start.16 = (bf16[40,2048]{1,0:T(8,128)(2,1)S(1)}, bf16[40,2048]{1,0:T(8,128)(2,1)S(1)}, u32[]{:S(2)}, u32[]{:S(2)}) collective-permute-start(bf16[40,2048]{1,0:T(8,128)(2,1)S(1)} %get-tuple-element.88), channel_id=1, source_target_pairs={{0,3},{1,0},{2,1},{3,2},{4,7},{5,4},{6,5},{7,6},{8,11},{9,8},{10,9... | collective-permute-start | bytes 491528 | tf_op jit(solution)/shard_map/ppermute | solution.py:379
  55.5 12.5 %collective-permute-start.17 = (bf16[40,2048]{1,0:T(8,128)(2,1)S(1)}, bf16[40,2048]{1,0:T(8,128)(2,1)S(1)}, u32[]{:S(2)}, u32[]{:S(2)}) collective-permute-start(bf16[40,2048]{1,0:T(8,128)(2,1)S(1)} %get-tuple-element.89), channel_id=1, source_target_pairs={{0,1},{1,2},{2,3},{3,0},{4,5},{5,6},{6,7},{7,4},{8,9},{9,10},{10,1... | collective-permute-start | bytes 491528 | tf_op jit(solution)/shard_map/ppermute | solution.py:379
  55.5 12.5 %copy-start.4 = (f32[1,128,1]{1,2,0:T(1,128)S(1)}, f32[1,128,1]{1,2,0:T(1,128)}, u32[]{:S(2)}) copy-start(f32[1,128,1]{1,2,0:T(1,128)} %param.14) | copy-start | bytes 1540
  55.5 5.4 %collective-permute-start.20 = (bf16[80,768]{1,0:T(8,128)(2,1)S(1)}, bf16[80,768]{1,0:T(8,128)(2,1)S(1)}, u32[]{:S(2)}, u32[]{:S(2)}) collective-permute-start(bf16[80,768]{1,0:T(8,128)(2,1)S(1)} %get-tuple-element.93), channel_id=1, source_target_pairs={{0,8},{4,12},{8,0},{12,4},{1,9},{5,13},{9,1},{13,5},{2,10},{6,14},... | collective-permute-start | bytes 368648 | tf_op jit(solution)/shard_map/ppermute | solution.py:311
  58.4 14.6 %collective-permute-start.18 = (bf16[40,2048]{1,0:T(8,128)(2,1)S(1)}, bf16[40,2048]{1,0:T(8,128)(2,1)S(1)}, u32[]{:S(2)}, u32[]{:S(2)}) collective-permute-start(bf16[40,2048]{1,0:T(8,128)(2,1)S(1)} %get-tuple-element.91), channel_id=1, source_target_pairs={{0,10},{1,11},{2,8},{3,9},{4,14},{5,15},{6,12},{7,13},{8,2},{9,3},... | collective-permute-start | bytes 491528 | tf_op jit(solution)/shard_map/ppermute | solution.py:379
  61.0 13.4 %collective-permute-start.19 = (bf16[40,2048]{1,0:T(8,128)(2,1)S(1)}, bf16[40,2048]{1,0:T(8,128)(2,1)S(1)}, u32[]{:S(2)}, u32[]{:S(2)}) collective-permute-start(bf16[40,2048]{1,0:T(8,128)(2,1)S(1)} %get-tuple-element.92), channel_id=1, source_target_pairs={{0,8},{1,9},{2,10},{3,11},{4,12},{5,13},{6,14},{7,15},{8,0},{9,1},... | collective-permute-start | bytes 491528 | tf_op jit(solution)/shard_map/ppermute | solution.py:379
  64.2 10.2 %collective-permute-start.21 = (bf16[40,2048]{1,0:T(8,128)(2,1)S(1)}, bf16[40,2048]{1,0:T(8,128)(2,1)S(1)}, u32[]{:S(2)}, u32[]{:S(2)}) collective-permute-start(bf16[40,2048]{1,0:T(8,128)(2,1)S(1)} %get-tuple-element.94), channel_id=1, source_target_pairs={{0,11},{1,8},{2,9},{3,10},{4,15},{5,12},{6,13},{7,14},{8,3},{9,0},... | collective-permute-start | bytes 491528 | tf_op jit(solution)/shard_map/ppermute | solution.py:379
  68.0 8.1 %collective-permute-start.22 = (bf16[40,2048]{1,0:T(8,128)(2,1)S(1)}, bf16[40,2048]{1,0:T(8,128)(2,1)S(1)}, u32[]{:S(2)}, u32[]{:S(2)}) collective-permute-start(bf16[40,2048]{1,0:T(8,128)(2,1)S(1)} %get-tuple-element.95), channel_id=1, source_target_pairs={{0,9},{1,10},{2,11},{3,8},{4,13},{5,14},{6,15},{7,12},{8,1},{9,2},... | collective-permute-start | bytes 491528 | tf_op jit(solution)/shard_map/ppermute | solution.py:379

commit v9 on v8

--- a/solution.py
+++ b/solution.py
@@ -401,9 +401,9 @@
     for i, far in enumerate(far_sums):
         rows = [after(r, made, *hiddens) for r in rows_a[i * pair : (i + 1) * pair]]
         sums, squares = products(meta, gain, rows, w_ins, row_at, False)
-        sums = after(sums, *moved)
+        hold = moved
         hidden, blocks = finish(meta, sums, squares, [far], w_outs, col_at, width, len(rows))
-        out_a += blocks
+        out_a += [after(b, *hold) for b in blocks] if hold else blocks
         hiddens.append(hidden)
         moved.append(swap(hidden, "ctx", n_ctx, top))
     back_a = send(out_a, True, False)

time: 77.9 us -> 77 us (0.988)
  waiting for transfers between devices: 22.4 us -> 21.6 us
    ppermute x14, waiting for transfers between devices: 17.7 us -> 16.3 us  [send(): moved.append(block if still else lax.ppermute(block, ('ctx', 'exp'), pairs))]
  transfers between devices with their start and end apart: 23 -> 23, of which waited for: 9 -> 8; matrix products, arithmetic and copies ran while one was open for 2% -> 2% of each run, Pallas kernels for 24% -> 25%
where the time goes in v9:
time: 77 us; the launch traced here: 76.7 us
  starting transfers between devices  31.1 us (40%)
  waiting for transfers between devices  21.6 us (28%)
  Pallas kernels  20.4 us (26%)
  local copies, waits for them, and re-layouts  2.58 us (3%)
  other arithmetic  0.88 us (1%)
    ppermute x14, starting transfers between devices, send(): moved.append(block if still else lax.ppermute(block, ('ctx', 'exp'), pairs))  22.7 us
    pallas_call x13, Pallas kernels, call(): pl.pallas_call(kernel, in_specs=specs, out_specs=[pl.BlockSpec(memory_spa...  20.4 us
    ppermute x14, waiting for transfers between devices, send(): moved.append(block if still else lax.ppermute(block, ('ctx', 'exp'), pairs))  16.3 us
    ppermute x9, starting transfers between devices, swap(): return lax.ppermute(array, axis, [(i, i ^ bit) for i in range(size)])  8.43 us
    ppermute x9, waiting for transfers between devices, swap(): return lax.ppermute(array, axis, [(i, i ^ bit) for i in range(size)])  5.31 us
    unnamed x14, local copies, waits for them, and re-layouts  1.85 us
  transfers between devices with their start and end apart: 23, of which 8 were waited for; matrix products, arithmetic and copies ran while one was open for 2% of the time, Pallas kernels for 25%

profile of v9, /device:TPU:0, one launch (start us, length us, event | category | flops | bytes accessed | tf_op | source)
XLA Modules:
  0.0 76.7 jit_solution(17377986548937004588)
XLA Ops:
  0.9 3.0 %collective-permute-start.1 = (bf16[128,512]{1,0:T(8,128)(2,1)S(1)}, bf16[128,512]{1,0:T(8,128)(2,1)S(1)}, u32[]{:S(2)}, u32[]{:S(2)}) collective-permute-start(bf16[128,512]{1,0:T(8,128)(2,1)S(1)} %pad_maximum_fusion.refs_0_), channel_id=1, source_target_pairs={{0,8},{4,12},{8,0},{12,4},{1,9},{5,13},{9,1},{13,5},{2,10},{6,14},... | collective-permute-start | bytes 393224 | tf_op jit(solution)/shard_map/ppermute | solution.py:311
  6.1 1.3 %collective-permute-done.1.refs_2_ = bf16[128,512]{1,0:T(8,128)(2,1)S(1)} collective-permute-done((bf16[128,512]{1,0:T(8,128)(2,1)S(1)}, bf16[128,512]{1,0:T(8,128)(2,1)S(1)}, u32[]{:S(2)}, u32[]{:S(2)}) %collective-permute-start.1) | collective-permute-done | bytes 131104 | tf_op jit(solution)/shard_map/ppermute | solution.py:311
  7.4 1.3 %collective-permute-done.2.refs_3_ = bf16[128,512]{1,0:T(8,128)(2,1)S(1)} collective-permute-done((bf16[128,512]{1,0:T(8,128)(2,1)S(1)}, bf16[128,512]{1,0:T(8,128)(2,1)S(1)}, u32[]{:S(2)}, u32[]{:S(2)}) %collective-permute-start.2) | collective-permute-done | bytes 131104 | tf_op jit(solution)/shard_map/ppermute | solution.py:311
  8.9 2.3 %attend_b.1 = (bf16[128,2048]{1,0:T(8,128)(2,1)S(1)}, bf16[40,2048]{1,0:T(8,128)(2,1)S(1)}, bf16[40,2048]{1,0:T(8,128)(2,1)S(1)}, bf16[40,2048]{1,0:T(8,128)(2,1)S(1)}, bf16[40,2048]{1,0:T(8,128)(2,1)S(1)}) custom-call(s32[11]{0:T(128)S(1)} %concatenate.6.meta, bf16[128,4096]{1,0:T(8,128)(2,1)S(1)} %bitcast.36, ...), custom_call_target="tpu_custom_call" | custom-call | flops 2000000000 | bytes 1000 | tf_op jit(solution)/shard_map/attend_b/pallas_call | solution.py:21
  11.2 3.8 %collective-permute-start.3 = (bf16[40,2048]{1,0:T(8,128)(2,1)S(1)}, bf16[40,2048]{1,0:T(8,128)(2,1)S(1)}, u32[]{:S(2)}, u32[]{:S(2)}) collective-permute-start(bf16[40,2048]{1,0:T(8,128)(2,1)S(1)} %get-tuple-element.56), channel_id=1, source_target_pairs={{0,10},{1,11},{2,8},{3,9},{4,14},{5,15},{6,12},{7,13},{8,2},{9,3},... | collective-permute-start | bytes 491528 | tf_op jit(solution)/shard_map/ppermute | solution.py:379
  16.2 2.3 %collective-permute-start.7 = (bf16[40,2048]{1,0:T(8,128)(2,1)S(1)}, bf16[40,2048]{1,0:T(8,128)(2,1)S(1)}, u32[]{:S(2)}, u32[]{:S(2)}) collective-permute-start(bf16[40,2048]{1,0:T(8,128)(2,1)S(1)} %get-tuple-element.65), channel_id=1, source_target_pairs={{0,11},{1,8},{2,9},{3,10},{4,15},{5,12},{6,13},{7,14},{8,3},{9,0},... | collective-permute-start | bytes 491528 | tf_op jit(solution)/shard_map/ppermute | solution.py:379
  19.2 4.5 %collective-permute-done.3.refs_0_ = bf16[40,2048]{1,0:T(8,128)(2,1)S(1)} collective-permute-done((bf16[40,2048]{1,0:T(8,128)(2,1)S(1)}, bf16[40,2048]{1,0:T(8,128)(2,1)S(1)}, u32[]{:S(2)}, u32[]{:S(2)}) %collective-permute-start.3) | collective-permute-done | bytes 163872 | tf_op jit(solution)/shard_map/ppermute | solution.py:379
  24.2 2.3 %attend_a.1 = (bf16[128,2048]{1,0:T(8,128)(2,1)S(1)}, bf16[40,2048]{1,0:T(8,128)(2,1)S(1)}, bf16[40,2048]{1,0:T(8,128)(2,1)S(1)}, bf16[40,2048]{1,0:T(8,128)(2,1)S(1)}, bf16[40,2048]{1,0:T(8,128)(2,1)S(1)}) custom-call(s32[11]{0:T(128)S(1)} %concatenate.6.meta, bf16[128,4096]{1,0:T(8,128)(2,1)S(1)} %bitcast.37, ...), custom_call_target="tpu_custom_call" | custom-call | flops 2000000000 | bytes 1000 | tf_op jit(solution)/shard_map/attend_a/pallas_call | solution.py:21
  26.9 4.4 %collective-permute-done.9.refs_1_ = bf16[40,2048]{1,0:T(8,128)(2,1)S(1)} collective-permute-done((bf16[40,2048]{1,0:T(8,128)(2,1)S(1)}, bf16[40,2048]{1,0:T(8,128)(2,1)S(1)}, u32[]{:S(2)}, u32[]{:S(2)}) %collective-permute-start.9) | collective-permute-done | bytes 163872 | tf_op jit(solution)/shard_map/ppermute | solution.py:379
  31.3 1.8 %products_b.3 = bf16[80,1664]{1,0:T(8,128)(2,1)S(1)} custom-call(s32[11]{0:T(128)S(1)} %concatenate.6.meta, f32[1,4096]{1,0:T(1,128)S(1)} %bitcast.32, bf16[40,2048]{1,0:T(8,128)(2,1)S(1)} %collective-permute-done.3.refs_0_, bf16[40,2048]{1,0:T(8,128)(2,1)S(1)} %collective-permute-done.9.refs_1_, bf16[1024,1536]{1,0:T(8,128)(2,1)S(1)} %bitcast.19, ...), custom_call_target="tpu_custom_call" | custom-call | flops 20000000000 | bytes 1000 | tf_op jit(solution)/shard_map/products_b/pallas_call | solution.py:21
  33.7 1.8 %products_b.2 = bf16[80,1664]{1,0:T(8,128)(2,1)S(1)} custom-call(s32[11]{0:T(128)S(1)} %concatenate.6.meta, f32[1,4096]{1,0:T(1,128)S(1)} %bitcast.33, bf16[40,2048]{1,0:T(8,128)(2,1)S(1)} %collective-permute-done.6.refs_0_, bf16[40,2048]{1,0:T(8,128)(2,1)S(1)} %collective-permute-done.7.refs_1_, bf16[1024,1536]{1,0:T(8,128)(2,1)S(1)} %bitcast.20, ...), custom_call_target="tpu_custom_call" | custom-call | flops 20000000000 | bytes 1000 | tf_op jit(solution)/shard_map/products_b/pallas_call | solution.py:21
  35.6 1.5 %collective-permute-start.14 = (bf16[80,1664]{1,0:T(8,128)(2,1)S(1)}, bf16[80,1664]{1,0:T(8,128)(2,1)S(1)}, u32[]{:S(2)}, u32[]{:S(2)}) collective-permute-start(bf16[80,1664]{1,0:T(8,128)(2,1)S(1)} %products_b.2), channel_id=1, source_target_pairs={{0,8},{4,12},{8,0},{12,4},{1,9},{5,13},{9,1},{13,5},{2,10},{6,14},... | collective-permute-start | bytes 798728 | tf_op jit(solution)/shard_map/ppermute | solution.py:311
  37.1 2.7 %collective-permute-start.12 = (bf16[40,2048]{1,0:T(8,128)(2,1)S(1)}, bf16[40,2048]{1,0:T(8,128)(2,1)S(1)}, u32[]{:S(2)}, u32[]{:S(2)}) collective-permute-start(bf16[40,2048]{1,0:T(8,128)(2,1)S(1)} %get-tuple-element.80), channel_id=1, source_target_pairs={{0,1},{1,2},{2,3},{3,0},{4,5},{5,6},{6,7},{7,4},{8,9},{9,10},{10,1... | collective-permute-start | bytes 491528 | tf_op jit(solution)/shard_map/ppermute | solution.py:379
  39.8 1.1 %collective-permute-start.13 = (bf16[40,2048]{1,0:T(8,128)(2,1)S(1)}, bf16[40,2048]{1,0:T(8,128)(2,1)S(1)}, u32[]{:S(2)}, u32[]{:S(2)}) collective-permute-start(bf16[40,2048]{1,0:T(8,128)(2,1)S(1)} %get-tuple-element.84), channel_id=1, source_target_pairs={{0,3},{1,0},{2,1},{3,2},{4,7},{5,4},{6,5},{7,6},{8,11},{9,8},{10,9... | collective-permute-start | bytes 491528 | tf_op jit(solution)/shard_map/ppermute | solution.py:379
  40.9 1.8 %products_a.2 = (f32[80,1536]{1,0:T(8,128)S(1)}, f32[80,128]{1,0:T(8,128)S(1)}) custom-call(s32[11]{0:T(128)S(1)} %concatenate.6.meta, f32[1,4096]{1,0:T(1,128)S(1)} %bitcast.34, bf16[40,2048]{1,0:T(8,128)(2,1)S(1)} %collective-permute-done.5.refs_0_, bf16[40,2048]{1,0:T(8,128)(2,1)S(1)} %get-tuple-element.71.refs_1_, bf16[1024,1536]{1,0:T(8,128)(2,1)S(1)} %bitcast.21, ...), custom_call_target="tpu_custom_call" | custom-call | flops 1000 | bytes 1000 | tf_op jit(solution)/shard_map/products_a/pallas_call | solution.py:21
  42.8 1.4 %hidden_down_a.2 = (bf16[80,768]{1,0:T(8,128)(2,1)S(1)}, bf16[40,2048]{1,0:T(8,128)(2,1)S(1)}, bf16[40,2048]{1,0:T(8,128)(2,1)S(1)}) custom-call(s32[11]{0:T(128)S(1)} %concatenate.6.meta, f32[80,1536]{1,0:T(8,128)S(1)} %get-tuple-element.72.sums_ref, f32[80,128]{1,0:T(8,128)S(1)} %get-tuple-element.73.squares_ref, ...), custom_call_target="tpu_custom_call" | custom-call | flops 1000 | bytes 1000 | tf_op jit(solution)/shard_map/hidden_down_a/pallas_call | solution.py:21
  44.2 1.5 %collective-permute-start.15 = (bf16[80,768]{1,0:T(8,128)(2,1)S(1)}, bf16[80,768]{1,0:T(8,128)(2,1)S(1)}, u32[]{:S(2)}, u32[]{:S(2)}) collective-permute-start(bf16[80,768]{1,0:T(8,128)(2,1)S(1)} %get-tuple-element.81), channel_id=1, source_target_pairs={{0,8},{4,12},{8,0},{12,4},{1,9},{5,13},{9,1},{13,5},{2,10},{6,14},... | collective-permute-start | bytes 368648 | tf_op jit(solution)/shard_map/ppermute | solution.py:311
  46.3 1.6 %collective-permute-done.13.refs_1_ = bf16[40,2048]{1,0:T(8,128)(2,1)S(1)} collective-permute-done((bf16[40,2048]{1,0:T(8,128)(2,1)S(1)}, bf16[40,2048]{1,0:T(8,128)(2,1)S(1)}, u32[]{:S(2)}, u32[]{:S(2)}) %collective-permute-start.13) | collective-permute-done | bytes 163872 | tf_op jit(solution)/shard_map/ppermute | solution.py:379
  47.9 1.8 %products_a.3 = (f32[80,1536]{1,0:T(8,128)S(1)}, f32[80,128]{1,0:T(8,128)S(1)}) custom-call(s32[11]{0:T(128)S(1)} %concatenate.6.meta, f32[1,4096]{1,0:T(1,128)S(1)} %bitcast.35, bf16[40,2048]{1,0:T(8,128)(2,1)S(1)} %collective-permute-done.12.refs_0_, bf16[40,2048]{1,0:T(8,128)(2,1)S(1)} %collective-permute-done.13.refs_1_, ...), custom_call_target="tpu_custom_call" | custom-call | flops 1000 | bytes 1000 | tf_op jit(solution)/shard_map/products_a/pallas_call | solution.py:21
  49.7 1.4 %hidden_down_a.3 = (bf16[80,768]{1,0:T(8,128)(2,1)S(1)}, bf16[40,2048]{1,0:T(8,128)(2,1)S(1)}, bf16[40,2048]{1,0:T(8,128)(2,1)S(1)}) custom-call(s32[11]{0:T(128)S(1)} %concatenate.6.meta, f32[80,1536]{1,0:T(8,128)S(1)} %get-tuple-element.86.sums_ref, f32[80,128]{1,0:T(8,128)S(1)} %get-tuple-element.87.squares_ref, ...), custom_call_target="tpu_custom_call" | custom-call | flops 1000 | bytes 1000 | tf_op jit(solution)/shard_map/hidden_down_a/pallas_call | solution.py:21
  51.1 1.6 %collective-permute-start.17 = (bf16[40,2048]{1,0:T(8,128)(2,1)S(1)}, bf16[40,2048]{1,0:T(8,128)(2,1)S(1)}, u32[]{:S(2)}, u32[]{:S(2)}) collective-permute-start(bf16[40,2048]{1,0:T(8,128)(2,1)S(1)} %get-tuple-element.91), channel_id=1, source_target_pairs={{0,1},{1,2},{2,3},{3,0},{4,5},{5,6},{6,7},{7,4},{8,9},{9,10},{10,1... | collective-permute-start | bytes 491528 | tf_op jit(solution)/shard_map/ppermute | solution.py:379
  52.7 2.9 %collective-permute-start.16 = (bf16[40,2048]{1,0:T(8,128)(2,1)S(1)}, bf16[40,2048]{1,0:T(8,128)(2,1)S(1)}, u32[]{:S(2)}, u32[]{:S(2)}) collective-permute-start(bf16[40,2048]{1,0:T(8,128)(2,1)S(1)} %get-tuple-element.89), channel_id=1, source_target_pairs={{0,3},{1,0},{2,1},{3,2},{4,7},{5,4},{6,5},{7,6},{8,11},{9,8},{10,9... | collective-permute-start | bytes 491528 | tf_op jit(solution)/shard_map/ppermute | solution.py:379
  55.6 1.6 %collective-permute-start.20 = (bf16[80,768]{1,0:T(8,128)(2,1)S(1)}, bf16[80,768]{1,0:T(8,128)(2,1)S(1)}, u32[]{:S(2)}, u32[]{:S(2)}) collective-permute-start(bf16[80,768]{1,0:T(8,128)(2,1)S(1)} %get-tuple-element.95), channel_id=1, source_target_pairs={{0,8},{4,12},{8,0},{12,4},{1,9},{5,13},{9,1},{13,5},{2,10},{6,14},... | collective-permute-start | bytes 368648 | tf_op jit(solution)/shard_map/ppermute | solution.py:311
  57.2 1.2 %down_b.2 = (bf16[40,2048]{1,0:T(8,128)(2,1)S(1)}, bf16[40,2048]{1,0:T(8,128)(2,1)S(1)}) custom-call(s32[11]{0:T(128)S(1)} %concatenate.6.meta, bf16[80,768]{1,0:T(8,128)(2,1)S(1)} %collective-permute-done.15.hidden_ref, bf16[768,1024]{1,0:T(8,128)(2,1)S(1)} %bitcast.30, bf16[768,1024]{1,0:T(8,128)(2,1)S(1)} %collective-permute-done.8.refs_2_.refs_1_), custom_call_target="tpu_custom_call" | custom-call | flops 1000 | bytes 1000 | tf_op jit(solution)/shard_map/down_b/pallas_call | solution.py:21
  58.9 2.6 %collective-permute-done.20.hidden_ref = bf16[80,768]{1,0:T(8,128)(2,1)S(1)} collective-permute-done((bf16[80,768]{1,0:T(8,128)(2,1)S(1)}, bf16[80,768]{1,0:T(8,128)(2,1)S(1)}, u32[]{:S(2)}, u32[]{:S(2)}) %collective-permute-start.20) | collective-permute-done | bytes 122912 | tf_op jit(solution)/shard_map/ppermute | solution.py:311
  61.5 1.5 %collective-permute-start.19 = (bf16[40,2048]{1,0:T(8,128)(2,1)S(1)}, bf16[40,2048]{1,0:T(8,128)(2,1)S(1)}, u32[]{:S(2)}, u32[]{:S(2)}) collective-permute-start(bf16[40,2048]{1,0:T(8,128)(2,1)S(1)} %get-tuple-element.94), channel_id=1, source_target_pairs={{0,8},{1,9},{2,10},{3,11},{4,12},{5,13},{6,14},{7,15},{8,0},{9,1},... | collective-permute-start | bytes 491528 | tf_op jit(solution)/shard_map/ppermute | solution.py:379
  63.0 1.2 %down_b.3 = (bf16[40,2048]{1,0:T(8,128)(2,1)S(1)}, bf16[40,2048]{1,0:T(8,128)(2,1)S(1)}) custom-call(s32[11]{0:T(128)S(1)} %concatenate.6.meta, bf16[80,768]{1,0:T(8,128)(2,1)S(1)} %collective-permute-done.20.hidden_ref, bf16[768,1024]{1,0:T(8,128)(2,1)S(1)} %bitcast.31, bf16[768,1024]{1,0:T(8,128)(2,1)S(1)} %collective-permute-done.8.refs_2_.refs_1_), custom_call_target="tpu_custom_call" | custom-call | flops 1000 | bytes 1000 | tf_op jit(solution)/shard_map/down_b/pallas_call | solution.py:21
  64.3 2.1 %collective-permute-start.21 = (bf16[40,2048]{1,0:T(8,128)(2,1)S(1)}, bf16[40,2048]{1,0:T(8,128)(2,1)S(1)}, u32[]{:S(2)}, u32[]{:S(2)}) collective-permute-start(bf16[40,2048]{1,0:T(8,128)(2,1)S(1)} %get-tuple-element.96), channel_id=1, source_target_pairs={{0,11},{1,8},{2,9},{3,10},{4,15},{5,12},{6,13},{7,14},{8,3},{9,0},... | collective-permute-start | bytes 491528 | tf_op jit(solution)/shard_map/ppermute | solution.py:379
  66.4 2.0 %collective-permute-start.22 = (bf16[40,2048]{1,0:T(8,128)(2,1)S(1)}, bf16[40,2048]{1,0:T(8,128)(2,1)S(1)}, u32[]{:S(2)}, u32[]{:S(2)}) collective-permute-start(bf16[40,2048]{1,0:T(8,128)(2,1)S(1)} %get-tuple-element.97), channel_id=1, source_target_pairs={{0,9},{1,10},{2,11},{3,8},{4,13},{5,14},{6,15},{7,12},{8,1},{9,2},... | collective-permute-start | bytes 491528 | tf_op jit(solution)/shard_map/ppermute | solution.py:379
  69.3 3.3 %collective-permute-done.18.refs_0_ = bf16[40,2048]{1,0:T(8,128)(2,1)S(1)} collective-permute-done((bf16[40,2048]{1,0:T(8,128)(2,1)S(1)}, bf16[40,2048]{1,0:T(8,128)(2,1)S(1)}, u32[]{:S(2)}, u32[]{:S(2)}) %collective-permute-start.18) | collective-permute-done | bytes 163872 | tf_op jit(solution)/shard_map/ppermute | solution.py:379
  72.6 2.6 %collective-permute-done.19.refs_1_ = bf16[40,2048]{1,0:T(8,128)(2,1)S(1)} collective-permute-done((bf16[40,2048]{1,0:T(8,128)(2,1)S(1)}, bf16[40,2048]{1,0:T(8,128)(2,1)S(1)}, u32[]{:S(2)}, u32[]{:S(2)}) %collective-permute-start.19) | collective-permute-done | bytes 163872 | tf_op jit(solution)/shard_map/ppermute | solution.py:379
  75.2 1.6 %combine_b.1 = bf16[128,4096]{1,0:T(8,128)(2,1)} custom-call(s32[11]{0:T(128)S(1)} %concatenate.6.meta, bf16[128,2048]{1,0:T(8,128)(2,1)S(1)} %get-tuple-element.54.att_ref, bf16[128,160]{1,0:T(8,128)(2,1)S(1)} %get-tuple-element.55.back_ref, f32[128,128]{1,0:T(8,128)S(1)} %get-tuple-element.92.weight_ref, ...), custom_call_target="tpu_custom_call" | custom-call | flops 20000000000 | bytes 1000 | tf_op jit(solution)/shard_map/combine_b/pallas_call | solution.py:21
  (43 shorter events, 8.5 us)
Async XLA Ops:
  0.9 6.5 %collective-permute-start.1 = (bf16[128,512]{1,0:T(8,128)(2,1)S(1)}, bf16[128,512]{1,0:T(8,128)(2,1)S(1)}, u32[]{:S(2)}, u32[]{:S(2)}) collective-permute-start(bf16[128,512]{1,0:T(8,128)(2,1)S(1)} %pad_maximum_fusion.refs_0_), channel_id=1, source_target_pairs={{0,8},{4,12},{8,0},{12,4},{1,9},{5,13},{9,1},{13,5},{2,10},{6,14},... | collective-permute-start | bytes 393224 | tf_op jit(solution)/shard_map/ppermute | solution.py:311
  3.9 3.5 %collective-permute-start = (bf16[128,512]{1,0:T(8,128)(2,1)S(1)}, bf16[128,512]{1,0:T(8,128)(2,1)S(1)}, u32[]{:S(2)}, u32[]{:S(2)}) collective-permute-start(bf16[128,512]{1,0:T(8,128)(2,1)S(1)} %pad_maximum_fusion.refs_0_), channel_id=1, source_target_pairs={{0,4},{4,0},{8,12},{12,8},{1,5},{5,1},{9,13},{13,9},{2,6},{6,2},{1... | collective-permute-start | bytes 393224 | tf_op jit(solution)/shard_map/ppermute | solution.py:311
  4.6 0.7 copy-start.3
  5.3 3.5 %copy-start.5 = (bf16[1,1024,2,768]{3,2,1,0:T(2,128)(2,1)S(1)}, bf16[1,1024,2,768]{3,2,1,0:T(2,128)(2,1)}, u32[]{:S(2)}) copy-start(bf16[1,1024,2,768]{3,2,1,0:T(2,128)(2,1)} %param.16) | copy-start | bytes 9437188
  5.3 3.6 %copy-start.2 = (bf16[1,128,4096]{2,1,0:T(8,128)(2,1)S(1)}, bf16[1,128,4096]{2,1,0:T(8,128)(2,1)}, u32[]{:S(2)}) copy-start(bf16[1,128,4096]{2,1,0:T(8,128)(2,1)} %param.9) | copy-start | bytes 3145732
  7.4 1.3 %collective-permute-start.2 = (bf16[128,512]{1,0:T(8,128)(2,1)S(1)}, bf16[128,512]{1,0:T(8,128)(2,1)S(1)}, u32[]{:S(2)}, u32[]{:S(2)}) collective-permute-start(bf16[128,512]{1,0:T(8,128)(2,1)S(1)} %collective-permute-done.1.refs_2_), channel_id=1, source_target_pairs={{0,4},{4,0},{8,12},{12,8},{1,5},{5,1},{9,13},{13,9},{2,6},{6,2},{1... | collective-permute-start | bytes 393224 | tf_op jit(solution)/shard_map/ppermute | solution.py:311
  8.7 14.9 %collective-permute-start.4 = (bf16[1024,2,768]{2,1,0:T(2,128)(2,1)S(1)}, bf16[1024,2,768]{2,1,0:T(2,128)(2,1)S(1)}, u32[]{:S(2)}, u32[]{:S(2)}) collective-permute-start(bf16[1024,2,768]{2,1,0:T(2,128)(2,1)S(1)} %bitcast.40), channel_id=1, source_target_pairs={{0,4},{4,0},{8,12},{12,8},{1,5},{5,1},{9,13},{13,9},{2,6},{6,2},{1... | collective-permute-start | bytes 9437192 | tf_op jit(solution)/shard_map/ppermute | solution.py:311
  11.2 12.4 %collective-permute-start.3 = (bf16[40,2048]{1,0:T(8,128)(2,1)S(1)}, bf16[40,2048]{1,0:T(8,128)(2,1)S(1)}, u32[]{:S(2)}, u32[]{:S(2)}) collective-permute-start(bf16[40,2048]{1,0:T(8,128)(2,1)S(1)} %get-tuple-element.56), channel_id=1, source_target_pairs={{0,10},{1,11},{2,8},{3,9},{4,14},{5,15},{6,12},{7,13},{8,2},{9,3},... | collective-permute-start | bytes 491528 | tf_op jit(solution)/shard_map/ppermute | solution.py:379
  15.0 8.6 %copy-start = (bf16[1,768,1024]{2,1,0:T(8,128)(2,1)S(1)}, bf16[1,768,1024]{2,1,0:T(8,128)(2,1)}, u32[]{:S(2)}) copy-start(bf16[1,768,1024]{2,1,0:T(8,128)(2,1)} %param.17) | copy-start | bytes 4718596
  15.6 15.6 %collective-permute-start.9 = (bf16[40,2048]{1,0:T(8,128)(2,1)S(1)}, bf16[40,2048]{1,0:T(8,128)(2,1)S(1)}, u32[]{:S(2)}, u32[]{:S(2)}) collective-permute-start(bf16[40,2048]{1,0:T(8,128)(2,1)S(1)} %get-tuple-element.75), channel_id=1, source_target_pairs={{0,8},{1,9},{2,10},{3,11},{4,12},{5,13},{6,14},{7,15},{8,0},{9,1},... | collective-permute-start | bytes 491528 | tf_op jit(solution)/shard_map/ppermute | solution.py:379
  16.2 17.5 %collective-permute-start.7 = (bf16[40,2048]{1,0:T(8,128)(2,1)S(1)}, bf16[40,2048]{1,0:T(8,128)(2,1)S(1)}, u32[]{:S(2)}, u32[]{:S(2)}) collective-permute-start(bf16[40,2048]{1,0:T(8,128)(2,1)S(1)} %get-tuple-element.65), channel_id=1, source_target_pairs={{0,11},{1,8},{2,9},{3,10},{4,15},{5,12},{6,13},{7,14},{8,3},{9,0},... | collective-permute-start | bytes 491528 | tf_op jit(solution)/shard_map/ppermute | solution.py:379
  18.5 15.2 %collective-permute-start.6 = (bf16[40,2048]{1,0:T(8,128)(2,1)S(1)}, bf16[40,2048]{1,0:T(8,128)(2,1)S(1)}, u32[]{:S(2)}, u32[]{:S(2)}) collective-permute-start(bf16[40,2048]{1,0:T(8,128)(2,1)S(1)} %get-tuple-element.63), channel_id=1, source_target_pairs={{0,9},{1,10},{2,11},{3,8},{4,13},{5,14},{6,15},{7,12},{8,1},{9,2},... | collective-permute-start | bytes 491528 | tf_op jit(solution)/shard_map/ppermute | solution.py:379
  23.6 10.1 %collective-permute-start.8 = (bf16[768,1024]{1,0:T(8,128)(2,1)S(1)}, bf16[768,1024]{1,0:T(8,128)(2,1)S(1)}, u32[]{:S(2)}, u32[]{:S(2)}) collective-permute-start(bf16[768,1024]{1,0:T(8,128)(2,1)S(1)} %bitcast.27), channel_id=1, source_target_pairs={{0,4},{4,0},{8,12},{12,8},{1,5},{5,1},{9,13},{13,9},{2,6},{6,2},{1... | collective-permute-start | bytes 4718600 | tf_op jit(solution)/shard_map/ppermute | solution.py:311
  24.2 7.0 %copy-start.1 = (f32[4096]{0:T(1024)S(1)}, f32[4096]{0:T(1024)}, u32[]{:S(2)}) copy-start(f32[4096]{0:T(1024)} %param.15) | copy-start | bytes 49156
  26.6 13.2 %collective-permute-start.5 = (bf16[40,2048]{1,0:T(8,128)(2,1)S(1)}, bf16[40,2048]{1,0:T(8,128)(2,1)S(1)}, u32[]{:S(2)}, u32[]{:S(2)}) collective-permute-start(bf16[40,2048]{1,0:T(8,128)(2,1)S(1)} %get-tuple-element.62), channel_id=1, source_target_pairs={{0,2},{1,3},{2,0},{3,1},{4,6},{5,7},{6,4},{7,5},{8,10},{9,11},{10,... | collective-permute-start | bytes 491528 | tf_op jit(solution)/shard_map/ppermute | solution.py:379
  33.1 9.7 %collective-permute-start.10 = (bf16[80,1664]{1,0:T(8,128)(2,1)S(1)}, bf16[80,1664]{1,0:T(8,128)(2,1)S(1)}, u32[]{:S(2)}, u32[]{:S(2)}) collective-permute-start(bf16[80,1664]{1,0:T(8,128)(2,1)S(1)} %products_b.3), channel_id=1, source_target_pairs={{0,8},{4,12},{8,0},{12,4},{1,9},{5,13},{9,1},{13,5},{2,10},{6,14},... | collective-permute-start | bytes 798728 | tf_op jit(solution)/shard_map/ppermute | solution.py:311
  35.6 14.1 %collective-permute-start.14 = (bf16[80,1664]{1,0:T(8,128)(2,1)S(1)}, bf16[80,1664]{1,0:T(8,128)(2,1)S(1)}, u32[]{:S(2)}, u32[]{:S(2)}) collective-permute-start(bf16[80,1664]{1,0:T(8,128)(2,1)S(1)} %products_b.2), channel_id=1, source_target_pairs={{0,8},{4,12},{8,0},{12,4},{1,9},{5,13},{9,1},{13,5},{2,10},{6,14},... | collective-permute-start | bytes 798728 | tf_op jit(solution)/shard_map/ppermute | solution.py:311
  37.1 8.6 %collective-permute-start.12 = (bf16[40,2048]{1,0:T(8,128)(2,1)S(1)}, bf16[40,2048]{1,0:T(8,128)(2,1)S(1)}, u32[]{:S(2)}, u32[]{:S(2)}) collective-permute-start(bf16[40,2048]{1,0:T(8,128)(2,1)S(1)} %get-tuple-element.80), channel_id=1, source_target_pairs={{0,1},{1,2},{2,3},{3,0},{4,5},{5,6},{6,7},{7,4},{8,9},{9,10},{10,1... | collective-permute-start | bytes 491528 | tf_op jit(solution)/shard_map/ppermute | solution.py:379
  39.8 8.1 %collective-permute-start.13 = (bf16[40,2048]{1,0:T(8,128)(2,1)S(1)}, bf16[40,2048]{1,0:T(8,128)(2,1)S(1)}, u32[]{:S(2)}, u32[]{:S(2)}) collective-permute-start(bf16[40,2048]{1,0:T(8,128)(2,1)S(1)} %get-tuple-element.84), channel_id=1, source_target_pairs={{0,3},{1,0},{2,1},{3,2},{4,7},{5,4},{6,5},{7,6},{8,11},{9,8},{10,9... | collective-permute-start | bytes 491528 | tf_op jit(solution)/shard_map/ppermute | solution.py:379
  44.2 6.9 %collective-permute-start.15 = (bf16[80,768]{1,0:T(8,128)(2,1)S(1)}, bf16[80,768]{1,0:T(8,128)(2,1)S(1)}, u32[]{:S(2)}, u32[]{:S(2)}) collective-permute-start(bf16[80,768]{1,0:T(8,128)(2,1)S(1)} %get-tuple-element.81), channel_id=1, source_target_pairs={{0,8},{4,12},{8,0},{12,4},{1,9},{5,13},{9,1},{13,5},{2,10},{6,14},... | collective-permute-start | bytes 368648 | tf_op jit(solution)/shard_map/ppermute | solution.py:311
  45.7 18.5 %collective-permute-start.11 = (bf16[40,2048]{1,0:T(8,128)(2,1)S(1)}, bf16[40,2048]{1,0:T(8,128)(2,1)S(1)}, u32[]{:S(2)}, u32[]{:S(2)}) collective-permute-start(bf16[40,2048]{1,0:T(8,128)(2,1)S(1)} %get-tuple-element.77), channel_id=1, source_target_pairs={{0,2},{1,3},{2,0},{3,1},{4,6},{5,7},{6,4},{7,5},{8,10},{9,11},{10,... | collective-permute-start | bytes 491528 | tf_op jit(solution)/shard_map/ppermute | solution.py:379
  51.1 15.3 %collective-permute-start.17 = (bf16[40,2048]{1,0:T(8,128)(2,1)S(1)}, bf16[40,2048]{1,0:T(8,128)(2,1)S(1)}, u32[]{:S(2)}, u32[]{:S(2)}) collective-permute-start(bf16[40,2048]{1,0:T(8,128)(2,1)S(1)} %get-tuple-element.91), channel_id=1, source_target_pairs={{0,1},{1,2},{2,3},{3,0},{4,5},{5,6},{6,7},{7,4},{8,9},{9,10},{10,1... | collective-permute-start | bytes 491528 | tf_op jit(solution)/shard_map/ppermute | solution.py:379
  52.7 15.7 %collective-permute-start.16 = (bf16[40,2048]{1,0:T(8,128)(2,1)S(1)}, bf16[40,2048]{1,0:T(8,128)(2,1)S(1)}, u32[]{:S(2)}, u32[]{:S(2)}) collective-permute-start(bf16[40,2048]{1,0:T(8,128)(2,1)S(1)} %get-tuple-element.89), channel_id=1, source_target_pairs={{0,3},{1,0},{2,1},{3,2},{4,7},{5,4},{6,5},{7,6},{8,11},{9,8},{10,9... | collective-permute-start | bytes 491528 | tf_op jit(solution)/shard_map/ppermute | solution.py:379
  55.6 12.8 %copy-start.4 = (f32[1,128,1]{1,2,0:T(1,128)S(1)}, f32[1,128,1]{1,2,0:T(1,128)}, u32[]{:S(2)}) copy-start(f32[1,128,1]{1,2,0:T(1,128)} %param.14) | copy-start | bytes 1540
  55.6 5.9 %collective-permute-start.20 = (bf16[80,768]{1,0:T(8,128)(2,1)S(1)}, bf16[80,768]{1,0:T(8,128)(2,1)S(1)}, u32[]{:S(2)}, u32[]{:S(2)}) collective-permute-start(bf16[80,768]{1,0:T(8,128)(2,1)S(1)} %get-tuple-element.95), channel_id=1, source_target_pairs={{0,8},{4,12},{8,0},{12,4},{1,9},{5,13},{9,1},{13,5},{2,10},{6,14},... | collective-permute-start | bytes 368648 | tf_op jit(solution)/shard_map/ppermute | solution.py:311
  58.4 14.2 %collective-permute-start.18 = (bf16[40,2048]{1,0:T(8,128)(2,1)S(1)}, bf16[40,2048]{1,0:T(8,128)(2,1)S(1)}, u32[]{:S(2)}, u32[]{:S(2)}) collective-permute-start(bf16[40,2048]{1,0:T(8,128)(2,1)S(1)} %get-tuple-element.93), channel_id=1, source_target_pairs={{0,10},{1,11},{2,8},{3,9},{4,14},{5,15},{6,12},{7,13},{8,2},{9,3},... | collective-permute-start | bytes 491528 | tf_op jit(solution)/shard_map/ppermute | solution.py:379
  61.5 13.7 %collective-permute-start.19 = (bf16[40,2048]{1,0:T(8,128)(2,1)S(1)}, bf16[40,2048]{1,0:T(8,128)(2,1)S(1)}, u32[]{:S(2)}, u32[]{:S(2)}) collective-permute-start(bf16[40,2048]{1,0:T(8,128)(2,1)S(1)} %get-tuple-element.94), channel_id=1, source_target_pairs={{0,8},{1,9},{2,10},{3,11},{4,12},{5,13},{6,14},{7,15},{8,0},{9,1},... | collective-permute-start | bytes 491528 | tf_op jit(solution)/shard_map/ppermute | solution.py:379
  64.3 10.9 %collective-permute-start.21 = (bf16[40,2048]{1,0:T(8,128)(2,1)S(1)}, bf16[40,2048]{1,0:T(8,128)(2,1)S(1)}, u32[]{:S(2)}, u32[]{:S(2)}) collective-permute-start(bf16[40,2048]{1,0:T(8,128)(2,1)S(1)} %get-tuple-element.96), channel_id=1, source_target_pairs={{0,11},{1,8},{2,9},{3,10},{4,15},{5,12},{6,13},{7,14},{8,3},{9,0},... | collective-permute-start | bytes 491528 | tf_op jit(solution)/shard_map/ppermute | solution.py:379
  66.4 8.7 %collective-permute-start.22 = (bf16[40,2048]{1,0:T(8,128)(2,1)S(1)}, bf16[40,2048]{1,0:T(8,128)(2,1)S(1)}, u32[]{:S(2)}, u32[]{:S(2)}) collective-permute-start(bf16[40,2048]{1,0:T(8,128)(2,1)S(1)} %get-tuple-element.97), channel_id=1, source_target_pairs={{0,9},{1,10},{2,11},{3,8},{4,13},{5,14},{6,15},{7,12},{8,1},{9,2},... | collective-permute-start | bytes 491528 | tf_op jit(solution)/shard_map/ppermute | solution.py:379

commit v10 on v9

--- a/solution.py
+++ b/solution.py
@@ -263,13 +263,13 @@
         )
         weight = jnp.sum(jnp.where(diagonal, weight_ref[...], 0.0), axis=1, keepdims=True)
         refs[1][...] = jnp.broadcast_to(weight, refs[1].shape)
-    rows = jnp.concatenate([r[...].astype(jnp.float32) for r in row_refs], axis=0)
-    rows = rows.astype(jnp.bfloat16)
     parts = 4 if last else 1
     step = half_width // parts
     for i in range(parts):
         columns = slice(i * step, (i + 1) * step)
-        mine = jnp.dot(back_ref[...], rows[:, columns], preferred_element_type=jnp.float32)
+        rows = jnp.concatenate([r[:, columns].astype(jnp.float32) for r in row_refs], axis=0)
+        rows = rows.astype(jnp.bfloat16)
+        mine = jnp.dot(back_ref[...], rows, preferred_element_type=jnp.float32)
         value = att_ref[:, columns].astype(jnp.float32) + mine * weight
         value = value.astype(jnp.bfloat16)
         if last:

time: 77 us -> 77 us (level)
  no operation moved by 1% of the time
where the time goes in v10:
time: 77 us; the launch traced here: 76.7 us
  starting transfers between devices  31.1 us (40%)
  waiting for transfers between devices  21.6 us (28%)
  Pallas kernels  20.4 us (26%)
  local copies, waits for them, and re-layouts  2.58 us (3%)
  other arithmetic  0.88 us (1%)
    ppermute x14, starting transfers between devices, send(): moved.append(block if still else lax.ppermute(block, ('ctx', 'exp'), pairs))  22.7 us
    pallas_call x13, Pallas kernels, call(): pl.pallas_call(kernel, in_specs=specs, out_specs=[pl.BlockSpec(memory_spa...  20.4 us
    ppermute x14, waiting for transfers between devices, send(): moved.append(block if still else lax.ppermute(block, ('ctx', 'exp'), pairs))  16.3 us
    ppermute x9, starting transfers between devices, swap(): return lax.ppermute(array, axis, [(i, i ^ bit) for i in range(size)])  8.43 us
    ppermute x9, waiting for transfers between devices, swap(): return lax.ppermute(array, axis, [(i, i ^ bit) for i in range(size)])  5.31 us
    unnamed x14, local copies, waits for them, and re-layouts  1.85 us
  transfers between devices with their start and end apart: 23, of which 8 were waited for; matrix products, arithmetic and copies ran while one was open for 2% of the time, Pallas kernels for 25%

profile of v10, /device:TPU:0, one launch (start us, length us, event | category | flops | bytes accessed | tf_op | source)
XLA Modules:
  0.0 76.7 jit_solution(17377986548937004588)
XLA Ops:
  0.9 3.0 %collective-permute-start.1 = (bf16[128,512]{1,0:T(8,128)(2,1)S(1)}, bf16[128,512]{1,0:T(8,128)(2,1)S(1)}, u32[]{:S(2)}, u32[]{:S(2)}) collective-permute-start(bf16[128,512]{1,0:T(8,128)(2,1)S(1)} %pad_maximum_fusion.refs_0_), channel_id=1, source_target_pairs={{0,8},{4,12},{8,0},{12,4},{1,9},{5,13},{9,1},{13,5},{2,10},{6,14},... | collective-permute-start | bytes 393224 | tf_op jit(solution)/shard_map/ppermute | solution.py:311
  6.1 1.3 %collective-permute-done.1.refs_2_ = bf16[128,512]{1,0:T(8,128)(2,1)S(1)} collective-permute-done((bf16[128,512]{1,0:T(8,128)(2,1)S(1)}, bf16[128,512]{1,0:T(8,128)(2,1)S(1)}, u32[]{:S(2)}, u32[]{:S(2)}) %collective-permute-start.1) | collective-permute-done | bytes 131104 | tf_op jit(solution)/shard_map/ppermute | solution.py:311
  7.4 1.3 %collective-permute-done.2.refs_3_ = bf16[128,512]{1,0:T(8,128)(2,1)S(1)} collective-permute-done((bf16[128,512]{1,0:T(8,128)(2,1)S(1)}, bf16[128,512]{1,0:T(8,128)(2,1)S(1)}, u32[]{:S(2)}, u32[]{:S(2)}) %collective-permute-start.2) | collective-permute-done | bytes 131104 | tf_op jit(solution)/shard_map/ppermute | solution.py:311
  8.9 2.3 %attend_b.1 = (bf16[128,2048]{1,0:T(8,128)(2,1)S(1)}, bf16[40,2048]{1,0:T(8,128)(2,1)S(1)}, bf16[40,2048]{1,0:T(8,128)(2,1)S(1)}, bf16[40,2048]{1,0:T(8,128)(2,1)S(1)}, bf16[40,2048]{1,0:T(8,128)(2,1)S(1)}) custom-call(s32[11]{0:T(128)S(1)} %concatenate.6.meta, bf16[128,4096]{1,0:T(8,128)(2,1)S(1)} %bitcast.36, ...), custom_call_target="tpu_custom_call" | custom-call | flops 2000000000 | bytes 1000 | tf_op jit(solution)/shard_map/attend_b/pallas_call | solution.py:21
  11.2 3.8 %collective-permute-start.3 = (bf16[40,2048]{1,0:T(8,128)(2,1)S(1)}, bf16[40,2048]{1,0:T(8,128)(2,1)S(1)}, u32[]{:S(2)}, u32[]{:S(2)}) collective-permute-start(bf16[40,2048]{1,0:T(8,128)(2,1)S(1)} %get-tuple-element.56), channel_id=1, source_target_pairs={{0,10},{1,11},{2,8},{3,9},{4,14},{5,15},{6,12},{7,13},{8,2},{9,3},... | collective-permute-start | bytes 491528 | tf_op jit(solution)/shard_map/ppermute | solution.py:379
  16.2 2.3 %collective-permute-start.7 = (bf16[40,2048]{1,0:T(8,128)(2,1)S(1)}, bf16[40,2048]{1,0:T(8,128)(2,1)S(1)}, u32[]{:S(2)}, u32[]{:S(2)}) collective-permute-start(bf16[40,2048]{1,0:T(8,128)(2,1)S(1)} %get-tuple-element.65), channel_id=1, source_target_pairs={{0,11},{1,8},{2,9},{3,10},{4,15},{5,12},{6,13},{7,14},{8,3},{9,0},... | collective-permute-start | bytes 491528 | tf_op jit(solution)/shard_map/ppermute | solution.py:379
  19.2 4.5 %collective-permute-done.3.refs_0_ = bf16[40,2048]{1,0:T(8,128)(2,1)S(1)} collective-permute-done((bf16[40,2048]{1,0:T(8,128)(2,1)S(1)}, bf16[40,2048]{1,0:T(8,128)(2,1)S(1)}, u32[]{:S(2)}, u32[]{:S(2)}) %collective-permute-start.3) | collective-permute-done | bytes 163872 | tf_op jit(solution)/shard_map/ppermute | solution.py:379
  24.2 2.3 %attend_a.1 = (bf16[128,2048]{1,0:T(8,128)(2,1)S(1)}, bf16[40,2048]{1,0:T(8,128)(2,1)S(1)}, bf16[40,2048]{1,0:T(8,128)(2,1)S(1)}, bf16[40,2048]{1,0:T(8,128)(2,1)S(1)}, bf16[40,2048]{1,0:T(8,128)(2,1)S(1)}) custom-call(s32[11]{0:T(128)S(1)} %concatenate.6.meta, bf16[128,4096]{1,0:T(8,128)(2,1)S(1)} %bitcast.37, ...), custom_call_target="tpu_custom_call" | custom-call | flops 2000000000 | bytes 1000 | tf_op jit(solution)/shard_map/attend_a/pallas_call | solution.py:21
  26.9 4.4 %collective-permute-done.9.refs_1_ = bf16[40,2048]{1,0:T(8,128)(2,1)S(1)} collective-permute-done((bf16[40,2048]{1,0:T(8,128)(2,1)S(1)}, bf16[40,2048]{1,0:T(8,128)(2,1)S(1)}, u32[]{:S(2)}, u32[]{:S(2)}) %collective-permute-start.9) | collective-permute-done | bytes 163872 | tf_op jit(solution)/shard_map/ppermute | solution.py:379
  31.3 1.8 %products_b.3 = bf16[80,1664]{1,0:T(8,128)(2,1)S(1)} custom-call(s32[11]{0:T(128)S(1)} %concatenate.6.meta, f32[1,4096]{1,0:T(1,128)S(1)} %bitcast.32, bf16[40,2048]{1,0:T(8,128)(2,1)S(1)} %collective-permute-done.3.refs_0_, bf16[40,2048]{1,0:T(8,128)(2,1)S(1)} %collective-permute-done.9.refs_1_, bf16[1024,1536]{1,0:T(8,128)(2,1)S(1)} %bitcast.19, ...), custom_call_target="tpu_custom_call" | custom-call | flops 20000000000 | bytes 1000 | tf_op jit(solution)/shard_map/products_b/pallas_call | solution.py:21
  33.7 1.8 %products_b.2 = bf16[80,1664]{1,0:T(8,128)(2,1)S(1)} custom-call(s32[11]{0:T(128)S(1)} %concatenate.6.meta, f32[1,4096]{1,0:T(1,128)S(1)} %bitcast.33, bf16[40,2048]{1,0:T(8,128)(2,1)S(1)} %collective-permute-done.6.refs_0_, bf16[40,2048]{1,0:T(8,128)(2,1)S(1)} %collective-permute-done.7.refs_1_, bf16[1024,1536]{1,0:T(8,128)(2,1)S(1)} %bitcast.20, ...), custom_call_target="tpu_custom_call" | custom-call | flops 20000000000 | bytes 1000 | tf_op jit(solution)/shard_map/products_b/pallas_call | solution.py:21
  35.6 1.5 %collective-permute-start.14 = (bf16[80,1664]{1,0:T(8,128)(2,1)S(1)}, bf16[80,1664]{1,0:T(8,128)(2,1)S(1)}, u32[]{:S(2)}, u32[]{:S(2)}) collective-permute-start(bf16[80,1664]{1,0:T(8,128)(2,1)S(1)} %products_b.2), channel_id=1, source_target_pairs={{0,8},{4,12},{8,0},{12,4},{1,9},{5,13},{9,1},{13,5},{2,10},{6,14},... | collective-permute-start | bytes 798728 | tf_op jit(solution)/shard_map/ppermute | solution.py:311
  37.1 2.7 %collective-permute-start.12 = (bf16[40,2048]{1,0:T(8,128)(2,1)S(1)}, bf16[40,2048]{1,0:T(8,128)(2,1)S(1)}, u32[]{:S(2)}, u32[]{:S(2)}) collective-permute-start(bf16[40,2048]{1,0:T(8,128)(2,1)S(1)} %get-tuple-element.80), channel_id=1, source_target_pairs={{0,1},{1,2},{2,3},{3,0},{4,5},{5,6},{6,7},{7,4},{8,9},{9,10},{10,1... | collective-permute-start | bytes 491528 | tf_op jit(solution)/shard_map/ppermute | solution.py:379
  39.8 1.1 %collective-permute-start.13 = (bf16[40,2048]{1,0:T(8,128)(2,1)S(1)}, bf16[40,2048]{1,0:T(8,128)(2,1)S(1)}, u32[]{:S(2)}, u32[]{:S(2)}) collective-permute-start(bf16[40,2048]{1,0:T(8,128)(2,1)S(1)} %get-tuple-element.84), channel_id=1, source_target_pairs={{0,3},{1,0},{2,1},{3,2},{4,7},{5,4},{6,5},{7,6},{8,11},{9,8},{10,9... | collective-permute-start | bytes 491528 | tf_op jit(solution)/shard_map/ppermute | solution.py:379
  40.9 1.8 %products_a.2 = (f32[80,1536]{1,0:T(8,128)S(1)}, f32[80,128]{1,0:T(8,128)S(1)}) custom-call(s32[11]{0:T(128)S(1)} %concatenate.6.meta, f32[1,4096]{1,0:T(1,128)S(1)} %bitcast.34, bf16[40,2048]{1,0:T(8,128)(2,1)S(1)} %collective-permute-done.5.refs_0_, bf16[40,2048]{1,0:T(8,128)(2,1)S(1)} %get-tuple-element.71.refs_1_, bf16[1024,1536]{1,0:T(8,128)(2,1)S(1)} %bitcast.21, ...), custom_call_target="tpu_custom_call" | custom-call | flops 1000 | bytes 1000 | tf_op jit(solution)/shard_map/products_a/pallas_call | solution.py:21
  42.8 1.4 %hidden_down_a.2 = (bf16[80,768]{1,0:T(8,128)(2,1)S(1)}, bf16[40,2048]{1,0:T(8,128)(2,1)S(1)}, bf16[40,2048]{1,0:T(8,128)(2,1)S(1)}) custom-call(s32[11]{0:T(128)S(1)} %concatenate.6.meta, f32[80,1536]{1,0:T(8,128)S(1)} %get-tuple-element.72.sums_ref, f32[80,128]{1,0:T(8,128)S(1)} %get-tuple-element.73.squares_ref, ...), custom_call_target="tpu_custom_call" | custom-call | flops 1000 | bytes 1000 | tf_op jit(solution)/shard_map/hidden_down_a/pallas_call | solution.py:21
  44.2 1.5 %collective-permute-start.15 = (bf16[80,768]{1,0:T(8,128)(2,1)S(1)}, bf16[80,768]{1,0:T(8,128)(2,1)S(1)}, u32[]{:S(2)}, u32[]{:S(2)}) collective-permute-start(bf16[80,768]{1,0:T(8,128)(2,1)S(1)} %get-tuple-element.81), channel_id=1, source_target_pairs={{0,8},{4,12},{8,0},{12,4},{1,9},{5,13},{9,1},{13,5},{2,10},{6,14},... | collective-permute-start | bytes 368648 | tf_op jit(solution)/shard_map/ppermute | solution.py:311
  46.3 1.6 %collective-permute-done.13.refs_1_ = bf16[40,2048]{1,0:T(8,128)(2,1)S(1)} collective-permute-done((bf16[40,2048]{1,0:T(8,128)(2,1)S(1)}, bf16[40,2048]{1,0:T(8,128)(2,1)S(1)}, u32[]{:S(2)}, u32[]{:S(2)}) %collective-permute-start.13) | collective-permute-done | bytes 163872 | tf_op jit(solution)/shard_map/ppermute | solution.py:379
  47.9 1.8 %products_a.3 = (f32[80,1536]{1,0:T(8,128)S(1)}, f32[80,128]{1,0:T(8,128)S(1)}) custom-call(s32[11]{0:T(128)S(1)} %concatenate.6.meta, f32[1,4096]{1,0:T(1,128)S(1)} %bitcast.35, bf16[40,2048]{1,0:T(8,128)(2,1)S(1)} %collective-permute-done.12.refs_0_, bf16[40,2048]{1,0:T(8,128)(2,1)S(1)} %collective-permute-done.13.refs_1_, ...), custom_call_target="tpu_custom_call" | custom-call | flops 1000 | bytes 1000 | tf_op jit(solution)/shard_map/products_a/pallas_call | solution.py:21
  49.7 1.4 %hidden_down_a.3 = (bf16[80,768]{1,0:T(8,128)(2,1)S(1)}, bf16[40,2048]{1,0:T(8,128)(2,1)S(1)}, bf16[40,2048]{1,0:T(8,128)(2,1)S(1)}) custom-call(s32[11]{0:T(128)S(1)} %concatenate.6.meta, f32[80,1536]{1,0:T(8,128)S(1)} %get-tuple-element.86.sums_ref, f32[80,128]{1,0:T(8,128)S(1)} %get-tuple-element.87.squares_ref, ...), custom_call_target="tpu_custom_call" | custom-call | flops 1000 | bytes 1000 | tf_op jit(solution)/shard_map/hidden_down_a/pallas_call | solution.py:21
  51.1 1.6 %collective-permute-start.17 = (bf16[40,2048]{1,0:T(8,128)(2,1)S(1)}, bf16[40,2048]{1,0:T(8,128)(2,1)S(1)}, u32[]{:S(2)}, u32[]{:S(2)}) collective-permute-start(bf16[40,2048]{1,0:T(8,128)(2,1)S(1)} %get-tuple-element.91), channel_id=1, source_target_pairs={{0,1},{1,2},{2,3},{3,0},{4,5},{5,6},{6,7},{7,4},{8,9},{9,10},{10,1... | collective-permute-start | bytes 491528 | tf_op jit(solution)/shard_map/ppermute | solution.py:379
  52.7 2.9 %collective-permute-start.16 = (bf16[40,2048]{1,0:T(8,128)(2,1)S(1)}, bf16[40,2048]{1,0:T(8,128)(2,1)S(1)}, u32[]{:S(2)}, u32[]{:S(2)}) collective-permute-start(bf16[40,2048]{1,0:T(8,128)(2,1)S(1)} %get-tuple-element.89), channel_id=1, source_target_pairs={{0,3},{1,0},{2,1},{3,2},{4,7},{5,4},{6,5},{7,6},{8,11},{9,8},{10,9... | collective-permute-start | bytes 491528 | tf_op jit(solution)/shard_map/ppermute | solution.py:379
  55.6 1.6 %collective-permute-start.20 = (bf16[80,768]{1,0:T(8,128)(2,1)S(1)}, bf16[80,768]{1,0:T(8,128)(2,1)S(1)}, u32[]{:S(2)}, u32[]{:S(2)}) collective-permute-start(bf16[80,768]{1,0:T(8,128)(2,1)S(1)} %get-tuple-element.95), channel_id=1, source_target_pairs={{0,8},{4,12},{8,0},{12,4},{1,9},{5,13},{9,1},{13,5},{2,10},{6,14},... | collective-permute-start | bytes 368648 | tf_op jit(solution)/shard_map/ppermute | solution.py:311
  57.2 1.2 %down_b.2 = (bf16[40,2048]{1,0:T(8,128)(2,1)S(1)}, bf16[40,2048]{1,0:T(8,128)(2,1)S(1)}) custom-call(s32[11]{0:T(128)S(1)} %concatenate.6.meta, bf16[80,768]{1,0:T(8,128)(2,1)S(1)} %collective-permute-done.15.hidden_ref, bf16[768,1024]{1,0:T(8,128)(2,1)S(1)} %bitcast.30, bf16[768,1024]{1,0:T(8,128)(2,1)S(1)} %collective-permute-done.8.refs_2_.refs_1_), custom_call_target="tpu_custom_call" | custom-call | flops 1000 | bytes 1000 | tf_op jit(solution)/shard_map/down_b/pallas_call | solution.py:21
  58.9 2.6 %collective-permute-done.20.hidden_ref = bf16[80,768]{1,0:T(8,128)(2,1)S(1)} collective-permute-done((bf16[80,768]{1,0:T(8,128)(2,1)S(1)}, bf16[80,768]{1,0:T(8,128)(2,1)S(1)}, u32[]{:S(2)}, u32[]{:S(2)}) %collective-permute-start.20) | collective-permute-done | bytes 122912 | tf_op jit(solution)/shard_map/ppermute | solution.py:311
  61.5 1.5 %collective-permute-start.19 = (bf16[40,2048]{1,0:T(8,128)(2,1)S(1)}, bf16[40,2048]{1,0:T(8,128)(2,1)S(1)}, u32[]{:S(2)}, u32[]{:S(2)}) collective-permute-start(bf16[40,2048]{1,0:T(8,128)(2,1)S(1)} %get-tuple-element.94), channel_id=1, source_target_pairs={{0,8},{1,9},{2,10},{3,11},{4,12},{5,13},{6,14},{7,15},{8,0},{9,1},... | collective-permute-start | bytes 491528 | tf_op jit(solution)/shard_map/ppermute | solution.py:379
  63.0 1.2 %down_b.3 = (bf16[40,2048]{1,0:T(8,128)(2,1)S(1)}, bf16[40,2048]{1,0:T(8,128)(2,1)S(1)}) custom-call(s32[11]{0:T(128)S(1)} %concatenate.6.meta, bf16[80,768]{1,0:T(8,128)(2,1)S(1)} %collective-permute-done.20.hidden_ref, bf16[768,1024]{1,0:T(8,128)(2,1)S(1)} %bitcast.31, bf16[768,1024]{1,0:T(8,128)(2,1)S(1)} %collective-permute-done.8.refs_2_.refs_1_), custom_call_target="tpu_custom_call" | custom-call | flops 1000 | bytes 1000 | tf_op jit(solution)/shard_map/down_b/pallas_call | solution.py:21
  64.3 2.1 %collective-permute-start.21 = (bf16[40,2048]{1,0:T(8,128)(2,1)S(1)}, bf16[40,2048]{1,0:T(8,128)(2,1)S(1)}, u32[]{:S(2)}, u32[]{:S(2)}) collective-permute-start(bf16[40,2048]{1,0:T(8,128)(2,1)S(1)} %get-tuple-element.96), channel_id=1, source_target_pairs={{0,11},{1,8},{2,9},{3,10},{4,15},{5,12},{6,13},{7,14},{8,3},{9,0},... | collective-permute-start | bytes 491528 | tf_op jit(solution)/shard_map/ppermute | solution.py:379
  66.4 2.0 %collective-permute-start.22 = (bf16[40,2048]{1,0:T(8,128)(2,1)S(1)}, bf16[40,2048]{1,0:T(8,128)(2,1)S(1)}, u32[]{:S(2)}, u32[]{:S(2)}) collective-permute-start(bf16[40,2048]{1,0:T(8,128)(2,1)S(1)} %get-tuple-element.97), channel_id=1, source_target_pairs={{0,9},{1,10},{2,11},{3,8},{4,13},{5,14},{6,15},{7,12},{8,1},{9,2},... | collective-permute-start | bytes 491528 | tf_op jit(solution)/shard_map/ppermute | solution.py:379
  69.3 3.3 %collective-permute-done.18.refs_0_ = bf16[40,2048]{1,0:T(8,128)(2,1)S(1)} collective-permute-done((bf16[40,2048]{1,0:T(8,128)(2,1)S(1)}, bf16[40,2048]{1,0:T(8,128)(2,1)S(1)}, u32[]{:S(2)}, u32[]{:S(2)}) %collective-permute-start.18) | collective-permute-done | bytes 163872 | tf_op jit(solution)/shard_map/ppermute | solution.py:379
  72.6 2.6 %collective-permute-done.19.refs_1_ = bf16[40,2048]{1,0:T(8,128)(2,1)S(1)} collective-permute-done((bf16[40,2048]{1,0:T(8,128)(2,1)S(1)}, bf16[40,2048]{1,0:T(8,128)(2,1)S(1)}, u32[]{:S(2)}, u32[]{:S(2)}) %collective-permute-start.19) | collective-permute-done | bytes 163872 | tf_op jit(solution)/shard_map/ppermute | solution.py:379
  75.2 1.6 %combine_b.1 = bf16[128,4096]{1,0:T(8,128)(2,1)} custom-call(s32[11]{0:T(128)S(1)} %concatenate.6.meta, bf16[128,2048]{1,0:T(8,128)(2,1)S(1)} %get-tuple-element.54.att_ref, bf16[128,160]{1,0:T(8,128)(2,1)S(1)} %get-tuple-element.55.back_ref, f32[128,128]{1,0:T(8,128)S(1)} %get-tuple-element.92.weight_ref, ...), custom_call_target="tpu_custom_call" | custom-call | flops 20000000000 | bytes 1000 | tf_op jit(solution)/shard_map/combine_b/pallas_call | solution.py:21
  (43 shorter events, 8.5 us)
Async XLA Ops:
  0.9 6.5 %collective-permute-start.1 = (bf16[128,512]{1,0:T(8,128)(2,1)S(1)}, bf16[128,512]{1,0:T(8,128)(2,1)S(1)}, u32[]{:S(2)}, u32[]{:S(2)}) collective-permute-start(bf16[128,512]{1,0:T(8,128)(2,1)S(1)} %pad_maximum_fusion.refs_0_), channel_id=1, source_target_pairs={{0,8},{4,12},{8,0},{12,4},{1,9},{5,13},{9,1},{13,5},{2,10},{6,14},... | collective-permute-start | bytes 393224 | tf_op jit(solution)/shard_map/ppermute | solution.py:311
  3.9 3.5 %collective-permute-start = (bf16[128,512]{1,0:T(8,128)(2,1)S(1)}, bf16[128,512]{1,0:T(8,128)(2,1)S(1)}, u32[]{:S(2)}, u32[]{:S(2)}) collective-permute-start(bf16[128,512]{1,0:T(8,128)(2,1)S(1)} %pad_maximum_fusion.refs_0_), channel_id=1, source_target_pairs={{0,4},{4,0},{8,12},{12,8},{1,5},{5,1},{9,13},{13,9},{2,6},{6,2},{1... | collective-permute-start | bytes 393224 | tf_op jit(solution)/shard_map/ppermute | solution.py:311
  4.6 0.7 copy-start.3
  5.3 3.5 %copy-start.5 = (bf16[1,1024,2,768]{3,2,1,0:T(2,128)(2,1)S(1)}, bf16[1,1024,2,768]{3,2,1,0:T(2,128)(2,1)}, u32[]{:S(2)}) copy-start(bf16[1,1024,2,768]{3,2,1,0:T(2,128)(2,1)} %param.16) | copy-start | bytes 9437188
  5.3 3.6 %copy-start.2 = (bf16[1,128,4096]{2,1,0:T(8,128)(2,1)S(1)}, bf16[1,128,4096]{2,1,0:T(8,128)(2,1)}, u32[]{:S(2)}) copy-start(bf16[1,128,4096]{2,1,0:T(8,128)(2,1)} %param.9) | copy-start | bytes 3145732
  7.4 1.3 %collective-permute-start.2 = (bf16[128,512]{1,0:T(8,128)(2,1)S(1)}, bf16[128,512]{1,0:T(8,128)(2,1)S(1)}, u32[]{:S(2)}, u32[]{:S(2)}) collective-permute-start(bf16[128,512]{1,0:T(8,128)(2,1)S(1)} %collective-permute-done.1.refs_2_), channel_id=1, source_target_pairs={{0,4},{4,0},{8,12},{12,8},{1,5},{5,1},{9,13},{13,9},{2,6},{6,2},{1... | collective-permute-start | bytes 393224 | tf_op jit(solution)/shard_map/ppermute | solution.py:311
  8.7 14.9 %collective-permute-start.4 = (bf16[1024,2,768]{2,1,0:T(2,128)(2,1)S(1)}, bf16[1024,2,768]{2,1,0:T(2,128)(2,1)S(1)}, u32[]{:S(2)}, u32[]{:S(2)}) collective-permute-start(bf16[1024,2,768]{2,1,0:T(2,128)(2,1)S(1)} %bitcast.40), channel_id=1, source_target_pairs={{0,4},{4,0},{8,12},{12,8},{1,5},{5,1},{9,13},{13,9},{2,6},{6,2},{1... | collective-permute-start | bytes 9437192 | tf_op jit(solution)/shard_map/ppermute | solution.py:311
  11.2 12.4 %collective-permute-start.3 = (bf16[40,2048]{1,0:T(8,128)(2,1)S(1)}, bf16[40,2048]{1,0:T(8,128)(2,1)S(1)}, u32[]{:S(2)}, u32[]{:S(2)}) collective-permute-start(bf16[40,2048]{1,0:T(8,128)(2,1)S(1)} %get-tuple-element.56), channel_id=1, source_target_pairs={{0,10},{1,11},{2,8},{3,9},{4,14},{5,15},{6,12},{7,13},{8,2},{9,3},... | collective-permute-start | bytes 491528 | tf_op jit(solution)/shard_map/ppermute | solution.py:379
  15.0 8.6 %copy-start = (bf16[1,768,1024]{2,1,0:T(8,128)(2,1)S(1)}, bf16[1,768,1024]{2,1,0:T(8,128)(2,1)}, u32[]{:S(2)}) copy-start(bf16[1,768,1024]{2,1,0:T(8,128)(2,1)} %param.17) | copy-start | bytes 4718596
  15.6 15.6 %collective-permute-start.9 = (bf16[40,2048]{1,0:T(8,128)(2,1)S(1)}, bf16[40,2048]{1,0:T(8,128)(2,1)S(1)}, u32[]{:S(2)}, u32[]{:S(2)}) collective-permute-start(bf16[40,2048]{1,0:T(8,128)(2,1)S(1)} %get-tuple-element.75), channel_id=1, source_target_pairs={{0,8},{1,9},{2,10},{3,11},{4,12},{5,13},{6,14},{7,15},{8,0},{9,1},... | collective-permute-start | bytes 491528 | tf_op jit(solution)/shard_map/ppermute | solution.py:379
  16.2 17.5 %collective-permute-start.7 = (bf16[40,2048]{1,0:T(8,128)(2,1)S(1)}, bf16[40,2048]{1,0:T(8,128)(2,1)S(1)}, u32[]{:S(2)}, u32[]{:S(2)}) collective-permute-start(bf16[40,2048]{1,0:T(8,128)(2,1)S(1)} %get-tuple-element.65), channel_id=1, source_target_pairs={{0,11},{1,8},{2,9},{3,10},{4,15},{5,12},{6,13},{7,14},{8,3},{9,0},... | collective-permute-start | bytes 491528 | tf_op jit(solution)/shard_map/ppermute | solution.py:379
  18.5 15.2 %collective-permute-start.6 = (bf16[40,2048]{1,0:T(8,128)(2,1)S(1)}, bf16[40,2048]{1,0:T(8,128)(2,1)S(1)}, u32[]{:S(2)}, u32[]{:S(2)}) collective-permute-start(bf16[40,2048]{1,0:T(8,128)(2,1)S(1)} %get-tuple-element.63), channel_id=1, source_target_pairs={{0,9},{1,10},{2,11},{3,8},{4,13},{5,14},{6,15},{7,12},{8,1},{9,2},... | collective-permute-start | bytes 491528 | tf_op jit(solution)/shard_map/ppermute | solution.py:379
  23.6 10.1 %collective-permute-start.8 = (bf16[768,1024]{1,0:T(8,128)(2,1)S(1)}, bf16[768,1024]{1,0:T(8,128)(2,1)S(1)}, u32[]{:S(2)}, u32[]{:S(2)}) collective-permute-start(bf16[768,1024]{1,0:T(8,128)(2,1)S(1)} %bitcast.27), channel_id=1, source_target_pairs={{0,4},{4,0},{8,12},{12,8},{1,5},{5,1},{9,13},{13,9},{2,6},{6,2},{1... | collective-permute-start | bytes 4718600 | tf_op jit(solution)/shard_map/ppermute | solution.py:311
  24.2 7.0 %copy-start.1 = (f32[4096]{0:T(1024)S(1)}, f32[4096]{0:T(1024)}, u32[]{:S(2)}) copy-start(f32[4096]{0:T(1024)} %param.15) | copy-start | bytes 49156
  26.6 13.2 %collective-permute-start.5 = (bf16[40,2048]{1,0:T(8,128)(2,1)S(1)}, bf16[40,2048]{1,0:T(8,128)(2,1)S(1)}, u32[]{:S(2)}, u32[]{:S(2)}) collective-permute-start(bf16[40,2048]{1,0:T(8,128)(2,1)S(1)} %get-tuple-element.62), channel_id=1, source_target_pairs={{0,2},{1,3},{2,0},{3,1},{4,6},{5,7},{6,4},{7,5},{8,10},{9,11},{10,... | collective-permute-start | bytes 491528 | tf_op jit(solution)/shard_map/ppermute | solution.py:379
  33.1 9.7 %collective-permute-start.10 = (bf16[80,1664]{1,0:T(8,128)(2,1)S(1)}, bf16[80,1664]{1,0:T(8,128)(2,1)S(1)}, u32[]{:S(2)}, u32[]{:S(2)}) collective-permute-start(bf16[80,1664]{1,0:T(8,128)(2,1)S(1)} %products_b.3), channel_id=1, source_target_pairs={{0,8},{4,12},{8,0},{12,4},{1,9},{5,13},{9,1},{13,5},{2,10},{6,14},... | collective-permute-start | bytes 798728 | tf_op jit(solution)/shard_map/ppermute | solution.py:311
  35.6 14.1 %collective-permute-start.14 = (bf16[80,1664]{1,0:T(8,128)(2,1)S(1)}, bf16[80,1664]{1,0:T(8,128)(2,1)S(1)}, u32[]{:S(2)}, u32[]{:S(2)}) collective-permute-start(bf16[80,1664]{1,0:T(8,128)(2,1)S(1)} %products_b.2), channel_id=1, source_target_pairs={{0,8},{4,12},{8,0},{12,4},{1,9},{5,13},{9,1},{13,5},{2,10},{6,14},... | collective-permute-start | bytes 798728 | tf_op jit(solution)/shard_map/ppermute | solution.py:311
  37.1 8.6 %collective-permute-start.12 = (bf16[40,2048]{1,0:T(8,128)(2,1)S(1)}, bf16[40,2048]{1,0:T(8,128)(2,1)S(1)}, u32[]{:S(2)}, u32[]{:S(2)}) collective-permute-start(bf16[40,2048]{1,0:T(8,128)(2,1)S(1)} %get-tuple-element.80), channel_id=1, source_target_pairs={{0,1},{1,2},{2,3},{3,0},{4,5},{5,6},{6,7},{7,4},{8,9},{9,10},{10,1... | collective-permute-start | bytes 491528 | tf_op jit(solution)/shard_map/ppermute | solution.py:379
  39.8 8.1 %collective-permute-start.13 = (bf16[40,2048]{1,0:T(8,128)(2,1)S(1)}, bf16[40,2048]{1,0:T(8,128)(2,1)S(1)}, u32[]{:S(2)}, u32[]{:S(2)}) collective-permute-start(bf16[40,2048]{1,0:T(8,128)(2,1)S(1)} %get-tuple-element.84), channel_id=1, source_target_pairs={{0,3},{1,0},{2,1},{3,2},{4,7},{5,4},{6,5},{7,6},{8,11},{9,8},{10,9... | collective-permute-start | bytes 491528 | tf_op jit(solution)/shard_map/ppermute | solution.py:379
  44.2 6.9 %collective-permute-start.15 = (bf16[80,768]{1,0:T(8,128)(2,1)S(1)}, bf16[80,768]{1,0:T(8,128)(2,1)S(1)}, u32[]{:S(2)}, u32[]{:S(2)}) collective-permute-start(bf16[80,768]{1,0:T(8,128)(2,1)S(1)} %get-tuple-element.81), channel_id=1, source_target_pairs={{0,8},{4,12},{8,0},{12,4},{1,9},{5,13},{9,1},{13,5},{2,10},{6,14},... | collective-permute-start | bytes 368648 | tf_op jit(solution)/shard_map/ppermute | solution.py:311
  45.7 18.5 %collective-permute-start.11 = (bf16[40,2048]{1,0:T(8,128)(2,1)S(1)}, bf16[40,2048]{1,0:T(8,128)(2,1)S(1)}, u32[]{:S(2)}, u32[]{:S(2)}) collective-permute-start(bf16[40,2048]{1,0:T(8,128)(2,1)S(1)} %get-tuple-element.77), channel_id=1, source_target_pairs={{0,2},{1,3},{2,0},{3,1},{4,6},{5,7},{6,4},{7,5},{8,10},{9,11},{10,... | collective-permute-start | bytes 491528 | tf_op jit(solution)/shard_map/ppermute | solution.py:379
  51.1 15.3 %collective-permute-start.17 = (bf16[40,2048]{1,0:T(8,128)(2,1)S(1)}, bf16[40,2048]{1,0:T(8,128)(2,1)S(1)}, u32[]{:S(2)}, u32[]{:S(2)}) collective-permute-start(bf16[40,2048]{1,0:T(8,128)(2,1)S(1)} %get-tuple-element.91), channel_id=1, source_target_pairs={{0,1},{1,2},{2,3},{3,0},{4,5},{5,6},{6,7},{7,4},{8,9},{9,10},{10,1... | collective-permute-start | bytes 491528 | tf_op jit(solution)/shard_map/ppermute | solution.py:379
  52.7 15.7 %collective-permute-start.16 = (bf16[40,2048]{1,0:T(8,128)(2,1)S(1)}, bf16[40,2048]{1,0:T(8,128)(2,1)S(1)}, u32[]{:S(2)}, u32[]{:S(2)}) collective-permute-start(bf16[40,2048]{1,0:T(8,128)(2,1)S(1)} %get-tuple-element.89), channel_id=1, source_target_pairs={{0,3},{1,0},{2,1},{3,2},{4,7},{5,4},{6,5},{7,6},{8,11},{9,8},{10,9... | collective-permute-start | bytes 491528 | tf_op jit(solution)/shard_map/ppermute | solution.py:379
  55.6 12.8 %copy-start.4 = (f32[1,128,1]{1,2,0:T(1,128)S(1)}, f32[1,128,1]{1,2,0:T(1,128)}, u32[]{:S(2)}) copy-start(f32[1,128,1]{1,2,0:T(1,128)} %param.14) | copy-start | bytes 1540
  55.6 5.9 %collective-permute-start.20 = (bf16[80,768]{1,0:T(8,128)(2,1)S(1)}, bf16[80,768]{1,0:T(8,128)(2,1)S(1)}, u32[]{:S(2)}, u32[]{:S(2)}) collective-permute-start(bf16[80,768]{1,0:T(8,128)(2,1)S(1)} %get-tuple-element.95), channel_id=1, source_target_pairs={{0,8},{4,12},{8,0},{12,4},{1,9},{5,13},{9,1},{13,5},{2,10},{6,14},... | collective-permute-start | bytes 368648 | tf_op jit(solution)/shard_map/ppermute | solution.py:311
  58.4 14.2 %collective-permute-start.18 = (bf16[40,2048]{1,0:T(8,128)(2,1)S(1)}, bf16[40,2048]{1,0:T(8,128)(2,1)S(1)}, u32[]{:S(2)}, u32[]{:S(2)}) collective-permute-start(bf16[40,2048]{1,0:T(8,128)(2,1)S(1)} %get-tuple-element.93), channel_id=1, source_target_pairs={{0,10},{1,11},{2,8},{3,9},{4,14},{5,15},{6,12},{7,13},{8,2},{9,3},... | collective-permute-start | bytes 491528 | tf_op jit(solution)/shard_map/ppermute | solution.py:379
  61.5 13.7 %collective-permute-start.19 = (bf16[40,2048]{1,0:T(8,128)(2,1)S(1)}, bf16[40,2048]{1,0:T(8,128)(2,1)S(1)}, u32[]{:S(2)}, u32[]{:S(2)}) collective-permute-start(bf16[40,2048]{1,0:T(8,128)(2,1)S(1)} %get-tuple-element.94), channel_id=1, source_target_pairs={{0,8},{1,9},{2,10},{3,11},{4,12},{5,13},{6,14},{7,15},{8,0},{9,1},... | collective-permute-start | bytes 491528 | tf_op jit(solution)/shard_map/ppermute | solution.py:379
  64.3 10.9 %collective-permute-start.21 = (bf16[40,2048]{1,0:T(8,128)(2,1)S(1)}, bf16[40,2048]{1,0:T(8,128)(2,1)S(1)}, u32[]{:S(2)}, u32[]{:S(2)}) collective-permute-start(bf16[40,2048]{1,0:T(8,128)(2,1)S(1)} %get-tuple-element.96), channel_id=1, source_target_pairs={{0,11},{1,8},{2,9},{3,10},{4,15},{5,12},{6,13},{7,14},{8,3},{9,0},... | collective-permute-start | bytes 491528 | tf_op jit(solution)/shard_map/ppermute | solution.py:379
  66.4 8.7 %collective-permute-start.22 = (bf16[40,2048]{1,0:T(8,128)(2,1)S(1)}, bf16[40,2048]{1,0:T(8,128)(2,1)S(1)}, u32[]{:S(2)}, u32[]{:S(2)}) collective-permute-start(bf16[40,2048]{1,0:T(8,128)(2,1)S(1)} %get-tuple-element.97), channel_id=1, source_target_pairs={{0,9},{1,10},{2,11},{3,8},{4,13},{5,14},{6,15},{7,12},{8,1},{9,2},... | collective-permute-start | bytes 491528 | tf_op jit(solution)/shard_map/ppermute | solution.py:379
